TPU v7x, 32 devices: a whole 2x2x4 slice. The times are simulated.
32 devices in a mesh: sx: 4 (over z), sy: 8 (over y, x, core).
Axes of the slice: x: 2, y: 2, z: 4, core: 2. Of those that a mesh axis runs over, the one named last changes fastest.
Arguments:
- fine_matrix: bfloat16 [8, 16, 2, 7, 64, 64], P('sx', 'sy'), may hold values from -0.75 to 0.75
- prolongator: bfloat16 [8, 16, 2, 7, 64, 64], P('sx', 'sy'), may hold values from -2.5 to 2.5
- aggregate: int32 [8, 16, 2], P('sx', 'sy'), may hold values from 0 to 31, as said below
- face_links: int32 [8, 16, 2, 6], P('sx', 'sy'), may hold values from 0 to 1, as said below
Outputs:
- coarse: bfloat16 [4, 8, 7, 7, 64, 64], P('sx', 'sy')
Inputs may be any that keep to these rules, and one draw needn't show every extreme that they name: aggregate[i] is the id bx 8 + by of a box of 2 x 2 x 2 elements: the box that holds element i, or the box beside it across a box face on which element i lies (faces along x or y). face_links[i, f] is the same on both sides of a face, and 0 on the outer faces of the grid.
All inputs are finite; a program needn't handle non-finite values.
Results may differ from a plain program's by a relative error of at most 0.007.
Values may be sent and summed in bfloat16 or wider, within the bound.
No kernel may reach another device: no remote copies, remote signals or barrier semaphores. Data moves between devices by JAX's collectives and lax.ppermute only.
A program may use at most 320 MiB of HBM per device.

v0:
```python
import jax
import jax.numpy as jnp
from jax import lax
from jax.sharding import PartitionSpec as P


def extended_2(cells, sides, width):
    for axis, dim in sides:
        count = lax.axis_size(axis)
        ends = count - 1
        head = lax.slice_in_dim(cells, 0, width, axis=dim)
        tail = lax.slice_in_dim(cells, cells.shape[dim] - width, cells.shape[dim], axis=dim)
        cells = jnp.concatenate(
            [
                lax.ppermute(tail, axis, [(i, (i + 1) % count) for i in range(ends)]),
                cells,
                lax.ppermute(head, axis, [((i + 1) % count, i) for i in range(ends)]),
            ],
            axis=dim,
        )
    return cells


def from_behind(value, axis, by):
    size = lax.axis_size(axis)
    pairs = [(i, i + by) for i in range(size) if 0 <= i + by < size]
    return lax.ppermute(value, axis, pairs)


def neighbour_views(extended):
    padded = jnp.pad(extended, [(0, 0), (0, 0), (1, 1)] + [(0, 0)] * (extended.ndim - 3))
    return [
        padded[1:-1, 1:-1, 1:3],
        padded[:-2, 1:-1, 1:3],
        padded[2:, 1:-1, 1:3],
        padded[1:-1, :-2, 1:3],
        padded[1:-1, 2:, 1:3],
        padded[1:-1, 1:-1, 0:2],
        padded[1:-1, 1:-1, 2:4],
    ]


def slot_ids(aggregate_ext, face_links, first_x, first_y, boxes_y):
    neighbours = jnp.stack(neighbour_views(aggregate_ext), axis=-1)
    count_x, count_y = (face_links.shape[0], face_links.shape[1])
    box_x = ((first_x + jnp.arange(count_x, dtype=jnp.int32)) // 2)[:, None, None, None]
    box_y = ((first_y + jnp.arange(count_y, dtype=jnp.int32)) // 2)[None, :, None, None]
    target_x = neighbours // boxes_y
    target_y = neighbours % boxes_y
    within = (target_x - box_x + 1) * 3 + (target_y - box_y + 1)
    present = jnp.concatenate([jnp.ones_like(face_links[..., :1]), face_links], axis=-1) == 1
    return jnp.where(present, within, -1)


def combine_rows(slot_table, blocks):
    selector = (slot_table[..., None] == jnp.arange(9, dtype=jnp.int32)).astype(blocks.dtype)
    combined = jnp.einsum(
        "xyzmt,xyzmpq->xyztpq", selector, blocks, preferred_element_type=jnp.float32
    )
    return combined.astype(jnp.bfloat16)


def box_step(direction, parity_x, parity_y):
    shift_x = 0
    shift_y = 0
    if direction == 1 and parity_x == 0:
        shift_x = -1
    if direction == 2 and parity_x == 1:
        shift_x = 1
    if direction == 3 and parity_y == 0:
        shift_y = -1
    if direction == 4 and parity_y == 1:
        shift_y = 1
    return (shift_x, shift_y)


def image_blocks(fine_matrix, face_links, box_ext):
    views = neighbour_views(box_ext)
    count_x, count_y = (fine_matrix.shape[0], fine_matrix.shape[1])
    half_x, half_y = (count_x // 2, count_y // 2)
    width, coarse_width = (fine_matrix.shape[-1], box_ext.shape[-1])
    total = jnp.zeros((half_x, 2, half_y, 2, 2, 5, 5, width, coarse_width), jnp.float32)
    for direction in range(7):
        product = jnp.einsum(
            "xyzpq,xyztqr->xyztpr",
            fine_matrix[:, :, :, direction],
            views[direction],
            preferred_element_type=jnp.float32,
        )
        if direction > 0:
            product = product * face_links[:, :, :, direction - 1, None, None, None].astype(
                jnp.float32
            )
        product = product.reshape(half_x, 2, half_y, 2, 2, 3, 3, width, coarse_width)
        for parity_x in range(2):
            for parity_y in range(2):
                shift_x, shift_y = box_step(direction, parity_x, parity_y)
                total = total.at[
                    :,
                    parity_x,
                    :,
                    parity_y,
                    :,
                    1 + shift_x : 4 + shift_x,
                    1 + shift_y : 4 + shift_y,
                ].add(product[:, parity_x, :, parity_y])
    return total.astype(jnp.bfloat16).reshape(half_x, 2, half_y, 2, 2, 25, width, coarse_width)


def place_blocks(contrib):
    half_x, half_y = (contrib.shape[0], contrib.shape[1])
    coarse_width = contrib.shape[-1]
    buffer = jnp.zeros((half_x + 2, half_y + 2, 7, 7, coarse_width, coarse_width), jnp.float32)
    for offset_x in range(3):
        for offset_y in range(3):
            piece = contrib[:, :, 3 * offset_x + offset_y].reshape(
                half_x, half_y, 5, 5, coarse_width, coarse_width
            )
            buffer = buffer.at[
                offset_x : offset_x + half_x,
                offset_y : offset_y + half_y,
                2 - offset_x : 7 - offset_x,
                2 - offset_y : 7 - offset_y,
            ].add(piece)
    return buffer


def per_device(fine_matrix, prolongator, aggregate, face_links):
    count_x, count_y = (aggregate.shape[0], aggregate.shape[1])
    half_x, half_y = (count_x // 2, count_y // 2)
    width, coarse_width = (fine_matrix.shape[-1], prolongator.shape[-1])
    first_x = lax.axis_index("sx") * count_x
    first_y = lax.axis_index("sy") * count_y
    boxes_y = count_y * lax.axis_size("sy") // 2
    aggregate_ext = extended_2(aggregate, (("sx", 0), ("sy", 1)), 1)
    slot_table = slot_ids(aggregate_ext, face_links, first_x, first_y, boxes_y)
    ghost_blocks = extended_2(prolongator, (("sx", 0), ("sy", 1)), 1)
    ghost_table = extended_2(slot_table, (("sx", 0), ("sy", 1)), 1)
    box_ext = combine_rows(ghost_table, ghost_blocks)
    box_own = box_ext[1:-1, 1:-1]
    image = image_blocks(fine_matrix, face_links, box_ext)
    left = box_own.reshape(half_x, 2, half_y, 2, 2, 9, width, coarse_width)
    contrib = jnp.einsum(
        "abcderkp,abcdeskq->acrspq", left, image, preferred_element_type=jnp.float32
    )
    buffer = place_blocks(contrib)
    lower_y = buffer[:, 0]
    upper_y = buffer[:, half_y + 1]
    from_right = from_behind(lower_y, "sy", -1)
    from_left = from_behind(upper_y, "sy", 1)
    inner = buffer[:, 1 : half_y + 1]
    inner = inner.at[:, half_y - 1].add(from_right)
    inner = inner.at[:, 0].add(from_left)
    lower_x = inner[0]
    upper_x = inner[half_x + 1]
    from_above = from_behind(lower_x.astype(jnp.bfloat16), "sx", -1).astype(lower_x.dtype)
    from_below = from_behind(upper_x.astype(jnp.bfloat16), "sx", 1).astype(upper_x.dtype)
    owned = inner[1 : half_x + 1]
    owned = owned.at[half_x - 1].add(from_above)
    owned = owned.at[0].add(from_below)
    return owned.astype(jnp.bfloat16)


def solution(mesh):
    return jax.shard_map(
        per_device,
        mesh=mesh,
        in_specs=(
            P("sx", "sy", None, None, None, None),
            P("sx", "sy", None, None, None, None),
            P("sx", "sy", None),
            P("sx", "sy", None, None),
        ),
        out_specs=P("sx", "sy", None, None, None, None),
        check_vma=False,
    )
```

profile of v0, /device:TPU:20, one launch (start us, length us, event | category | flops | bytes accessed | tf_op | source)
XLA Modules:
  0.0 252.3 jit_solution(5392627108378936249)
XLA Ops:
  0.0 0.9 copy.123
  0.9 2.3 collective-permute-start.1
  3.3 3.5 %collective-permute-start = (s32[1,2,2]{0,2,1:T(2,128)S(1)}, s32[1,2,2]{0,2,1:T(2,128)S(1)}, u32[]{:S(2)}, u32[]{:S(2)}) collective-permute-start(s32[1,2,2]{0,2,1:T(2,128)S(1)} %get-tuple-element.543), channel_id=1, source_target_pairs={{0,8},{8,16},{16,24},{1,9},{9,17},{17,25},{2,10},{10,18},{18,26},{... | collective-permute-start | bytes 56 | tf_op jit(solution)/shard_map/ppermute | solution.py:15
  6.8 1.2 fusion.81
  8.3 1.9 collective-permute-start.8
  10.6 3.9 %collective-permute-start.9 = (bf16[1,2,2,7,64,64]{5,3,4,2,1,0:T(8,128)(2,1)S(1)}, bf16[1,2,2,7,64,64]{5,3,4,2,1,0:T(8,128)(2,1)S(1)}, u32[]{:S(2)}, u32[]{:S(2)}) collective-permute-start(bf16[1,2,2,7,64,64]{5,3,4,2,1,0:T(8,128)(2,1)S(1)} %copy.219), channel_id=1, source_target_pairs={{8,0},{16,8},{24,16},{9,1},{17,9},{25,17},{10,2},{18,10},{26,18},{... | collective-permute-start | bytes 688136 | tf_op jit(solution)/shard_map/ppermute | solution.py:17
  14.5 0.8 copy.132
  15.6 0.7 fusion.74
  16.5 1.9 collective-permute-start.3
  18.4 2.4 collective-permute-start.2
  20.9 3.4 %collective-permute-done.2 = s32[4,1,2]{0,2,1:T(2,128)S(1)} collective-permute-done((s32[4,1,2]{0,2,1:T(2,128)S(1)}, s32[4,1,2]{0,2,1:T(2,128)S(1)}, u32[]{:S(2)}, u32[]{:S(2)}) %collective-permute-start.2) | collective-permute-done | bytes 64 | tf_op jit(solution)/shard_map/ppermute | solution.py:15
  25.0 0.8 compare_select_fusion
  25.8 2.0 collective-permute-start.4
  27.8 3.9 %collective-permute-start.5 = (s32[1,2,2,7]{3,2,1,0:T(2,128)S(1)}, s32[1,2,2,7]{3,2,1,0:T(2,128)S(1)}, u32[]{:S(2)}, u32[]{:S(2)}) collective-permute-start(s32[1,2,2,7]{3,2,1,0:T(2,128)S(1)} %get-tuple-element.535), channel_id=1, source_target_pairs={{8,0},{16,8},{24,16},{9,1},{17,9},{25,17},{10,2},{18,10},{26,18},{... | collective-permute-start | bytes 344 | tf_op jit(solution)/shard_map/ppermute | solution.py:17
  33.2 1.9 collective-permute-start.11
  35.1 2.4 collective-permute-start.10
  37.6 2.1 collective-permute-start.6
  39.7 4.3 %collective-permute-start.7 = (s32[4,1,2,7]{3,2,1,0:T(2,128)S(1)}, s32[4,1,2,7]{3,2,1,0:T(2,128)S(1)}, u32[]{:S(2)}, u32[]{:S(2)}) collective-permute-start(s32[4,1,2,7]{3,2,1,0:T(2,128)S(1)} %get-tuple-element.531), channel_id=1, source_target_pairs={{1,0},{2,1},{3,2},{4,3},{5,4},{6,5},{7,6},{9,8},{10,9},{11,10},{12... | collective-permute-start | bytes 680 | tf_op jit(solution)/shard_map/ppermute | solution.py:17
  44.2 12.7 %collective-permute-done.6 = s32[4,1,2,7]{3,2,1,0:T(2,128)S(1)} collective-permute-done((s32[4,1,2,7]{3,2,1,0:T(2,128)S(1)}, s32[4,1,2,7]{3,2,1,0:T(2,128)S(1)}, u32[]{:S(2)}, u32[]{:S(2)}) %collective-permute-start.6) | collective-permute-done | bytes 256 | tf_op jit(solution)/shard_map/ppermute | solution.py:15
  58.2 5.5 %convolution_convert_fusion = bf16[4,4,2,9,64,64]{5,3,4,2,1,0:T(8,128)(2,1)S(1)} fusion(bf16[4,1,2,7,64,64]{5,3,4,2,1,0:T(8,128)(2,1)S(1)} %copy.145, bf16[4,2,2,7,64,64]{5,3,4,2,1,0:T(8,128)(2,1)S(1)} %constant_dynamic-update-slice_fusion.1, bf16[4,1,2,7,64,64]{5,3,4,2,1,0:T(8,128)(2,1)S(1)} %copy.144, s32[4,4,2,7]{3,2,1,0:T(2,128)S(1)} %pad_add_fusion), kind=kOutput, calls=%fused_computation.3 | convolution fusion | flops 23201760 | bytes 4195200 | tf_op jit(solution)/shard_map/xyzmt,xyzmpq->xyztpq/dot_general | solution.py:57
  63.7 5.7 %slice_bitcast_fusion.4 = (bf16[2,2,2,9,64,64,1]{5,3,4,2,1,0,6:T(8,128)(2,1)}, bf16[2,2,2,9,64,64]{5,3,4,2,1,0:T(8,128)(2,1)S(1)}, bf16[2,2,2,9,64,64]{5,3,4,2,1...) fusion(bf16[4,4,2,9,64,64]{5,3,4,2,1,0:T(8,128)(2,1)S(1)} %conv, ...), kind=kLoop, calls=%fused_computation.165 | loop fusion | bytes 23592960 | tf_op jit(solution)/shard_map/slice | solution.py:33
  69.4 1.4 fusion.17
  70.9 0.8 scatter-add.124
  79.7 0.8 convert_element_type.117
  80.5 0.7 copy.160
  81.3 0.8 copy-done.8
  82.1 2.8 %fusion.9 = f32[25,64,9,64,1,1,1]{3,1,6,5,0,2,4:T(8,128)S(1)} fusion(bf16[2,2,2,25,64,64,1]{4,5,2,1,3,6,0:T(8,128)(2,1)S(1)} %bitcast.182, bf16[2,2,2,9,64,64,1]{5,3,4,2,1,0,6:T(8,128)(2,1)S(1)} %copy-done.8), kind=kOutput, calls=%fused_computation.23 | convolution fusion | flops 943718400 | bytes 5914624 | tf_op jit(solution)/shard_map/abcderkp,abcdeskq->acrspq/dot_general | solution.py:143
  84.9 1.4 copy.220
  86.3 2.4 fusion.79
  88.7 2.3 copy.170
  91.0 2.4 copy.169
  93.4 2.3 copy.168
  95.7 2.3 copy.167
  98.0 2.3 copy.166
  100.4 1.2 copy.165
  102.4 1.8 scatter-add.170
  107.0 5.3 %slice_bitcast_fusion.1 = (f32[3,7,7,64,64]{4,3,2,1,0:T(8,128)}, f32[3,7,7,64,64]{4,3,2,1,0:T(8,128)}) fusion(f32[3,3,7,7,64,64]{5,4,3,2,0,1:T(8,128)S(1)} %fusion.19), kind=kLoop, calls=%fused_computation.5 | loop fusion | bytes 9633792 | tf_op jit(solution)/shard_map/squeeze | solution.py:147
  112.3 3.5 %copy-done = f32[3,3,7,7,64,64]{5,4,3,2,0,1:T(8,128)} copy-done((f32[3,3,7,7,64,64]{5,4,3,2,0,1:T(8,128)}, f32[3,3,7,7,64,64]{5,4,3,2,0,1:T(8,128)S(1)}, u32[]{:S(2)}) %copy-start) | copy-done | bytes 7225368
  115.8 1.9 collective-permute-start.12
  117.7 2.4 collective-permute-start.13
  120.1 99.3 %collective-permute-done.12 = f32[3,7,7,64,64]{4,3,2,1,0:T(8,128)S(1)} collective-permute-done((f32[3,7,7,64,64]{4,3,2,1,0:T(8,128)}, f32[3,7,7,64,64]{4,3,2,1,0:T(8,128)S(1)}, u32[]{:S(2)}, u32[]{:S(2)}) %collective-permute-start.12) | collective-permute-done | bytes 2408480 | tf_op jit(solution)/shard_map/ppermute | solution.py:27
  219.4 1.0 collective-permute-done.13
  220.4 6.2 %fusion.77 = (bf16[3,1,7,7,64,64]{5,4,3,2,1,0:T(8,128)(2,1)S(1)}, f32[3,1,7,7,64,64]{5,4,3,2,1,0:T(8,128)S(1)}) fusion(f32[3,7,7,64,64]{4,3,2,1,0:T(8,128)} %collective-permute-done.13, f32[3,7,7,64,64]{4,3,2,1,0:T(8,128)S(1)} %collective-permute-done.12, f32[3,3,7,7,64,64]{5,4,3,2,0,1:T(8,128)} %copy-done), kind=kLoop, calls=%fused_computation.166 | loop fusion | flops 1806336 | bytes 10838016 | tf_op jit(solution)/shard_map/convert.3
  226.7 2.4 collective-permute-start.14
  229.1 3.5 %collective-permute-start.15 = (bf16[1,7,7,64,64]{4,3,2,1,0:T(8,128)(2,1)S(1)}, bf16[1,7,7,64,64]{4,3,2,1,0:T(8,128)(2,1)S(1)}, u32[]{:S(2)}, u32[]{:S(2)}) collective-permute-start(bf16[1,7,7,64,64]{4,3,2,1,0:T(8,128)(2,1)S(1)} %get-tuple-element.525), channel_id=1, source_target_pairs={{0,8},{8,16},{16,24},{1,9},{9,17},{17,25},{2,10},{10,18},{18,26},{... | collective-permute-start | bytes 1204232 | tf_op jit(solution)/shard_map/ppermute | solution.py:27
  232.6 15.7 %collective-permute-done.14 = bf16[1,7,7,64,64]{4,3,2,1,0:T(8,128)(2,1)S(1)} collective-permute-done((bf16[1,7,7,64,64]{4,3,2,1,0:T(8,128)(2,1)S(1)}, bf16[1,7,7,64,64]{4,3,2,1,0:T(8,128)(2,1)S(1)}, u32[]{:S(2)}, u32[]{:S(2)}) %collective-permute-start.14) | collective-permute-done | bytes 401440 | tf_op jit(solution)/shard_map/ppermute | solution.py:27
  248.3 2.7 %collective-permute-done.15 = bf16[1,7,7,64,64]{4,3,2,1,0:T(8,128)(2,1)S(1)} collective-permute-done((bf16[1,7,7,64,64]{4,3,2,1,0:T(8,128)(2,1)S(1)}, bf16[1,7,7,64,64]{4,3,2,1,0:T(8,128)(2,1)S(1)}, u32[]{:S(2)}, u32[]{:S(2)}) %collective-permute-start.15) | collective-permute-done | bytes 401440 | tf_op jit(solution)/shard_map/ppermute | solution.py:27
  251.0 1.3 fusion.8
  (107 shorter events, 16.3 us)
Async XLA Ops:
  0.0 31.7 %copy-start.1 = (bf16[2,2,2,7,64,64]{5,4,3,2,1,0:T(8,128)(2,1)S(1)}, bf16[2,2,2,7,64,64]{5,4,3,2,1,0:T(8,128)(2,1)}, u32[]{:S(2)}) copy-start(bf16[2,2,2,7,64,64]{5,4,3,2,1,0:T(8,128)(2,1)} %param.87) | copy-start | bytes 1376260
  0.9 14.4 %collective-permute-start.1 = (s32[1,2,2]{0,2,1:T(2,128)S(1)}, s32[1,2,2]{0,2,1:T(2,128)S(1)}, u32[]{:S(2)}, u32[]{:S(2)}) collective-permute-start(s32[1,2,2]{0,2,1:T(2,128)S(1)} %get-tuple-element.542), channel_id=1, source_target_pairs={{8,0},{16,8},{24,16},{9,1},{17,9},{25,17},{10,2},{18,10},{26,18},{... | collective-permute-start | bytes 56 | tf_op jit(solution)/shard_map/ppermute | solution.py:17
  3.3 12.0 %collective-permute-start = (s32[1,2,2]{0,2,1:T(2,128)S(1)}, s32[1,2,2]{0,2,1:T(2,128)S(1)}, u32[]{:S(2)}, u32[]{:S(2)}) collective-permute-start(s32[1,2,2]{0,2,1:T(2,128)S(1)} %get-tuple-element.543), channel_id=1, source_target_pairs={{0,8},{8,16},{16,24},{1,9},{9,17},{17,25},{2,10},{10,18},{18,26},{... | collective-permute-start | bytes 56 | tf_op jit(solution)/shard_map/ppermute | solution.py:15
  8.3 23.4 %collective-permute-start.8 = (bf16[1,2,2,7,64,64]{5,3,4,2,1,0:T(8,128)(2,1)S(1)}, bf16[1,2,2,7,64,64]{5,3,4,2,1,0:T(8,128)(2,1)S(1)}, u32[]{:S(2)}, u32[]{:S(2)}) collective-permute-start(bf16[1,2,2,7,64,64]{5,3,4,2,1,0:T(8,128)(2,1)S(1)} %copy.218), channel_id=1, source_target_pairs={{0,8},{8,16},{16,24},{1,9},{9,17},{17,25},{2,10},{10,18},{18,26},{... | collective-permute-start | bytes 688136 | tf_op jit(solution)/shard_map/ppermute | solution.py:15
  10.6 21.9 %collective-permute-start.9 = (bf16[1,2,2,7,64,64]{5,3,4,2,1,0:T(8,128)(2,1)S(1)}, bf16[1,2,2,7,64,64]{5,3,4,2,1,0:T(8,128)(2,1)S(1)}, u32[]{:S(2)}, u32[]{:S(2)}) collective-permute-start(bf16[1,2,2,7,64,64]{5,3,4,2,1,0:T(8,128)(2,1)S(1)} %copy.219), channel_id=1, source_target_pairs={{8,0},{16,8},{24,16},{9,1},{17,9},{25,17},{10,2},{18,10},{26,18},{... | collective-permute-start | bytes 688136 | tf_op jit(solution)/shard_map/ppermute | solution.py:17
  16.5 4.3 %collective-permute-start.3 = (s32[4,1,2]{0,2,1:T(2,128)S(1)}, s32[4,1,2]{0,2,1:T(2,128)S(1)}, u32[]{:S(2)}, u32[]{:S(2)}) collective-permute-start(s32[4,1,2]{0,2,1:T(2,128)S(1)} %get-tuple-element.538), channel_id=1, source_target_pairs={{1,0},{2,1},{3,2},{4,3},{5,4},{6,5},{7,6},{9,8},{10,9},{11,10},{12... | collective-permute-start | bytes 104 | tf_op jit(solution)/shard_map/ppermute | solution.py:17
  18.4 5.8 %collective-permute-start.2 = (s32[4,1,2]{0,2,1:T(2,128)S(1)}, s32[4,1,2]{0,2,1:T(2,128)S(1)}, u32[]{:S(2)}, u32[]{:S(2)}) collective-permute-start(s32[4,1,2]{0,2,1:T(2,128)S(1)} %get-tuple-element.539), channel_id=1, source_target_pairs={{0,1},{1,2},{2,3},{3,4},{4,5},{5,6},{6,7},{8,9},{9,10},{10,11},{11... | collective-permute-start | bytes 104 | tf_op jit(solution)/shard_map/ppermute | solution.py:15
  25.8 11.7 %collective-permute-start.4 = (s32[1,2,2,7]{3,2,1,0:T(2,128)S(1)}, s32[1,2,2,7]{3,2,1,0:T(2,128)S(1)}, u32[]{:S(2)}, u32[]{:S(2)}) collective-permute-start(s32[1,2,2,7]{3,2,1,0:T(2,128)S(1)} %get-tuple-element.534), channel_id=1, source_target_pairs={{0,8},{8,16},{16,24},{1,9},{9,17},{17,25},{2,10},{10,18},{18,26},{... | collective-permute-start | bytes 344 | tf_op jit(solution)/shard_map/ppermute | solution.py:15
  27.8 9.7 %collective-permute-start.5 = (s32[1,2,2,7]{3,2,1,0:T(2,128)S(1)}, s32[1,2,2,7]{3,2,1,0:T(2,128)S(1)}, u32[]{:S(2)}, u32[]{:S(2)}) collective-permute-start(s32[1,2,2,7]{3,2,1,0:T(2,128)S(1)} %get-tuple-element.535), channel_id=1, source_target_pairs={{8,0},{16,8},{24,16},{9,1},{17,9},{25,17},{10,2},{18,10},{26,18},{... | collective-permute-start | bytes 344 | tf_op jit(solution)/shard_map/ppermute | solution.py:17
  32.4 11.6 %copy-start.10 = (s32[2,2,2,6]{3,2,1,0:T(2,128)S(1)}, s32[2,2,2,6]{3,2,1,0:T(2,128)}, u32[]{:S(2)}) copy-start(s32[2,2,2,6]{3,2,1,0:T(2,128)} %param.89) | copy-start | bytes 580
  33.2 23.7 %collective-permute-start.11 = (bf16[4,1,2,7,64,64]{5,4,3,2,1,0:T(8,128)(2,1)S(1)}, bf16[4,1,2,7,64,64]{5,4,3,2,1,0:T(8,128)(2,1)S(1)}, u32[]{:S(2)}, u32[]{:S(2)}) collective-permute-start(bf16[4,1,2,7,64,64]{5,4,3,2,1,0:T(8,128)(2,1)S(1)} %copy.143), channel_id=1, source_target_pairs={{1,0},{2,1},{3,2},{4,3},{5,4},{6,5},{7,6},{9,8},{10,9},{11,10},{12... | collective-permute-start | bytes 1376264 | tf_op jit(solution)/shard_map/ppermute | solution.py:17
  35.1 22.5 %collective-permute-start.10 = (bf16[4,1,2,7,64,64]{5,4,3,2,1,0:T(8,128)(2,1)S(1)}, bf16[4,1,2,7,64,64]{5,4,3,2,1,0:T(8,128)(2,1)S(1)}, u32[]{:S(2)}, u32[]{:S(2)}) collective-permute-start(bf16[4,1,2,7,64,64]{5,4,3,2,1,0:T(8,128)(2,1)S(1)} %copy.142), channel_id=1, source_target_pairs={{0,1},{1,2},{2,3},{3,4},{4,5},{5,6},{6,7},{8,9},{9,10},{10,11},{11... | collective-permute-start | bytes 1376264 | tf_op jit(solution)/shard_map/ppermute | solution.py:15
  37.6 19.3 %collective-permute-start.6 = (s32[4,1,2,7]{3,2,1,0:T(2,128)S(1)}, s32[4,1,2,7]{3,2,1,0:T(2,128)S(1)}, u32[]{:S(2)}, u32[]{:S(2)}) collective-permute-start(s32[4,1,2,7]{3,2,1,0:T(2,128)S(1)} %get-tuple-element.530), channel_id=1, source_target_pairs={{0,1},{1,2},{2,3},{3,4},{4,5},{5,6},{6,7},{8,9},{9,10},{10,11},{11... | collective-permute-start | bytes 680 | tf_op jit(solution)/shard_map/ppermute | solution.py:15
  39.7 17.2 %collective-permute-start.7 = (s32[4,1,2,7]{3,2,1,0:T(2,128)S(1)}, s32[4,1,2,7]{3,2,1,0:T(2,128)S(1)}, u32[]{:S(2)}, u32[]{:S(2)}) collective-permute-start(s32[4,1,2,7]{3,2,1,0:T(2,128)S(1)} %get-tuple-element.531), channel_id=1, source_target_pairs={{1,0},{2,1},{3,2},{4,3},{5,4},{6,5},{7,6},{9,8},{10,9},{11,10},{12... | collective-permute-start | bytes 680 | tf_op jit(solution)/shard_map/ppermute | solution.py:17
  70.9 1.2 copy-start.9
  80.5 1.6 copy-start.8
  102.4 2.2 copy-start.7
  104.3 1.2 copy-start.6
  104.3 1.4 copy-start.5
  104.4 1.6 copy-start.4
  104.7 1.6 copy-start.3
  105.4 1.3 copy-start.2
  107.0 8.8 %copy-start = (f32[3,3,7,7,64,64]{5,4,3,2,0,1:T(8,128)}, f32[3,3,7,7,64,64]{5,4,3,2,0,1:T(8,128)S(1)}, u32[]{:S(2)}) copy-start(f32[3,3,7,7,64,64]{5,4,3,2,0,1:T(8,128)S(1)} %fusion.19) | copy-start | bytes 21676036
  115.8 103.6 %collective-permute-start.12 = (f32[3,7,7,64,64]{4,3,2,1,0:T(8,128)}, f32[3,7,7,64,64]{4,3,2,1,0:T(8,128)S(1)}, u32[]{:S(2)}, u32[]{:S(2)}) collective-permute-start(f32[3,7,7,64,64]{4,3,2,1,0:T(8,128)} %get-tuple-element.505), channel_id=1, source_target_pairs={{1,0},{2,1},{3,2},{4,3},{5,4},{6,5},{7,6},{9,8},{10,9},{11,10},{12... | collective-permute-start | bytes 7225352 | tf_op jit(solution)/shard_map/ppermute | solution.py:27
  117.7 102.7 %collective-permute-start.13 = (f32[3,7,7,64,64]{4,3,2,1,0:T(8,128)}, f32[3,7,7,64,64]{4,3,2,1,0:T(8,128)}, u32[]{:S(2)}, u32[]{:S(2)}) collective-permute-start(f32[3,7,7,64,64]{4,3,2,1,0:T(8,128)} %get-tuple-element.506), channel_id=1, source_target_pairs={{0,1},{1,2},{2,3},{3,4},{4,5},{5,6},{6,7},{8,9},{9,10},{10,11},{11... | collective-permute-start | bytes 7225352 | tf_op jit(solution)/shard_map/ppermute | solution.py:27
  226.7 21.6 %collective-permute-start.14 = (bf16[1,7,7,64,64]{4,3,2,1,0:T(8,128)(2,1)S(1)}, bf16[1,7,7,64,64]{4,3,2,1,0:T(8,128)(2,1)S(1)}, u32[]{:S(2)}, u32[]{:S(2)}) collective-permute-start(bf16[1,7,7,64,64]{4,3,2,1,0:T(8,128)(2,1)S(1)} %get-tuple-element.524), channel_id=1, source_target_pairs={{8,0},{16,8},{24,16},{9,1},{17,9},{25,17},{10,2},{18,10},{26,18},{... | collective-permute-start | bytes 1204232 | tf_op jit(solution)/shard_map/ppermute | solution.py:27
  229.1 21.9 %collective-permute-start.15 = (bf16[1,7,7,64,64]{4,3,2,1,0:T(8,128)(2,1)S(1)}, bf16[1,7,7,64,64]{4,3,2,1,0:T(8,128)(2,1)S(1)}, u32[]{:S(2)}, u32[]{:S(2)}) collective-permute-start(bf16[1,7,7,64,64]{4,3,2,1,0:T(8,128)(2,1)S(1)} %get-tuple-element.525), channel_id=1, source_target_pairs={{0,8},{8,16},{16,24},{1,9},{9,17},{17,25},{2,10},{10,18},{18,26},{... | collective-permute-start | bytes 1204232 | tf_op jit(solution)/shard_map/ppermute | solution.py:27
where the time goes:
time: 254 us; the launch traced here: 252 us
  waiting for transfers between devices  135 us (53%)
  local copies, waits for them, and re-layouts  44.5 us (18%)
  starting transfers between devices  42.8 us (17%)
  other arithmetic  16 us (6%)
  matrix products  13.4 us (5%)
    ppermute x4, waiting for transfers between devices, from_behind(): return lax.ppermute(value, axis, pairs)  119 us
    ppermute x6, starting transfers between devices, extended_2(): lax.ppermute(head, axis, [((i + 1) % count, i) for i in range(ends)])  18.3 us
    ppermute x6, waiting for transfers between devices, extended_2(): lax.ppermute(tail, axis, [(i, (i + 1) % count) for i in range(ends)])  16 us
    ppermute x6, starting transfers between devices, extended_2(): lax.ppermute(tail, axis, [(i, (i + 1) % count) for i in range(ends)])  14.3 us
    another operation x7, local copies, waits for them, and re-layouts  13.1 us
    ppermute x4, starting transfers between devices, from_behind(): return lax.ppermute(value, axis, pairs)  10.2 us
    unnamed x27, local copies, waits for them, and re-layouts  7.34 us
    another operation x1, other arithmetic  6.2 us
  transfers between devices with their start and end apart: 16, of which 6 were waited for; matrix products, arithmetic and copies ran while one was open for 3% of the time, Pallas kernels for 0%

commit v1 on v0

v1 whole, which is shorter than its diff:
```python
import functools

import jax
import jax.numpy as jnp
from jax import lax
from jax.experimental import pallas as pl
from jax.experimental.pallas import tpu as pltpu
from jax.sharding import PartitionSpec as P

B = 64
PAIR = 2 * B
BLOCK_ROWS = 7 * B
BODY = 2 * BLOCK_ROWS
VMEM_LIMIT = 48 * 1024 * 1024

FACES = [(0, 0), (-1, 0), (1, 0), (0, -1), (0, 1), (0, 0), (0, 0)]
COLUMNS = [(0, 0), (0, 1), (1, 0), (1, 1)]


def targets(px, py):
    table = []
    for dx, dy in FACES:
        ox, nx = divmod(px + dx, 2)
        oy, ny = divmod(py + dy, 2)
        table.append([(ox, oy), (ox + 2 * nx - 1, oy), (ox, oy + 2 * ny - 1)])
    return table


def box_set(px, py):
    return sorted({t for row in targets(px, py) for t in row})


def around(px, py):
    found = [((0, 0), (0, 0), (px, py))]
    for m in (2, 1) if px == 0 else (1, 2):
        ox, nx = divmod(px + FACES[m][0], 2)
        found.append(((m, m), (ox, 0), (nx, py)))
    for m in (4, 3) if py == 0 else (3, 4):
        oy, ny = divmod(py + FACES[m][1], 2)
        found.append(((m, m), (0, oy), (px, ny)))
    found.append(((6, 5), (0, 0), (px, py)))
    return found


def image_set(px, py):
    found = set()
    for _, (ox, oy), column in around(px, py):
        found |= {(ox + tx, oy + ty) for tx, ty in box_set(*column)}
    return sorted(found)


IMAGE = sorted({s for column in COLUMNS for s in image_set(*column)})
IMAGE_PAIRS = (len(IMAGE) + 1) // 2
STAR = [(0, 1), (0, -1), (0, 0), (1, 0), (-1, 0)]


def corner_of(tx, ty):
    return ((tx + 1) // 2, (ty + 1) // 2)


def blocks_of(tx, ty):
    return IMAGE if (tx, ty) in STAR else image_set(*corner_of(tx, ty))


def relay_list(ty):
    return [(tx, s) for tx in (0, -1, 1) for s in blocks_of(tx, ty)]


def coarse_list(tx):
    found = {(sx - tx, sy) for sx, sy in blocks_of(tx, 0)}
    for ty in (-1, 1):
        found |= {(sx - tx, sy - ty) for sx, sy in blocks_of(tx, ty)}
    return sorted(found)


def own_list():
    found = set(IMAGE)
    for ty in (-1, 1):
        found |= {(sx, sy - ty) for sx, sy in IMAGE}
    return sorted(found)


def low_half(shape):
    return lax.broadcasted_iota(jnp.int32, shape, len(shape) - 1) < B


def swap_halves(value):
    return pltpu.roll(value, B, value.ndim - 1)


def pair_lanes(left, right):
    return jnp.concatenate([left, right], axis=-1)


def state_of(aggregate_ref, px, py, z, own, boxes_y):
    shift = aggregate_ref[px, py, z] - own
    across_x = (shift == boxes_y) | (shift == -boxes_y)
    return jnp.where(shift == 0, 0, jnp.where(across_x, 1, 2)).astype(jnp.float32)


def fill_rows(rows, values):
    shape = (rows, PAIR)
    row = lax.broadcasted_iota(jnp.int32, shape, 0)
    half = low_half(shape)
    filled = jnp.zeros(shape, jnp.float32)
    for index, (low, high) in enumerate(values):
        filled = jnp.where(row == index, jnp.where(half, low, high), filled)
    return filled


def pack_kernel(boxes_y, place_ref, aggregate_ref, links_ref, p_ref, rows_ref, meta_ref, first_ref, second_ref):
    x = place_ref[0]
    own = x * boxes_y + place_ref[1]
    states = [
        tuple(state_of(aggregate_ref, px, py, z, own, boxes_y) for z in (0, 1)) for px, py in COLUMNS
    ]

    def link(px, py, face):
        return tuple(links_ref[px, py, z, face].astype(jnp.float32) for z in (0, 1))

    own_links = [link(px, py, face) for px, py in COLUMNS for face in range(6)]
    meta_ref[...] = fill_rows(32, states + own_links)
    for px, py in COLUMNS:
        for m in range(7):
            rows_ref[px, py, m * B : (m + 1) * B, :] = pair_lanes(p_ref[px, py, 0, m], p_ref[px, py, 1, m])
    for ref, face in ((first_ref, 1 - x % 2), (second_ref, x % 2)):
        ref[0:BLOCK_ROWS, :] = rows_ref[face, 0]
        ref[BLOCK_ROWS:BODY, :] = rows_ref[face, 1]
        face_links = [link(face, py, side) for py in (0, 1) for side in range(6)]
        ref[BODY : BODY + 16, :] = fill_rows(16, states + face_links).astype(jnp.bfloat16)


def pack_y_kernel(place_ref, links_ref, rows_ref, meta_ref, first_in, second_in, first_ref, second_ref):
    y = place_ref[1]

    def link(px, py, face):
        return tuple(links_ref[px, py, z, face].astype(jnp.float32) for z in (0, 1))

    row = lax.broadcasted_iota(jnp.int32, (16, PAIR), 0)
    from_first = first_in[BODY : BODY + 16, :].astype(jnp.float32)
    from_second = pltpu.roll(second_in[BODY : BODY + 16, :].astype(jnp.float32), 4, 0)
    corners = jnp.where(row < 4, from_first, from_second).astype(jnp.bfloat16)
    states = meta_ref[0:16, :]
    for ref, face in ((first_ref, 1 - y % 2), (second_ref, y % 2)):
        ref[0:BLOCK_ROWS, :] = rows_ref[0, face]
        ref[BLOCK_ROWS:BODY, :] = rows_ref[1, face]
        face_links = [link(px, face, side) for px in (0, 1) for side in range(6)]
        linked = fill_rows(16, [(0.0, 0.0)] * 4 + face_links)
        ref[BODY : BODY + 16, :] = jnp.where(row < 4, states, linked).astype(jnp.bfloat16)
        ref[BODY + 16 : BODY + 32, :] = corners


def pack_matrix_kernel(links_ref, a_ref, out_ref):
    for index, (px, py) in enumerate(COLUMNS):
        for z in (0, 1):
            blocks = []
            for slots, _, _ in around(px, py):
                m = slots[z]
                block = a_ref[px, py, z, m]
                if m > 0:
                    present = links_ref[px, py, z, m - 1] == 1
                    block = jnp.where(present, block, jnp.zeros_like(block))
                blocks.append(block)
            for pair in range(3):
                out_ref[index, z * B : (z + 1) * B, pair * PAIR : (pair + 1) * PAIR] = pair_lanes(
                    blocks[2 * pair], blocks[2 * pair + 1]
                )


def main_kernel(
    place_ref,
    a_ref,
    rows_ref,
    meta_ref,
    x_first,
    x_second,
    y_first,
    y_second,
    to_y_first,
    to_y_second,
    rest_ref,
    right,
    image,
    left_star,
    left_corner,
):
    x_even = place_ref[0] % 2 == 0
    y_even = place_ref[1] % 2 == 0

    def from_x(ox, rows):
        return jnp.where(x_even == (ox > 0), x_first[rows, :], x_second[rows, :])

    def from_y(oy, rows):
        return jnp.where(y_even == (oy > 0), y_first[rows, :], y_second[rows, :])

    tail = pl.ds(BODY, 16)
    tail_2 = pl.ds(BODY + 16, 16)
    own_meta = meta_ref[...]
    notes = {(0, 0): own_meta}
    for side in (-1, 1):
        notes[side, 0] = from_x(side, tail).astype(jnp.float32)
        notes[0, side] = from_y(side, tail).astype(jnp.float32)
    corner_notes = {side: from_y(side, tail_2).astype(jnp.float32) for side in (-1, 1)}

    def state_row(ox, oy, px, py):
        index = 2 * px + py
        if ox and oy:
            both = corner_notes[oy]
            first = both[index : index + 1]
            second = both[4 + index : 5 + index]
            return jnp.where(x_even == (ox > 0), first, second)
        return notes[ox, oy][index : index + 1]

    def link_row(ox, oy, px, py, face):
        if (ox, oy) == (0, 0):
            index = 4 + 6 * (2 * px + py) + face
        else:
            index = 4 + 6 * (py if ox else px) + face
        return notes[ox, oy][index : index + 1]

    def block(ox, oy, px, py, m, chunk):
        start = m * B + chunk * 16
        if (ox, oy) == (0, 0):
            return rows_ref[px, py, start : start + 16, :]
        start += (py if ox else px) * BLOCK_ROWS
        return (from_x(ox, pl.ds(start, 16)) if ox else from_y(oy, pl.ds(start, 16)))

    def box_rows(ox, oy, px, py):
        weights = []
        for m, (dx, dy) in enumerate(FACES):
            bx, nx = divmod(2 * ox + px + dx, 2)
            by, ny = divmod(2 * oy + py + dy, 2)
            state = state_row(bx, by, nx, ny)
            if m >= 5:
                state = swap_halves(state)
            rows = []
            for kind in range(3):
                weight = jnp.where(state == kind, 1.0, 0.0)
                if m > 0:
                    weight = weight * link_row(ox, oy, px, py, m - 1)
                rows.append(jnp.broadcast_to(weight, (16, PAIR)))
            weights.append(rows)
        reach = targets(px, py)
        chunks = {t: [] for t in box_set(px, py)}
        for chunk in range(4):
            values = [block(ox, oy, px, py, m, chunk).astype(jnp.float32) for m in range(7)]
            for t in chunks:
                total = None
                for m in range(7):
                    for kind in range(3):
                        if reach[m][kind] == t:
                            term = values[m] * weights[m][kind]
                            total = term if total is None else total + term
                chunks[t].append(total)
        return {t: jnp.concatenate(parts, axis=0) for t, parts in chunks.items()}

    images = {column: image_set(*column) for column in COLUMNS}
    users = {}
    for index, column in enumerate(COLUMNS):
        for place, (_, box, other) in enumerate(around(*column)):
            users.setdefault((box, other), []).append((index, column, place, box))
            reached = {(box[0] + tx, box[1] + ty) for tx, ty in box_set(*other)}
            for position, s in enumerate(images[column]):
                if s not in reached:
                    right[index, place * B : (place + 1) * B, position * PAIR : (position + 1) * PAIR] = jnp.zeros(
                        (B, PAIR), jnp.bfloat16
                    )
    for (box, other), uses in users.items():
        found = box_rows(*box, *other)
        own = COLUMNS.index(other)
        for t, value in found.items():
            rounded = value.astype(jnp.bfloat16)
            for index, column, place, _ in uses:
                position = images[column].index((box[0] + t[0], box[1] + t[1]))
                stored = swap_halves(value).astype(jnp.bfloat16) if place == 5 else rounded
                right[index, place * B : (place + 1) * B, position * PAIR : (position + 1) * PAIR] = stored
            if box == (0, 0):
                turned = value.T
                turned = pair_lanes(turned[:B], turned[B:]).astype(jnp.bfloat16)
                if t in STAR:
                    left_star[STAR.index(t) * B : (STAR.index(t) + 1) * B, own * PAIR : (own + 1) * PAIR] = turned
                else:
                    left_corner[own] = turned
    half = low_half((B, PAIR))
    for index, column in enumerate(COLUMNS):
        product = jnp.dot(a_ref[index], right[index], preferred_element_type=jnp.float32)

        def part(s, z):
            if s not in images[column]:
                return jnp.zeros((B, PAIR), jnp.float32)
            position = images[column].index(s)
            return product[z * B : (z + 1) * B, position * PAIR : (position + 1) * PAIR]

        for pair in range(IMAGE_PAIRS):
            one = IMAGE[2 * pair]
            two = IMAGE[2 * pair + 1] if 2 * pair + 1 < len(IMAGE) else None
            low = jnp.where(half, part(one, 0), swap_halves(part(two, 0)))
            high = jnp.where(half, swap_halves(part(one, 1)), part(two, 1))
            start = index * PAIR
            lanes = slice(pair * PAIR, (pair + 1) * PAIR)
            image[start : start + B, lanes] = low.astype(jnp.bfloat16)
            image[start + B : start + PAIR, lanes] = high.astype(jnp.bfloat16)
    folded_half = low_half((B // 2, PAIR))

    def fold(product):
        blocks = {}
        for pair in range(IMAGE_PAIRS):
            tile = product[:, pair * PAIR : (pair + 1) * PAIR]
            top, bottom = tile[: B // 2], tile[B // 2 :]
            blocks[IMAGE[2 * pair]] = jnp.where(folded_half, top, swap_halves(bottom))
            if 2 * pair + 1 < len(IMAGE):
                blocks[IMAGE[2 * pair + 1]] = jnp.where(folded_half, swap_halves(top), bottom)
        return blocks

    def contribution(tx, ty):
        if (tx, ty) in STAR:
            rows = STAR.index((tx, ty)) * B
            product = jnp.dot(left_star[rows : rows + B, :], image[...], preferred_element_type=jnp.float32)
        else:
            index = COLUMNS.index(corner_of(tx, ty))
            product = jnp.dot(
                left_corner[index], image[index * PAIR : (index + 1) * PAIR, :], preferred_element_type=jnp.float32
            )
        return fold(product)

    for ty in (-1, 1):
        parts = {tx: contribution(tx, ty) for tx in (0, -1, 1)}
        for position, (tx, s) in enumerate(relay_list(ty)):
            value = parts[tx][s].astype(jnp.bfloat16)
            rows = slice(position * (B // 2), (position + 1) * (B // 2))

            if ty > 0:
                goes_first = y_even
            else:
                goes_first = jnp.logical_not(y_even)

            @pl.when(goes_first)
            def _(rows=rows, value=value):
                to_y_first[rows, :] = value

            @pl.when(jnp.logical_not(goes_first))
            def _(rows=rows, value=value):
                to_y_second[rows, :] = value

    for group, tx in enumerate((0, -1, 1)):
        parts = contribution(tx, 0)
        for position, s in enumerate(IMAGE):
            rest_ref[group, position] = parts[s]


HALF = B // 2


def relay_kernel(place_ref, rest_ref, y_first, y_second, to_x_first, to_x_second, own_ref):
    x_even = place_ref[0] % 2 == 0
    y_even = place_ref[1] % 2 == 0

    def from_y(oy, tx, s):
        position = relay_list(-oy).index((tx, s))
        rows = pl.ds(position * HALF, HALF)
        value = jnp.where(y_even == (oy > 0), y_first[rows, :], y_second[rows, :]).astype(jnp.float32)
        return value * (place_ref[3] if oy > 0 else place_ref[2]).astype(jnp.float32)

    def total(tx, block):
        jx, jy = block
        terms = []
        if (jx + tx, jy) in IMAGE:
            terms.append(rest_ref[(0, -1, 1).index(tx), IMAGE.index((jx + tx, jy))])
        for oy in (-1, 1):
            s = (jx + tx, jy - oy)
            if (tx, s) in relay_list(-oy):
                terms.append(from_y(oy, tx, s))
        value = terms[0]
        for term in terms[1:]:
            value = value + term
        return value

    for tx in (-1, 1):
        goes_first = x_even if tx > 0 else jnp.logical_not(x_even)
        for position, block in enumerate(coarse_list(tx)):
            value = total(tx, block).astype(jnp.bfloat16)
            rows = slice(position * HALF, (position + 1) * HALF)

            @pl.when(goes_first)
            def _(rows=rows, value=value):
                to_x_first[rows, :] = value

            @pl.when(jnp.logical_not(goes_first))
            def _(rows=rows, value=value):
                to_x_second[rows, :] = value

    for position, block in enumerate(own_list()):
        own_ref[position] = total(0, block)


def finish_kernel(place_ref, own_ref, x_first, x_second, out_ref):
    x_even = place_ref[0] % 2 == 0
    own = own_list()
    lists = {ox: coarse_list(-ox) for ox in (-1, 1)}
    for jx in range(-3, 4):
        for jy in range(-3, 4):
            terms = []
            if (jx, jy) in own:
                terms.append(own_ref[own.index((jx, jy))])
            for ox in (-1, 1):
                if (jx, jy) in lists[ox]:
                    rows = pl.ds(lists[ox].index((jx, jy)) * HALF, HALF)
                    value = jnp.where(x_even == (ox > 0), x_first[rows, :], x_second[rows, :]).astype(jnp.float32)
                    terms.append(value * (place_ref[5] if ox > 0 else place_ref[4]).astype(jnp.float32))
            if not terms:
                out_ref[jx + 3, jy + 3] = jnp.zeros((B, B), jnp.bfloat16)
                continue
            value = terms[0]
            for term in terms[1:]:
                value = value + term
            out_ref[jx + 3, jy + 3, 0:HALF, :] = value[:, :B].astype(jnp.bfloat16)
            out_ref[jx + 3, jy + 3, HALF:B, :] = swap_halves(value)[:, :B].astype(jnp.bfloat16)


def swapped(value, axis, offset):
    count_x, count_y = lax.axis_size("sx"), lax.axis_size("sy")
    pairs = []
    for x in range(count_x):
        for y in range(count_y):
            if axis == "sx":
                partner = ((x + offset) ^ 1) - offset
                other = (partner, y) if 0 <= partner < count_x else (x, y ^ 1)
            else:
                partner = ((y + offset) ^ 1) - offset
                other = (x, partner) if 0 <= partner < count_y else (x ^ 1, y)
            pairs.append((x * count_y + y, other[0] * count_y + other[1]))
    return lax.ppermute(value, ("sx", "sy"), pairs)


SMEM = pl.BlockSpec(memory_space=pltpu.SMEM)
VMEM = pl.BlockSpec(memory_space=pltpu.VMEM)


def call(kernel, in_specs, outs, scratch=()):
    return pl.pallas_call(
        kernel,
        out_shape=[jax.ShapeDtypeStruct(shape, dtype) for shape, dtype in outs],
        in_specs=in_specs,
        out_specs=[VMEM] * len(outs),
        scratch_shapes=list(scratch),
        compiler_params=pltpu.CompilerParams(vmem_limit_bytes=VMEM_LIMIT),
    )


def per_device(fine_matrix, prolongator, aggregate, face_links):
    x, y = lax.axis_index("sx"), lax.axis_index("sy")
    count_x, count_y = lax.axis_size("sx"), lax.axis_size("sy")
    place = jnp.stack([x, y, y > 0, y < count_y - 1, x > 0, x < count_x - 1]).astype(jnp.int32)
    bf16, f32 = jnp.bfloat16, jnp.float32
    message = ((BODY + 16, PAIR), bf16)
    rows, meta, first, second = call(
        functools.partial(pack_kernel, count_y),
        [SMEM, SMEM, SMEM, VMEM],
        [((2, 2, BLOCK_ROWS, PAIR), bf16), ((32, PAIR), f32), message, message],
    )(place, aggregate, face_links, prolongator)
    x_first, x_second = swapped(first, "sx", 0), swapped(second, "sx", 1)
    (matrix,) = call(pack_matrix_kernel, [SMEM, VMEM], [((4, PAIR, 6 * B), bf16)])(face_links, fine_matrix)
    message = ((BODY + 32, PAIR), bf16)
    first, second = call(pack_y_kernel, [SMEM, SMEM, VMEM, VMEM, VMEM, VMEM], [message, message])(
        place, face_links, rows, meta, x_first, x_second
    )
    y_first, y_second = swapped(first, "sy", 0), swapped(second, "sy", 1)
    relay = ((len(relay_list(1)) * HALF, PAIR), bf16)
    first, second, rest = call(
        main_kernel,
        [SMEM] + [VMEM] * 7,
        [relay, relay, ((3, len(IMAGE), HALF, PAIR), f32)],
        [
            pltpu.VMEM((4, 6 * B, 10 * PAIR), bf16),
            pltpu.VMEM((4 * PAIR, IMAGE_PAIRS * PAIR), bf16),
            pltpu.VMEM((len(STAR) * B, 4 * PAIR), bf16),
            pltpu.VMEM((4, B, PAIR), bf16),
        ],
    )(place, matrix, rows, meta, x_first, x_second, y_first, y_second)
    y_first, y_second = swapped(first, "sy", 0), swapped(second, "sy", 1)
    sent = ((len(coarse_list(1)) * HALF, PAIR), bf16)
    first, second, own = call(
        relay_kernel, [SMEM] + [VMEM] * 3, [sent, sent, ((len(own_list()), HALF, PAIR), f32)]
    )(place, rest, y_first, y_second)
    x_first, x_second = swapped(first, "sx", 0), swapped(second, "sx", 1)
    (out,) = call(finish_kernel, [SMEM] + [VMEM] * 3, [((7, 7, B, B), bf16)])(place, own, x_first, x_second)
    return out[None, None]


def solution(mesh):
    return jax.shard_map(
        per_device,
        mesh=mesh,
        in_specs=(
            P("sx", "sy", None, None, None, None),
            P("sx", "sy", None, None, None, None),
            P("sx", "sy", None),
            P("sx", "sy", None, None),
        ),
        out_specs=P("sx", "sy", None, None, None, None),
        check_vma=False,
    )
```

time: 254 us -> 42.9 us (0.17)
  waiting for transfers between devices: 135 us -> 26.1 us
  local copies, waits for them, and re-layouts: 44.5 us -> 1.88 us
  starting transfers between devices: 42.8 us -> 5.07 us
  other arithmetic: 16 us -> 0 us
  matrix products: 13.4 us -> 0 us
  Pallas kernels: 0 us -> 9.57 us
    ppermute x16 -> x8, waiting for transfers between devices: 135 us -> 26.1 us  [swapped(): return lax.ppermute(value, ('sx', 'sy'), pairs)]
    ppermute x16 -> x8, starting transfers between devices: 42.8 us -> 5.07 us  [swapped(): return lax.ppermute(value, ('sx', 'sy'), pairs)]
    another operation x16 -> x1, local copies, waits for them, and re-layouts: 14.8 us -> 0.08 us  [per_device(): jnp.stack([x, y, y > 0, y < count_y - 1, x > 0, x < count_x - 1])]
    dot_general x9 -> x0, matrix products: 13.4 us -> none  [the longest x1 5.55 us: combine_rows(): jnp.einsum('xyzmt,xyzmpq->xyztpq', selector, blocks, preferred_element_ty...]
    slice x11 -> x0, local copies, waits for them, and re-layouts: 10 us -> none  [the longest x1 5.67 us: neighbour_views(): padded[1:-1, 1:-1, 1:3]]
    pallas_call x0 -> x6, Pallas kernels: none -> 9.57 us  [the longest x1 4.68 us: per_device(): call(main_kernel, [SMEM] + [VMEM] * 7, [relay, relay, ((3, len(IMAGE), HA...]
    another operation x3 -> x0, other arithmetic: 6.97 us -> none
    scatter-add x33 -> x0, other arithmetic: 5.8 us -> none  [the longest x26 4.07 us: image_blocks(): total = total.at[:, parity_x, :, parity_y, :, 1 + shift_x:4 + shift_x, 1...]
  transfers between devices with their start and end apart: 16 -> 8, of which waited for: 6 -> 7; matrix products, arithmetic and copies ran while one was open for 3% -> 0% of each run, Pallas kernels for 0% -> 2%
where the time goes in v1:
time: 42.9 us; the launch traced here: 42.7 us
  waiting for transfers between devices  26.1 us (61%)
  Pallas kernels  9.57 us (22%)
  starting transfers between devices  5.07 us (12%)
  local copies, waits for them, and re-layouts  1.88 us (4%)
    ppermute x8, waiting for transfers between devices, swapped(): return lax.ppermute(value, ('sx', 'sy'), pairs)  26.1 us
    ppermute x8, starting transfers between devices, swapped(): return lax.ppermute(value, ('sx', 'sy'), pairs)  5.07 us
    pallas_call x1, Pallas kernels, per_device(): call(main_kernel, [SMEM] + [VMEM] * 7, [relay, relay, ((3, len(IMAGE), HA...  4.68 us
    unnamed x8, local copies, waits for them, and re-layouts  1.79 us
    pallas_call x1, Pallas kernels, per_device(): call(finish_kernel, [SMEM] + [VMEM] * 3, [((7, 7, B, B), bf16)])  1.61 us
    pallas_call x1, Pallas kernels, per_device(): call(relay_kernel, [SMEM] + [VMEM] * 3, [sent, sent, ((len(own_list()), H...  0.94 us
    pallas_call x1, Pallas kernels, per_device(): call(functools.partial(pack_kernel, count_y), [SMEM, SMEM, SMEM, VMEM], [...  0.91 us
  transfers between devices with their start and end apart: 8, of which 7 were waited for; matrix products, arithmetic and copies ran while one was open for 0% of the time, Pallas kernels for 2%

profile of v1, /device:TPU:20, one launch (start us, length us, event | category | flops | bytes accessed | tf_op | source)
XLA Modules:
  0.0 42.7 jit_solution(8566694668354956619)
XLA Ops:
  0.0 0.0 copy-start.2
  0.0 0.0 copy-start.3
  0.0 0.1 stack.43.place_ref
  0.1 0.6 %copy-done.2 = s32[2,2,2,6]{3,2,1,0:T(2,128)S(1)} copy-done((s32[2,2,2,6]{3,2,1,0:T(2,128)S(1)}, s32[2,2,2,6]{3,2,1,0:T(2,128)}, u32[]{:S(2)}) %copy-start.2) | copy-done | bytes 216
  0.7 0.0 copy-done.3
  0.7 0.0 copy-start.1
  0.7 1.2 %copy-done.1 = bf16[2,2,2,7,64,64]{5,4,3,2,1,0:T(8,128)(2,1)S(1)} copy-done((bf16[2,2,2,7,64,64]{5,4,3,2,1,0:T(8,128)(2,1)S(1)}, bf16[2,2,2,7,64,64]{5,4,3,2,1,0:T(8,128)(2,1)}, u32[]{:S(2)}) %copy-start.1) | copy-done | bytes 458776
  1.9 0.0 copy-start
  1.9 0.9 %shard_map.47 = (bf16[2,2,448,128]{3,2,1,0:T(8,128)(2,1)S(1)}, f32[32,128]{1,0:T(8,128)S(1)}, bf16[912,128]{1,0:T(8,128)(2,1)S(1)}, bf16[912,128]{1,0:T(8,128)(2,1)S(1)}) custom-call(s32[6]{0:T(128)S(1)} %stack.43.place_ref, s32[2,2,2]{2,1,0:T(2,128)S(1)} %copy-done.3, s32[2,2,2,6]{3,2,1,0:T(2,128)S(1)} %copy-done.2, bf16[2,2,2,7,64,64]{5,4,3,2,1,0:T(8,128)(2,1)S(1)} %copy-done.1), custom_call_target="tpu_custom_call" | custom-call | tf_op jit(solution)/shard_map/pallas_call | solution.py:456
  2.8 1.6 %collective-permute-start = (bf16[912,128]{1,0:T(8,128)(2,1)S(1)}, bf16[912,128]{1,0:T(8,128)(2,1)S(1)}, u32[]{:S(2)}, u32[]{:S(2)}) collective-permute-start(bf16[912,128]{1,0:T(8,128)(2,1)S(1)} %get-tuple-element.19), channel_id=1, source_target_pairs={{0,8},{1,9},{2,10},{3,11},{4,12},{5,13},{6,14},{7,15},{8,0},{9,1},... | collective-permute-start | bytes 700424 | tf_op jit(solution)/shard_map/ppermute | solution.py:432
  4.4 0.0 collective-permute-start.1
  4.4 5.9 %collective-permute-done.first_in.x_first = bf16[912,128]{1,0:T(8,128)(2,1)S(1)} collective-permute-done((bf16[912,128]{1,0:T(8,128)(2,1)S(1)}, bf16[912,128]{1,0:T(8,128)(2,1)S(1)}, u32[]{:S(2)}, u32[]{:S(2)}) %collective-permute-start) | collective-permute-done | bytes 233504 | tf_op jit(solution)/shard_map/ppermute | solution.py:432
  10.3 1.3 %collective-permute-done.1.second_in.x_second = bf16[912,128]{1,0:T(8,128)(2,1)S(1)} collective-permute-done((bf16[912,128]{1,0:T(8,128)(2,1)S(1)}, bf16[912,128]{1,0:T(8,128)(2,1)S(1)}, u32[]{:S(2)}, u32[]{:S(2)}) %collective-permute-start.1) | collective-permute-done | bytes 233504 | tf_op jit(solution)/shard_map/ppermute | solution.py:432
  11.6 0.7 %shard_map.48 = (bf16[928,128]{1,0:T(8,128)(2,1)S(1)}, bf16[928,128]{1,0:T(8,128)(2,1)S(1)}) custom-call(s32[6]{0:T(128)S(1)} %stack.43.place_ref, s32[2,2,2,6]{3,2,1,0:T(2,128)S(1)} %copy-done.2, bf16[2,2,448,128]{3,2,1,0:T(8,128)(2,1)S(1)} %get-tuple-element.17.rows_ref, f32[32,128]{1,0:T(8,128)S(1)} %get-tuple-element.18.meta_ref, ...), custom_call_target="tpu_custom_call" | custom-call | tf_op jit(solution)/shard_map/pallas_call | solution.py:464
  12.3 0.1 collective-permute-start.2
  12.3 1.5 %collective-permute-start.3 = (bf16[928,128]{1,0:T(8,128)(2,1)S(1)}, bf16[928,128]{1,0:T(8,128)(2,1)S(1)}, u32[]{:S(2)}, u32[]{:S(2)}) collective-permute-start(bf16[928,128]{1,0:T(8,128)(2,1)S(1)} %get-tuple-element.22), channel_id=1, source_target_pairs={{0,8},{1,2},{2,1},{3,4},{4,3},{5,6},{6,5},{7,15},{8,0},{9,10},{10,... | collective-permute-start | bytes 712712 | tf_op jit(solution)/shard_map/ppermute | solution.py:432
  13.9 0.0 copy-done
  13.9 0.8 %shard_map.46.a_ref = bf16[4,128,384]{2,1,0:T(8,128)(2,1)S(1)} custom-call(s32[2,2,2,6]{3,2,1,0:T(2,128)S(1)} %copy-done.2, bf16[2,2,2,7,64,64]{5,4,3,2,1,0:T(8,128)(2,1)S(1)} %copy-done), custom_call_target="tpu_custom_call" | custom-call | tf_op jit(solution)/shard_map/pallas_call | solution.py:462
  14.6 0.0 collective-permute-done.2.y_first
  14.7 6.4 %collective-permute-done.3.y_second = bf16[928,128]{1,0:T(8,128)(2,1)S(1)} collective-permute-done((bf16[928,128]{1,0:T(8,128)(2,1)S(1)}, bf16[928,128]{1,0:T(8,128)(2,1)S(1)}, u32[]{:S(2)}, u32[]{:S(2)}) %collective-permute-start.3) | collective-permute-done | bytes 237600 | tf_op jit(solution)/shard_map/ppermute | solution.py:432
  21.0 4.7 %shard_map.49 = (bf16[1056,128]{1,0:T(8,128)(2,1)S(1)}, bf16[1056,128]{1,0:T(8,128)(2,1)S(1)}, f32[3,13,32,128]{3,2,1,0:T(8,128)S(1)}) custom-call(s32[6]{0:T(128)S(1)} %stack.43.place_ref, bf16[4,128,384]{2,1,0:T(8,128)(2,1)S(1)} %shard_map.46.a_ref, bf16[2,2,448,128]{3,2,1,0:T(8,128)(2,1)S(1)} %get-tuple-element.17.rows_ref, ...), custom_call_target="tpu_custom_call" | custom-call | tf_op jit(solution)/shard_map/pallas_call | solution.py:469
  25.7 0.1 collective-permute-start.4
  25.8 1.3 %collective-permute-start.5 = (bf16[1056,128]{1,0:T(8,128)(2,1)S(1)}, bf16[1056,128]{1,0:T(8,128)(2,1)S(1)}, u32[]{:S(2)}, u32[]{:S(2)}) collective-permute-start(bf16[1056,128]{1,0:T(8,128)(2,1)S(1)} %get-tuple-element.25), channel_id=1, source_target_pairs={{0,8},{1,2},{2,1},{3,4},{4,3},{5,6},{6,5},{7,15},{8,0},{9,10},{10,... | collective-permute-start | bytes 811016 | tf_op jit(solution)/shard_map/ppermute | solution.py:432
  27.1 0.2 collective-permute-done.4.y_first
  27.3 7.4 %collective-permute-done.5.y_second = bf16[1056,128]{1,0:T(8,128)(2,1)S(1)} collective-permute-done((bf16[1056,128]{1,0:T(8,128)(2,1)S(1)}, bf16[1056,128]{1,0:T(8,128)(2,1)S(1)}, u32[]{:S(2)}, u32[]{:S(2)}) %collective-permute-start.5) | collective-permute-done | bytes 270368 | tf_op jit(solution)/shard_map/ppermute | solution.py:432
  34.8 0.9 %shard_map.50 = (bf16[544,128]{1,0:T(8,128)(2,1)S(1)}, bf16[544,128]{1,0:T(8,128)(2,1)S(1)}, f32[23,32,128]{2,1,0:T(8,128)S(1)}) custom-call(s32[6]{0:T(128)S(1)} %stack.43.place_ref, f32[3,13,32,128]{3,2,1,0:T(8,128)S(1)} %get-tuple-element.23.rest_ref, bf16[1056,128]{1,0:T(8,128)(2,1)S(1)} %collective-permute-done.4.y_first, ...), custom_call_target="tpu_custom_call" | custom-call | tf_op jit(solution)/shard_map/pallas_call | solution.py:482
  35.7 0.3 collective-permute-start.6
  36.1 0.1 collective-permute-start.7
  36.1 4.7 %collective-permute-done.6.x_first = bf16[544,128]{1,0:T(8,128)(2,1)S(1)} collective-permute-done((bf16[544,128]{1,0:T(8,128)(2,1)S(1)}, bf16[544,128]{1,0:T(8,128)(2,1)S(1)}, u32[]{:S(2)}, u32[]{:S(2)}) %collective-permute-start.6) | collective-permute-done | bytes 139296 | tf_op jit(solution)/shard_map/ppermute | solution.py:432
  40.8 0.3 collective-permute-done.7.x_second
  41.1 1.6 %shard_map.51 = bf16[7,7,64,64]{3,2,1,0:T(8,128)(2,1)} custom-call(s32[6]{0:T(128)S(1)} %stack.43.place_ref, f32[23,32,128]{2,1,0:T(8,128)S(1)} %get-tuple-element.26.own_ref, bf16[544,128]{1,0:T(8,128)(2,1)S(1)} %collective-permute-done.6.x_first, bf16[544,128]{1,0:T(8,128)(2,1)S(1)} %collective-permute-done.7.x_second), custom_call_target="tpu_custom_call" | custom-call | tf_op jit(solution)/shard_map/pallas_call | solution.py:486
Async XLA Ops:
  0.0 0.7 %copy-start.2 = (s32[2,2,2,6]{3,2,1,0:T(2,128)S(1)}, s32[2,2,2,6]{3,2,1,0:T(2,128)}, u32[]{:S(2)}) copy-start(s32[2,2,2,6]{3,2,1,0:T(2,128)} %links_ref.5) | copy-start | bytes 580
  0.0 0.7 %copy-start.3 = (s32[2,2,2]{2,1,0:T(2,128)S(1)}, s32[2,2,2]{2,1,0:T(2,128)}, u32[]{:S(2)}) copy-start(s32[2,2,2]{2,1,0:T(2,128)} %aggregate_ref.1) | copy-start | bytes 100
  0.7 1.2 %copy-start.1 = (bf16[2,2,2,7,64,64]{5,4,3,2,1,0:T(8,128)(2,1)S(1)}, bf16[2,2,2,7,64,64]{5,4,3,2,1,0:T(8,128)(2,1)}, u32[]{:S(2)}) copy-start(bf16[2,2,2,7,64,64]{5,4,3,2,1,0:T(8,128)(2,1)} %p_ref.1) | copy-start | bytes 1376260
  1.9 12.0 %copy-start = (bf16[2,2,2,7,64,64]{5,4,3,2,1,0:T(8,128)(2,1)S(1)}, bf16[2,2,2,7,64,64]{5,4,3,2,1,0:T(8,128)(2,1)}, u32[]{:S(2)}) copy-start(bf16[2,2,2,7,64,64]{5,4,3,2,1,0:T(8,128)(2,1)} %a_ref.1) | copy-start | bytes 1376260
  2.8 7.5 %collective-permute-start = (bf16[912,128]{1,0:T(8,128)(2,1)S(1)}, bf16[912,128]{1,0:T(8,128)(2,1)S(1)}, u32[]{:S(2)}, u32[]{:S(2)}) collective-permute-start(bf16[912,128]{1,0:T(8,128)(2,1)S(1)} %get-tuple-element.19), channel_id=1, source_target_pairs={{0,8},{1,9},{2,10},{3,11},{4,12},{5,13},{6,14},{7,15},{8,0},{9,1},... | collective-permute-start | bytes 700424 | tf_op jit(solution)/shard_map/ppermute | solution.py:432
  4.4 7.2 %collective-permute-start.1 = (bf16[912,128]{1,0:T(8,128)(2,1)S(1)}, bf16[912,128]{1,0:T(8,128)(2,1)S(1)}, u32[]{:S(2)}, u32[]{:S(2)}) collective-permute-start(bf16[912,128]{1,0:T(8,128)(2,1)S(1)} %get-tuple-element.20), channel_id=1, source_target_pairs={{0,1},{1,0},{2,3},{3,2},{4,5},{5,4},{6,7},{7,6},{8,16},{9,17},{10,... | collective-permute-start | bytes 700424 | tf_op jit(solution)/shard_map/ppermute | solution.py:432
  12.3 2.4 %collective-permute-start.2 = (bf16[928,128]{1,0:T(8,128)(2,1)S(1)}, bf16[928,128]{1,0:T(8,128)(2,1)S(1)}, u32[]{:S(2)}, u32[]{:S(2)}) collective-permute-start(bf16[928,128]{1,0:T(8,128)(2,1)S(1)} %get-tuple-element.21), channel_id=1, source_target_pairs={{0,1},{1,0},{2,3},{3,2},{4,5},{5,4},{6,7},{7,6},{8,9},{9,8},{10,11... | collective-permute-start | bytes 712712 | tf_op jit(solution)/shard_map/ppermute | solution.py:432
  12.3 8.7 %collective-permute-start.3 = (bf16[928,128]{1,0:T(8,128)(2,1)S(1)}, bf16[928,128]{1,0:T(8,128)(2,1)S(1)}, u32[]{:S(2)}, u32[]{:S(2)}) collective-permute-start(bf16[928,128]{1,0:T(8,128)(2,1)S(1)} %get-tuple-element.22), channel_id=1, source_target_pairs={{0,8},{1,2},{2,1},{3,4},{4,3},{5,6},{6,5},{7,15},{8,0},{9,10},{10,... | collective-permute-start | bytes 712712 | tf_op jit(solution)/shard_map/ppermute | solution.py:432
  25.7 1.6 %collective-permute-start.4 = (bf16[1056,128]{1,0:T(8,128)(2,1)S(1)}, bf16[1056,128]{1,0:T(8,128)(2,1)S(1)}, u32[]{:S(2)}, u32[]{:S(2)}) collective-permute-start(bf16[1056,128]{1,0:T(8,128)(2,1)S(1)} %get-tuple-element.24), channel_id=1, source_target_pairs={{0,1},{1,0},{2,3},{3,2},{4,5},{5,4},{6,7},{7,6},{8,9},{9,8},{10,11... | collective-permute-start | bytes 811016 | tf_op jit(solution)/shard_map/ppermute | solution.py:432
  25.8 9.0 %collective-permute-start.5 = (bf16[1056,128]{1,0:T(8,128)(2,1)S(1)}, bf16[1056,128]{1,0:T(8,128)(2,1)S(1)}, u32[]{:S(2)}, u32[]{:S(2)}) collective-permute-start(bf16[1056,128]{1,0:T(8,128)(2,1)S(1)} %get-tuple-element.25), channel_id=1, source_target_pairs={{0,8},{1,2},{2,1},{3,4},{4,3},{5,6},{6,5},{7,15},{8,0},{9,10},{10,... | collective-permute-start | bytes 811016 | tf_op jit(solution)/shard_map/ppermute | solution.py:432
  35.7 5.1 %collective-permute-start.6 = (bf16[544,128]{1,0:T(8,128)(2,1)S(1)}, bf16[544,128]{1,0:T(8,128)(2,1)S(1)}, u32[]{:S(2)}, u32[]{:S(2)}) collective-permute-start(bf16[544,128]{1,0:T(8,128)(2,1)S(1)} %get-tuple-element.27), channel_id=1, source_target_pairs={{0,8},{1,9},{2,10},{3,11},{4,12},{5,13},{6,14},{7,15},{8,0},{9,1},... | collective-permute-start | bytes 417800 | tf_op jit(solution)/shard_map/ppermute | solution.py:432
  36.1 5.1 %collective-permute-start.7 = (bf16[544,128]{1,0:T(8,128)(2,1)S(1)}, bf16[544,128]{1,0:T(8,128)(2,1)S(1)}, u32[]{:S(2)}, u32[]{:S(2)}) collective-permute-start(bf16[544,128]{1,0:T(8,128)(2,1)S(1)} %get-tuple-element.28), channel_id=1, source_target_pairs={{0,1},{1,0},{2,3},{3,2},{4,5},{5,4},{6,7},{7,6},{8,16},{9,17},{10,... | collective-permute-start | bytes 417800 | tf_op jit(solution)/shard_map/ppermute | solution.py:432

commit v2 on v1

v2 whole, which is shorter than its diff:
```python
import functools

import jax
import jax.numpy as jnp
from jax import lax
from jax.experimental import pallas as pl
from jax.experimental.pallas import tpu as pltpu
from jax.sharding import PartitionSpec as P


B = 64
HALF = B // 2
PAIR = 2 * B
BLOCK_ROWS = 7 * B
BODY = 2 * BLOCK_ROWS
TAIL = 16
VMEM_LIMIT = 48 * 1024 * 1024

FACES = [(0, 0), (-1, 0), (1, 0), (0, -1), (0, 1), (0, 0), (0, 0)]
COLUMNS = [(0, 0), (0, 1), (1, 0), (1, 1)]
SIDES_X = (0, 2, 1, 3, 4, 5, 6)
SIDES_Y = (0, 1, 2, 4, 3, 5, 6)


def targets(px, py):
    table = []
    for dx, dy in FACES:
        ox, nx = divmod(px + dx, 2)
        oy, ny = divmod(py + dy, 2)
        table.append([(ox, oy), (ox + 2 * nx - 1, oy), (ox, oy + 2 * ny - 1)])
    return table


def box_set(px, py):
    return sorted({t for row in targets(px, py) for t in row})


def around(px, py):
    found = [((0, 0), (0, 0), (px, py))]
    for m in (2, 1) if px == 0 else (1, 2):
        ox, nx = divmod(px + FACES[m][0], 2)
        found.append(((m, m), (ox, 0), (nx, py)))
    for m in (4, 3) if py == 0 else (3, 4):
        oy, ny = divmod(py + FACES[m][1], 2)
        found.append(((m, m), (0, oy), (px, ny)))
    found.append(((6, 5), (0, 0), (px, py)))
    return found


def image_set(px, py):
    found = set()
    for _, (ox, oy), column in around(px, py):
        found |= {(ox + tx, oy + ty) for tx, ty in box_set(*column)}
    return sorted(found)


IMAGE = sorted({s for column in COLUMNS for s in image_set(*column)})
IMAGE_PAIRS = (len(IMAGE) + 1) // 2
STAR = [(0, 1), (0, -1), (0, 0), (1, 0), (-1, 0)]


def column_of(tx, ty):
    return ((tx + 1) // 2, (ty + 1) // 2)


def blocks_of(tx, ty):
    return IMAGE if (tx, ty) in STAR else image_set(*column_of(tx, ty))


TO_Y_FIRST = [((tx, 1), s) for tx in (0, -1, 1) for s in blocks_of(tx, 1)]
TO_Y_SECOND = [((0, -1), s) for s in blocks_of(0, -1)]
TO_C_FIRST = [((1, -1), s) for s in blocks_of(1, -1)]
TO_C_SECOND = [((-1, -1), s) for s in blocks_of(-1, -1)]


def relayed(tx):
    return {(s[0], 1 - s[1]): row for row, (t, s) in enumerate(TO_Y_FIRST) if t[0] == tx}


TO_X = {tx: sorted(set(IMAGE) | set(relayed(tx))) for tx in (1, -1)}
OWN = sorted(set(IMAGE) | set(relayed(0)))
STENCIL = [(jx, jy) for jx in range(-3, 4) for jy in range(-3, 4) if abs(jx) + abs(jy) <= 3]


def low_half(shape):
    return lax.broadcasted_iota(jnp.int32, shape, len(shape) - 1) < B


def swap_halves(value):
    return pltpu.roll(value, B, value.ndim - 1)


def pair_lanes(left, right):
    return jnp.concatenate([left, right], axis=-1)


def mirrored():
    return lax.axis_index("sx") % 2, lax.axis_index("sy") % 2


def slot_here(m, odd_x, odd_y):
    if m in (1, 2):
        return jnp.where(odd_x == 1, 3 - m, m)
    if m in (3, 4):
        return jnp.where(odd_y == 1, 7 - m, m)
    return m


def fill_rows(rows, values):
    shape = (rows, PAIR)
    row = lax.broadcasted_iota(jnp.int32, shape, 0)
    half = low_half(shape)
    filled = jnp.zeros(shape, jnp.float32)
    for index, (low, high) in enumerate(values):
        filled = jnp.where(row == index, jnp.where(half, low, high), filled)
    return filled


def pack_kernel(
    boxes_y,
    aggregate_hbm,
    links_hbm,
    p_hbm,
    rows_ref,
    meta_ref,
    x_first,
    x_second,
    y_first,
    y_second,
    p_ref,
    aggregate_ref,
    links_ref,
    p_sems,
    sems,
):
    odd_x, odd_y = mirrored()
    own = lax.axis_index("sx") * boxes_y + lax.axis_index("sy")
    place = {(px, py): (px ^ odd_x, py ^ odd_y) for px, py in COLUMNS}
    copies = [
        pltpu.make_async_copy(p_hbm.at[place[column]], p_ref.at[index], p_sems.at[index])
        for index, column in enumerate(COLUMNS)
    ]
    small = [
        pltpu.make_async_copy(aggregate_hbm, aggregate_ref, sems.at[0]),
        pltpu.make_async_copy(links_hbm, links_ref, sems.at[1]),
    ]
    for copy in small + copies:
        copy.start()
    for copy in small:
        copy.wait()

    def state(column, z):
        shift = aggregate_ref[place[column] + (z,)] - own
        across_x = (shift == boxes_y) | (shift == -boxes_y)
        return jnp.where(shift == 0, 0, jnp.where(across_x, 1, 2)).astype(jnp.float32)

    def link(column, m):
        face = slot_here(m, odd_x, odd_y) - 1
        return tuple(links_ref[place[column] + (z, face)].astype(jnp.float32) for z in (0, 1))

    states = [tuple(state(column, z) for z in (0, 1)) for column in COLUMNS]
    links = {column: [link(column, m) for m in range(1, 7)] for column in COLUMNS}
    meta_ref[...] = fill_rows(32, states + sum((links[column] for column in COLUMNS), []))
    messages = (
        (x_first, ((1, 0), (1, 1))),
        (x_second, ((0, 0), (0, 1))),
        (y_first, ((0, 1), (1, 1))),
        (y_second, ((0, 0), (1, 0))),
    )
    for ref, columns in messages:
        tail = fill_rows(TAIL, states + links[columns[0]] + links[columns[1]])
        ref[BODY : BODY + TAIL, :] = tail.astype(jnp.bfloat16)
    for index, column in enumerate(COLUMNS):
        copies[index].wait()
        for m in range(7):
            slot = slot_here(m, odd_x, odd_y)
            packed = pair_lanes(p_ref[index, 0, slot], p_ref[index, 1, slot])
            rows_ref[index, m * B : (m + 1) * B, :] = packed
            for ref, columns in messages:
                if column in columns:
                    start = columns.index(column) * BLOCK_ROWS + m * B
                    ref[start : start + B, :] = packed


def pack_matrix_kernel(links_ref, a_ref, out_ref):
    odd_x, odd_y = mirrored()
    for index, (px, py) in enumerate(COLUMNS):
        place = (px ^ odd_x, py ^ odd_y)
        for z in (0, 1):
            blocks = []
            for slots, _, _ in around(px, py):
                slot = slot_here(slots[z], odd_x, odd_y)
                block = a_ref[place + (z, slot)]
                if slots[z] > 0:
                    present = links_ref[place + (z, slot - 1)] == 1
                    block = jnp.where(present, block, jnp.zeros_like(block))
                blocks.append(block)
            for pair in range(3):
                out_ref[index, z * B : (z + 1) * B, pair * PAIR : (pair + 1) * PAIR] = pair_lanes(
                    blocks[2 * pair], blocks[2 * pair + 1]
                )


def main_kernel(
    a_ref,
    rows_ref,
    meta_ref,
    x_first,
    x_second,
    y_first,
    y_second,
    c_first,
    c_second,
    to_y_first,
    to_y_second,
    to_c_first,
    to_c_second,
    rest_ref,
    right,
    image,
    left_star,
    left_corner,
):
    from_x = {1: x_first, -1: x_second}
    from_y = {1: y_first, -1: y_second}
    notes = {(0, 0): meta_ref[...]}
    corner_notes = {}
    for side in (-1, 1):
        notes[side, 0] = from_x[side][BODY : BODY + TAIL, :].astype(jnp.float32)
        notes[0, side] = from_y[side][BODY : BODY + TAIL, :].astype(jnp.float32)
    for ref, oy in ((c_first, 1), (c_second, -1)):
        corner_notes[1, oy] = ref[0:TAIL, :].astype(jnp.float32)
        corner_notes[-1, oy] = ref[TAIL : 2 * TAIL, :].astype(jnp.float32)

    def there(ox, oy, px, py):
        return (1 - px if ox else px, 1 - py if oy else py)

    def slot_there(ox, oy, m):
        m = SIDES_X[m] if ox else m
        return SIDES_Y[m] if oy else m

    def state_row(ox, oy, px, py):
        index = COLUMNS.index(there(ox, oy, px, py))
        note = corner_notes[ox, oy] if ox and oy else notes[ox, oy]
        return note[index : index + 1]

    def link_row(ox, oy, px, py, m):
        if (ox, oy) == (0, 0):
            index = 6 * COLUMNS.index((px, py))
        else:
            index = 6 * (py if ox else px)
        index += 4 + slot_there(ox, oy, m) - 1
        return notes[ox, oy][index : index + 1]

    def block(ox, oy, px, py, m, chunk):
        start = slot_there(ox, oy, m) * B + chunk * 16
        if (ox, oy) == (0, 0):
            return rows_ref[COLUMNS.index((px, py)), start : start + 16, :]
        start += (py if ox else px) * BLOCK_ROWS
        ref = from_x[ox] if ox else from_y[oy]
        return ref[start : start + 16, :]

    def box_rows(ox, oy, px, py):
        weights = []
        for m, (dx, dy) in enumerate(FACES):
            bx, nx = divmod(2 * ox + px + dx, 2)
            by, ny = divmod(2 * oy + py + dy, 2)
            state = state_row(bx, by, nx, ny)
            if m >= 5:
                state = swap_halves(state)
            rows = []
            for kind in range(3):
                weight = jnp.where(state == kind, 1.0, 0.0)
                if m > 0:
                    weight = weight * link_row(ox, oy, px, py, m)
                rows.append(jnp.broadcast_to(weight, (16, PAIR)))
            weights.append(rows)
        reach = targets(px, py)
        chunks = {t: [] for t in box_set(px, py)}
        for chunk in range(4):
            values = [block(ox, oy, px, py, m, chunk).astype(jnp.float32) for m in range(7)]
            for t in chunks:
                total = None
                for m in range(7):
                    for kind in range(3):
                        if reach[m][kind] == t:
                            term = values[m] * weights[m][kind]
                            total = term if total is None else total + term
                chunks[t].append(total)
        return {t: jnp.concatenate(parts, axis=0) for t, parts in chunks.items()}

    images = {column: image_set(*column) for column in COLUMNS}
    users = {}
    for index, column in enumerate(COLUMNS):
        for place, (_, box, other) in enumerate(around(*column)):
            users.setdefault((box, other), []).append((index, column, place))
            reached = {(box[0] + tx, box[1] + ty) for tx, ty in box_set(*other)}
            for position, s in enumerate(images[column]):
                if s not in reached:
                    right[index, place * B : (place + 1) * B, position * PAIR : (position + 1) * PAIR] = jnp.zeros(
                        (B, PAIR), jnp.bfloat16
                    )
    for (box, other), uses in users.items():
        found = box_rows(*box, *other)
        own = COLUMNS.index(other)
        for t, value in found.items():
            rounded = value.astype(jnp.bfloat16)
            for index, column, place in uses:
                position = images[column].index((box[0] + t[0], box[1] + t[1]))
                stored = swap_halves(value).astype(jnp.bfloat16) if place == 5 else rounded
                right[index, place * B : (place + 1) * B, position * PAIR : (position + 1) * PAIR] = stored
            if box == (0, 0):
                turned = value.T
                turned = pair_lanes(turned[:B], turned[B:]).astype(jnp.bfloat16)
                if t in STAR:
                    left_star[STAR.index(t) * B : (STAR.index(t) + 1) * B, own * PAIR : (own + 1) * PAIR] = turned
                else:
                    left_corner[own] = turned
    half = low_half((B, PAIR))
    for index, column in enumerate(COLUMNS):
        product = jnp.dot(a_ref[index], right[index], preferred_element_type=jnp.float32)

        def part(s, z):
            if s not in images[column]:
                return jnp.zeros((B, PAIR), jnp.float32)
            position = images[column].index(s)
            return product[z * B : (z + 1) * B, position * PAIR : (position + 1) * PAIR]

        for pair in range(IMAGE_PAIRS):
            one = IMAGE[2 * pair]
            two = IMAGE[2 * pair + 1] if 2 * pair + 1 < len(IMAGE) else None
            low = jnp.where(half, part(one, 0), swap_halves(part(two, 0)))
            high = jnp.where(half, swap_halves(part(one, 1)), part(two, 1))
            start = index * PAIR
            lanes = slice(pair * PAIR, (pair + 1) * PAIR)
            image[start : start + B, lanes] = low.astype(jnp.bfloat16)
            image[start + B : start + PAIR, lanes] = high.astype(jnp.bfloat16)
    folded_half = low_half((HALF, PAIR))

    def fold(product):
        blocks = {}
        for pair in range(IMAGE_PAIRS):
            tile = product[:, pair * PAIR : (pair + 1) * PAIR]
            top, bottom = tile[:HALF], tile[HALF:]
            blocks[IMAGE[2 * pair]] = jnp.where(folded_half, top, swap_halves(bottom))
            if 2 * pair + 1 < len(IMAGE):
                blocks[IMAGE[2 * pair + 1]] = jnp.where(folded_half, swap_halves(top), bottom)
        return blocks

    def contribution(t):
        if t in STAR:
            rows = STAR.index(t) * B
            product = jnp.dot(left_star[rows : rows + B, :], image[...], preferred_element_type=jnp.float32)
        else:
            index = COLUMNS.index(column_of(*t))
            product = jnp.dot(
                left_corner[index], image[index * PAIR : (index + 1) * PAIR, :], preferred_element_type=jnp.float32
            )
        return fold(product)

    for ref, sent in (
        (to_y_first, TO_Y_FIRST),
        (to_y_second, TO_Y_SECOND),
        (to_c_first, TO_C_FIRST),
        (to_c_second, TO_C_SECOND),
    ):
        parts = {t: contribution(t) for t in sorted({t for t, _ in sent})}
        for row, (t, s) in enumerate(sent):
            ref[row * HALF : (row + 1) * HALF, :] = parts[t][s].astype(jnp.bfloat16)
    for group, tx in enumerate((0, -1, 1)):
        parts = contribution((tx, 0))
        for position, s in enumerate(IMAGE):
            rest_ref[group, position] = parts[s]


def message_block(ref, row):
    return ref[row * HALF : (row + 1) * HALF, :].astype(jnp.float32)


def relay_kernel(rest_ref, y_first, x_first, x_second):
    for ref, tx in ((x_first, 1), (x_second, -1)):
        arrived = relayed(tx)
        for row, s in enumerate(TO_X[tx]):
            value = None
            if s in IMAGE:
                value = rest_ref[(0, -1, 1).index(tx), IMAGE.index(s)]
            if s in arrived:
                more = message_block(y_first, arrived[s])
                value = more if value is None else value + more
            ref[row * HALF : (row + 1) * HALF, :] = value.astype(jnp.bfloat16)


def own_kernel(rest_ref, y_first, own_ref, out_hbm, zeros, sems):
    zeros[...] = jnp.zeros(zeros.shape, zeros.dtype)
    copies = []
    for jx in range(-3, 4):
        width = abs(jx)
        if width:
            for start in (0, 7 - width):
                copies.append(
                    pltpu.make_async_copy(
                        zeros.at[pl.ds(0, width)], out_hbm.at[jx + 3, pl.ds(start, width)], sems.at[len(copies)]
                    )
                )
    for copy in copies:
        copy.start()
    arrived = relayed(0)
    for position, s in enumerate(OWN):
        value = None
        if s in IMAGE:
            value = rest_ref[0, IMAGE.index(s)]
        if s in arrived:
            more = message_block(y_first, arrived[s])
            value = more if value is None else value + more
        own_ref[position] = value
    for copy in copies:
        copy.wait()


def finish_kernel(own_ref, y_second, c_first, c_second, x_first, x_second, _, out_hbm, rows, sems):
    odd_x, odd_y = mirrored()
    x, y = lax.axis_index("sx"), lax.axis_index("sy")
    has_x = ((x > 0) & (x < lax.axis_size("sx") - 1)).astype(jnp.float32)
    has_y = ((y > 0) & (y < lax.axis_size("sy") - 1)).astype(jnp.float32)
    terms = {block: [] for block in STENCIL}
    for position, block in enumerate(OWN):
        terms[block].append((own_ref, position, None))
    for row, s in enumerate(TO_X[1]):
        terms[1 - s[0], s[1]].append((x_first, row, None))
    for row, s in enumerate(TO_X[-1]):
        terms[-1 - s[0], s[1]].append((x_second, row, has_x))
    for row, (_, s) in enumerate(TO_Y_SECOND):
        terms[s[0], -1 - s[1]].append((y_second, row, has_y))
    for row, (_, s) in enumerate(TO_C_FIRST):
        terms[1 - s[0], -1 - s[1]].append((c_first, row, has_y))
    for row, (_, s) in enumerate(TO_C_SECOND):
        terms[-1 - s[0], -1 - s[1]].append((c_second, row, has_x * has_y))
    copies = []
    for jx in (0, 1, -1, 2, -2, 3, -3):
        row_here = jnp.where(odd_x == 1, 3 - jx, 3 + jx)
        reach = 3 - abs(jx)
        for jy in range(-reach, reach + 1):
            value = None
            for ref, row, flag in terms[jx, jy]:
                more = ref[row] if ref is own_ref else message_block(ref, row)
                if flag is not None:
                    more = more * flag
                value = more if value is None else value + more
            column_here = jnp.where(odd_y == 1, 3 - jy, 3 + jy)
            rows[jx + 3, column_here, 0:HALF, :] = value[:, :B].astype(jnp.bfloat16)
            rows[jx + 3, column_here, HALF:B, :] = swap_halves(value)[:, :B].astype(jnp.bfloat16)
        span = pl.ds(3 - reach, 2 * reach + 1)
        copy = pltpu.make_async_copy(rows.at[jx + 3, span], out_hbm.at[row_here, span], sems.at[jx + 3])
        copy.start()
        copies.append(copy)
    for copy in copies:
        copy.wait()


def swapped(value, move_x, move_y):
    count_x, count_y = lax.axis_size("sx"), lax.axis_size("sy")

    def partner(index, move, count):
        if move == 0:
            return index
        found = index ^ 1 if move == 1 else ((index + 1) ^ 1) - 1
        return found if 0 <= found < count else None

    pairs = []
    for x in range(count_x):
        for y in range(count_y):
            to_x, to_y = partner(x, move_x, count_x), partner(y, move_y, count_y)
            if to_x is None and to_y is None:
                to_x, to_y = x, count_y - 1 - y
            elif to_x is None:
                to_x, to_y = x, (y ^ 1 if move_y == 0 else to_y)
            elif to_y is None:
                to_x, to_y = (x ^ 1 if move_x == 0 else to_x), y
            pairs.append((x * count_y + y, to_x * count_y + to_y))
    return lax.ppermute(value, ("sx", "sy"), pairs)


SMEM = pl.BlockSpec(memory_space=pltpu.SMEM)
VMEM = pl.BlockSpec(memory_space=pltpu.VMEM)
HBM = pl.BlockSpec(memory_space=pl.ANY)


def call(kernel, in_specs, outs, scratch=(), out_specs=None, aliases=None):
    return pl.pallas_call(
        kernel,
        out_shape=[jax.ShapeDtypeStruct(shape, dtype) for shape, dtype in outs],
        in_specs=in_specs,
        out_specs=out_specs or [VMEM] * len(outs),
        scratch_shapes=list(scratch),
        input_output_aliases=aliases or {},
        compiler_params=pltpu.CompilerParams(vmem_limit_bytes=VMEM_LIMIT),
    )


def per_device(fine_matrix, prolongator, aggregate, face_links):
    bf16, f32 = jnp.bfloat16, jnp.float32
    message = ((BODY + TAIL, PAIR), bf16)
    rows, meta, x_first, x_second, y_first, y_second = call(
        functools.partial(pack_kernel, lax.axis_size("sy")),
        [HBM, HBM, HBM],
        [((4, BLOCK_ROWS, PAIR), bf16), ((32, PAIR), f32), message, message, message, message],
        [
            pltpu.VMEM((4, 2, 7, B, B), bf16),
            pltpu.SMEM((2, 2, 2), jnp.int32),
            pltpu.SMEM((2, 2, 2, 6), jnp.int32),
            pltpu.SemaphoreType.DMA((4,)),
            pltpu.SemaphoreType.DMA((2,)),
        ],
    )(aggregate, face_links, prolongator)
    x_first, x_second = swapped(x_first, 1, 0), swapped(x_second, 2, 0)
    y_first, y_second = swapped(y_first, 0, 1), swapped(y_second, 0, 2)
    notes = jnp.concatenate([x_first[BODY:], x_second[BODY:]], axis=0)
    c_first, c_second = swapped(notes, 0, 1), swapped(notes, 0, 2)
    (matrix,) = call(pack_matrix_kernel, [SMEM, VMEM], [((4, PAIR, 6 * B), bf16)])(face_links, fine_matrix)

    def sent(blocks):
        return ((len(blocks) * HALF, PAIR), bf16)

    y_first, y_second, c_first, c_second, rest = call(
        main_kernel,
        [VMEM] * 9,
        [
            sent(TO_Y_FIRST),
            sent(TO_Y_SECOND),
            sent(TO_C_FIRST),
            sent(TO_C_SECOND),
            ((3, len(IMAGE), HALF, PAIR), f32),
        ],
        [
            pltpu.VMEM((4, 6 * B, 10 * PAIR), bf16),
            pltpu.VMEM((4 * PAIR, IMAGE_PAIRS * PAIR), bf16),
            pltpu.VMEM((len(STAR) * B, 4 * PAIR), bf16),
            pltpu.VMEM((4, B, PAIR), bf16),
        ],
    )(matrix, rows, meta, x_first, x_second, y_first, y_second, c_first, c_second)
    y_second = swapped(y_second, 0, 2)
    c_first, c_second = swapped(c_first, 1, 2), swapped(c_second, 2, 2)
    y_first = swapped(y_first, 0, 1)
    x_first, x_second = call(relay_kernel, [VMEM] * 2, [sent(TO_X[1]), sent(TO_X[-1])])(rest, y_first)
    x_first, x_second = swapped(x_first, 1, 0), swapped(x_second, 2, 0)
    whole = ((7, 7, B, B), bf16)
    own, out = call(
        own_kernel,
        [VMEM] * 2,
        [((len(OWN), HALF, PAIR), f32), whole],
        [pltpu.VMEM((3, B, B), bf16), pltpu.SemaphoreType.DMA((12,))],
        [VMEM, HBM],
    )(rest, y_first)
    (out,) = call(
        finish_kernel,
        [VMEM] * 6 + [HBM],
        [whole],
        [pltpu.VMEM((7, 7, B, B), bf16), pltpu.SemaphoreType.DMA((7,))],
        [HBM],
        {6: 0},
    )(own, y_second, c_first, c_second, x_first, x_second, out)
    return out[None, None]


def solution(mesh):
    return jax.shard_map(
        per_device,
        mesh=mesh,
        in_specs=(
            P("sx", "sy", None, None, None, None),
            P("sx", "sy", None, None, None, None),
            P("sx", "sy", None),
            P("sx", "sy", None, None),
        ),
        out_specs=P("sx", "sy", None, None, None, None),
        check_vma=False,
    )
```

time: 42.9 us -> 33.8 us (0.79)
  the two profiles are of different devices: /device:TPU:20 before, /device:TPU:11 now
where the time goes in v2:
time: 33.8 us; the launch traced here: 33.6 us
  starting transfers between devices  15.3 us (45%)
  waiting for transfers between devices  8.05 us (24%)
  Pallas kernels  7.54 us (22%)
  local copies, waits for them, and re-layouts  2.55 us (8%)
    ppermute x12, starting transfers between devices, swapped(): return lax.ppermute(value, ('sx', 'sy'), pairs)  15.3 us
    ppermute x12, waiting for transfers between devices, swapped(): return lax.ppermute(value, ('sx', 'sy'), pairs)  8.05 us
    pallas_call x1, Pallas kernels, per_device(): call(main_kernel, [VMEM] * 9, [sent(TO_Y_FIRST), sent(TO_Y_SECOND), sent(...  3.1 us
    unnamed x8, local copies, waits for them, and re-layouts  2.55 us
    pallas_call x1, Pallas kernels, per_device(): call(functools.partial(pack_kernel, lax.axis_size('sy')), [HBM, HBM, HBM]...  1.81 us
    pallas_call x1, Pallas kernels, per_device(): call(finish_kernel, [VMEM] * 6 + [HBM], [whole], [pltpu.VMEM((7, 7, B, B)...  0.94 us
    pallas_call x1, Pallas kernels, per_device(): call(own_kernel, [VMEM] * 2, [((len(OWN), HALF, PAIR), f32), whole], [plt...  0.84 us
    pallas_call x1, Pallas kernels, per_device(): call(pack_matrix_kernel, [SMEM, VMEM], [((4, PAIR, 6 * B), bf16)])  0.82 us
  transfers between devices with their start and end apart: 12, of which 7 were waited for; matrix products, arithmetic and copies ran while one was open for 0% of the time, Pallas kernels for 5%

profile of v2, /device:TPU:11, one launch (start us, length us, event | category | flops | bytes accessed | tf_op | source)
XLA Modules:
  0.0 33.6 jit_solution(1109817037866133376)
XLA Ops:
  0.0 0.0 copy-start
  0.0 1.2 %copy-done = bf16[2,2,2,7,64,64]{5,4,3,2,1,0:T(8,128)(2,1)S(1)} copy-done((bf16[2,2,2,7,64,64]{5,4,3,2,1,0:T(8,128)(2,1)S(1)}, bf16[2,2,2,7,64,64]{5,4,3,2,1,0:T(8,128)(2,1)}, u32[]{:S(2)}) %copy-start) | copy-done | bytes 458776
  1.2 0.0 copy-start.2
  1.2 0.7 %copy-done.2 = s32[2,2,2,6]{3,2,1,0:T(2,128)S(1)} copy-done((s32[2,2,2,6]{3,2,1,0:T(2,128)S(1)}, s32[2,2,2,6]{3,2,1,0:T(2,128)}, u32[]{:S(2)}) %copy-start.2) | copy-done | bytes 216
  1.9 0.0 copy-start.3
  1.9 0.7 %copy-done.3 = s32[2,2,2]{2,1,0:T(2,128)S(1)} copy-done((s32[2,2,2]{2,1,0:T(2,128)S(1)}, s32[2,2,2]{2,1,0:T(2,128)}, u32[]{:S(2)}) %copy-start.3) | copy-done | bytes 56
  2.5 0.0 copy-start.1
  2.6 1.8 %shard_map.47 = (bf16[4,448,128]{2,1,0:T(8,128)(2,1)S(1)}, f32[32,128]{1,0:T(8,128)S(1)}, bf16[912,128]{1,0:T(8,128)(2,1)S(1)}, bf16[912,128]{1,0:T(8,128)(2,1)S...) custom-call(s32[2,2,2]{2,1,0:T(2,128)S(1)} %copy-done.3, s32[2,2,2,6]{3,2,1,0:T(2,128)S(1)} %copy-done.2, ...), custom_call_target="tpu_custom_call" | custom-call | tf_op jit(solution)/shard_map/pallas_call | solution.py:503
  4.4 0.2 collective-permute-start
  4.6 2.4 %collective-permute-start.1 = (bf16[912,128]{1,0:T(8,128)(2,1)S(1)}, bf16[912,128]{1,0:T(8,128)(2,1)S(1)}, u32[]{:S(2)}, u32[]{:S(2)}) collective-permute-start(bf16[912,128]{1,0:T(8,128)(2,1)S(1)} %get-tuple-element.23), channel_id=1, source_target_pairs={{0,1},{1,0},{2,3},{3,2},{4,5},{5,4},{6,7},{7,6},{8,16},{9,17},{10,... | collective-permute-start | bytes 700424 | tf_op jit(solution)/shard_map/ppermute | solution.py:480
  7.0 1.2 %collective-permute-start.2 = (bf16[912,128]{1,0:T(8,128)(2,1)S(1)}, bf16[912,128]{1,0:T(8,128)(2,1)S(1)}, u32[]{:S(2)}, u32[]{:S(2)}) collective-permute-start(bf16[912,128]{1,0:T(8,128)(2,1)S(1)} %get-tuple-element.24), channel_id=1, source_target_pairs={{0,1},{1,0},{2,3},{3,2},{4,5},{5,4},{6,7},{7,6},{8,9},{9,8},{10,11... | collective-permute-start | bytes 700424 | tf_op jit(solution)/shard_map/ppermute | solution.py:480
  8.3 1.1 %collective-permute-start.3 = (bf16[912,128]{1,0:T(8,128)(2,1)S(1)}, bf16[912,128]{1,0:T(8,128)(2,1)S(1)}, u32[]{:S(2)}, u32[]{:S(2)}) collective-permute-start(bf16[912,128]{1,0:T(8,128)(2,1)S(1)} %get-tuple-element.25), channel_id=1, source_target_pairs={{0,8},{1,2},{2,1},{3,4},{4,3},{5,6},{6,5},{7,15},{8,0},{9,10},{10,... | collective-permute-start | bytes 700424 | tf_op jit(solution)/shard_map/ppermute | solution.py:480
  9.4 1.6 %collective-permute-done.x_first = bf16[912,128]{1,0:T(8,128)(2,1)S(1)} collective-permute-done((bf16[912,128]{1,0:T(8,128)(2,1)S(1)}, bf16[912,128]{1,0:T(8,128)(2,1)S(1)}, u32[]{:S(2)}, u32[]{:S(2)}) %collective-permute-start) | collective-permute-done | bytes 233504 | tf_op jit(solution)/shard_map/ppermute | solution.py:480
  11.0 1.1 %collective-permute-done.1.x_second = bf16[912,128]{1,0:T(8,128)(2,1)S(1)} collective-permute-done((bf16[912,128]{1,0:T(8,128)(2,1)S(1)}, bf16[912,128]{1,0:T(8,128)(2,1)S(1)}, u32[]{:S(2)}, u32[]{:S(2)}) %collective-permute-start.1) | collective-permute-done | bytes 233504 | tf_op jit(solution)/shard_map/ppermute | solution.py:480
  12.1 2.6 %collective-permute-start.5 = (bf16[32,128]{1,0:T(8,128)(2,1)S(1)}, bf16[32,128]{1,0:T(8,128)(2,1)S(1)}, u32[]{:S(2)}, u32[]{:S(2)}) collective-permute-start(bf16[32,128]{1,0:T(8,128)(2,1)S(1)} %pad_maximum_fusion), channel_id=1, source_target_pairs={{0,8},{1,2},{2,1},{3,4},{4,3},{5,6},{6,5},{7,15},{8,0},{9,10},{10,... | collective-permute-start | bytes 24584 | tf_op jit(solution)/shard_map/ppermute | solution.py:480
  14.8 0.0 collective-permute-start.4
  14.8 0.0 copy-done.1
  14.8 0.8 %shard_map.46.a_ref = bf16[4,128,384]{2,1,0:T(8,128)(2,1)S(1)} custom-call(s32[2,2,2,6]{3,2,1,0:T(2,128)S(1)} %copy-done.2, bf16[2,2,2,7,64,64]{5,4,3,2,1,0:T(8,128)(2,1)S(1)} %copy-done.1), custom_call_target="tpu_custom_call" | custom-call | tf_op jit(solution)/shard_map/pallas_call | solution.py:519
  15.6 0.0 collective-permute-done.2.y_first
  15.6 0.9 %collective-permute-done.3.y_second = bf16[912,128]{1,0:T(8,128)(2,1)S(1)} collective-permute-done((bf16[912,128]{1,0:T(8,128)(2,1)S(1)}, bf16[912,128]{1,0:T(8,128)(2,1)S(1)}, u32[]{:S(2)}, u32[]{:S(2)}) %collective-permute-start.3) | collective-permute-done | bytes 233504 | tf_op jit(solution)/shard_map/ppermute | solution.py:480
  16.5 0.1 collective-permute-done.5.c_second
  16.6 0.0 collective-permute-done.4.c_first
  16.6 3.1 %shard_map.48 = (bf16[1056,128]{1,0:T(8,128)(2,1)S(1)}, bf16[416,128]{1,0:T(8,128)(2,1)S(1)}, bf16[320,128]{1,0:T(8,128)(2,1)S(1)}, bf16[320,128]{1,0:T(8,128)(2,1)S(1)}, f32[3,13,32,128]{3,2,1,0:T(8,128)S(1)}) custom-call(bf16[4,128,384]{2,1,0:T(8,128)(2,1)S(1)} %shard_map.46.a_ref, bf16[4,448,128]{2,1,0:T(8,128)(2,1)S(1)} %get-tuple-element.20.rows_ref, ...), custom_call_target="tpu_custom_call" | custom-call | tf_op jit(solution)/shard_map/pallas_call | solution.py:524
  19.7 0.2 collective-permute-start.6
  19.9 1.4 %collective-permute-done.6.y_first = bf16[1056,128]{1,0:T(8,128)(2,1)S(1)} collective-permute-done((bf16[1056,128]{1,0:T(8,128)(2,1)S(1)}, bf16[1056,128]{1,0:T(8,128)(2,1)S(1)}, u32[]{:S(2)}, u32[]{:S(2)}) %collective-permute-start.6) | collective-permute-done | bytes 270368 | tf_op jit(solution)/shard_map/ppermute | solution.py:480
  21.4 0.1 collective-permute-start.10
  21.5 1.3 %collective-permute-start.11 = (bf16[480,128]{1,0:T(8,128)(2,1)S(1)}, bf16[480,128]{1,0:T(8,128)(2,1)S(1)}, u32[]{:S(2)}, u32[]{:S(2)}) collective-permute-start(bf16[480,128]{1,0:T(8,128)(2,1)S(1)} %get-tuple-element.33), channel_id=1, source_target_pairs={{0,1},{1,0},{2,3},{3,2},{4,5},{5,4},{6,7},{7,6},{8,16},{9,17},{10,... | collective-permute-start | bytes 368648 | tf_op jit(solution)/shard_map/ppermute | solution.py:480
  22.8 2.9 %collective-permute-start.7 = (bf16[416,128]{1,0:T(8,128)(2,1)S(1)}, bf16[416,128]{1,0:T(8,128)(2,1)S(1)}, u32[]{:S(2)}, u32[]{:S(2)}) collective-permute-start(bf16[416,128]{1,0:T(8,128)(2,1)S(1)} %get-tuple-element.29), channel_id=1, source_target_pairs={{0,8},{1,2},{2,1},{3,4},{4,3},{5,6},{6,5},{7,15},{8,0},{9,10},{10,... | collective-permute-start | bytes 319496 | tf_op jit(solution)/shard_map/ppermute | solution.py:480
  25.7 0.0 collective-permute-start.8
  25.7 3.2 %collective-permute-start.9 = (bf16[320,128]{1,0:T(8,128)(2,1)S(1)}, bf16[320,128]{1,0:T(8,128)(2,1)S(1)}, u32[]{:S(2)}, u32[]{:S(2)}) collective-permute-start(bf16[320,128]{1,0:T(8,128)(2,1)S(1)} %get-tuple-element.31), channel_id=1, source_target_pairs={{0,7},{1,2},{2,1},{3,4},{4,3},{5,6},{6,5},{7,0},{8,16},{9,18},{10,... | collective-permute-start | bytes 245768 | tf_op jit(solution)/shard_map/ppermute | solution.py:480
  28.9 0.8 %shard_map.49 = (f32[18,32,128]{2,1,0:T(8,128)S(1)}, bf16[7,7,64,64]{3,2,1,0:T(8,128)(2,1)}) custom-call(f32[3,13,32,128]{3,2,1,0:T(8,128)S(1)} %get-tuple-element.26.rest_ref, bf16[1056,128]{1,0:T(8,128)(2,1)S(1)} %collective-permute-done.6.y_first), custom_call_target="tpu_custom_call" | custom-call | tf_op jit(solution)/shard_map/pallas_call | solution.py:547
  29.7 2.8 %collective-permute-done.8.c_first = bf16[320,128]{1,0:T(8,128)(2,1)S(1)} collective-permute-done((bf16[320,128]{1,0:T(8,128)(2,1)S(1)}, bf16[320,128]{1,0:T(8,128)(2,1)S(1)}, u32[]{:S(2)}, u32[]{:S(2)}) %collective-permute-start.8) | collective-permute-done | bytes 81952 | tf_op jit(solution)/shard_map/ppermute | solution.py:480
  32.5 0.1 collective-permute-done.9.c_second
  32.6 0.0 collective-permute-done.7.y_second
  32.6 0.0 collective-permute-done.10.x_first
  32.6 0.0 collective-permute-done.11.x_second
  32.6 0.9 %shard_map.51 = bf16[7,7,64,64]{3,2,1,0:T(8,128)(2,1)} custom-call(f32[18,32,128]{2,1,0:T(8,128)S(1)} %get-tuple-element.28.own_ref, bf16[416,128]{1,0:T(8,128)(2,1)S(1)} %collective-permute-done.7.y_second, bf16[320,128]{1,0:T(8,128)(2,1)S(1)} %collective-permute-done.8.c_first, ...), custom_call_target="tpu_custom_call", output_to_operand_aliasing={{}: (6, {})} | custom-call | tf_op jit(solution)/shard_map/pallas_call | solution.py:554
  (4 shorter events, 0.0 us)
Async XLA Ops:
  0.0 1.2 %copy-start = (bf16[2,2,2,7,64,64]{5,4,3,2,1,0:T(8,128)(2,1)S(1)}, bf16[2,2,2,7,64,64]{5,4,3,2,1,0:T(8,128)(2,1)}, u32[]{:S(2)}) copy-start(bf16[2,2,2,7,64,64]{5,4,3,2,1,0:T(8,128)(2,1)} %p_hbm.1) | copy-start | bytes 1376260
  1.2 0.7 %copy-start.2 = (s32[2,2,2,6]{3,2,1,0:T(2,128)S(1)}, s32[2,2,2,6]{3,2,1,0:T(2,128)}, u32[]{:S(2)}) copy-start(s32[2,2,2,6]{3,2,1,0:T(2,128)} %links_hbm.1) | copy-start | bytes 580
  1.9 0.7 %copy-start.3 = (s32[2,2,2]{2,1,0:T(2,128)S(1)}, s32[2,2,2]{2,1,0:T(2,128)}, u32[]{:S(2)}) copy-start(s32[2,2,2]{2,1,0:T(2,128)} %aggregate_hbm.1) | copy-start | bytes 100
  2.5 12.2 %copy-start.1 = (bf16[2,2,2,7,64,64]{5,4,3,2,1,0:T(8,128)(2,1)S(1)}, bf16[2,2,2,7,64,64]{5,4,3,2,1,0:T(8,128)(2,1)}, u32[]{:S(2)}) copy-start(bf16[2,2,2,7,64,64]{5,4,3,2,1,0:T(8,128)(2,1)} %a_ref.1) | copy-start | bytes 1376260
  4.4 6.6 %collective-permute-start = (bf16[912,128]{1,0:T(8,128)(2,1)S(1)}, bf16[912,128]{1,0:T(8,128)(2,1)S(1)}, u32[]{:S(2)}, u32[]{:S(2)}) collective-permute-start(bf16[912,128]{1,0:T(8,128)(2,1)S(1)} %get-tuple-element.22), channel_id=1, source_target_pairs={{0,8},{1,9},{2,10},{3,11},{4,12},{5,13},{6,14},{7,15},{8,0},{9,1},... | collective-permute-start | bytes 700424 | tf_op jit(solution)/shard_map/ppermute | solution.py:480
  4.6 7.5 %collective-permute-start.1 = (bf16[912,128]{1,0:T(8,128)(2,1)S(1)}, bf16[912,128]{1,0:T(8,128)(2,1)S(1)}, u32[]{:S(2)}, u32[]{:S(2)}) collective-permute-start(bf16[912,128]{1,0:T(8,128)(2,1)S(1)} %get-tuple-element.23), channel_id=1, source_target_pairs={{0,1},{1,0},{2,3},{3,2},{4,5},{5,4},{6,7},{7,6},{8,16},{9,17},{10,... | collective-permute-start | bytes 700424 | tf_op jit(solution)/shard_map/ppermute | solution.py:480
  7.0 8.6 %collective-permute-start.2 = (bf16[912,128]{1,0:T(8,128)(2,1)S(1)}, bf16[912,128]{1,0:T(8,128)(2,1)S(1)}, u32[]{:S(2)}, u32[]{:S(2)}) collective-permute-start(bf16[912,128]{1,0:T(8,128)(2,1)S(1)} %get-tuple-element.24), channel_id=1, source_target_pairs={{0,1},{1,0},{2,3},{3,2},{4,5},{5,4},{6,7},{7,6},{8,9},{9,8},{10,11... | collective-permute-start | bytes 700424 | tf_op jit(solution)/shard_map/ppermute | solution.py:480
  8.3 8.3 %collective-permute-start.3 = (bf16[912,128]{1,0:T(8,128)(2,1)S(1)}, bf16[912,128]{1,0:T(8,128)(2,1)S(1)}, u32[]{:S(2)}, u32[]{:S(2)}) collective-permute-start(bf16[912,128]{1,0:T(8,128)(2,1)S(1)} %get-tuple-element.25), channel_id=1, source_target_pairs={{0,8},{1,2},{2,1},{3,4},{4,3},{5,6},{6,5},{7,15},{8,0},{9,10},{10,... | collective-permute-start | bytes 700424 | tf_op jit(solution)/shard_map/ppermute | solution.py:480
  12.1 4.5 %collective-permute-start.5 = (bf16[32,128]{1,0:T(8,128)(2,1)S(1)}, bf16[32,128]{1,0:T(8,128)(2,1)S(1)}, u32[]{:S(2)}, u32[]{:S(2)}) collective-permute-start(bf16[32,128]{1,0:T(8,128)(2,1)S(1)} %pad_maximum_fusion), channel_id=1, source_target_pairs={{0,8},{1,2},{2,1},{3,4},{4,3},{5,6},{6,5},{7,15},{8,0},{9,10},{10,... | collective-permute-start | bytes 24584 | tf_op jit(solution)/shard_map/ppermute | solution.py:480
  14.8 1.8 %collective-permute-start.4 = (bf16[32,128]{1,0:T(8,128)(2,1)S(1)}, bf16[32,128]{1,0:T(8,128)(2,1)S(1)}, u32[]{:S(2)}, u32[]{:S(2)}) collective-permute-start(bf16[32,128]{1,0:T(8,128)(2,1)S(1)} %pad_maximum_fusion), channel_id=1, source_target_pairs={{0,1},{1,0},{2,3},{3,2},{4,5},{5,4},{6,7},{7,6},{8,9},{9,8},{10,11... | collective-permute-start | bytes 24584 | tf_op jit(solution)/shard_map/ppermute | solution.py:480
  19.7 1.6 %collective-permute-start.6 = (bf16[1056,128]{1,0:T(8,128)(2,1)S(1)}, bf16[1056,128]{1,0:T(8,128)(2,1)S(1)}, u32[]{:S(2)}, u32[]{:S(2)}) collective-permute-start(bf16[1056,128]{1,0:T(8,128)(2,1)S(1)} %get-tuple-element.27), channel_id=1, source_target_pairs={{0,1},{1,0},{2,3},{3,2},{4,5},{5,4},{6,7},{7,6},{8,9},{9,8},{10,11... | collective-permute-start | bytes 811016 | tf_op jit(solution)/shard_map/ppermute | solution.py:480
  21.4 11.2 %collective-permute-start.10 = (bf16[480,128]{1,0:T(8,128)(2,1)S(1)}, bf16[480,128]{1,0:T(8,128)(2,1)S(1)}, u32[]{:S(2)}, u32[]{:S(2)}) collective-permute-start(bf16[480,128]{1,0:T(8,128)(2,1)S(1)} %get-tuple-element.32), channel_id=1, source_target_pairs={{0,8},{1,9},{2,10},{3,11},{4,12},{5,13},{6,14},{7,15},{8,0},{9,1},... | collective-permute-start | bytes 368648 | tf_op jit(solution)/shard_map/ppermute | solution.py:480
  21.5 11.2 %collective-permute-start.11 = (bf16[480,128]{1,0:T(8,128)(2,1)S(1)}, bf16[480,128]{1,0:T(8,128)(2,1)S(1)}, u32[]{:S(2)}, u32[]{:S(2)}) collective-permute-start(bf16[480,128]{1,0:T(8,128)(2,1)S(1)} %get-tuple-element.33), channel_id=1, source_target_pairs={{0,1},{1,0},{2,3},{3,2},{4,5},{5,4},{6,7},{7,6},{8,16},{9,17},{10,... | collective-permute-start | bytes 368648 | tf_op jit(solution)/shard_map/ppermute | solution.py:480
  22.8 9.8 %collective-permute-start.7 = (bf16[416,128]{1,0:T(8,128)(2,1)S(1)}, bf16[416,128]{1,0:T(8,128)(2,1)S(1)}, u32[]{:S(2)}, u32[]{:S(2)}) collective-permute-start(bf16[416,128]{1,0:T(8,128)(2,1)S(1)} %get-tuple-element.29), channel_id=1, source_target_pairs={{0,8},{1,2},{2,1},{3,4},{4,3},{5,6},{6,5},{7,15},{8,0},{9,10},{10,... | collective-permute-start | bytes 319496 | tf_op jit(solution)/shard_map/ppermute | solution.py:480
  25.7 6.9 %collective-permute-start.8 = (bf16[320,128]{1,0:T(8,128)(2,1)S(1)}, bf16[320,128]{1,0:T(8,128)(2,1)S(1)}, u32[]{:S(2)}, u32[]{:S(2)}) collective-permute-start(bf16[320,128]{1,0:T(8,128)(2,1)S(1)} %get-tuple-element.30), channel_id=1, source_target_pairs={{0,8},{1,10},{2,9},{3,12},{4,11},{5,14},{6,13},{7,15},{8,0},{9,2},... | collective-permute-start | bytes 245768 | tf_op jit(solution)/shard_map/ppermute | solution.py:480
  25.7 6.9 %collective-permute-start.9 = (bf16[320,128]{1,0:T(8,128)(2,1)S(1)}, bf16[320,128]{1,0:T(8,128)(2,1)S(1)}, u32[]{:S(2)}, u32[]{:S(2)}) collective-permute-start(bf16[320,128]{1,0:T(8,128)(2,1)S(1)} %get-tuple-element.31), channel_id=1, source_target_pairs={{0,7},{1,2},{2,1},{3,4},{4,3},{5,6},{6,5},{7,0},{8,16},{9,18},{10,... | collective-permute-start | bytes 245768 | tf_op jit(solution)/shard_map/ppermute | solution.py:480

commit v3 on v2

--- a/solution.py
+++ b/solution.py
@@ -11,15 +11,16 @@
 B = 64
 HALF = B // 2
 PAIR = 2 * B
-BLOCK_ROWS = 7 * B
+SLOTS = 6
+BLOCK_ROWS = SLOTS * B
 BODY = 2 * BLOCK_ROWS
 TAIL = 16
 VMEM_LIMIT = 48 * 1024 * 1024
 
-FACES = [(0, 0), (-1, 0), (1, 0), (0, -1), (0, 1), (0, 0), (0, 0)]
+FACES = [(0, 0), (-1, 0), (1, 0), (0, -1), (0, 1), (0, 0)]
 COLUMNS = [(0, 0), (0, 1), (1, 0), (1, 1)]
-SIDES_X = (0, 2, 1, 3, 4, 5, 6)
-SIDES_Y = (0, 1, 2, 4, 3, 5, 6)
+SIDES_X = (0, 2, 1, 3, 4, 5)
+SIDES_Y = (0, 1, 2, 4, 3, 5)
 
 
 def targets(px, py):
@@ -36,14 +37,14 @@
 
 
 def around(px, py):
-    found = [((0, 0), (0, 0), (px, py))]
+    found = [(0, (0, 0), (px, py))]
     for m in (2, 1) if px == 0 else (1, 2):
         ox, nx = divmod(px + FACES[m][0], 2)
-        found.append(((m, m), (ox, 0), (nx, py)))
+        found.append((m, (ox, 0), (nx, py)))
     for m in (4, 3) if py == 0 else (3, 4):
         oy, ny = divmod(py + FACES[m][1], 2)
-        found.append(((m, m), (0, oy), (px, ny)))
-    found.append(((6, 5), (0, 0), (px, py)))
+        found.append((m, (0, oy), (px, ny)))
+    found.append((5, (0, 0), (px, py)))
     return found
 
 
@@ -78,8 +79,14 @@
 
 
 TO_X = {tx: sorted(set(IMAGE) | set(relayed(tx))) for tx in (1, -1)}
-OWN = sorted(set(IMAGE) | set(relayed(0)))
 STENCIL = [(jx, jy) for jx in range(-3, 4) for jy in range(-3, 4) if abs(jx) + abs(jy) <= 3]
+OWN = sorted(
+    set(IMAGE)
+    | set(relayed(0))
+    | {(s[0], -1 - s[1]) for _, s in TO_Y_SECOND}
+    | {(1 - s[0], -1 - s[1]) for _, s in TO_C_FIRST}
+    | {(-1 - s[0], -1 - s[1]) for _, s in TO_C_SECOND}
+)
 
 
 def low_half(shape):
@@ -98,12 +105,12 @@
     return lax.axis_index("sx") % 2, lax.axis_index("sy") % 2
 
 
-def slot_here(m, odd_x, odd_y):
+def slot_here(m, z, odd_x, odd_y):
     if m in (1, 2):
         return jnp.where(odd_x == 1, 3 - m, m)
     if m in (3, 4):
         return jnp.where(odd_y == 1, 7 - m, m)
-    return m
+    return 6 - z if m == 5 else m
 
 
 def fill_rows(rows, values):
@@ -155,11 +162,11 @@
         return jnp.where(shift == 0, 0, jnp.where(across_x, 1, 2)).astype(jnp.float32)
 
     def link(column, m):
-        face = slot_here(m, odd_x, odd_y) - 1
-        return tuple(links_ref[place[column] + (z, face)].astype(jnp.float32) for z in (0, 1))
+        faces = [slot_here(m, z, odd_x, odd_y) - 1 for z in (0, 1)]
+        return tuple(links_ref[place[column] + (z, faces[z])].astype(jnp.float32) for z in (0, 1))
 
     states = [tuple(state(column, z) for z in (0, 1)) for column in COLUMNS]
-    links = {column: [link(column, m) for m in range(1, 7)] for column in COLUMNS}
+    links = {column: [link(column, m) for m in range(1, SLOTS)] for column in COLUMNS}
     meta_ref[...] = fill_rows(32, states + sum((links[column] for column in COLUMNS), []))
     messages = (
         (x_first, ((1, 0), (1, 1))),
@@ -172,9 +179,8 @@
         ref[BODY : BODY + TAIL, :] = tail.astype(jnp.bfloat16)
     for index, column in enumerate(COLUMNS):
         copies[index].wait()
-        for m in range(7):
-            slot = slot_here(m, odd_x, odd_y)
-            packed = pair_lanes(p_ref[index, 0, slot], p_ref[index, 1, slot])
+        for m in range(SLOTS):
+            packed = pair_lanes(*(p_ref[index, z, slot_here(m, z, odd_x, odd_y)] for z in (0, 1)))
             rows_ref[index, m * B : (m + 1) * B, :] = packed
             for ref, columns in messages:
                 if column in columns:
@@ -188,10 +194,10 @@
         place = (px ^ odd_x, py ^ odd_y)
         for z in (0, 1):
             blocks = []
-            for slots, _, _ in around(px, py):
-                slot = slot_here(slots[z], odd_x, odd_y)
+            for m, _, _ in around(px, py):
+                slot = slot_here(m, z, odd_x, odd_y)
                 block = a_ref[place + (z, slot)]
-                if slots[z] > 0:
+                if m > 0:
                     present = links_ref[place + (z, slot - 1)] == 1
                     block = jnp.where(present, block, jnp.zeros_like(block))
                 blocks.append(block)
@@ -246,9 +252,9 @@
 
     def link_row(ox, oy, px, py, m):
         if (ox, oy) == (0, 0):
-            index = 6 * COLUMNS.index((px, py))
+            index = (SLOTS - 1) * COLUMNS.index((px, py))
         else:
-            index = 6 * (py if ox else px)
+            index = (SLOTS - 1) * (py if ox else px)
         index += 4 + slot_there(ox, oy, m) - 1
         return notes[ox, oy][index : index + 1]
 
@@ -266,7 +272,7 @@
             bx, nx = divmod(2 * ox + px + dx, 2)
             by, ny = divmod(2 * oy + py + dy, 2)
             state = state_row(bx, by, nx, ny)
-            if m >= 5:
+            if m == 5:
                 state = swap_halves(state)
             rows = []
             for kind in range(3):
@@ -278,10 +284,10 @@
         reach = targets(px, py)
         chunks = {t: [] for t in box_set(px, py)}
         for chunk in range(4):
-            values = [block(ox, oy, px, py, m, chunk).astype(jnp.float32) for m in range(7)]
+            values = [block(ox, oy, px, py, m, chunk).astype(jnp.float32) for m in range(SLOTS)]
             for t in chunks:
                 total = None
-                for m in range(7):
+                for m in range(SLOTS):
                     for kind in range(3):
                         if reach[m][kind] == t:
                             term = values[m] * weights[m][kind]
@@ -390,7 +396,25 @@
             ref[row * HALF : (row + 1) * HALF, :] = value.astype(jnp.bfloat16)
 
 
-def own_kernel(rest_ref, y_first, own_ref, out_hbm, zeros, sems):
+def gathered(terms):
+    total = None
+    for ref, row, flag in terms:
+        value = message_block(ref, row) if row is not None else ref
+        if flag is not None:
+            value = value * flag
+        total = value if total is None else total + value
+    return total
+
+
+def inside():
+    x, y = lax.axis_index("sx"), lax.axis_index("sy")
+    return (
+        ((x > 0) & (x < lax.axis_size("sx") - 1)).astype(jnp.float32),
+        ((y > 0) & (y < lax.axis_size("sy") - 1)).astype(jnp.float32),
+    )
+
+
+def own_kernel(rest_ref, y_first, y_second, c_first, c_second, own_ref, out_hbm, zeros, sems):
     zeros[...] = jnp.zeros(zeros.shape, zeros.dtype)
     copies = []
     for jx in range(-3, 4):
@@ -404,48 +428,40 @@
                 )
     for copy in copies:
         copy.start()
-    arrived = relayed(0)
-    for position, s in enumerate(OWN):
-        value = None
-        if s in IMAGE:
-            value = rest_ref[0, IMAGE.index(s)]
-        if s in arrived:
-            more = message_block(y_first, arrived[s])
-            value = more if value is None else value + more
-        own_ref[position] = value
-    for copy in copies:
-        copy.wait()
-
-
-def finish_kernel(own_ref, y_second, c_first, c_second, x_first, x_second, _, out_hbm, rows, sems):
-    odd_x, odd_y = mirrored()
-    x, y = lax.axis_index("sx"), lax.axis_index("sy")
-    has_x = ((x > 0) & (x < lax.axis_size("sx") - 1)).astype(jnp.float32)
-    has_y = ((y > 0) & (y < lax.axis_size("sy") - 1)).astype(jnp.float32)
+    has_x, has_y = inside()
     terms = {block: [] for block in STENCIL}
-    for position, block in enumerate(OWN):
-        terms[block].append((own_ref, position, None))
-    for row, s in enumerate(TO_X[1]):
-        terms[1 - s[0], s[1]].append((x_first, row, None))
-    for row, s in enumerate(TO_X[-1]):
-        terms[-1 - s[0], s[1]].append((x_second, row, has_x))
+    for position, s in enumerate(IMAGE):
+        terms[s].append((rest_ref[0, position], None, None))
+    for s, row in relayed(0).items():
+        terms[s].append((y_first, row, None))
     for row, (_, s) in enumerate(TO_Y_SECOND):
         terms[s[0], -1 - s[1]].append((y_second, row, has_y))
     for row, (_, s) in enumerate(TO_C_FIRST):
         terms[1 - s[0], -1 - s[1]].append((c_first, row, has_y))
     for row, (_, s) in enumerate(TO_C_SECOND):
         terms[-1 - s[0], -1 - s[1]].append((c_second, row, has_x * has_y))
+    for position, block in enumerate(OWN):
+        own_ref[position] = gathered(terms[block])
+    for copy in copies:
+        copy.wait()
+
+
+def finish_kernel(own_ref, x_first, x_second, _, out_hbm, rows, sems):
+    odd_x, odd_y = mirrored()
+    has_x, _ = inside()
+    terms = {block: [] for block in STENCIL}
+    for position, block in enumerate(OWN):
+        terms[block].append((own_ref[position], None, None))
+    for row, s in enumerate(TO_X[1]):
+        terms[1 - s[0], s[1]].append((x_first, row, None))
+    for row, s in enumerate(TO_X[-1]):
+        terms[-1 - s[0], s[1]].append((x_second, row, has_x))
     copies = []
     for jx in (0, 1, -1, 2, -2, 3, -3):
         row_here = jnp.where(odd_x == 1, 3 - jx, 3 + jx)
         reach = 3 - abs(jx)
         for jy in range(-reach, reach + 1):
-            value = None
-            for ref, row, flag in terms[jx, jy]:
-                more = ref[row] if ref is own_ref else message_block(ref, row)
-                if flag is not None:
-                    more = more * flag
-                value = more if value is None else value + more
+            value = gathered(terms[jx, jy])
             column_here = jnp.where(odd_y == 1, 3 - jy, 3 + jy)
             rows[jx + 3, column_here, 0:HALF, :] = value[:, :B].astype(jnp.bfloat16)
             rows[jx + 3, column_here, HALF:B, :] = swap_halves(value)[:, :B].astype(jnp.bfloat16)
@@ -482,10 +498,10 @@
 
 SMEM = pl.BlockSpec(memory_space=pltpu.SMEM)
 VMEM = pl.BlockSpec(memory_space=pltpu.VMEM)
-HBM = pl.BlockSpec(memory_space=pl.ANY)
-
-
-def call(kernel, in_specs, outs, scratch=(), out_specs=None, aliases=None):
+HBM = pl.BlockSpec(memory_space=pltpu.HBM)
+
+
+def call(kernel, in_specs, outs, scratch=(), out_specs=None, aliases=None, cost=None):
     return pl.pallas_call(
         kernel,
         out_shape=[jax.ShapeDtypeStruct(shape, dtype) for shape, dtype in outs],
@@ -494,6 +510,7 @@
         scratch_shapes=list(scratch),
         input_output_aliases=aliases or {},
         compiler_params=pltpu.CompilerParams(vmem_limit_bytes=VMEM_LIMIT),
+        cost_estimate=None if cost is None else pl.CostEstimate(flops=0, bytes_accessed=cost, transcendentals=0),
     )
 
 
@@ -511,9 +528,10 @@
             pltpu.SemaphoreType.DMA((4,)),
             pltpu.SemaphoreType.DMA((2,)),
         ],
-    )(aggregate, face_links, prolongator)
+    )(*(pltpu.with_memory_space_constraint(value, pltpu.HBM) for value in (aggregate, face_links, prolongator)))
+    y_second = swapped(y_second, 0, 2)
     x_first, x_second = swapped(x_first, 1, 0), swapped(x_second, 2, 0)
-    y_first, y_second = swapped(y_first, 0, 1), swapped(y_second, 0, 2)
+    y_first = swapped(y_first, 0, 1)
     notes = jnp.concatenate([x_first[BODY:], x_second[BODY:]], axis=0)
     c_first, c_second = swapped(notes, 0, 1), swapped(notes, 0, 2)
     (matrix,) = call(pack_matrix_kernel, [SMEM, VMEM], [((4, PAIR, 6 * B), bf16)])(face_links, fine_matrix)
@@ -541,24 +559,27 @@
     y_second = swapped(y_second, 0, 2)
     c_first, c_second = swapped(c_first, 1, 2), swapped(c_second, 2, 2)
     y_first = swapped(y_first, 0, 1)
-    x_first, x_second = call(relay_kernel, [VMEM] * 2, [sent(TO_X[1]), sent(TO_X[-1])])(rest, y_first)
+    x_first, x_second = call(relay_kernel, [VMEM] * 2, [sent(TO_X[1]), sent(TO_X[-1])], cost=100_000_000)(
+        rest, y_first
+    )
     x_first, x_second = swapped(x_first, 1, 0), swapped(x_second, 2, 0)
     whole = ((7, 7, B, B), bf16)
     own, out = call(
         own_kernel,
-        [VMEM] * 2,
+        [VMEM] * 5,
         [((len(OWN), HALF, PAIR), f32), whole],
         [pltpu.VMEM((3, B, B), bf16), pltpu.SemaphoreType.DMA((12,))],
         [VMEM, HBM],
-    )(rest, y_first)
+        cost=1,
+    )(rest, y_first, y_second, c_first, c_second)
     (out,) = call(
         finish_kernel,
-        [VMEM] * 6 + [HBM],
+        [VMEM] * 3 + [HBM],
         [whole],
         [pltpu.VMEM((7, 7, B, B), bf16), pltpu.SemaphoreType.DMA((7,))],
         [HBM],
-        {6: 0},
-    )(own, y_second, c_first, c_second, x_first, x_second, out)
+        {3: 0},
+    )(own, x_first, x_second, out)
     return out[None, None]
 
 

time: 33.8 us -> 30.9 us (0.914)
  local copies, waits for them, and re-layouts: 2.55 us -> 0.01 us
  Pallas kernels: 7.54 us -> 7.09 us
    unnamed x8 -> x4, local copies, waits for them, and re-layouts: 2.55 us -> 0.01 us
  transfers between devices with their start and end apart: 12 -> 12, of which waited for: 7 -> 6; matrix products, arithmetic and copies ran while one was open for 0% -> 0% of each run, Pallas kernels for 5% -> 5%
where the time goes in v3:
time: 30.9 us; the launch traced here: 30.7 us
  starting transfers between devices  15.3 us (50%)
  waiting for transfers between devices  8.21 us (27%)
  Pallas kernels  7.09 us (23%)
    ppermute x12, starting transfers between devices, swapped(): return lax.ppermute(value, ('sx', 'sy'), pairs)  15.3 us
    ppermute x12, waiting for transfers between devices, swapped(): return lax.ppermute(value, ('sx', 'sy'), pairs)  8.21 us
    pallas_call x1, Pallas kernels, per_device(): call(main_kernel, [VMEM] * 9, [sent(TO_Y_FIRST), sent(TO_Y_SECOND), sent(...  2.98 us
    pallas_call x1, Pallas kernels, per_device(): call(functools.partial(pack_kernel, lax.axis_size('sy')), [HBM, HBM, HBM]...  1.51 us
    pallas_call x1, Pallas kernels, per_device(): call(finish_kernel, [VMEM] * 3 + [HBM], [whole], [pltpu.VMEM((7, 7, B, B)...  0.9 us
    pallas_call x1, Pallas kernels, per_device(): call(own_kernel, [VMEM] * 5, [((len(OWN), HALF, PAIR), f32), whole], [plt...  0.84 us
    pallas_call x1, Pallas kernels, per_device(): call(pack_matrix_kernel, [SMEM, VMEM], [((4, PAIR, 6 * B), bf16)])  0.82 us
  transfers between devices with their start and end apart: 12, of which 6 were waited for; matrix products, arithmetic and copies ran while one was open for 0% of the time, Pallas kernels for 5%

profile of v3, /device:TPU:11, one launch (start us, length us, event | category | flops | bytes accessed | tf_op | source)
XLA Modules:
  0.0 30.7 jit_solution(8711395275347833813)
XLA Ops:
  0.0 0.0 copy-start
  0.0 1.5 %shard_map.47 = (bf16[4,384,128]{2,1,0:T(8,128)(2,1)S(1)}, f32[32,128]{1,0:T(8,128)S(1)}, bf16[784,128]{1,0:T(8,128)(2,1)S(1)}, bf16[784,128]{1,0:T(8,128)(2,1)S...) custom-call(s32[2,2,2]{2,1,0:T(2,128)} %aggregate_hbm.1, s32[2,2,2,6]{3,2,1,0:T(2,128)} %links_hbm.1, ...), custom_call_target="tpu_custom_call" | custom-call | tf_op jit(solution)/shard_map/pallas_call | solution.py:520
  1.5 0.2 collective-permute-start
  1.8 2.4 %collective-permute-start.1 = (bf16[784,128]{1,0:T(8,128)(2,1)S(1)}, bf16[784,128]{1,0:T(8,128)(2,1)S(1)}, u32[]{:S(2)}, u32[]{:S(2)}) collective-permute-start(bf16[784,128]{1,0:T(8,128)(2,1)S(1)} %get-tuple-element.23), channel_id=1, source_target_pairs={{0,1},{1,0},{2,3},{3,2},{4,5},{5,4},{6,7},{7,6},{8,16},{9,17},{10,... | collective-permute-start | bytes 602120 | tf_op jit(solution)/shard_map/ppermute | solution.py:496
  4.2 1.2 %collective-permute-start.2 = (bf16[784,128]{1,0:T(8,128)(2,1)S(1)}, bf16[784,128]{1,0:T(8,128)(2,1)S(1)}, u32[]{:S(2)}, u32[]{:S(2)}) collective-permute-start(bf16[784,128]{1,0:T(8,128)(2,1)S(1)} %get-tuple-element.24), channel_id=1, source_target_pairs={{0,1},{1,0},{2,3},{3,2},{4,5},{5,4},{6,7},{7,6},{8,9},{9,8},{10,11... | collective-permute-start | bytes 602120 | tf_op jit(solution)/shard_map/ppermute | solution.py:496
  5.4 1.1 %collective-permute-start.3 = (bf16[784,128]{1,0:T(8,128)(2,1)S(1)}, bf16[784,128]{1,0:T(8,128)(2,1)S(1)}, u32[]{:S(2)}, u32[]{:S(2)}) collective-permute-start(bf16[784,128]{1,0:T(8,128)(2,1)S(1)} %get-tuple-element.25), channel_id=1, source_target_pairs={{0,8},{1,2},{2,1},{3,4},{4,3},{5,6},{6,5},{7,15},{8,0},{9,10},{10,... | collective-permute-start | bytes 602120 | tf_op jit(solution)/shard_map/ppermute | solution.py:496
  6.5 0.9 %collective-permute-done.x_first = bf16[784,128]{1,0:T(8,128)(2,1)S(1)} collective-permute-done((bf16[784,128]{1,0:T(8,128)(2,1)S(1)}, bf16[784,128]{1,0:T(8,128)(2,1)S(1)}, u32[]{:S(2)}, u32[]{:S(2)}) %collective-permute-start) | collective-permute-done | bytes 200736 | tf_op jit(solution)/shard_map/ppermute | solution.py:496
  7.4 1.1 %collective-permute-done.1.x_second = bf16[784,128]{1,0:T(8,128)(2,1)S(1)} collective-permute-done((bf16[784,128]{1,0:T(8,128)(2,1)S(1)}, bf16[784,128]{1,0:T(8,128)(2,1)S(1)}, u32[]{:S(2)}, u32[]{:S(2)}) %collective-permute-start.1) | collective-permute-done | bytes 200736 | tf_op jit(solution)/shard_map/ppermute | solution.py:496
  8.6 0.0 copy-start.1
  8.6 2.6 %collective-permute-start.5 = (bf16[32,128]{1,0:T(8,128)(2,1)S(1)}, bf16[32,128]{1,0:T(8,128)(2,1)S(1)}, u32[]{:S(2)}, u32[]{:S(2)}) collective-permute-start(bf16[32,128]{1,0:T(8,128)(2,1)S(1)} %pad_maximum_fusion), channel_id=1, source_target_pairs={{0,8},{1,2},{2,1},{3,4},{4,3},{5,6},{6,5},{7,15},{8,0},{9,10},{10,... | collective-permute-start | bytes 24584 | tf_op jit(solution)/shard_map/ppermute | solution.py:496
  11.2 0.0 collective-permute-start.4
  11.2 0.0 copy-done
  11.2 0.0 copy-done.1
  11.2 0.8 %shard_map.46.a_ref = bf16[4,128,384]{2,1,0:T(8,128)(2,1)S(1)} custom-call(s32[2,2,2,6]{3,2,1,0:T(2,128)S(1)} %copy-done.1, bf16[2,2,2,7,64,64]{5,4,3,2,1,0:T(8,128)(2,1)S(1)} %copy-done), custom_call_target="tpu_custom_call" | custom-call | tf_op jit(solution)/shard_map/pallas_call | solution.py:537
  12.1 0.0 collective-permute-done.2.y_first
  12.1 0.9 %collective-permute-done.3.y_second = bf16[784,128]{1,0:T(8,128)(2,1)S(1)} collective-permute-done((bf16[784,128]{1,0:T(8,128)(2,1)S(1)}, bf16[784,128]{1,0:T(8,128)(2,1)S(1)}, u32[]{:S(2)}, u32[]{:S(2)}) %collective-permute-start.3) | collective-permute-done | bytes 200736 | tf_op jit(solution)/shard_map/ppermute | solution.py:496
  13.0 0.1 collective-permute-done.5.c_second
  13.1 0.0 collective-permute-done.4.c_first
  13.1 3.0 %shard_map.48 = (bf16[1056,128]{1,0:T(8,128)(2,1)S(1)}, bf16[416,128]{1,0:T(8,128)(2,1)S(1)}, bf16[320,128]{1,0:T(8,128)(2,1)S(1)}, bf16[320,128]{1,0:T(8,128)(2,1)S(1)}, f32[3,13,32,128]{3,2,1,0:T(8,128)S(1)}) custom-call(bf16[4,128,384]{2,1,0:T(8,128)(2,1)S(1)} %shard_map.46.a_ref, bf16[4,384,128]{2,1,0:T(8,128)(2,1)S(1)} %get-tuple-element.20.rows_ref, ...), custom_call_target="tpu_custom_call" | custom-call | tf_op jit(solution)/shard_map/pallas_call | solution.py:542
  16.1 0.2 collective-permute-start.6
  16.3 1.4 %collective-permute-done.6.y_first = bf16[1056,128]{1,0:T(8,128)(2,1)S(1)} collective-permute-done((bf16[1056,128]{1,0:T(8,128)(2,1)S(1)}, bf16[1056,128]{1,0:T(8,128)(2,1)S(1)}, u32[]{:S(2)}, u32[]{:S(2)}) %collective-permute-start.6) | collective-permute-done | bytes 270368 | tf_op jit(solution)/shard_map/ppermute | solution.py:496
  17.7 0.1 collective-permute-start.10
  17.8 1.3 %collective-permute-start.11 = (bf16[480,128]{1,0:T(8,128)(2,1)S(1)}, bf16[480,128]{1,0:T(8,128)(2,1)S(1)}, u32[]{:S(2)}, u32[]{:S(2)}) collective-permute-start(bf16[480,128]{1,0:T(8,128)(2,1)S(1)} %get-tuple-element.33), channel_id=1, source_target_pairs={{0,1},{1,0},{2,3},{3,2},{4,5},{5,4},{6,7},{7,6},{8,16},{9,17},{10,... | collective-permute-start | bytes 368648 | tf_op jit(solution)/shard_map/ppermute | solution.py:496
  19.1 2.9 %collective-permute-start.7 = (bf16[416,128]{1,0:T(8,128)(2,1)S(1)}, bf16[416,128]{1,0:T(8,128)(2,1)S(1)}, u32[]{:S(2)}, u32[]{:S(2)}) collective-permute-start(bf16[416,128]{1,0:T(8,128)(2,1)S(1)} %get-tuple-element.28), channel_id=1, source_target_pairs={{0,8},{1,2},{2,1},{3,4},{4,3},{5,6},{6,5},{7,15},{8,0},{9,10},{10,... | collective-permute-start | bytes 319496 | tf_op jit(solution)/shard_map/ppermute | solution.py:496
  22.0 0.0 collective-permute-start.8
  22.0 3.2 %collective-permute-start.9 = (bf16[320,128]{1,0:T(8,128)(2,1)S(1)}, bf16[320,128]{1,0:T(8,128)(2,1)S(1)}, u32[]{:S(2)}, u32[]{:S(2)}) collective-permute-start(bf16[320,128]{1,0:T(8,128)(2,1)S(1)} %get-tuple-element.30), channel_id=1, source_target_pairs={{0,7},{1,2},{2,1},{3,4},{4,3},{5,6},{6,5},{7,0},{8,16},{9,18},{10,... | collective-permute-start | bytes 245768 | tf_op jit(solution)/shard_map/ppermute | solution.py:496
  25.2 3.7 %collective-permute-done.8.c_first = bf16[320,128]{1,0:T(8,128)(2,1)S(1)} collective-permute-done((bf16[320,128]{1,0:T(8,128)(2,1)S(1)}, bf16[320,128]{1,0:T(8,128)(2,1)S(1)}, u32[]{:S(2)}, u32[]{:S(2)}) %collective-permute-start.8) | collective-permute-done | bytes 81952 | tf_op jit(solution)/shard_map/ppermute | solution.py:496
  28.9 0.0 collective-permute-done.9.c_second
  28.9 0.0 collective-permute-done.7.y_second
  28.9 0.8 %shard_map.49 = (f32[23,32,128]{2,1,0:T(8,128)S(1)}, bf16[7,7,64,64]{3,2,1,0:T(8,128)(2,1)}) custom-call(f32[3,13,32,128]{3,2,1,0:T(8,128)S(1)} %get-tuple-element.26.rest_ref, bf16[1056,128]{1,0:T(8,128)(2,1)S(1)} %collective-permute-done.6.y_first, bf16[416,128]{1,0:T(8,128)(2,1)S(1)} %collective-permute-done.7.y_second, ...), custom_call_target="tpu_custom_call" | custom-call | bytes 1 | tf_op jit(solution)/shard_map/pallas_call | solution.py:567
  29.8 0.0 collective-permute-done.10.x_first
  29.8 0.0 collective-permute-done.11.x_second
  29.8 0.9 %shard_map.51 = bf16[7,7,64,64]{3,2,1,0:T(8,128)(2,1)} custom-call(f32[23,32,128]{2,1,0:T(8,128)S(1)} %get-tuple-element.31.own_ref, bf16[480,128]{1,0:T(8,128)(2,1)S(1)} %collective-permute-done.10.x_first, bf16[480,128]{1,0:T(8,128)(2,1)S(1)} %collective-permute-done.11.x_second, ...), custom_call_target="tpu_custom_call", output_to_operand_aliasing={{}: (3, {})} | custom-call | tf_op jit(solution)/shard_map/pallas_call | solution.py:575
  (4 shorter events, 0.0 us)
Async XLA Ops:
  0.0 11.2 %copy-start = (bf16[2,2,2,7,64,64]{5,4,3,2,1,0:T(8,128)(2,1)S(1)}, bf16[2,2,2,7,64,64]{5,4,3,2,1,0:T(8,128)(2,1)}, u32[]{:S(2)}) copy-start(bf16[2,2,2,7,64,64]{5,4,3,2,1,0:T(8,128)(2,1)} %a_ref.1) | copy-start | bytes 1376260
  1.5 5.9 %collective-permute-start = (bf16[784,128]{1,0:T(8,128)(2,1)S(1)}, bf16[784,128]{1,0:T(8,128)(2,1)S(1)}, u32[]{:S(2)}, u32[]{:S(2)}) collective-permute-start(bf16[784,128]{1,0:T(8,128)(2,1)S(1)} %get-tuple-element.22), channel_id=1, source_target_pairs={{0,8},{1,9},{2,10},{3,11},{4,12},{5,13},{6,14},{7,15},{8,0},{9,1},... | collective-permute-start | bytes 602120 | tf_op jit(solution)/shard_map/ppermute | solution.py:496
  1.8 6.8 %collective-permute-start.1 = (bf16[784,128]{1,0:T(8,128)(2,1)S(1)}, bf16[784,128]{1,0:T(8,128)(2,1)S(1)}, u32[]{:S(2)}, u32[]{:S(2)}) collective-permute-start(bf16[784,128]{1,0:T(8,128)(2,1)S(1)} %get-tuple-element.23), channel_id=1, source_target_pairs={{0,1},{1,0},{2,3},{3,2},{4,5},{5,4},{6,7},{7,6},{8,16},{9,17},{10,... | collective-permute-start | bytes 602120 | tf_op jit(solution)/shard_map/ppermute | solution.py:496
  4.2 7.9 %collective-permute-start.2 = (bf16[784,128]{1,0:T(8,128)(2,1)S(1)}, bf16[784,128]{1,0:T(8,128)(2,1)S(1)}, u32[]{:S(2)}, u32[]{:S(2)}) collective-permute-start(bf16[784,128]{1,0:T(8,128)(2,1)S(1)} %get-tuple-element.24), channel_id=1, source_target_pairs={{0,1},{1,0},{2,3},{3,2},{4,5},{5,4},{6,7},{7,6},{8,9},{9,8},{10,11... | collective-permute-start | bytes 602120 | tf_op jit(solution)/shard_map/ppermute | solution.py:496
  5.4 7.6 %collective-permute-start.3 = (bf16[784,128]{1,0:T(8,128)(2,1)S(1)}, bf16[784,128]{1,0:T(8,128)(2,1)S(1)}, u32[]{:S(2)}, u32[]{:S(2)}) collective-permute-start(bf16[784,128]{1,0:T(8,128)(2,1)S(1)} %get-tuple-element.25), channel_id=1, source_target_pairs={{0,8},{1,2},{2,1},{3,4},{4,3},{5,6},{6,5},{7,15},{8,0},{9,10},{10,... | collective-permute-start | bytes 602120 | tf_op jit(solution)/shard_map/ppermute | solution.py:496
  8.6 2.7 %copy-start.1 = (s32[2,2,2,6]{3,2,1,0:T(2,128)S(1)}, s32[2,2,2,6]{3,2,1,0:T(2,128)}, u32[]{:S(2)}) copy-start(s32[2,2,2,6]{3,2,1,0:T(2,128)} %links_hbm.1) | copy-start | bytes 580
  8.6 4.5 %collective-permute-start.5 = (bf16[32,128]{1,0:T(8,128)(2,1)S(1)}, bf16[32,128]{1,0:T(8,128)(2,1)S(1)}, u32[]{:S(2)}, u32[]{:S(2)}) collective-permute-start(bf16[32,128]{1,0:T(8,128)(2,1)S(1)} %pad_maximum_fusion), channel_id=1, source_target_pairs={{0,8},{1,2},{2,1},{3,4},{4,3},{5,6},{6,5},{7,15},{8,0},{9,10},{10,... | collective-permute-start | bytes 24584 | tf_op jit(solution)/shard_map/ppermute | solution.py:496
  11.2 1.8 %collective-permute-start.4 = (bf16[32,128]{1,0:T(8,128)(2,1)S(1)}, bf16[32,128]{1,0:T(8,128)(2,1)S(1)}, u32[]{:S(2)}, u32[]{:S(2)}) collective-permute-start(bf16[32,128]{1,0:T(8,128)(2,1)S(1)} %pad_maximum_fusion), channel_id=1, source_target_pairs={{0,1},{1,0},{2,3},{3,2},{4,5},{5,4},{6,7},{7,6},{8,9},{9,8},{10,11... | collective-permute-start | bytes 24584 | tf_op jit(solution)/shard_map/ppermute | solution.py:496
  16.1 1.6 %collective-permute-start.6 = (bf16[1056,128]{1,0:T(8,128)(2,1)S(1)}, bf16[1056,128]{1,0:T(8,128)(2,1)S(1)}, u32[]{:S(2)}, u32[]{:S(2)}) collective-permute-start(bf16[1056,128]{1,0:T(8,128)(2,1)S(1)} %get-tuple-element.27), channel_id=1, source_target_pairs={{0,1},{1,0},{2,3},{3,2},{4,5},{5,4},{6,7},{7,6},{8,9},{9,8},{10,11... | collective-permute-start | bytes 811016 | tf_op jit(solution)/shard_map/ppermute | solution.py:496
  17.7 12.1 %collective-permute-start.10 = (bf16[480,128]{1,0:T(8,128)(2,1)S(1)}, bf16[480,128]{1,0:T(8,128)(2,1)S(1)}, u32[]{:S(2)}, u32[]{:S(2)}) collective-permute-start(bf16[480,128]{1,0:T(8,128)(2,1)S(1)} %get-tuple-element.32), channel_id=1, source_target_pairs={{0,8},{1,9},{2,10},{3,11},{4,12},{5,13},{6,14},{7,15},{8,0},{9,1},... | collective-permute-start | bytes 368648 | tf_op jit(solution)/shard_map/ppermute | solution.py:496
  17.8 12.0 %collective-permute-start.11 = (bf16[480,128]{1,0:T(8,128)(2,1)S(1)}, bf16[480,128]{1,0:T(8,128)(2,1)S(1)}, u32[]{:S(2)}, u32[]{:S(2)}) collective-permute-start(bf16[480,128]{1,0:T(8,128)(2,1)S(1)} %get-tuple-element.33), channel_id=1, source_target_pairs={{0,1},{1,0},{2,3},{3,2},{4,5},{5,4},{6,7},{7,6},{8,16},{9,17},{10,... | collective-permute-start | bytes 368648 | tf_op jit(solution)/shard_map/ppermute | solution.py:496
  19.1 9.9 %collective-permute-start.7 = (bf16[416,128]{1,0:T(8,128)(2,1)S(1)}, bf16[416,128]{1,0:T(8,128)(2,1)S(1)}, u32[]{:S(2)}, u32[]{:S(2)}) collective-permute-start(bf16[416,128]{1,0:T(8,128)(2,1)S(1)} %get-tuple-element.28), channel_id=1, source_target_pairs={{0,8},{1,2},{2,1},{3,4},{4,3},{5,6},{6,5},{7,15},{8,0},{9,10},{10,... | collective-permute-start | bytes 319496 | tf_op jit(solution)/shard_map/ppermute | solution.py:496
  22.0 6.9 %collective-permute-start.8 = (bf16[320,128]{1,0:T(8,128)(2,1)S(1)}, bf16[320,128]{1,0:T(8,128)(2,1)S(1)}, u32[]{:S(2)}, u32[]{:S(2)}) collective-permute-start(bf16[320,128]{1,0:T(8,128)(2,1)S(1)} %get-tuple-element.29), channel_id=1, source_target_pairs={{0,8},{1,10},{2,9},{3,12},{4,11},{5,14},{6,13},{7,15},{8,0},{9,2},... | collective-permute-start | bytes 245768 | tf_op jit(solution)/shard_map/ppermute | solution.py:496
  22.0 6.9 %collective-permute-start.9 = (bf16[320,128]{1,0:T(8,128)(2,1)S(1)}, bf16[320,128]{1,0:T(8,128)(2,1)S(1)}, u32[]{:S(2)}, u32[]{:S(2)}) collective-permute-start(bf16[320,128]{1,0:T(8,128)(2,1)S(1)} %get-tuple-element.30), channel_id=1, source_target_pairs={{0,7},{1,2},{2,1},{3,4},{4,3},{5,6},{6,5},{7,0},{8,16},{9,18},{10,... | collective-permute-start | bytes 245768 | tf_op jit(solution)/shard_map/ppermute | solution.py:496

commit v4 on v3

--- a/solution.py
+++ b/solution.py
@@ -188,7 +188,20 @@
                     ref[start : start + B, :] = packed
 
 
-def pack_matrix_kernel(links_ref, a_ref, out_ref):
+def pack_matrix_kernel(links_ref, a_ref, out_ref, whole_hbm, zeros, sems):
+    zeros[...] = jnp.zeros(zeros.shape, zeros.dtype)
+    copies = []
+    for jx in range(-3, 4):
+        width = abs(jx)
+        if width:
+            for start in (0, 7 - width):
+                copies.append(
+                    pltpu.make_async_copy(
+                        zeros.at[pl.ds(0, width)], whole_hbm.at[jx + 3, pl.ds(start, width)], sems.at[len(copies)]
+                    )
+                )
+    for copy in copies:
+        copy.start()
     odd_x, odd_y = mirrored()
     for index, (px, py) in enumerate(COLUMNS):
         place = (px ^ odd_x, py ^ odd_y)
@@ -205,6 +218,8 @@
                 out_ref[index, z * B : (z + 1) * B, pair * PAIR : (pair + 1) * PAIR] = pair_lanes(
                     blocks[2 * pair], blocks[2 * pair + 1]
                 )
+    for copy in copies:
+        copy.wait()
 
 
 def main_kernel(
@@ -414,20 +429,7 @@
     )
 
 
-def own_kernel(rest_ref, y_first, y_second, c_first, c_second, own_ref, out_hbm, zeros, sems):
-    zeros[...] = jnp.zeros(zeros.shape, zeros.dtype)
-    copies = []
-    for jx in range(-3, 4):
-        width = abs(jx)
-        if width:
-            for start in (0, 7 - width):
-                copies.append(
-                    pltpu.make_async_copy(
-                        zeros.at[pl.ds(0, width)], out_hbm.at[jx + 3, pl.ds(start, width)], sems.at[len(copies)]
-                    )
-                )
-    for copy in copies:
-        copy.start()
+def own_kernel(rest_ref, y_first, y_second, c_first, c_second, own_ref):
     has_x, has_y = inside()
     terms = {block: [] for block in STENCIL}
     for position, s in enumerate(IMAGE):
@@ -442,8 +444,6 @@
         terms[-1 - s[0], -1 - s[1]].append((c_second, row, has_x * has_y))
     for position, block in enumerate(OWN):
         own_ref[position] = gathered(terms[block])
-    for copy in copies:
-        copy.wait()
 
 
 def finish_kernel(own_ref, x_first, x_second, _, out_hbm, rows, sems):
@@ -510,7 +510,7 @@
         scratch_shapes=list(scratch),
         input_output_aliases=aliases or {},
         compiler_params=pltpu.CompilerParams(vmem_limit_bytes=VMEM_LIMIT),
-        cost_estimate=None if cost is None else pl.CostEstimate(flops=0, bytes_accessed=cost, transcendentals=0),
+        cost_estimate=None if cost is None else pl.CostEstimate(flops=cost, bytes_accessed=1, transcendentals=0),
     )
 
 
@@ -534,7 +534,14 @@
     y_first = swapped(y_first, 0, 1)
     notes = jnp.concatenate([x_first[BODY:], x_second[BODY:]], axis=0)
     c_first, c_second = swapped(notes, 0, 1), swapped(notes, 0, 2)
-    (matrix,) = call(pack_matrix_kernel, [SMEM, VMEM], [((4, PAIR, 6 * B), bf16)])(face_links, fine_matrix)
+    whole = ((7, 7, B, B), bf16)
+    matrix, out = call(
+        pack_matrix_kernel,
+        [SMEM, VMEM],
+        [((4, PAIR, 6 * B), bf16), whole],
+        [pltpu.VMEM((3, B, B), bf16), pltpu.SemaphoreType.DMA((12,))],
+        [VMEM, HBM],
+    )(face_links, fine_matrix)
 
     def sent(blocks):
         return ((len(blocks) * HALF, PAIR), bf16)
@@ -559,19 +566,11 @@
     y_second = swapped(y_second, 0, 2)
     c_first, c_second = swapped(c_first, 1, 2), swapped(c_second, 2, 2)
     y_first = swapped(y_first, 0, 1)
-    x_first, x_second = call(relay_kernel, [VMEM] * 2, [sent(TO_X[1]), sent(TO_X[-1])], cost=100_000_000)(
-        rest, y_first
+    x_first, x_second = call(relay_kernel, [VMEM] * 2, [sent(TO_X[1]), sent(TO_X[-1])])(rest, y_first)
+    x_first, x_second = swapped(x_first, 1, 0), swapped(x_second, 2, 0)
+    (own,) = call(own_kernel, [VMEM] * 5, [((len(OWN), HALF, PAIR), f32)], cost=1_000_000_000_000)(
+        rest, y_first, y_second, c_first, c_second
     )
-    x_first, x_second = swapped(x_first, 1, 0), swapped(x_second, 2, 0)
-    whole = ((7, 7, B, B), bf16)
-    own, out = call(
-        own_kernel,
-        [VMEM] * 5,
-        [((len(OWN), HALF, PAIR), f32), whole],
-        [pltpu.VMEM((3, B, B), bf16), pltpu.SemaphoreType.DMA((12,))],
-        [VMEM, HBM],
-        cost=1,
-    )(rest, y_first, y_second, c_first, c_second)
     (out,) = call(
         finish_kernel,
         [VMEM] * 3 + [HBM],

time: 30.9 us -> 30.1 us (0.974)
  the two profiles are of different devices: /device:TPU:11 before, /device:TPU:0 now
where the time goes in v4:
time: 30.1 us; the launch traced here: 29.9 us
  starting transfers between devices  15 us (50%)
  Pallas kernels  8.76 us (29%)
  waiting for transfers between devices  6.04 us (20%)
    ppermute x12, starting transfers between devices, swapped(): return lax.ppermute(value, ('sx', 'sy'), pairs)  15 us
    ppermute x12, waiting for transfers between devices, swapped(): return lax.ppermute(value, ('sx', 'sy'), pairs)  6.04 us
    pallas_call x1, Pallas kernels, per_device(): call(main_kernel, [VMEM] * 9, [sent(TO_Y_FIRST), sent(TO_Y_SECOND), sent(...  3 us
    pallas_call x1, Pallas kernels, per_device(): call(finish_kernel, [VMEM] * 3 + [HBM], [whole], [pltpu.VMEM((7, 7, B, B)...  1.85 us
    pallas_call x1, Pallas kernels, per_device(): call(pack_matrix_kernel, [SMEM, VMEM], [((4, PAIR, 6 * B), bf16), whole],...  1.61 us
    pallas_call x1, Pallas kernels, per_device(): call(functools.partial(pack_kernel, lax.axis_size('sy')), [HBM, HBM, HBM]...  1.51 us
    pallas_call x1, Pallas kernels, per_device(): call(relay_kernel, [VMEM] * 2, [sent(TO_X[1]), sent(TO_X[-1])])  0.72 us
  transfers between devices with their start and end apart: 12, of which 4 were waited for; matrix products, arithmetic and copies ran while one was open for 0% of the time, Pallas kernels for 8%

profile of v4, /device:TPU:0, one launch (start us, length us, event | category | flops | bytes accessed | tf_op | source)
XLA Modules:
  0.0 29.9 jit_solution(3122174735255865210)
XLA Ops:
  0.0 0.0 copy-start
  0.0 1.5 %shard_map.47 = (bf16[4,384,128]{2,1,0:T(8,128)(2,1)S(1)}, f32[32,128]{1,0:T(8,128)S(1)}, bf16[784,128]{1,0:T(8,128)(2,1)S(1)}, bf16[784,128]{1,0:T(8,128)(2,1)S...) custom-call(s32[2,2,2]{2,1,0:T(2,128)} %aggregate_hbm.1, s32[2,2,2,6]{3,2,1,0:T(2,128)} %links_hbm.1, ...), custom_call_target="tpu_custom_call" | custom-call | tf_op jit(solution)/shard_map/pallas_call | solution.py:520
  1.5 3.1 %collective-permute-start = (bf16[784,128]{1,0:T(8,128)(2,1)S(1)}, bf16[784,128]{1,0:T(8,128)(2,1)S(1)}, u32[]{:S(2)}, u32[]{:S(2)}) collective-permute-start(bf16[784,128]{1,0:T(8,128)(2,1)S(1)} %get-tuple-element.23), channel_id=1, source_target_pairs={{0,8},{1,9},{2,10},{3,11},{4,12},{5,13},{6,14},{7,15},{8,0},{9,1},... | collective-permute-start | bytes 602120 | tf_op jit(solution)/shard_map/ppermute | solution.py:496
  4.6 0.0 collective-permute-start.1
  4.6 0.5 %collective-permute-start.2 = (bf16[784,128]{1,0:T(8,128)(2,1)S(1)}, bf16[784,128]{1,0:T(8,128)(2,1)S(1)}, u32[]{:S(2)}, u32[]{:S(2)}) collective-permute-start(bf16[784,128]{1,0:T(8,128)(2,1)S(1)} %get-tuple-element.25), channel_id=1, source_target_pairs={{0,1},{1,0},{2,3},{3,2},{4,5},{5,4},{6,7},{7,6},{8,9},{9,8},{10,11... | collective-permute-start | bytes 602120 | tf_op jit(solution)/shard_map/ppermute | solution.py:496
  5.1 2.6 %collective-permute-start.3 = (bf16[784,128]{1,0:T(8,128)(2,1)S(1)}, bf16[784,128]{1,0:T(8,128)(2,1)S(1)}, u32[]{:S(2)}, u32[]{:S(2)}) collective-permute-start(bf16[784,128]{1,0:T(8,128)(2,1)S(1)} %get-tuple-element.26), channel_id=1, source_target_pairs={{0,8},{1,2},{2,1},{3,4},{4,3},{5,6},{6,5},{7,15},{8,0},{9,10},{10,... | collective-permute-start | bytes 602120 | tf_op jit(solution)/shard_map/ppermute | solution.py:496
  7.8 1.8 %collective-permute-done.x_first = bf16[784,128]{1,0:T(8,128)(2,1)S(1)} collective-permute-done((bf16[784,128]{1,0:T(8,128)(2,1)S(1)}, bf16[784,128]{1,0:T(8,128)(2,1)S(1)}, u32[]{:S(2)}, u32[]{:S(2)}) %collective-permute-start) | collective-permute-done | bytes 200736 | tf_op jit(solution)/shard_map/ppermute | solution.py:496
  9.6 0.0 collective-permute-done.1.x_second
  9.6 0.0 copy-start.1
  9.6 2.9 %collective-permute-start.5 = (bf16[32,128]{1,0:T(8,128)(2,1)S(1)}, bf16[32,128]{1,0:T(8,128)(2,1)S(1)}, u32[]{:S(2)}, u32[]{:S(2)}) collective-permute-start(bf16[32,128]{1,0:T(8,128)(2,1)S(1)} %pad_maximum_fusion), channel_id=1, source_target_pairs={{0,8},{1,2},{2,1},{3,4},{4,3},{5,6},{6,5},{7,15},{8,0},{9,10},{10,... | collective-permute-start | bytes 24584 | tf_op jit(solution)/shard_map/ppermute | solution.py:496
  12.5 0.0 collective-permute-start.4
  12.5 0.0 copy-done
  12.5 0.0 copy-done.1
  12.5 1.6 %shard_map.46 = (bf16[4,128,384]{2,1,0:T(8,128)(2,1)S(1)}, bf16[7,7,64,64]{3,2,1,0:T(8,128)(2,1)}) custom-call(s32[2,2,2,6]{3,2,1,0:T(2,128)S(1)} %copy-done.1, bf16[2,2,2,7,64,64]{5,4,3,2,1,0:T(8,128)(2,1)S(1)} %copy-done), custom_call_target="tpu_custom_call" | custom-call | tf_op jit(solution)/shard_map/pallas_call | solution.py:538
  14.1 0.0 collective-permute-done.2.y_first
  14.1 0.0 collective-permute-done.3.y_second
  14.1 0.0 collective-permute-done.5.c_second
  14.1 0.0 collective-permute-done.4.c_first
  14.1 3.0 %shard_map.48 = (bf16[1056,128]{1,0:T(8,128)(2,1)S(1)}, bf16[416,128]{1,0:T(8,128)(2,1)S(1)}, bf16[320,128]{1,0:T(8,128)(2,1)S(1)}, bf16[320,128]{1,0:T(8,128)(2,1)S(1)}, f32[3,13,32,128]{3,2,1,0:T(8,128)S(1)}) custom-call(bf16[4,128,384]{2,1,0:T(8,128)(2,1)S(1)} %get-tuple-element.20.a_ref, bf16[4,384,128]{2,1,0:T(8,128)(2,1)S(1)} %get-tuple-element.21.rows_ref, ...), custom_call_target="tpu_custom_call" | custom-call | tf_op jit(solution)/shard_map/pallas_call | solution.py:549
  17.2 0.6 %collective-permute-start.6 = (bf16[1056,128]{1,0:T(8,128)(2,1)S(1)}, bf16[1056,128]{1,0:T(8,128)(2,1)S(1)}, u32[]{:S(2)}, u32[]{:S(2)}) collective-permute-start(bf16[1056,128]{1,0:T(8,128)(2,1)S(1)} %get-tuple-element.28), channel_id=1, source_target_pairs={{0,1},{1,0},{2,3},{3,2},{4,5},{5,4},{6,7},{7,6},{8,9},{9,8},{10,11... | collective-permute-start | bytes 811016 | tf_op jit(solution)/shard_map/ppermute | solution.py:496
  17.7 1.6 %collective-permute-start.7 = (bf16[416,128]{1,0:T(8,128)(2,1)S(1)}, bf16[416,128]{1,0:T(8,128)(2,1)S(1)}, u32[]{:S(2)}, u32[]{:S(2)}) collective-permute-start(bf16[416,128]{1,0:T(8,128)(2,1)S(1)} %get-tuple-element.29), channel_id=1, source_target_pairs={{0,8},{1,2},{2,1},{3,4},{4,3},{5,6},{6,5},{7,15},{8,0},{9,10},{10,... | collective-permute-start | bytes 319496 | tf_op jit(solution)/shard_map/ppermute | solution.py:496
  19.3 0.5 %collective-permute-start.8 = (bf16[320,128]{1,0:T(8,128)(2,1)S(1)}, bf16[320,128]{1,0:T(8,128)(2,1)S(1)}, u32[]{:S(2)}, u32[]{:S(2)}) collective-permute-start(bf16[320,128]{1,0:T(8,128)(2,1)S(1)} %get-tuple-element.30), channel_id=1, source_target_pairs={{0,8},{1,10},{2,9},{3,12},{4,11},{5,14},{6,13},{7,15},{8,0},{9,2},... | collective-permute-start | bytes 245768 | tf_op jit(solution)/shard_map/ppermute | solution.py:496
  19.7 1.2 %collective-permute-start.9 = (bf16[320,128]{1,0:T(8,128)(2,1)S(1)}, bf16[320,128]{1,0:T(8,128)(2,1)S(1)}, u32[]{:S(2)}, u32[]{:S(2)}) collective-permute-start(bf16[320,128]{1,0:T(8,128)(2,1)S(1)} %get-tuple-element.31), channel_id=1, source_target_pairs={{0,7},{1,2},{2,1},{3,4},{4,3},{5,6},{6,5},{7,0},{8,16},{9,18},{10,... | collective-permute-start | bytes 245768 | tf_op jit(solution)/shard_map/ppermute | solution.py:496
  20.9 0.0 collective-permute-done.6.y_first
  20.9 0.7 %shard_map.50 = (bf16[480,128]{1,0:T(8,128)(2,1)}, bf16[480,128]{1,0:T(8,128)(2,1)}) custom-call(f32[3,13,32,128]{3,2,1,0:T(8,128)S(1)} %get-tuple-element.27.rest_ref, bf16[1056,128]{1,0:T(8,128)(2,1)S(1)} %collective-permute-done.6.y_first), custom_call_target="tpu_custom_call" | custom-call | tf_op jit(solution)/shard_map/pallas_call | solution.py:569
  21.7 2.1 %collective-permute-start.10 = (bf16[480,128]{1,0:T(8,128)(2,1)}, bf16[480,128]{1,0:T(8,128)(2,1)}, u32[]{:S(2)}, u32[]{:S(2)}) collective-permute-start(bf16[480,128]{1,0:T(8,128)(2,1)} %get-tuple-element.32), channel_id=1, source_target_pairs={{0,8},{1,9},{2,10},{3,11},{4,12},{5,13},{6,14},{7,15},{8,0},{9,1},... | collective-permute-start | bytes 368648 | tf_op jit(solution)/shard_map/ppermute | solution.py:496
  23.8 0.0 collective-permute-start.11
  23.8 0.4 %collective-permute-done.8.c_first = bf16[320,128]{1,0:T(8,128)(2,1)S(1)} collective-permute-done((bf16[320,128]{1,0:T(8,128)(2,1)S(1)}, bf16[320,128]{1,0:T(8,128)(2,1)S(1)}, u32[]{:S(2)}, u32[]{:S(2)}) %collective-permute-start.8) | collective-permute-done | bytes 81952 | tf_op jit(solution)/shard_map/ppermute | solution.py:496
  24.2 1.2 %collective-permute-done.9.c_second = bf16[320,128]{1,0:T(8,128)(2,1)S(1)} collective-permute-done((bf16[320,128]{1,0:T(8,128)(2,1)S(1)}, bf16[320,128]{1,0:T(8,128)(2,1)S(1)}, u32[]{:S(2)}, u32[]{:S(2)}) %collective-permute-start.9) | collective-permute-done | bytes 81952 | tf_op jit(solution)/shard_map/ppermute | solution.py:496
  25.4 0.0 collective-permute-done.7.y_second
  25.4 0.1 shard_map.49.own_ref
  25.5 2.6 %collective-permute-done.10.x_first = bf16[480,128]{1,0:T(8,128)(2,1)} collective-permute-done((bf16[480,128]{1,0:T(8,128)(2,1)}, bf16[480,128]{1,0:T(8,128)(2,1)}, u32[]{:S(2)}, u32[]{:S(2)}) %collective-permute-start.10) | collective-permute-done | bytes 122912 | tf_op jit(solution)/shard_map/ppermute | solution.py:496
  28.0 0.0 collective-permute-done.11.x_second
  28.0 1.9 %shard_map.51 = bf16[7,7,64,64]{3,2,1,0:T(8,128)(2,1)} custom-call(f32[23,32,128]{2,1,0:T(8,128)S(1)} %shard_map.49.own_ref, bf16[480,128]{1,0:T(8,128)(2,1)} %collective-permute-done.10.x_first, bf16[480,128]{1,0:T(8,128)(2,1)} %collective-permute-done.11.x_second, bf16[7,7,64,64]{3,2,1,0:T(8,128)(2,1)} %get-tuple-element.34._), custom_call_target="tpu_custom_call", output_to_operand_aliasing={{}: (3, {})} | custom-call | tf_op jit(solution)/shard_map/pallas_call | solution.py:574
  (3 shorter events, 0.0 us)
Async XLA Ops:
  0.0 12.5 %copy-start = (bf16[2,2,2,7,64,64]{5,4,3,2,1,0:T(8,128)(2,1)S(1)}, bf16[2,2,2,7,64,64]{5,4,3,2,1,0:T(8,128)(2,1)}, u32[]{:S(2)}) copy-start(bf16[2,2,2,7,64,64]{5,4,3,2,1,0:T(8,128)(2,1)} %a_ref.1) | copy-start | bytes 1376260
  1.5 8.1 %collective-permute-start = (bf16[784,128]{1,0:T(8,128)(2,1)S(1)}, bf16[784,128]{1,0:T(8,128)(2,1)S(1)}, u32[]{:S(2)}, u32[]{:S(2)}) collective-permute-start(bf16[784,128]{1,0:T(8,128)(2,1)S(1)} %get-tuple-element.23), channel_id=1, source_target_pairs={{0,8},{1,9},{2,10},{3,11},{4,12},{5,13},{6,14},{7,15},{8,0},{9,1},... | collective-permute-start | bytes 602120 | tf_op jit(solution)/shard_map/ppermute | solution.py:496
  4.6 5.0 %collective-permute-start.1 = (bf16[784,128]{1,0:T(8,128)(2,1)S(1)}, bf16[784,128]{1,0:T(8,128)(2,1)S(1)}, u32[]{:S(2)}, u32[]{:S(2)}) collective-permute-start(bf16[784,128]{1,0:T(8,128)(2,1)S(1)} %get-tuple-element.24), channel_id=1, source_target_pairs={{0,1},{1,0},{2,3},{3,2},{4,5},{5,4},{6,7},{7,6},{8,16},{9,17},{10,... | collective-permute-start | bytes 602120 | tf_op jit(solution)/shard_map/ppermute | solution.py:496
  4.6 9.5 %collective-permute-start.2 = (bf16[784,128]{1,0:T(8,128)(2,1)S(1)}, bf16[784,128]{1,0:T(8,128)(2,1)S(1)}, u32[]{:S(2)}, u32[]{:S(2)}) collective-permute-start(bf16[784,128]{1,0:T(8,128)(2,1)S(1)} %get-tuple-element.25), channel_id=1, source_target_pairs={{0,1},{1,0},{2,3},{3,2},{4,5},{5,4},{6,7},{7,6},{8,9},{9,8},{10,11... | collective-permute-start | bytes 602120 | tf_op jit(solution)/shard_map/ppermute | solution.py:496
  5.1 9.0 %collective-permute-start.3 = (bf16[784,128]{1,0:T(8,128)(2,1)S(1)}, bf16[784,128]{1,0:T(8,128)(2,1)S(1)}, u32[]{:S(2)}, u32[]{:S(2)}) collective-permute-start(bf16[784,128]{1,0:T(8,128)(2,1)S(1)} %get-tuple-element.26), channel_id=1, source_target_pairs={{0,8},{1,2},{2,1},{3,4},{4,3},{5,6},{6,5},{7,15},{8,0},{9,10},{10,... | collective-permute-start | bytes 602120 | tf_op jit(solution)/shard_map/ppermute | solution.py:496
  9.6 2.9 %copy-start.1 = (s32[2,2,2,6]{3,2,1,0:T(2,128)S(1)}, s32[2,2,2,6]{3,2,1,0:T(2,128)}, u32[]{:S(2)}) copy-start(s32[2,2,2,6]{3,2,1,0:T(2,128)} %links_hbm.1) | copy-start | bytes 580
  9.6 4.5 %collective-permute-start.5 = (bf16[32,128]{1,0:T(8,128)(2,1)S(1)}, bf16[32,128]{1,0:T(8,128)(2,1)S(1)}, u32[]{:S(2)}, u32[]{:S(2)}) collective-permute-start(bf16[32,128]{1,0:T(8,128)(2,1)S(1)} %pad_maximum_fusion), channel_id=1, source_target_pairs={{0,8},{1,2},{2,1},{3,4},{4,3},{5,6},{6,5},{7,15},{8,0},{9,10},{10,... | collective-permute-start | bytes 24584 | tf_op jit(solution)/shard_map/ppermute | solution.py:496
  12.5 1.7 %collective-permute-start.4 = (bf16[32,128]{1,0:T(8,128)(2,1)S(1)}, bf16[32,128]{1,0:T(8,128)(2,1)S(1)}, u32[]{:S(2)}, u32[]{:S(2)}) collective-permute-start(bf16[32,128]{1,0:T(8,128)(2,1)S(1)} %pad_maximum_fusion), channel_id=1, source_target_pairs={{0,1},{1,0},{2,3},{3,2},{4,5},{5,4},{6,7},{7,6},{8,9},{9,8},{10,11... | collective-permute-start | bytes 24584 | tf_op jit(solution)/shard_map/ppermute | solution.py:496
  17.2 3.8 %collective-permute-start.6 = (bf16[1056,128]{1,0:T(8,128)(2,1)S(1)}, bf16[1056,128]{1,0:T(8,128)(2,1)S(1)}, u32[]{:S(2)}, u32[]{:S(2)}) collective-permute-start(bf16[1056,128]{1,0:T(8,128)(2,1)S(1)} %get-tuple-element.28), channel_id=1, source_target_pairs={{0,1},{1,0},{2,3},{3,2},{4,5},{5,4},{6,7},{7,6},{8,9},{9,8},{10,11... | collective-permute-start | bytes 811016 | tf_op jit(solution)/shard_map/ppermute | solution.py:496
  17.7 7.7 %collective-permute-start.7 = (bf16[416,128]{1,0:T(8,128)(2,1)S(1)}, bf16[416,128]{1,0:T(8,128)(2,1)S(1)}, u32[]{:S(2)}, u32[]{:S(2)}) collective-permute-start(bf16[416,128]{1,0:T(8,128)(2,1)S(1)} %get-tuple-element.29), channel_id=1, source_target_pairs={{0,8},{1,2},{2,1},{3,4},{4,3},{5,6},{6,5},{7,15},{8,0},{9,10},{10,... | collective-permute-start | bytes 319496 | tf_op jit(solution)/shard_map/ppermute | solution.py:496
  19.3 4.9 %collective-permute-start.8 = (bf16[320,128]{1,0:T(8,128)(2,1)S(1)}, bf16[320,128]{1,0:T(8,128)(2,1)S(1)}, u32[]{:S(2)}, u32[]{:S(2)}) collective-permute-start(bf16[320,128]{1,0:T(8,128)(2,1)S(1)} %get-tuple-element.30), channel_id=1, source_target_pairs={{0,8},{1,10},{2,9},{3,12},{4,11},{5,14},{6,13},{7,15},{8,0},{9,2},... | collective-permute-start | bytes 245768 | tf_op jit(solution)/shard_map/ppermute | solution.py:496
  19.7 5.6 %collective-permute-start.9 = (bf16[320,128]{1,0:T(8,128)(2,1)S(1)}, bf16[320,128]{1,0:T(8,128)(2,1)S(1)}, u32[]{:S(2)}, u32[]{:S(2)}) collective-permute-start(bf16[320,128]{1,0:T(8,128)(2,1)S(1)} %get-tuple-element.31), channel_id=1, source_target_pairs={{0,7},{1,2},{2,1},{3,4},{4,3},{5,6},{6,5},{7,0},{8,16},{9,18},{10,... | collective-permute-start | bytes 245768 | tf_op jit(solution)/shard_map/ppermute | solution.py:496
  21.7 6.4 %collective-permute-start.10 = (bf16[480,128]{1,0:T(8,128)(2,1)}, bf16[480,128]{1,0:T(8,128)(2,1)}, u32[]{:S(2)}, u32[]{:S(2)}) collective-permute-start(bf16[480,128]{1,0:T(8,128)(2,1)} %get-tuple-element.32), channel_id=1, source_target_pairs={{0,8},{1,9},{2,10},{3,11},{4,12},{5,13},{6,14},{7,15},{8,0},{9,1},... | collective-permute-start | bytes 368648 | tf_op jit(solution)/shard_map/ppermute | solution.py:496
  23.8 4.3 %collective-permute-start.11 = (bf16[480,128]{1,0:T(8,128)(2,1)}, bf16[480,128]{1,0:T(8,128)(2,1)}, u32[]{:S(2)}, u32[]{:S(2)}) collective-permute-start(bf16[480,128]{1,0:T(8,128)(2,1)} %get-tuple-element.33), channel_id=1, source_target_pairs={{0,1},{1,0},{2,3},{3,2},{4,5},{5,4},{6,7},{7,6},{8,16},{9,17},{10,... | collective-permute-start | bytes 368648 | tf_op jit(solution)/shard_map/ppermute | solution.py:496

commit v5 on v4

--- a/solution.py
+++ b/solution.py
@@ -188,20 +188,7 @@
                     ref[start : start + B, :] = packed
 
 
-def pack_matrix_kernel(links_ref, a_ref, out_ref, whole_hbm, zeros, sems):
-    zeros[...] = jnp.zeros(zeros.shape, zeros.dtype)
-    copies = []
-    for jx in range(-3, 4):
-        width = abs(jx)
-        if width:
-            for start in (0, 7 - width):
-                copies.append(
-                    pltpu.make_async_copy(
-                        zeros.at[pl.ds(0, width)], whole_hbm.at[jx + 3, pl.ds(start, width)], sems.at[len(copies)]
-                    )
-                )
-    for copy in copies:
-        copy.start()
+def pack_matrix_kernel(links_ref, a_ref, out_ref):
     odd_x, odd_y = mirrored()
     for index, (px, py) in enumerate(COLUMNS):
         place = (px ^ odd_x, py ^ odd_y)
@@ -218,8 +205,6 @@
                 out_ref[index, z * B : (z + 1) * B, pair * PAIR : (pair + 1) * PAIR] = pair_lanes(
                     blocks[2 * pair], blocks[2 * pair + 1]
                 )
-    for copy in copies:
-        copy.wait()
 
 
 def main_kernel(
@@ -237,11 +222,27 @@
     to_c_first,
     to_c_second,
     rest_ref,
+    whole_hbm,
     right,
     image,
     left_star,
     left_corner,
+    zeros,
+    sems,
 ):
+    zeros[...] = jnp.zeros(zeros.shape, zeros.dtype)
+    copies = []
+    for jx in range(-3, 4):
+        width = abs(jx)
+        if width:
+            for start in (0, 7 - width):
+                copies.append(
+                    pltpu.make_async_copy(
+                        zeros.at[pl.ds(0, width)], whole_hbm.at[jx + 3, pl.ds(start, width)], sems.at[len(copies)]
+                    )
+                )
+    for copy in copies:
+        copy.start()
     from_x = {1: x_first, -1: x_second}
     from_y = {1: y_first, -1: y_second}
     notes = {(0, 0): meta_ref[...]}
@@ -392,6 +393,8 @@
         parts = contribution((tx, 0))
         for position, s in enumerate(IMAGE):
             rest_ref[group, position] = parts[s]
+    for copy in copies:
+        copy.wait()
 
 
 def message_block(ref, row):
@@ -534,19 +537,13 @@
     y_first = swapped(y_first, 0, 1)
     notes = jnp.concatenate([x_first[BODY:], x_second[BODY:]], axis=0)
     c_first, c_second = swapped(notes, 0, 1), swapped(notes, 0, 2)
+    (matrix,) = call(pack_matrix_kernel, [SMEM, VMEM], [((4, PAIR, 6 * B), bf16)])(face_links, fine_matrix)
     whole = ((7, 7, B, B), bf16)
-    matrix, out = call(
-        pack_matrix_kernel,
-        [SMEM, VMEM],
-        [((4, PAIR, 6 * B), bf16), whole],
-        [pltpu.VMEM((3, B, B), bf16), pltpu.SemaphoreType.DMA((12,))],
-        [VMEM, HBM],
-    )(face_links, fine_matrix)
 
     def sent(blocks):
         return ((len(blocks) * HALF, PAIR), bf16)
 
-    y_first, y_second, c_first, c_second, rest = call(
+    y_first, y_second, c_first, c_second, rest, out = call(
         main_kernel,
         [VMEM] * 9,
         [
@@ -555,20 +552,24 @@
             sent(TO_C_FIRST),
             sent(TO_C_SECOND),
             ((3, len(IMAGE), HALF, PAIR), f32),
+            whole,
         ],
         [
             pltpu.VMEM((4, 6 * B, 10 * PAIR), bf16),
             pltpu.VMEM((4 * PAIR, IMAGE_PAIRS * PAIR), bf16),
             pltpu.VMEM((len(STAR) * B, 4 * PAIR), bf16),
             pltpu.VMEM((4, B, PAIR), bf16),
+            pltpu.VMEM((3, B, B), bf16),
+            pltpu.SemaphoreType.DMA((12,)),
         ],
+        [VMEM] * 5 + [HBM],
     )(matrix, rows, meta, x_first, x_second, y_first, y_second, c_first, c_second)
     y_second = swapped(y_second, 0, 2)
     c_first, c_second = swapped(c_first, 1, 2), swapped(c_second, 2, 2)
     y_first = swapped(y_first, 0, 1)
     x_first, x_second = call(relay_kernel, [VMEM] * 2, [sent(TO_X[1]), sent(TO_X[-1])])(rest, y_first)
     x_first, x_second = swapped(x_first, 1, 0), swapped(x_second, 2, 0)
-    (own,) = call(own_kernel, [VMEM] * 5, [((len(OWN), HALF, PAIR), f32)], cost=1_000_000_000_000)(
+    (own,) = call(own_kernel, [VMEM] * 5, [((len(OWN), HALF, PAIR), f32)], cost=3_000_000_000)(
         rest, y_first, y_second, c_first, c_second
     )
     (out,) = call(

time: 30.1 us -> 28.9 us (0.960)
  the two profiles are of different devices: /device:TPU:0 before, /device:TPU:20 now
where the time goes in v5:
time: 28.9 us; the launch traced here: 28.7 us
  waiting for transfers between devices  11.5 us (40%)
  starting transfers between devices  9.98 us (35%)
  Pallas kernels  7.07 us (24%)
    ppermute x12, waiting for transfers between devices, swapped(): return lax.ppermute(value, ('sx', 'sy'), pairs)  11.5 us
    ppermute x12, starting transfers between devices, swapped(): return lax.ppermute(value, ('sx', 'sy'), pairs)  9.98 us
    pallas_call x1, Pallas kernels, per_device(): call(main_kernel, [VMEM] * 9, [sent(TO_Y_FIRST), sent(TO_Y_SECOND), sent(...  3.75 us
    pallas_call x1, Pallas kernels, per_device(): call(functools.partial(pack_kernel, lax.axis_size('sy')), [HBM, HBM, HBM]...  1.51 us
    pallas_call x1, Pallas kernels, per_device(): call(finish_kernel, [VMEM] * 3 + [HBM], [whole], [pltpu.VMEM((7, 7, B, B)...  0.89 us
    pallas_call x1, Pallas kernels, per_device(): call(pack_matrix_kernel, [SMEM, VMEM], [((4, PAIR, 6 * B), bf16)])  0.82 us
  transfers between devices with their start and end apart: 12, of which 7 were waited for; matrix products, arithmetic and copies ran while one was open for 0% of the time, Pallas kernels for 3%

profile of v5, /device:TPU:20, one launch (start us, length us, event | category | flops | bytes accessed | tf_op | source)
XLA Modules:
  0.0 28.7 jit_solution(13013118673875811347)
XLA Ops:
  0.0 0.0 copy-start
  0.0 1.5 %shard_map.47 = (bf16[4,384,128]{2,1,0:T(8,128)(2,1)S(1)}, f32[32,128]{1,0:T(8,128)S(1)}, bf16[784,128]{1,0:T(8,128)(2,1)S(1)}, bf16[784,128]{1,0:T(8,128)(2,1)S...) custom-call(s32[2,2,2]{2,1,0:T(2,128)} %aggregate_hbm.1, s32[2,2,2,6]{3,2,1,0:T(2,128)} %links_hbm.1, ...), custom_call_target="tpu_custom_call" | custom-call | tf_op jit(solution)/shard_map/pallas_call | solution.py:523
  1.5 1.6 %collective-permute-start = (bf16[784,128]{1,0:T(8,128)(2,1)S(1)}, bf16[784,128]{1,0:T(8,128)(2,1)S(1)}, u32[]{:S(2)}, u32[]{:S(2)}) collective-permute-start(bf16[784,128]{1,0:T(8,128)(2,1)S(1)} %get-tuple-element.21), channel_id=1, source_target_pairs={{0,8},{1,9},{2,10},{3,11},{4,12},{5,13},{6,14},{7,15},{8,0},{9,1},... | collective-permute-start | bytes 602120 | tf_op jit(solution)/shard_map/ppermute | solution.py:499
  3.2 0.0 collective-permute-start.1
  3.2 0.0 collective-permute-start.2
  3.2 1.5 %collective-permute-start.3 = (bf16[784,128]{1,0:T(8,128)(2,1)S(1)}, bf16[784,128]{1,0:T(8,128)(2,1)S(1)}, u32[]{:S(2)}, u32[]{:S(2)}) collective-permute-start(bf16[784,128]{1,0:T(8,128)(2,1)S(1)} %get-tuple-element.24), channel_id=1, source_target_pairs={{0,8},{1,2},{2,1},{3,4},{4,3},{5,6},{6,5},{7,15},{8,0},{9,10},{10,... | collective-permute-start | bytes 602120 | tf_op jit(solution)/shard_map/ppermute | solution.py:499
  4.7 3.6 %collective-permute-done.x_first = bf16[784,128]{1,0:T(8,128)(2,1)S(1)} collective-permute-done((bf16[784,128]{1,0:T(8,128)(2,1)S(1)}, bf16[784,128]{1,0:T(8,128)(2,1)S(1)}, u32[]{:S(2)}, u32[]{:S(2)}) %collective-permute-start) | collective-permute-done | bytes 200736 | tf_op jit(solution)/shard_map/ppermute | solution.py:499
  8.3 1.3 %collective-permute-done.1.x_second = bf16[784,128]{1,0:T(8,128)(2,1)S(1)} collective-permute-done((bf16[784,128]{1,0:T(8,128)(2,1)S(1)}, bf16[784,128]{1,0:T(8,128)(2,1)S(1)}, u32[]{:S(2)}, u32[]{:S(2)}) %collective-permute-start.1) | collective-permute-done | bytes 200736 | tf_op jit(solution)/shard_map/ppermute | solution.py:499
  9.6 0.0 copy-start.1
  9.6 0.0 collective-permute-start.5
  9.6 1.6 %collective-permute-start.4 = (bf16[32,128]{1,0:T(8,128)(2,1)S(1)}, bf16[32,128]{1,0:T(8,128)(2,1)S(1)}, u32[]{:S(2)}, u32[]{:S(2)}) collective-permute-start(bf16[32,128]{1,0:T(8,128)(2,1)S(1)} %pad_maximum_fusion), channel_id=1, source_target_pairs={{0,1},{1,0},{2,3},{3,2},{4,5},{5,4},{6,7},{7,6},{8,9},{9,8},{10,11... | collective-permute-start | bytes 24584 | tf_op jit(solution)/shard_map/ppermute | solution.py:499
  11.3 0.0 copy-done
  11.3 0.0 copy-done.1
  11.3 0.8 %shard_map.46.a_ref = bf16[4,128,384]{2,1,0:T(8,128)(2,1)S(1)} custom-call(s32[2,2,2,6]{3,2,1,0:T(2,128)S(1)} %copy-done.1, bf16[2,2,2,7,64,64]{5,4,3,2,1,0:T(8,128)(2,1)S(1)} %copy-done), custom_call_target="tpu_custom_call" | custom-call | tf_op jit(solution)/shard_map/pallas_call | solution.py:540
  12.1 0.0 collective-permute-done.2.y_first
  12.1 0.0 collective-permute-done.3.y_second
  12.1 1.5 %collective-permute-done.5.c_second = bf16[32,128]{1,0:T(8,128)(2,1)S(1)} collective-permute-done((bf16[32,128]{1,0:T(8,128)(2,1)S(1)}, bf16[32,128]{1,0:T(8,128)(2,1)S(1)}, u32[]{:S(2)}, u32[]{:S(2)}) %collective-permute-start.5) | collective-permute-done | bytes 8224 | tf_op jit(solution)/shard_map/ppermute | solution.py:499
  13.6 0.0 collective-permute-done.4.c_first
  13.6 3.7 %shard_map.48 = (bf16[1056,128]{1,0:T(8,128)(2,1)S(1)}, bf16[416,128]{1,0:T(8,128)(2,1)S(1)}, bf16[320,128]{1,0:T(8,128)(2,1)S(1)}, bf16[320,128]{1,0:T(8,128)(2...) custom-call(bf16[4,128,384]{2,1,0:T(8,128)(2,1)S(1)} %shard_map.46.a_ref, ...), custom_call_target="tpu_custom_call" | custom-call | tf_op jit(solution)/shard_map/pallas_call | solution.py:546
  17.4 0.1 collective-permute-start.6
  17.4 0.6 %collective-permute-start.7 = (bf16[416,128]{1,0:T(8,128)(2,1)S(1)}, bf16[416,128]{1,0:T(8,128)(2,1)S(1)}, u32[]{:S(2)}, u32[]{:S(2)}) collective-permute-start(bf16[416,128]{1,0:T(8,128)(2,1)S(1)} %get-tuple-element.27), channel_id=1, source_target_pairs={{0,8},{1,2},{2,1},{3,4},{4,3},{5,6},{6,5},{7,15},{8,0},{9,10},{10,... | collective-permute-start | bytes 319496 | tf_op jit(solution)/shard_map/ppermute | solution.py:499
  18.1 1.9 %collective-permute-start.8 = (bf16[320,128]{1,0:T(8,128)(2,1)S(1)}, bf16[320,128]{1,0:T(8,128)(2,1)S(1)}, u32[]{:S(2)}, u32[]{:S(2)}) collective-permute-start(bf16[320,128]{1,0:T(8,128)(2,1)S(1)} %get-tuple-element.28), channel_id=1, source_target_pairs={{0,8},{1,10},{2,9},{3,12},{4,11},{5,14},{6,13},{7,15},{8,0},{9,2},... | collective-permute-start | bytes 245768 | tf_op jit(solution)/shard_map/ppermute | solution.py:499
  20.0 0.0 collective-permute-start.9
  20.0 0.0 collective-permute-done.6.y_first
  20.0 2.3 %collective-permute-start.10 = (bf16[480,128]{1,0:T(8,128)(2,1)S(1)}, bf16[480,128]{1,0:T(8,128)(2,1)S(1)}, u32[]{:S(2)}, u32[]{:S(2)}) collective-permute-start(bf16[480,128]{1,0:T(8,128)(2,1)S(1)} %get-tuple-element.30), channel_id=1, source_target_pairs={{0,8},{1,9},{2,10},{3,11},{4,12},{5,13},{6,14},{7,15},{8,0},{9,1},... | collective-permute-start | bytes 368648 | tf_op jit(solution)/shard_map/ppermute | solution.py:499
  22.3 0.3 collective-permute-start.11
  22.6 2.4 %collective-permute-done.8.c_first = bf16[320,128]{1,0:T(8,128)(2,1)S(1)} collective-permute-done((bf16[320,128]{1,0:T(8,128)(2,1)S(1)}, bf16[320,128]{1,0:T(8,128)(2,1)S(1)}, u32[]{:S(2)}, u32[]{:S(2)}) %collective-permute-start.8) | collective-permute-done | bytes 81952 | tf_op jit(solution)/shard_map/ppermute | solution.py:499
  24.9 0.9 %collective-permute-done.9.c_second = bf16[320,128]{1,0:T(8,128)(2,1)S(1)} collective-permute-done((bf16[320,128]{1,0:T(8,128)(2,1)S(1)}, bf16[320,128]{1,0:T(8,128)(2,1)S(1)}, u32[]{:S(2)}, u32[]{:S(2)}) %collective-permute-start.9) | collective-permute-done | bytes 81952 | tf_op jit(solution)/shard_map/ppermute | solution.py:499
  25.8 0.7 %collective-permute-done.7.y_second = bf16[416,128]{1,0:T(8,128)(2,1)S(1)} collective-permute-done((bf16[416,128]{1,0:T(8,128)(2,1)S(1)}, bf16[416,128]{1,0:T(8,128)(2,1)S(1)}, u32[]{:S(2)}, u32[]{:S(2)}) %collective-permute-start.7) | collective-permute-done | bytes 106528 | tf_op jit(solution)/shard_map/ppermute | solution.py:499
  26.5 0.1 shard_map.49.own_ref
  26.6 0.0 collective-permute-done.10.x_first
  26.6 1.2 %collective-permute-done.11.x_second = bf16[480,128]{1,0:T(8,128)(2,1)S(1)} collective-permute-done((bf16[480,128]{1,0:T(8,128)(2,1)S(1)}, bf16[480,128]{1,0:T(8,128)(2,1)S(1)}, u32[]{:S(2)}, u32[]{:S(2)}) %collective-permute-start.11) | collective-permute-done | bytes 122912 | tf_op jit(solution)/shard_map/ppermute | solution.py:499
  27.8 0.9 %shard_map.51 = bf16[7,7,64,64]{3,2,1,0:T(8,128)(2,1)} custom-call(f32[23,32,128]{2,1,0:T(8,128)S(1)} %shard_map.49.own_ref, bf16[480,128]{1,0:T(8,128)(2,1)S(1)} %collective-permute-done.10.x_first, bf16[480,128]{1,0:T(8,128)(2,1)S(1)} %collective-permute-done.11.x_second, bf16[7,7,64,64]{3,2,1,0:T(8,128)(2,1)} %get-tuple-element.32._), custom_call_target="tpu_custom_call", output_to_operand_aliasing={{}: (3, {})} | custom-call | tf_op jit(solution)/shard_map/pallas_call | solution.py:575
  (4 shorter events, 0.0 us)
Async XLA Ops:
  0.0 11.3 %copy-start = (bf16[2,2,2,7,64,64]{5,4,3,2,1,0:T(8,128)(2,1)S(1)}, bf16[2,2,2,7,64,64]{5,4,3,2,1,0:T(8,128)(2,1)}, u32[]{:S(2)}) copy-start(bf16[2,2,2,7,64,64]{5,4,3,2,1,0:T(8,128)(2,1)} %a_ref.1) | copy-start | bytes 1376260
  1.5 6.8 %collective-permute-start = (bf16[784,128]{1,0:T(8,128)(2,1)S(1)}, bf16[784,128]{1,0:T(8,128)(2,1)S(1)}, u32[]{:S(2)}, u32[]{:S(2)}) collective-permute-start(bf16[784,128]{1,0:T(8,128)(2,1)S(1)} %get-tuple-element.21), channel_id=1, source_target_pairs={{0,8},{1,9},{2,10},{3,11},{4,12},{5,13},{6,14},{7,15},{8,0},{9,1},... | collective-permute-start | bytes 602120 | tf_op jit(solution)/shard_map/ppermute | solution.py:499
  3.2 6.4 %collective-permute-start.1 = (bf16[784,128]{1,0:T(8,128)(2,1)S(1)}, bf16[784,128]{1,0:T(8,128)(2,1)S(1)}, u32[]{:S(2)}, u32[]{:S(2)}) collective-permute-start(bf16[784,128]{1,0:T(8,128)(2,1)S(1)} %get-tuple-element.22), channel_id=1, source_target_pairs={{0,1},{1,0},{2,3},{3,2},{4,5},{5,4},{6,7},{7,6},{8,16},{9,17},{10,... | collective-permute-start | bytes 602120 | tf_op jit(solution)/shard_map/ppermute | solution.py:499
  3.2 8.9 %collective-permute-start.2 = (bf16[784,128]{1,0:T(8,128)(2,1)S(1)}, bf16[784,128]{1,0:T(8,128)(2,1)S(1)}, u32[]{:S(2)}, u32[]{:S(2)}) collective-permute-start(bf16[784,128]{1,0:T(8,128)(2,1)S(1)} %get-tuple-element.23), channel_id=1, source_target_pairs={{0,1},{1,0},{2,3},{3,2},{4,5},{5,4},{6,7},{7,6},{8,9},{9,8},{10,11... | collective-permute-start | bytes 602120 | tf_op jit(solution)/shard_map/ppermute | solution.py:499
  3.2 8.9 %collective-permute-start.3 = (bf16[784,128]{1,0:T(8,128)(2,1)S(1)}, bf16[784,128]{1,0:T(8,128)(2,1)S(1)}, u32[]{:S(2)}, u32[]{:S(2)}) collective-permute-start(bf16[784,128]{1,0:T(8,128)(2,1)S(1)} %get-tuple-element.24), channel_id=1, source_target_pairs={{0,8},{1,2},{2,1},{3,4},{4,3},{5,6},{6,5},{7,15},{8,0},{9,10},{10,... | collective-permute-start | bytes 602120 | tf_op jit(solution)/shard_map/ppermute | solution.py:499
  9.6 1.6 %copy-start.1 = (s32[2,2,2,6]{3,2,1,0:T(2,128)S(1)}, s32[2,2,2,6]{3,2,1,0:T(2,128)}, u32[]{:S(2)}) copy-start(s32[2,2,2,6]{3,2,1,0:T(2,128)} %links_hbm.1) | copy-start | bytes 580
  9.6 4.0 %collective-permute-start.5 = (bf16[32,128]{1,0:T(8,128)(2,1)S(1)}, bf16[32,128]{1,0:T(8,128)(2,1)S(1)}, u32[]{:S(2)}, u32[]{:S(2)}) collective-permute-start(bf16[32,128]{1,0:T(8,128)(2,1)S(1)} %pad_maximum_fusion), channel_id=1, source_target_pairs={{0,8},{1,2},{2,1},{3,4},{4,3},{5,6},{6,5},{7,15},{8,0},{9,10},{10,... | collective-permute-start | bytes 24584 | tf_op jit(solution)/shard_map/ppermute | solution.py:499
  9.6 4.0 %collective-permute-start.4 = (bf16[32,128]{1,0:T(8,128)(2,1)S(1)}, bf16[32,128]{1,0:T(8,128)(2,1)S(1)}, u32[]{:S(2)}, u32[]{:S(2)}) collective-permute-start(bf16[32,128]{1,0:T(8,128)(2,1)S(1)} %pad_maximum_fusion), channel_id=1, source_target_pairs={{0,1},{1,0},{2,3},{3,2},{4,5},{5,4},{6,7},{7,6},{8,9},{9,8},{10,11... | collective-permute-start | bytes 24584 | tf_op jit(solution)/shard_map/ppermute | solution.py:499
  17.4 2.6 %collective-permute-start.6 = (bf16[1056,128]{1,0:T(8,128)(2,1)S(1)}, bf16[1056,128]{1,0:T(8,128)(2,1)S(1)}, u32[]{:S(2)}, u32[]{:S(2)}) collective-permute-start(bf16[1056,128]{1,0:T(8,128)(2,1)S(1)} %get-tuple-element.26), channel_id=1, source_target_pairs={{0,1},{1,0},{2,3},{3,2},{4,5},{5,4},{6,7},{7,6},{8,9},{9,8},{10,11... | collective-permute-start | bytes 811016 | tf_op jit(solution)/shard_map/ppermute | solution.py:499
  17.4 9.1 %collective-permute-start.7 = (bf16[416,128]{1,0:T(8,128)(2,1)S(1)}, bf16[416,128]{1,0:T(8,128)(2,1)S(1)}, u32[]{:S(2)}, u32[]{:S(2)}) collective-permute-start(bf16[416,128]{1,0:T(8,128)(2,1)S(1)} %get-tuple-element.27), channel_id=1, source_target_pairs={{0,8},{1,2},{2,1},{3,4},{4,3},{5,6},{6,5},{7,15},{8,0},{9,10},{10,... | collective-permute-start | bytes 319496 | tf_op jit(solution)/shard_map/ppermute | solution.py:499
  18.1 6.9 %collective-permute-start.8 = (bf16[320,128]{1,0:T(8,128)(2,1)S(1)}, bf16[320,128]{1,0:T(8,128)(2,1)S(1)}, u32[]{:S(2)}, u32[]{:S(2)}) collective-permute-start(bf16[320,128]{1,0:T(8,128)(2,1)S(1)} %get-tuple-element.28), channel_id=1, source_target_pairs={{0,8},{1,10},{2,9},{3,12},{4,11},{5,14},{6,13},{7,15},{8,0},{9,2},... | collective-permute-start | bytes 245768 | tf_op jit(solution)/shard_map/ppermute | solution.py:499
  20.0 5.9 %collective-permute-start.9 = (bf16[320,128]{1,0:T(8,128)(2,1)S(1)}, bf16[320,128]{1,0:T(8,128)(2,1)S(1)}, u32[]{:S(2)}, u32[]{:S(2)}) collective-permute-start(bf16[320,128]{1,0:T(8,128)(2,1)S(1)} %get-tuple-element.29), channel_id=1, source_target_pairs={{0,7},{1,2},{2,1},{3,4},{4,3},{5,6},{6,5},{7,0},{8,16},{9,18},{10,... | collective-permute-start | bytes 245768 | tf_op jit(solution)/shard_map/ppermute | solution.py:499
  20.0 6.6 %collective-permute-start.10 = (bf16[480,128]{1,0:T(8,128)(2,1)S(1)}, bf16[480,128]{1,0:T(8,128)(2,1)S(1)}, u32[]{:S(2)}, u32[]{:S(2)}) collective-permute-start(bf16[480,128]{1,0:T(8,128)(2,1)S(1)} %get-tuple-element.30), channel_id=1, source_target_pairs={{0,8},{1,9},{2,10},{3,11},{4,12},{5,13},{6,14},{7,15},{8,0},{9,1},... | collective-permute-start | bytes 368648 | tf_op jit(solution)/shard_map/ppermute | solution.py:499
  22.3 5.5 %collective-permute-start.11 = (bf16[480,128]{1,0:T(8,128)(2,1)S(1)}, bf16[480,128]{1,0:T(8,128)(2,1)S(1)}, u32[]{:S(2)}, u32[]{:S(2)}) collective-permute-start(bf16[480,128]{1,0:T(8,128)(2,1)S(1)} %get-tuple-element.31), channel_id=1, source_target_pairs={{0,1},{1,0},{2,3},{3,2},{4,5},{5,4},{6,7},{7,6},{8,16},{9,17},{10,... | collective-permute-start | bytes 368648 | tf_op jit(solution)/shard_map/ppermute | solution.py:499

commit v6 on v4

--- a/solution.py
+++ b/solution.py
@@ -321,6 +321,9 @@
                     right[index, place * B : (place + 1) * B, position * PAIR : (position + 1) * PAIR] = jnp.zeros(
                         (B, PAIR), jnp.bfloat16
                     )
+    square = (PAIR, PAIR)
+    diagonal = lax.broadcasted_iota(jnp.int32, square, 0) == lax.broadcasted_iota(jnp.int32, square, 1)
+    unit = jnp.where(diagonal, 1.0, 0.0).astype(jnp.bfloat16)
     for (box, other), uses in users.items():
         found = box_rows(*box, *other)
         own = COLUMNS.index(other)
@@ -331,8 +334,10 @@
                 stored = swap_halves(value).astype(jnp.bfloat16) if place == 5 else rounded
                 right[index, place * B : (place + 1) * B, position * PAIR : (position + 1) * PAIR] = stored
             if box == (0, 0):
-                turned = value.T
-                turned = pair_lanes(turned[:B], turned[B:]).astype(jnp.bfloat16)
+                turned = lax.dot_general(
+                    unit, rounded, (((1,), (1,)), ((), ())), preferred_element_type=jnp.float32
+                ).astype(jnp.bfloat16)
+                turned = pair_lanes(turned[:B], turned[B:])
                 if t in STAR:
                     left_star[STAR.index(t) * B : (STAR.index(t) + 1) * B, own * PAIR : (own + 1) * PAIR] = turned
                 else:
@@ -368,16 +373,17 @@
                 blocks[IMAGE[2 * pair + 1]] = jnp.where(folded_half, swap_halves(top), bottom)
         return blocks
 
+    star = jnp.dot(left_star[...], image[...], preferred_element_type=jnp.float32)
+
     def contribution(t):
         if t in STAR:
-            rows = STAR.index(t) * B
-            product = jnp.dot(left_star[rows : rows + B, :], image[...], preferred_element_type=jnp.float32)
-        else:
-            index = COLUMNS.index(column_of(*t))
-            product = jnp.dot(
+            return fold(star[STAR.index(t) * B : (STAR.index(t) + 1) * B])
+        index = COLUMNS.index(column_of(*t))
+        return fold(
+            jnp.dot(
                 left_corner[index], image[index * PAIR : (index + 1) * PAIR, :], preferred_element_type=jnp.float32
             )
-        return fold(product)
+        )
 
     for ref, sent in (
         (to_y_first, TO_Y_FIRST),
@@ -568,7 +574,7 @@
     y_first = swapped(y_first, 0, 1)
     x_first, x_second = call(relay_kernel, [VMEM] * 2, [sent(TO_X[1]), sent(TO_X[-1])])(rest, y_first)
     x_first, x_second = swapped(x_first, 1, 0), swapped(x_second, 2, 0)
-    (own,) = call(own_kernel, [VMEM] * 5, [((len(OWN), HALF, PAIR), f32)], cost=1_000_000_000_000)(
+    (own,) = call(own_kernel, [VMEM] * 5, [((len(OWN), HALF, PAIR), f32)], cost=3_000_000_000)(
         rest, y_first, y_second, c_first, c_second
     )
     (out,) = call(

time: 30.1 us -> 27.5 us (0.914)
  the two profiles are of different devices: /device:TPU:0 before, /device:TPU:20 now
where the time goes in v6:
time: 27.5 us; the launch traced here: 27.2 us
  waiting for transfers between devices  10.5 us (38%)
  starting transfers between devices  10.2 us (37%)
  Pallas kernels  6.43 us (23%)
    ppermute x12, waiting for transfers between devices, swapped(): return lax.ppermute(value, ('sx', 'sy'), pairs)  10.5 us
    ppermute x12, starting transfers between devices, swapped(): return lax.ppermute(value, ('sx', 'sy'), pairs)  10.2 us
    pallas_call x1, Pallas kernels, per_device(): call(main_kernel, [VMEM] * 9, [sent(TO_Y_FIRST), sent(TO_Y_SECOND), sent(...  2.32 us
    pallas_call x1, Pallas kernels, per_device(): call(pack_matrix_kernel, [SMEM, VMEM], [((4, PAIR, 6 * B), bf16), whole],...  1.6 us
    pallas_call x1, Pallas kernels, per_device(): call(functools.partial(pack_kernel, lax.axis_size('sy')), [HBM, HBM, HBM]...  1.51 us
    pallas_call x1, Pallas kernels, per_device(): call(finish_kernel, [VMEM] * 3 + [HBM], [whole], [pltpu.VMEM((7, 7, B, B)...  0.89 us
  transfers between devices with their start and end apart: 12, of which 6 were waited for; matrix products, arithmetic and copies ran while one was open for 0% of the time, Pallas kernels for 6%

profile of v6, /device:TPU:20, one launch (start us, length us, event | category | flops | bytes accessed | tf_op | source)
XLA Modules:
  0.0 27.2 jit_solution(13838433437927305485)
XLA Ops:
  0.0 0.0 copy-start
  0.0 1.5 %shard_map.47 = (bf16[4,384,128]{2,1,0:T(8,128)(2,1)S(1)}, f32[32,128]{1,0:T(8,128)S(1)}, bf16[784,128]{1,0:T(8,128)(2,1)S(1)}, bf16[784,128]{1,0:T(8,128)(2,1)S...) custom-call(s32[2,2,2]{2,1,0:T(2,128)} %aggregate_hbm.1, s32[2,2,2,6]{3,2,1,0:T(2,128)} %links_hbm.1, ...), custom_call_target="tpu_custom_call" | custom-call | tf_op jit(solution)/shard_map/pallas_call | solution.py:526
  1.5 1.6 %collective-permute-start = (bf16[784,128]{1,0:T(8,128)(2,1)S(1)}, bf16[784,128]{1,0:T(8,128)(2,1)S(1)}, u32[]{:S(2)}, u32[]{:S(2)}) collective-permute-start(bf16[784,128]{1,0:T(8,128)(2,1)S(1)} %get-tuple-element.23), channel_id=1, source_target_pairs={{0,8},{1,9},{2,10},{3,11},{4,12},{5,13},{6,14},{7,15},{8,0},{9,1},... | collective-permute-start | bytes 602120 | tf_op jit(solution)/shard_map/ppermute | solution.py:502
  3.2 0.0 collective-permute-start.1
  3.2 0.0 collective-permute-start.2
  3.2 1.5 %collective-permute-start.3 = (bf16[784,128]{1,0:T(8,128)(2,1)S(1)}, bf16[784,128]{1,0:T(8,128)(2,1)S(1)}, u32[]{:S(2)}, u32[]{:S(2)}) collective-permute-start(bf16[784,128]{1,0:T(8,128)(2,1)S(1)} %get-tuple-element.26), channel_id=1, source_target_pairs={{0,8},{1,2},{2,1},{3,4},{4,3},{5,6},{6,5},{7,15},{8,0},{9,10},{10,... | collective-permute-start | bytes 602120 | tf_op jit(solution)/shard_map/ppermute | solution.py:502
  4.7 3.6 %collective-permute-done.x_first = bf16[784,128]{1,0:T(8,128)(2,1)S(1)} collective-permute-done((bf16[784,128]{1,0:T(8,128)(2,1)S(1)}, bf16[784,128]{1,0:T(8,128)(2,1)S(1)}, u32[]{:S(2)}, u32[]{:S(2)}) %collective-permute-start) | collective-permute-done | bytes 200736 | tf_op jit(solution)/shard_map/ppermute | solution.py:502
  8.3 1.3 %collective-permute-done.1.x_second = bf16[784,128]{1,0:T(8,128)(2,1)S(1)} collective-permute-done((bf16[784,128]{1,0:T(8,128)(2,1)S(1)}, bf16[784,128]{1,0:T(8,128)(2,1)S(1)}, u32[]{:S(2)}, u32[]{:S(2)}) %collective-permute-start.1) | collective-permute-done | bytes 200736 | tf_op jit(solution)/shard_map/ppermute | solution.py:502
  9.6 0.0 copy-start.1
  9.6 0.0 collective-permute-start.5
  9.6 1.6 %collective-permute-start.4 = (bf16[32,128]{1,0:T(8,128)(2,1)S(1)}, bf16[32,128]{1,0:T(8,128)(2,1)S(1)}, u32[]{:S(2)}, u32[]{:S(2)}) collective-permute-start(bf16[32,128]{1,0:T(8,128)(2,1)S(1)} %pad_maximum_fusion), channel_id=1, source_target_pairs={{0,1},{1,0},{2,3},{3,2},{4,5},{5,4},{6,7},{7,6},{8,9},{9,8},{10,11... | collective-permute-start | bytes 24584 | tf_op jit(solution)/shard_map/ppermute | solution.py:502
  11.3 0.0 copy-done
  11.3 0.0 copy-done.1
  11.3 1.6 %shard_map.46 = (bf16[4,128,384]{2,1,0:T(8,128)(2,1)S(1)}, bf16[7,7,64,64]{3,2,1,0:T(8,128)(2,1)}) custom-call(s32[2,2,2,6]{3,2,1,0:T(2,128)S(1)} %copy-done.1, bf16[2,2,2,7,64,64]{5,4,3,2,1,0:T(8,128)(2,1)S(1)} %copy-done), custom_call_target="tpu_custom_call" | custom-call | tf_op jit(solution)/shard_map/pallas_call | solution.py:544
  12.9 0.0 collective-permute-done.2.y_first
  12.9 0.0 collective-permute-done.3.y_second
  12.9 0.7 %collective-permute-done.5.c_second = bf16[32,128]{1,0:T(8,128)(2,1)S(1)} collective-permute-done((bf16[32,128]{1,0:T(8,128)(2,1)S(1)}, bf16[32,128]{1,0:T(8,128)(2,1)S(1)}, u32[]{:S(2)}, u32[]{:S(2)}) %collective-permute-start.5) | collective-permute-done | bytes 8224 | tf_op jit(solution)/shard_map/ppermute | solution.py:502
  13.6 0.0 collective-permute-done.4.c_first
  13.6 2.3 %shard_map.48 = (bf16[1056,128]{1,0:T(8,128)(2,1)S(1)}, bf16[416,128]{1,0:T(8,128)(2,1)S(1)}, bf16[320,128]{1,0:T(8,128)(2,1)S(1)}, bf16[320,128]{1,0:T(8,128)(2,1)S(1)}, f32[3,13,32,128]{3,2,1,0:T(8,128)S(1)}) custom-call(bf16[4,128,384]{2,1,0:T(8,128)(2,1)S(1)} %get-tuple-element.20.a_ref, bf16[4,384,128]{2,1,0:T(8,128)(2,1)S(1)} %get-tuple-element.21.rows_ref, ...), custom_call_target="tpu_custom_call" | custom-call | tf_op jit(solution)/shard_map/pallas_call | solution.py:555
  15.9 0.1 collective-permute-start.6
  16.0 0.8 %collective-permute-start.7 = (bf16[416,128]{1,0:T(8,128)(2,1)S(1)}, bf16[416,128]{1,0:T(8,128)(2,1)S(1)}, u32[]{:S(2)}, u32[]{:S(2)}) collective-permute-start(bf16[416,128]{1,0:T(8,128)(2,1)S(1)} %get-tuple-element.29), channel_id=1, source_target_pairs={{0,8},{1,2},{2,1},{3,4},{4,3},{5,6},{6,5},{7,15},{8,0},{9,10},{10,... | collective-permute-start | bytes 319496 | tf_op jit(solution)/shard_map/ppermute | solution.py:502
  16.8 2.1 %collective-permute-start.8 = (bf16[320,128]{1,0:T(8,128)(2,1)S(1)}, bf16[320,128]{1,0:T(8,128)(2,1)S(1)}, u32[]{:S(2)}, u32[]{:S(2)}) collective-permute-start(bf16[320,128]{1,0:T(8,128)(2,1)S(1)} %get-tuple-element.30), channel_id=1, source_target_pairs={{0,8},{1,10},{2,9},{3,12},{4,11},{5,14},{6,13},{7,15},{8,0},{9,2},... | collective-permute-start | bytes 245768 | tf_op jit(solution)/shard_map/ppermute | solution.py:502
  18.9 0.0 collective-permute-start.9
  19.0 0.0 collective-permute-done.6.y_first
  19.0 2.1 %collective-permute-start.10 = (bf16[480,128]{1,0:T(8,128)(2,1)S(1)}, bf16[480,128]{1,0:T(8,128)(2,1)S(1)}, u32[]{:S(2)}, u32[]{:S(2)}) collective-permute-start(bf16[480,128]{1,0:T(8,128)(2,1)S(1)} %get-tuple-element.32), channel_id=1, source_target_pairs={{0,8},{1,9},{2,10},{3,11},{4,12},{5,13},{6,14},{7,15},{8,0},{9,1},... | collective-permute-start | bytes 368648 | tf_op jit(solution)/shard_map/ppermute | solution.py:502
  21.0 0.3 %collective-permute-start.11 = (bf16[480,128]{1,0:T(8,128)(2,1)S(1)}, bf16[480,128]{1,0:T(8,128)(2,1)S(1)}, u32[]{:S(2)}, u32[]{:S(2)}) collective-permute-start(bf16[480,128]{1,0:T(8,128)(2,1)S(1)} %get-tuple-element.33), channel_id=1, source_target_pairs={{0,1},{1,0},{2,3},{3,2},{4,5},{5,4},{6,7},{7,6},{8,16},{9,17},{10,... | collective-permute-start | bytes 368648 | tf_op jit(solution)/shard_map/ppermute | solution.py:502
  21.3 2.4 %collective-permute-done.8.c_first = bf16[320,128]{1,0:T(8,128)(2,1)S(1)} collective-permute-done((bf16[320,128]{1,0:T(8,128)(2,1)S(1)}, bf16[320,128]{1,0:T(8,128)(2,1)S(1)}, u32[]{:S(2)}, u32[]{:S(2)}) %collective-permute-start.8) | collective-permute-done | bytes 81952 | tf_op jit(solution)/shard_map/ppermute | solution.py:502
  23.7 1.4 %collective-permute-done.9.c_second = bf16[320,128]{1,0:T(8,128)(2,1)S(1)} collective-permute-done((bf16[320,128]{1,0:T(8,128)(2,1)S(1)}, bf16[320,128]{1,0:T(8,128)(2,1)S(1)}, u32[]{:S(2)}, u32[]{:S(2)}) %collective-permute-start.9) | collective-permute-done | bytes 81952 | tf_op jit(solution)/shard_map/ppermute | solution.py:502
  25.2 0.0 collective-permute-done.7.y_second
  25.2 0.1 shard_map.49.own_ref
  25.2 0.0 collective-permute-done.10.x_first
  25.2 1.1 %collective-permute-done.11.x_second = bf16[480,128]{1,0:T(8,128)(2,1)S(1)} collective-permute-done((bf16[480,128]{1,0:T(8,128)(2,1)S(1)}, bf16[480,128]{1,0:T(8,128)(2,1)S(1)}, u32[]{:S(2)}, u32[]{:S(2)}) %collective-permute-start.11) | collective-permute-done | bytes 122912 | tf_op jit(solution)/shard_map/ppermute | solution.py:502
  26.3 0.9 %shard_map.51 = bf16[7,7,64,64]{3,2,1,0:T(8,128)(2,1)} custom-call(f32[23,32,128]{2,1,0:T(8,128)S(1)} %shard_map.49.own_ref, bf16[480,128]{1,0:T(8,128)(2,1)S(1)} %collective-permute-done.10.x_first, bf16[480,128]{1,0:T(8,128)(2,1)S(1)} %collective-permute-done.11.x_second, bf16[7,7,64,64]{3,2,1,0:T(8,128)(2,1)} %get-tuple-element.34._), custom_call_target="tpu_custom_call", output_to_operand_aliasing={{}: (3, {})} | custom-call | tf_op jit(solution)/shard_map/pallas_call | solution.py:580
  (4 shorter events, 0.0 us)
Async XLA Ops:
  0.0 11.3 %copy-start = (bf16[2,2,2,7,64,64]{5,4,3,2,1,0:T(8,128)(2,1)S(1)}, bf16[2,2,2,7,64,64]{5,4,3,2,1,0:T(8,128)(2,1)}, u32[]{:S(2)}) copy-start(bf16[2,2,2,7,64,64]{5,4,3,2,1,0:T(8,128)(2,1)} %a_ref.1) | copy-start | bytes 1376260
  1.5 6.8 %collective-permute-start = (bf16[784,128]{1,0:T(8,128)(2,1)S(1)}, bf16[784,128]{1,0:T(8,128)(2,1)S(1)}, u32[]{:S(2)}, u32[]{:S(2)}) collective-permute-start(bf16[784,128]{1,0:T(8,128)(2,1)S(1)} %get-tuple-element.23), channel_id=1, source_target_pairs={{0,8},{1,9},{2,10},{3,11},{4,12},{5,13},{6,14},{7,15},{8,0},{9,1},... | collective-permute-start | bytes 602120 | tf_op jit(solution)/shard_map/ppermute | solution.py:502
  3.2 6.4 %collective-permute-start.1 = (bf16[784,128]{1,0:T(8,128)(2,1)S(1)}, bf16[784,128]{1,0:T(8,128)(2,1)S(1)}, u32[]{:S(2)}, u32[]{:S(2)}) collective-permute-start(bf16[784,128]{1,0:T(8,128)(2,1)S(1)} %get-tuple-element.24), channel_id=1, source_target_pairs={{0,1},{1,0},{2,3},{3,2},{4,5},{5,4},{6,7},{7,6},{8,16},{9,17},{10,... | collective-permute-start | bytes 602120 | tf_op jit(solution)/shard_map/ppermute | solution.py:502
  3.2 9.7 %collective-permute-start.2 = (bf16[784,128]{1,0:T(8,128)(2,1)S(1)}, bf16[784,128]{1,0:T(8,128)(2,1)S(1)}, u32[]{:S(2)}, u32[]{:S(2)}) collective-permute-start(bf16[784,128]{1,0:T(8,128)(2,1)S(1)} %get-tuple-element.25), channel_id=1, source_target_pairs={{0,1},{1,0},{2,3},{3,2},{4,5},{5,4},{6,7},{7,6},{8,9},{9,8},{10,11... | collective-permute-start | bytes 602120 | tf_op jit(solution)/shard_map/ppermute | solution.py:502
  3.2 9.7 %collective-permute-start.3 = (bf16[784,128]{1,0:T(8,128)(2,1)S(1)}, bf16[784,128]{1,0:T(8,128)(2,1)S(1)}, u32[]{:S(2)}, u32[]{:S(2)}) collective-permute-start(bf16[784,128]{1,0:T(8,128)(2,1)S(1)} %get-tuple-element.26), channel_id=1, source_target_pairs={{0,8},{1,2},{2,1},{3,4},{4,3},{5,6},{6,5},{7,15},{8,0},{9,10},{10,... | collective-permute-start | bytes 602120 | tf_op jit(solution)/shard_map/ppermute | solution.py:502
  9.6 1.6 %copy-start.1 = (s32[2,2,2,6]{3,2,1,0:T(2,128)S(1)}, s32[2,2,2,6]{3,2,1,0:T(2,128)}, u32[]{:S(2)}) copy-start(s32[2,2,2,6]{3,2,1,0:T(2,128)} %links_hbm.1) | copy-start | bytes 580
  9.6 4.0 %collective-permute-start.5 = (bf16[32,128]{1,0:T(8,128)(2,1)S(1)}, bf16[32,128]{1,0:T(8,128)(2,1)S(1)}, u32[]{:S(2)}, u32[]{:S(2)}) collective-permute-start(bf16[32,128]{1,0:T(8,128)(2,1)S(1)} %pad_maximum_fusion), channel_id=1, source_target_pairs={{0,8},{1,2},{2,1},{3,4},{4,3},{5,6},{6,5},{7,15},{8,0},{9,10},{10,... | collective-permute-start | bytes 24584 | tf_op jit(solution)/shard_map/ppermute | solution.py:502
  9.6 4.0 %collective-permute-start.4 = (bf16[32,128]{1,0:T(8,128)(2,1)S(1)}, bf16[32,128]{1,0:T(8,128)(2,1)S(1)}, u32[]{:S(2)}, u32[]{:S(2)}) collective-permute-start(bf16[32,128]{1,0:T(8,128)(2,1)S(1)} %pad_maximum_fusion), channel_id=1, source_target_pairs={{0,1},{1,0},{2,3},{3,2},{4,5},{5,4},{6,7},{7,6},{8,9},{9,8},{10,11... | collective-permute-start | bytes 24584 | tf_op jit(solution)/shard_map/ppermute | solution.py:502
  15.9 3.0 %collective-permute-start.6 = (bf16[1056,128]{1,0:T(8,128)(2,1)S(1)}, bf16[1056,128]{1,0:T(8,128)(2,1)S(1)}, u32[]{:S(2)}, u32[]{:S(2)}) collective-permute-start(bf16[1056,128]{1,0:T(8,128)(2,1)S(1)} %get-tuple-element.28), channel_id=1, source_target_pairs={{0,1},{1,0},{2,3},{3,2},{4,5},{5,4},{6,7},{7,6},{8,9},{9,8},{10,11... | collective-permute-start | bytes 811016 | tf_op jit(solution)/shard_map/ppermute | solution.py:502
  16.0 9.1 %collective-permute-start.7 = (bf16[416,128]{1,0:T(8,128)(2,1)S(1)}, bf16[416,128]{1,0:T(8,128)(2,1)S(1)}, u32[]{:S(2)}, u32[]{:S(2)}) collective-permute-start(bf16[416,128]{1,0:T(8,128)(2,1)S(1)} %get-tuple-element.29), channel_id=1, source_target_pairs={{0,8},{1,2},{2,1},{3,4},{4,3},{5,6},{6,5},{7,15},{8,0},{9,10},{10,... | collective-permute-start | bytes 319496 | tf_op jit(solution)/shard_map/ppermute | solution.py:502
  16.8 6.9 %collective-permute-start.8 = (bf16[320,128]{1,0:T(8,128)(2,1)S(1)}, bf16[320,128]{1,0:T(8,128)(2,1)S(1)}, u32[]{:S(2)}, u32[]{:S(2)}) collective-permute-start(bf16[320,128]{1,0:T(8,128)(2,1)S(1)} %get-tuple-element.30), channel_id=1, source_target_pairs={{0,8},{1,10},{2,9},{3,12},{4,11},{5,14},{6,13},{7,15},{8,0},{9,2},... | collective-permute-start | bytes 245768 | tf_op jit(solution)/shard_map/ppermute | solution.py:502
  18.9 6.2 %collective-permute-start.9 = (bf16[320,128]{1,0:T(8,128)(2,1)S(1)}, bf16[320,128]{1,0:T(8,128)(2,1)S(1)}, u32[]{:S(2)}, u32[]{:S(2)}) collective-permute-start(bf16[320,128]{1,0:T(8,128)(2,1)S(1)} %get-tuple-element.31), channel_id=1, source_target_pairs={{0,7},{1,2},{2,1},{3,4},{4,3},{5,6},{6,5},{7,0},{8,16},{9,18},{10,... | collective-permute-start | bytes 245768 | tf_op jit(solution)/shard_map/ppermute | solution.py:502
  19.0 6.2 %collective-permute-start.10 = (bf16[480,128]{1,0:T(8,128)(2,1)S(1)}, bf16[480,128]{1,0:T(8,128)(2,1)S(1)}, u32[]{:S(2)}, u32[]{:S(2)}) collective-permute-start(bf16[480,128]{1,0:T(8,128)(2,1)S(1)} %get-tuple-element.32), channel_id=1, source_target_pairs={{0,8},{1,9},{2,10},{3,11},{4,12},{5,13},{6,14},{7,15},{8,0},{9,1},... | collective-permute-start | bytes 368648 | tf_op jit(solution)/shard_map/ppermute | solution.py:502
  21.0 5.3 %collective-permute-start.11 = (bf16[480,128]{1,0:T(8,128)(2,1)S(1)}, bf16[480,128]{1,0:T(8,128)(2,1)S(1)}, u32[]{:S(2)}, u32[]{:S(2)}) collective-permute-start(bf16[480,128]{1,0:T(8,128)(2,1)S(1)} %get-tuple-element.33), channel_id=1, source_target_pairs={{0,1},{1,0},{2,3},{3,2},{4,5},{5,4},{6,7},{7,6},{8,16},{9,17},{10,... | collective-permute-start | bytes 368648 | tf_op jit(solution)/shard_map/ppermute | solution.py:502

commit v7 on v6

--- a/solution.py
+++ b/solution.py
@@ -15,7 +15,7 @@
 BLOCK_ROWS = SLOTS * B
 BODY = 2 * BLOCK_ROWS
 TAIL = 16
-VMEM_LIMIT = 48 * 1024 * 1024
+VMEM_LIMIT = 20 * 1024 * 1024
 
 FACES = [(0, 0), (-1, 0), (1, 0), (0, -1), (0, 1), (0, 0)]
 COLUMNS = [(0, 0), (0, 1), (1, 0), (1, 1)]
@@ -188,7 +188,21 @@
                     ref[start : start + B, :] = packed
 
 
-def pack_matrix_kernel(links_ref, a_ref, out_ref, whole_hbm, zeros, sems):
+def notes_kernel(x_first, x_second, _, notes_ref):
+    notes_ref[0:TAIL, :] = x_first[BODY : BODY + TAIL, :]
+    notes_ref[TAIL : 2 * TAIL, :] = x_second[BODY : BODY + TAIL, :]
+
+
+def pack_matrix_kernel(links_hbm, a_hbm, out_ref, whole_hbm, a_ref, links_ref, zeros, a_sems, sems):
+    fetches = [
+        pltpu.make_async_copy(links_hbm, links_ref, a_sems.at[4]),
+        *(
+            pltpu.make_async_copy(a_hbm.at[px, py], a_ref.at[px, py], a_sems.at[index])
+            for index, (px, py) in enumerate(COLUMNS)
+        ),
+    ]
+    for fetch in fetches:
+        fetch.start()
     zeros[...] = jnp.zeros(zeros.shape, zeros.dtype)
     copies = []
     for jx in range(-3, 4):
@@ -202,6 +216,8 @@
                 )
     for copy in copies:
         copy.start()
+    for fetch in fetches:
+        fetch.wait()
     odd_x, odd_y = mirrored()
     for index, (px, py) in enumerate(COLUMNS):
         place = (px ^ odd_x, py ^ odd_y)
@@ -222,126 +238,167 @@
         copy.wait()
 
 
+def there(ox, oy, px, py):
+    return (1 - px if ox else px, 1 - py if oy else py)
+
+
+def slot_there(ox, oy, m):
+    m = SIDES_X[m] if ox else m
+    return SIDES_Y[m] if oy else m
+
+
+class Rows:
+    def __init__(self, rows_ref, meta_ref, from_x, from_y, corners):
+        self.rows_ref, self.from_x, self.from_y = rows_ref, from_x, from_y
+        self.notes = {(0, 0): meta_ref[...]}
+        for side, ref in from_x.items():
+            self.notes[side, 0] = ref[BODY : BODY + TAIL, :].astype(jnp.float32)
+        for side, ref in from_y.items():
+            self.notes[0, side] = ref[BODY : BODY + TAIL, :].astype(jnp.float32)
+        for oy, ref in corners.items():
+            self.notes[1, oy] = ref[0:TAIL, :].astype(jnp.float32)
+            self.notes[-1, oy] = ref[TAIL : 2 * TAIL, :].astype(jnp.float32)
+
+    def state_row(self, ox, oy, px, py):
+        index = COLUMNS.index(there(ox, oy, px, py))
+        return self.notes[ox, oy][index : index + 1]
+
+    def link_row(self, ox, oy, px, py, m):
+        if (ox, oy) == (0, 0):
+            index = (SLOTS - 1) * COLUMNS.index((px, py))
+        else:
+            index = (SLOTS - 1) * (py if ox else px)
+        index += 4 + slot_there(ox, oy, m) - 1
+        return self.notes[ox, oy][index : index + 1]
+
+    def block(self, ox, oy, px, py, m, chunk):
+        start = slot_there(ox, oy, m) * B + chunk * 16
+        if (ox, oy) == (0, 0):
+            return self.rows_ref[COLUMNS.index((px, py)), start : start + 16, :]
+        start += (py if ox else px) * BLOCK_ROWS
+        ref = self.from_x[ox] if ox else self.from_y[oy]
+        return ref[start : start + 16, :]
+
+    def sums(self, box, column, slots, begun=None):
+        (ox, oy), (px, py) = box, column
+        weights = {}
+        for m in slots:
+            dx, dy = FACES[m]
+            bx, nx = divmod(2 * ox + px + dx, 2)
+            by, ny = divmod(2 * oy + py + dy, 2)
+            state = self.state_row(bx, by, nx, ny)
+            if m == 5:
+                state = swap_halves(state)
+            for kind in range(3):
+                weight = jnp.where(state == kind, 1.0, 0.0)
+                if m > 0:
+                    weight = weight * self.link_row(ox, oy, px, py, m)
+                weights[m, kind] = jnp.broadcast_to(weight, (16, PAIR))
+        reach = targets(px, py)
+        chunks = {}
+        for chunk in range(4):
+            values = {m: self.block(ox, oy, px, py, m, chunk).astype(jnp.float32) for m in slots}
+            for t in box_set(px, py):
+                total = begun[t][chunk * 16 : chunk * 16 + 16] if begun and t in begun else None
+                for m in slots:
+                    for kind in range(3):
+                        if reach[m][kind] == t:
+                            term = values[m] * weights[m, kind]
+                            total = term if total is None else total + term
+                if total is not None:
+                    chunks.setdefault(t, []).append(total)
+        return {t: jnp.concatenate(parts, axis=0) for t, parts in chunks.items()}
+
+
+IMAGES = {column: image_set(*column) for column in COLUMNS}
+USERS = {}
+for _index, _column in enumerate(COLUMNS):
+    for _place, (_, _box, _other) in enumerate(around(*_column)):
+        USERS.setdefault((_box, _other), []).append((_index, _column, _place))
+BEGUN = [key for key in USERS if key[1][1] == 0 and key[0][1] == 0]
+LATE = [key for key in USERS if key[0][1] == -1]
+BEGUN_SLOT = 3
+
+
+def place_rows(found, box, other, right, left_star, left_corner):
+    unit = None
+    if box == (0, 0):
+        square = (PAIR, PAIR)
+        diagonal = lax.broadcasted_iota(jnp.int32, square, 0) == lax.broadcasted_iota(jnp.int32, square, 1)
+        unit = jnp.where(diagonal, 1.0, 0.0).astype(jnp.bfloat16)
+    own = COLUMNS.index(other)
+    for t, value in found.items():
+        rounded = value.astype(jnp.bfloat16)
+        for index, column, place in USERS[box, other]:
+            position = IMAGES[column].index((box[0] + t[0], box[1] + t[1]))
+            stored = swap_halves(value).astype(jnp.bfloat16) if place == 5 else rounded
+            right[index, place * B : (place + 1) * B, position * PAIR : (position + 1) * PAIR] = stored
+        if box == (0, 0):
+            turned = lax.dot_general(
+                unit, rounded, (((1,), (1,)), ((), ())), preferred_element_type=jnp.float32
+            ).astype(jnp.bfloat16)
+            turned = pair_lanes(turned[:B], turned[B:])
+            if t in STAR:
+                left_star[STAR.index(t) * B : (STAR.index(t) + 1) * B, own * PAIR : (own + 1) * PAIR] = turned
+            else:
+                left_corner[own] = turned
+
+
+def begin_kernel(rows_ref, meta_ref, x_first, x_second, y_first, c_first, right, left_star, left_corner, begun_ref):
+    rows = Rows(rows_ref, meta_ref, {1: x_first, -1: x_second}, {1: y_first}, {1: c_first})
+    for index, column in enumerate(COLUMNS):
+        for place, (_, box, other) in enumerate(around(*column)):
+            reached = {(box[0] + tx, box[1] + ty) for tx, ty in box_set(*other)}
+            for position, s in enumerate(IMAGES[column]):
+                if s not in reached:
+                    right[index, place * B : (place + 1) * B, position * PAIR : (position + 1) * PAIR] = jnp.zeros(
+                        (B, PAIR), jnp.bfloat16
+                    )
+    for box, other in USERS:
+        if (box, other) in LATE:
+            continue
+        slots = list(range(SLOTS))
+        open_targets = []
+        if (box, other) in BEGUN:
+            slots.remove(BEGUN_SLOT)
+            open_targets = targets(*other)[BEGUN_SLOT]
+        found = rows.sums(box, other, slots)
+        for place, t in enumerate(open_targets):
+            begun_ref[BEGUN.index((box, other)), place] = found.pop(t)
+        place_rows(found, box, other, right, left_star, left_corner)
+
+
 def main_kernel(
     a_ref,
     rows_ref,
     meta_ref,
     x_first,
     x_second,
-    y_first,
     y_second,
-    c_first,
     c_second,
+    begun_ref,
+    right_in,
+    left_star_in,
+    left_corner_in,
     to_y_first,
     to_y_second,
     to_c_first,
     to_c_second,
     rest_ref,
     right,
-    image,
     left_star,
     left_corner,
+    image,
 ):
-    from_x = {1: x_first, -1: x_second}
-    from_y = {1: y_first, -1: y_second}
-    notes = {(0, 0): meta_ref[...]}
-    corner_notes = {}
-    for side in (-1, 1):
-        notes[side, 0] = from_x[side][BODY : BODY + TAIL, :].astype(jnp.float32)
-        notes[0, side] = from_y[side][BODY : BODY + TAIL, :].astype(jnp.float32)
-    for ref, oy in ((c_first, 1), (c_second, -1)):
-        corner_notes[1, oy] = ref[0:TAIL, :].astype(jnp.float32)
-        corner_notes[-1, oy] = ref[TAIL : 2 * TAIL, :].astype(jnp.float32)
-
-    def there(ox, oy, px, py):
-        return (1 - px if ox else px, 1 - py if oy else py)
-
-    def slot_there(ox, oy, m):
-        m = SIDES_X[m] if ox else m
-        return SIDES_Y[m] if oy else m
-
-    def state_row(ox, oy, px, py):
-        index = COLUMNS.index(there(ox, oy, px, py))
-        note = corner_notes[ox, oy] if ox and oy else notes[ox, oy]
-        return note[index : index + 1]
-
-    def link_row(ox, oy, px, py, m):
-        if (ox, oy) == (0, 0):
-            index = (SLOTS - 1) * COLUMNS.index((px, py))
-        else:
-            index = (SLOTS - 1) * (py if ox else px)
-        index += 4 + slot_there(ox, oy, m) - 1
-        return notes[ox, oy][index : index + 1]
-
-    def block(ox, oy, px, py, m, chunk):
-        start = slot_there(ox, oy, m) * B + chunk * 16
-        if (ox, oy) == (0, 0):
-            return rows_ref[COLUMNS.index((px, py)), start : start + 16, :]
-        start += (py if ox else px) * BLOCK_ROWS
-        ref = from_x[ox] if ox else from_y[oy]
-        return ref[start : start + 16, :]
-
-    def box_rows(ox, oy, px, py):
-        weights = []
-        for m, (dx, dy) in enumerate(FACES):
-            bx, nx = divmod(2 * ox + px + dx, 2)
-            by, ny = divmod(2 * oy + py + dy, 2)
-            state = state_row(bx, by, nx, ny)
-            if m == 5:
-                state = swap_halves(state)
-            rows = []
-            for kind in range(3):
-                weight = jnp.where(state == kind, 1.0, 0.0)
-                if m > 0:
-                    weight = weight * link_row(ox, oy, px, py, m)
-                rows.append(jnp.broadcast_to(weight, (16, PAIR)))
-            weights.append(rows)
-        reach = targets(px, py)
-        chunks = {t: [] for t in box_set(px, py)}
-        for chunk in range(4):
-            values = [block(ox, oy, px, py, m, chunk).astype(jnp.float32) for m in range(SLOTS)]
-            for t in chunks:
-                total = None
-                for m in range(SLOTS):
-                    for kind in range(3):
-                        if reach[m][kind] == t:
-                            term = values[m] * weights[m][kind]
-                            total = term if total is None else total + term
-                chunks[t].append(total)
-        return {t: jnp.concatenate(parts, axis=0) for t, parts in chunks.items()}
-
-    images = {column: image_set(*column) for column in COLUMNS}
-    users = {}
-    for index, column in enumerate(COLUMNS):
-        for place, (_, box, other) in enumerate(around(*column)):
-            users.setdefault((box, other), []).append((index, column, place))
-            reached = {(box[0] + tx, box[1] + ty) for tx, ty in box_set(*other)}
-            for position, s in enumerate(images[column]):
-                if s not in reached:
-                    right[index, place * B : (place + 1) * B, position * PAIR : (position + 1) * PAIR] = jnp.zeros(
-                        (B, PAIR), jnp.bfloat16
-                    )
-    square = (PAIR, PAIR)
-    diagonal = lax.broadcasted_iota(jnp.int32, square, 0) == lax.broadcasted_iota(jnp.int32, square, 1)
-    unit = jnp.where(diagonal, 1.0, 0.0).astype(jnp.bfloat16)
-    for (box, other), uses in users.items():
-        found = box_rows(*box, *other)
-        own = COLUMNS.index(other)
-        for t, value in found.items():
-            rounded = value.astype(jnp.bfloat16)
-            for index, column, place in uses:
-                position = images[column].index((box[0] + t[0], box[1] + t[1]))
-                stored = swap_halves(value).astype(jnp.bfloat16) if place == 5 else rounded
-                right[index, place * B : (place + 1) * B, position * PAIR : (position + 1) * PAIR] = stored
-            if box == (0, 0):
-                turned = lax.dot_general(
-                    unit, rounded, (((1,), (1,)), ((), ())), preferred_element_type=jnp.float32
-                ).astype(jnp.bfloat16)
-                turned = pair_lanes(turned[:B], turned[B:])
-                if t in STAR:
-                    left_star[STAR.index(t) * B : (STAR.index(t) + 1) * B, own * PAIR : (own + 1) * PAIR] = turned
-                else:
-                    left_corner[own] = turned
+    images = IMAGES
+    rows = Rows(rows_ref, meta_ref, {1: x_first, -1: x_second}, {-1: y_second}, {-1: c_second})
+    for box, other in BEGUN:
+        begun = {
+            t: begun_ref[BEGUN.index((box, other)), place] for place, t in enumerate(targets(*other)[BEGUN_SLOT])
+        }
+        place_rows(rows.sums(box, other, [BEGUN_SLOT], begun), box, other, right, left_star, left_corner)
+    for box, other in LATE:
+        place_rows(rows.sums(box, other, list(range(SLOTS))), box, other, right, left_star, left_corner)
     half = low_half((B, PAIR))
     for index, column in enumerate(COLUMNS):
         product = jnp.dot(a_ref[index], right[index], preferred_element_type=jnp.float32)
@@ -492,10 +549,8 @@
     for x in range(count_x):
         for y in range(count_y):
             to_x, to_y = partner(x, move_x, count_x), partner(y, move_y, count_y)
-            if to_x is None and to_y is None:
-                to_x, to_y = x, count_y - 1 - y
-            elif to_x is None:
-                to_x, to_y = x, (y ^ 1 if move_y == 0 else to_y)
+            if to_x is None:
+                to_x, to_y = x, y ^ 1
             elif to_y is None:
                 to_x, to_y = (x ^ 1 if move_x == 0 else to_x), y
             pairs.append((x * count_y + y, to_x * count_y + to_y))
@@ -505,6 +560,7 @@
 SMEM = pl.BlockSpec(memory_space=pltpu.SMEM)
 VMEM = pl.BlockSpec(memory_space=pltpu.VMEM)
 HBM = pl.BlockSpec(memory_space=pltpu.HBM)
+ANY = pl.BlockSpec(memory_space=pl.ANY)
 
 
 def call(kernel, in_specs, outs, scratch=(), out_specs=None, aliases=None, cost=None):
@@ -520,13 +576,18 @@
     )
 
 
+def in_hbm(*values):
+    return [pltpu.with_memory_space_constraint(value, pltpu.HBM) for value in values]
+
+
 def per_device(fine_matrix, prolongator, aggregate, face_links):
     bf16, f32 = jnp.bfloat16, jnp.float32
     message = ((BODY + TAIL, PAIR), bf16)
+    longer = ((BODY + 2 * TAIL, PAIR), bf16)
     rows, meta, x_first, x_second, y_first, y_second = call(
         functools.partial(pack_kernel, lax.axis_size("sy")),
         [HBM, HBM, HBM],
-        [((4, BLOCK_ROWS, PAIR), bf16), ((32, PAIR), f32), message, message, message, message],
+        [((4, BLOCK_ROWS, PAIR), bf16), ((32, PAIR), f32), message, message, message, longer],
         [
             pltpu.VMEM((4, 2, 7, B, B), bf16),
             pltpu.SMEM((2, 2, 2), jnp.int32),
@@ -534,41 +595,62 @@
             pltpu.SemaphoreType.DMA((4,)),
             pltpu.SemaphoreType.DMA((2,)),
         ],
-    )(*(pltpu.with_memory_space_constraint(value, pltpu.HBM) for value in (aggregate, face_links, prolongator)))
+    )(*in_hbm(aggregate, face_links, prolongator))
     y_second = swapped(y_second, 0, 2)
     x_first, x_second = swapped(x_first, 1, 0), swapped(x_second, 2, 0)
     y_first = swapped(y_first, 0, 1)
-    notes = jnp.concatenate([x_first[BODY:], x_second[BODY:]], axis=0)
-    c_first, c_second = swapped(notes, 0, 1), swapped(notes, 0, 2)
     whole = ((7, 7, B, B), bf16)
     matrix, out = call(
         pack_matrix_kernel,
-        [SMEM, VMEM],
+        [HBM, HBM],
         [((4, PAIR, 6 * B), bf16), whole],
-        [pltpu.VMEM((3, B, B), bf16), pltpu.SemaphoreType.DMA((12,))],
+        [
+            pltpu.VMEM((2, 2, 2, 7, B, B), bf16),
+            pltpu.SMEM((2, 2, 2, 6), jnp.int32),
+            pltpu.VMEM((3, B, B), bf16),
+            pltpu.SemaphoreType.DMA((5,)),
+            pltpu.SemaphoreType.DMA((12,)),
+        ],
         [VMEM, HBM],
-    )(face_links, fine_matrix)
+    )(*in_hbm(face_links, fine_matrix))
+    (notes,) = call(notes_kernel, [VMEM, VMEM, ANY], [((2 * TAIL, PAIR), bf16)])(x_first, x_second, matrix)
+    c_first, c_second = swapped(notes, 0, 1), swapped(notes, 0, 2)
 
     def sent(blocks):
         return ((len(blocks) * HALF, PAIR), bf16)
 
-    y_first, y_second, c_first, c_second, rest = call(
+    lefts = [
+        ((4, SLOTS * B, 10 * PAIR), bf16),
+        ((len(STAR) * B, 4 * PAIR), bf16),
+        ((4, B, PAIR), bf16),
+    ]
+    *lefts_begun, begun = call(begin_kernel, [VMEM] * 6, lefts + [((len(BEGUN), 3, B, PAIR), f32)])(
+        rows, meta, x_first, x_second, y_first, c_first
+    )
+    y_first, y_second, c_first, c_second, rest, *_ = call(
         main_kernel,
-        [VMEM] * 9,
+        [VMEM] * 11,
         [
             sent(TO_Y_FIRST),
             sent(TO_Y_SECOND),
             sent(TO_C_FIRST),
             sent(TO_C_SECOND),
             ((3, len(IMAGE), HALF, PAIR), f32),
-        ],
-        [
-            pltpu.VMEM((4, 6 * B, 10 * PAIR), bf16),
-            pltpu.VMEM((4 * PAIR, IMAGE_PAIRS * PAIR), bf16),
-            pltpu.VMEM((len(STAR) * B, 4 * PAIR), bf16),
-            pltpu.VMEM((4, B, PAIR), bf16),
-        ],
-    )(matrix, rows, meta, x_first, x_second, y_first, y_second, c_first, c_second)
+        ]
+        + lefts,
+        [pltpu.VMEM((4 * PAIR, IMAGE_PAIRS * PAIR), bf16)],
+        aliases={8: 5, 9: 6, 10: 7},
+    )(
+        matrix,
+        rows,
+        meta,
+        x_first,
+        x_second,
+        y_second,
+        c_second,
+        begun,
+        *(pltpu.with_memory_space_constraint(left, pltpu.VMEM) for left in lefts_begun),
+    )
     y_second = swapped(y_second, 0, 2)
     c_first, c_second = swapped(c_first, 1, 2), swapped(c_second, 2, 2)
     y_first = swapped(y_first, 0, 1)

time: 27.5 us -> 27 us (0.982)
  waiting for transfers between devices: 10.5 us -> 9.16 us
  Pallas kernels: 6.43 us -> 7 us
  starting transfers between devices: 10.2 us -> 10.5 us
    ppermute x12, waiting for transfers between devices: 10.5 us -> 9.16 us  [swapped(): return lax.ppermute(value, ('sx', 'sy'), pairs)]
    pallas_call x2 -> x4, Pallas kernels: 3.93 us -> 4.5 us  [the longest x1 1.78 us: per_device(): call(pack_matrix_kernel, [HBM, HBM], [((4, PAIR, 6 * B), bf16), whole], [...]
    ppermute x12, starting transfers between devices: 10.2 us -> 10.5 us  [swapped(): return lax.ppermute(value, ('sx', 'sy'), pairs)]
  transfers between devices with their start and end apart: 12 -> 12, of which waited for: 6 -> 5; matrix products, arithmetic and copies ran while one was open for 0% -> 0% of each run, Pallas kernels for 6% -> 11%
where the time goes in v7:
time: 27 us; the launch traced here: 26.7 us
  starting transfers between devices  10.5 us (39%)
  waiting for transfers between devices  9.16 us (34%)
  Pallas kernels  7 us (26%)
    ppermute x12, starting transfers between devices, swapped(): return lax.ppermute(value, ('sx', 'sy'), pairs)  10.5 us
    ppermute x12, waiting for transfers between devices, swapped(): return lax.ppermute(value, ('sx', 'sy'), pairs)  9.16 us
    pallas_call x1, Pallas kernels, per_device(): call(pack_matrix_kernel, [HBM, HBM], [((4, PAIR, 6 * B), bf16), whole], [...  1.78 us
    pallas_call x1, Pallas kernels, per_device(): call(main_kernel, [VMEM] * 11, [sent(TO_Y_FIRST), sent(TO_Y_SECOND), sent...  1.65 us
    pallas_call x1, Pallas kernels, per_device(): call(functools.partial(pack_kernel, lax.axis_size('sy')), [HBM, HBM, HBM]...  1.48 us
    pallas_call x1, Pallas kernels, per_device(): call(begin_kernel, [VMEM] * 6, lefts + [((len(BEGUN), 3, B, PAIR), f32)])  1.07 us
    pallas_call x1, Pallas kernels, per_device(): call(finish_kernel, [VMEM] * 3 + [HBM], [whole], [pltpu.VMEM((7, 7, B, B)...  0.89 us
  transfers between devices with their start and end apart: 12, of which 5 were waited for; matrix products, arithmetic and copies ran while one was open for 0% of the time, Pallas kernels for 11%

profile of v7, /device:TPU:20, one launch (start us, length us, event | category | flops | bytes accessed | tf_op | source)
XLA Modules:
  0.0 26.7 jit_solution(6992881051840572588)
XLA Ops:
  0.0 1.5 %shard_map.47 = (bf16[4,384,128]{2,1,0:T(8,128)(2,1)S(1)}, f32[32,128]{1,0:T(8,128)S(1)}, bf16[784,128]{1,0:T(8,128)(2,1)S(1)}, bf16[784,128]{1,0:T(8,128)(2,1)S...) custom-call(s32[2,2,2]{2,1,0:T(2,128)} %aggregate_hbm.1, s32[2,2,2,6]{3,2,1,0:T(2,128)} %links_hbm.3, ...), custom_call_target="tpu_custom_call" | custom-call | tf_op jit(solution)/shard_map/pallas_call | solution.py:587
  1.5 1.6 %collective-permute-start = (bf16[784,128]{1,0:T(8,128)(2,1)S(1)}, bf16[784,128]{1,0:T(8,128)(2,1)S(1)}, u32[]{:S(2)}, u32[]{:S(2)}) collective-permute-start(bf16[784,128]{1,0:T(8,128)(2,1)S(1)} %get-tuple-element.27), channel_id=1, source_target_pairs={{0,8},{1,9},{2,10},{3,11},{4,12},{5,13},{6,14},{7,15},{8,0},{9,1},... | collective-permute-start | bytes 602120 | tf_op jit(solution)/shard_map/ppermute | solution.py:557
  3.1 0.0 collective-permute-start.1
  3.1 0.6 %collective-permute-start.2 = (bf16[800,128]{1,0:T(8,128)(2,1)S(1)}, bf16[800,128]{1,0:T(8,128)(2,1)S(1)}, u32[]{:S(2)}, u32[]{:S(2)}) collective-permute-start(bf16[800,128]{1,0:T(8,128)(2,1)S(1)} %get-tuple-element.29), channel_id=1, source_target_pairs={{0,8},{1,2},{2,1},{3,4},{4,3},{5,6},{6,5},{7,15},{8,0},{9,10},{10,... | collective-permute-start | bytes 614408 | tf_op jit(solution)/shard_map/ppermute | solution.py:557
  3.7 1.0 %collective-permute-start.4 = (bf16[784,128]{1,0:T(8,128)(2,1)S(1)}, bf16[784,128]{1,0:T(8,128)(2,1)S(1)}, u32[]{:S(2)}, u32[]{:S(2)}) collective-permute-start(bf16[784,128]{1,0:T(8,128)(2,1)S(1)} %get-tuple-element.30), channel_id=1, source_target_pairs={{0,1},{1,0},{2,3},{3,2},{4,5},{5,4},{6,7},{7,6},{8,9},{9,8},{10,11... | collective-permute-start | bytes 602120 | tf_op jit(solution)/shard_map/ppermute | solution.py:557
  4.7 1.8 %shard_map.46 = (bf16[4,128,384]{2,1,0:T(8,128)(2,1)S(1)}, bf16[7,7,64,64]{3,2,1,0:T(8,128)(2,1)}) custom-call(s32[2,2,2,6]{3,2,1,0:T(2,128)} %links_hbm.3, bf16[2,2,2,7,64,64]{5,4,3,2,1,0:T(8,128)(2,1)} %a_hbm.1), custom_call_target="tpu_custom_call" | custom-call | tf_op jit(solution)/shard_map/pallas_call | solution.py:603
  6.5 1.8 %collective-permute-done.x_first = bf16[784,128]{1,0:T(8,128)(2,1)S(1)} collective-permute-done((bf16[784,128]{1,0:T(8,128)(2,1)S(1)}, bf16[784,128]{1,0:T(8,128)(2,1)S(1)}, u32[]{:S(2)}, u32[]{:S(2)}) %collective-permute-start) | collective-permute-done | bytes 200736 | tf_op jit(solution)/shard_map/ppermute | solution.py:557
  8.3 1.3 %collective-permute-done.1.x_second = bf16[784,128]{1,0:T(8,128)(2,1)S(1)} collective-permute-done((bf16[784,128]{1,0:T(8,128)(2,1)S(1)}, bf16[784,128]{1,0:T(8,128)(2,1)S(1)}, u32[]{:S(2)}, u32[]{:S(2)}) %collective-permute-start.1) | collective-permute-done | bytes 200736 | tf_op jit(solution)/shard_map/ppermute | solution.py:557
  9.6 0.0 collective-permute-start.5
  9.6 1.5 %collective-permute-start.3 = (bf16[32,128]{1,0:T(8,128)(2,1)S(1)}, bf16[32,128]{1,0:T(8,128)(2,1)S(1)}, u32[]{:S(2)}, u32[]{:S(2)}) collective-permute-start(bf16[32,128]{1,0:T(8,128)(2,1)S(1)} %shard_map.48), channel_id=1, source_target_pairs={{0,8},{1,2},{2,1},{3,4},{4,3},{5,6},{6,5},{7,15},{8,0},{9,10},{10,... | collective-permute-start | bytes 24584 | tf_op jit(solution)/shard_map/ppermute | solution.py:557
  11.1 0.0 collective-permute-done.4.y_first
  11.1 0.0 collective-permute-done.5.c_first
  11.1 1.1 %shard_map.49 = (bf16[4,384,1280]{2,1,0:T(8,128)(2,1)S(1)}, bf16[320,512]{1,0:T(8,128)(2,1)S(1)}, bf16[4,64,128]{2,1,0:T(8,128)(2,1)S(1)}, f32[4,3,64,128]{3,2,1,0:T(8,128)S(1)}) custom-call(bf16[4,384,128]{2,1,0:T(8,128)(2,1)S(1)} %get-tuple-element.25.rows_ref, f32[32,128]{1,0:T(8,128)S(1)} %get-tuple-element.26.meta_ref, ...), custom_call_target="tpu_custom_call" | custom-call | tf_op jit(solution)/shard_map/pallas_call | solution.py:627
  12.2 0.0 collective-permute-done.2.y_second
  12.2 1.3 %collective-permute-done.3.c_second = bf16[32,128]{1,0:T(8,128)(2,1)S(1)} collective-permute-done((bf16[32,128]{1,0:T(8,128)(2,1)S(1)}, bf16[32,128]{1,0:T(8,128)(2,1)S(1)}, u32[]{:S(2)}, u32[]{:S(2)}) %collective-permute-start.3) | collective-permute-done | bytes 8224 | tf_op jit(solution)/shard_map/ppermute | solution.py:557
  13.6 1.6 %shard_map.50 = (bf16[1056,128]{1,0:T(8,128)(2,1)S(1)}, bf16[416,128]{1,0:T(8,128)(2,1)S(1)}, bf16[320,128]{1,0:T(8,128)(2,1)S(1)}, bf16[320,128]{1,0:T(8,128)(2...) custom-call(bf16[4,128,384]{2,1,0:T(8,128)(2,1)S(1)} %get-tuple-elem, ...), custom_call_target="tpu_custom_call", output_to_operand_aliasing={{5}: (8, {}), {6}: (9, {}), {7}: (10, {})} | custom-call | tf_op jit(solution)/shard_map/pallas_call | solution.py:630
  15.2 0.1 collective-permute-start.6
  15.3 1.6 %collective-permute-start.7 = (bf16[416,128]{1,0:T(8,128)(2,1)S(1)}, bf16[416,128]{1,0:T(8,128)(2,1)S(1)}, u32[]{:S(2)}, u32[]{:S(2)}) collective-permute-start(bf16[416,128]{1,0:T(8,128)(2,1)S(1)} %get-tuple-element.37), channel_id=1, source_target_pairs={{0,8},{1,2},{2,1},{3,4},{4,3},{5,6},{6,5},{7,15},{8,0},{9,10},{10,... | collective-permute-start | bytes 319496 | tf_op jit(solution)/shard_map/ppermute | solution.py:557
  16.9 0.9 %collective-permute-start.8 = (bf16[320,128]{1,0:T(8,128)(2,1)S(1)}, bf16[320,128]{1,0:T(8,128)(2,1)S(1)}, u32[]{:S(2)}, u32[]{:S(2)}) collective-permute-start(bf16[320,128]{1,0:T(8,128)(2,1)S(1)} %get-tuple-element.38), channel_id=1, source_target_pairs={{0,8},{1,10},{2,9},{3,12},{4,11},{5,14},{6,13},{7,15},{8,0},{9,2},... | collective-permute-start | bytes 245768 | tf_op jit(solution)/shard_map/ppermute | solution.py:557
  17.8 0.2 collective-permute-start.9
  18.0 0.0 collective-permute-done.6.y_first
  18.1 1.5 %collective-permute-start.10 = (bf16[480,128]{1,0:T(8,128)(2,1)S(1)}, bf16[480,128]{1,0:T(8,128)(2,1)S(1)}, u32[]{:S(2)}, u32[]{:S(2)}) collective-permute-start(bf16[480,128]{1,0:T(8,128)(2,1)S(1)} %get-tuple-element.40), channel_id=1, source_target_pairs={{0,8},{1,9},{2,10},{3,11},{4,12},{5,13},{6,14},{7,15},{8,0},{9,1},... | collective-permute-start | bytes 368648 | tf_op jit(solution)/shard_map/ppermute | solution.py:557
  19.6 1.3 %collective-permute-start.11 = (bf16[480,128]{1,0:T(8,128)(2,1)S(1)}, bf16[480,128]{1,0:T(8,128)(2,1)S(1)}, u32[]{:S(2)}, u32[]{:S(2)}) collective-permute-start(bf16[480,128]{1,0:T(8,128)(2,1)S(1)} %get-tuple-element.41), channel_id=1, source_target_pairs={{0,1},{1,0},{2,3},{3,2},{4,5},{5,4},{6,7},{7,6},{8,16},{9,17},{10,... | collective-permute-start | bytes 368648 | tf_op jit(solution)/shard_map/ppermute | solution.py:557
  20.9 4.0 %collective-permute-done.8.c_first = bf16[320,128]{1,0:T(8,128)(2,1)S(1)} collective-permute-done((bf16[320,128]{1,0:T(8,128)(2,1)S(1)}, bf16[320,128]{1,0:T(8,128)(2,1)S(1)}, u32[]{:S(2)}, u32[]{:S(2)}) %collective-permute-start.8) | collective-permute-done | bytes 81952 | tf_op jit(solution)/shard_map/ppermute | solution.py:557
  24.9 0.0 collective-permute-done.9.c_second
  24.9 0.0 collective-permute-done.7.y_second
  24.9 0.1 shard_map.51.own_ref
  25.0 0.0 collective-permute-done.10.x_first
  25.0 0.8 %collective-permute-done.11.x_second = bf16[480,128]{1,0:T(8,128)(2,1)S(1)} collective-permute-done((bf16[480,128]{1,0:T(8,128)(2,1)S(1)}, bf16[480,128]{1,0:T(8,128)(2,1)S(1)}, u32[]{:S(2)}, u32[]{:S(2)}) %collective-permute-start.11) | collective-permute-done | bytes 122912 | tf_op jit(solution)/shard_map/ppermute | solution.py:557
  25.8 0.9 %shard_map.53 = bf16[7,7,64,64]{3,2,1,0:T(8,128)(2,1)} custom-call(f32[23,32,128]{2,1,0:T(8,128)S(1)} %shard_map.51.own_ref, bf16[480,128]{1,0:T(8,128)(2,1)S(1)} %collective-permute-done.10.x_first, bf16[480,128]{1,0:T(8,128)(2,1)S(1)} %collective-permute-done.11.x_second, bf16[7,7,64,64]{3,2,1,0:T(8,128)(2,1)} %get-tuple-element.42._), custom_call_target="tpu_custom_call", output_to_operand_aliasing={{}: (3, {})} | custom-call | tf_op jit(solution)/shard_map/pallas_call | solution.py:662
  (2 shorter events, 0.1 us)
Async XLA Ops:
  1.5 6.8 %collective-permute-start = (bf16[784,128]{1,0:T(8,128)(2,1)S(1)}, bf16[784,128]{1,0:T(8,128)(2,1)S(1)}, u32[]{:S(2)}, u32[]{:S(2)}) collective-permute-start(bf16[784,128]{1,0:T(8,128)(2,1)S(1)} %get-tuple-element.27), channel_id=1, source_target_pairs={{0,8},{1,9},{2,10},{3,11},{4,12},{5,13},{6,14},{7,15},{8,0},{9,1},... | collective-permute-start | bytes 602120 | tf_op jit(solution)/shard_map/ppermute | solution.py:557
  3.1 6.4 %collective-permute-start.1 = (bf16[784,128]{1,0:T(8,128)(2,1)S(1)}, bf16[784,128]{1,0:T(8,128)(2,1)S(1)}, u32[]{:S(2)}, u32[]{:S(2)}) collective-permute-start(bf16[784,128]{1,0:T(8,128)(2,1)S(1)} %get-tuple-element.28), channel_id=1, source_target_pairs={{0,1},{1,0},{2,3},{3,2},{4,5},{5,4},{6,7},{7,6},{8,16},{9,17},{10,... | collective-permute-start | bytes 602120 | tf_op jit(solution)/shard_map/ppermute | solution.py:557
  3.1 9.1 %collective-permute-start.2 = (bf16[800,128]{1,0:T(8,128)(2,1)S(1)}, bf16[800,128]{1,0:T(8,128)(2,1)S(1)}, u32[]{:S(2)}, u32[]{:S(2)}) collective-permute-start(bf16[800,128]{1,0:T(8,128)(2,1)S(1)} %get-tuple-element.29), channel_id=1, source_target_pairs={{0,8},{1,2},{2,1},{3,4},{4,3},{5,6},{6,5},{7,15},{8,0},{9,10},{10,... | collective-permute-start | bytes 614408 | tf_op jit(solution)/shard_map/ppermute | solution.py:557
  3.7 7.4 %collective-permute-start.4 = (bf16[784,128]{1,0:T(8,128)(2,1)S(1)}, bf16[784,128]{1,0:T(8,128)(2,1)S(1)}, u32[]{:S(2)}, u32[]{:S(2)}) collective-permute-start(bf16[784,128]{1,0:T(8,128)(2,1)S(1)} %get-tuple-element.30), channel_id=1, source_target_pairs={{0,1},{1,0},{2,3},{3,2},{4,5},{5,4},{6,7},{7,6},{8,9},{9,8},{10,11... | collective-permute-start | bytes 602120 | tf_op jit(solution)/shard_map/ppermute | solution.py:557
  9.6 1.6 %collective-permute-start.5 = (bf16[32,128]{1,0:T(8,128)(2,1)S(1)}, bf16[32,128]{1,0:T(8,128)(2,1)S(1)}, u32[]{:S(2)}, u32[]{:S(2)}) collective-permute-start(bf16[32,128]{1,0:T(8,128)(2,1)S(1)} %shard_map.48), channel_id=1, source_target_pairs={{0,1},{1,0},{2,3},{3,2},{4,5},{5,4},{6,7},{7,6},{8,9},{9,8},{10,11... | collective-permute-start | bytes 24584 | tf_op jit(solution)/shard_map/ppermute | solution.py:557
  9.6 4.0 %collective-permute-start.3 = (bf16[32,128]{1,0:T(8,128)(2,1)S(1)}, bf16[32,128]{1,0:T(8,128)(2,1)S(1)}, u32[]{:S(2)}, u32[]{:S(2)}) collective-permute-start(bf16[32,128]{1,0:T(8,128)(2,1)S(1)} %shard_map.48), channel_id=1, source_target_pairs={{0,8},{1,2},{2,1},{3,4},{4,3},{5,6},{6,5},{7,15},{8,0},{9,10},{10,... | collective-permute-start | bytes 24584 | tf_op jit(solution)/shard_map/ppermute | solution.py:557
  15.2 2.8 %collective-permute-start.6 = (bf16[1056,128]{1,0:T(8,128)(2,1)S(1)}, bf16[1056,128]{1,0:T(8,128)(2,1)S(1)}, u32[]{:S(2)}, u32[]{:S(2)}) collective-permute-start(bf16[1056,128]{1,0:T(8,128)(2,1)S(1)} %get-tuple-element.36), channel_id=1, source_target_pairs={{0,1},{1,0},{2,3},{3,2},{4,5},{5,4},{6,7},{7,6},{8,9},{9,8},{10,11... | collective-permute-start | bytes 811016 | tf_op jit(solution)/shard_map/ppermute | solution.py:557
  15.3 9.6 %collective-permute-start.7 = (bf16[416,128]{1,0:T(8,128)(2,1)S(1)}, bf16[416,128]{1,0:T(8,128)(2,1)S(1)}, u32[]{:S(2)}, u32[]{:S(2)}) collective-permute-start(bf16[416,128]{1,0:T(8,128)(2,1)S(1)} %get-tuple-element.37), channel_id=1, source_target_pairs={{0,8},{1,2},{2,1},{3,4},{4,3},{5,6},{6,5},{7,15},{8,0},{9,10},{10,... | collective-permute-start | bytes 319496 | tf_op jit(solution)/shard_map/ppermute | solution.py:557
  16.9 8.0 %collective-permute-start.8 = (bf16[320,128]{1,0:T(8,128)(2,1)S(1)}, bf16[320,128]{1,0:T(8,128)(2,1)S(1)}, u32[]{:S(2)}, u32[]{:S(2)}) collective-permute-start(bf16[320,128]{1,0:T(8,128)(2,1)S(1)} %get-tuple-element.38), channel_id=1, source_target_pairs={{0,8},{1,10},{2,9},{3,12},{4,11},{5,14},{6,13},{7,15},{8,0},{9,2},... | collective-permute-start | bytes 245768 | tf_op jit(solution)/shard_map/ppermute | solution.py:557
  17.8 7.1 %collective-permute-start.9 = (bf16[320,128]{1,0:T(8,128)(2,1)S(1)}, bf16[320,128]{1,0:T(8,128)(2,1)S(1)}, u32[]{:S(2)}, u32[]{:S(2)}) collective-permute-start(bf16[320,128]{1,0:T(8,128)(2,1)S(1)} %get-tuple-element.39), channel_id=1, source_target_pairs={{0,1},{1,0},{2,3},{3,2},{4,5},{5,4},{6,7},{7,6},{8,16},{9,18},{10,... | collective-permute-start | bytes 245768 | tf_op jit(solution)/shard_map/ppermute | solution.py:557
  18.1 6.9 %collective-permute-start.10 = (bf16[480,128]{1,0:T(8,128)(2,1)S(1)}, bf16[480,128]{1,0:T(8,128)(2,1)S(1)}, u32[]{:S(2)}, u32[]{:S(2)}) collective-permute-start(bf16[480,128]{1,0:T(8,128)(2,1)S(1)} %get-tuple-element.40), channel_id=1, source_target_pairs={{0,8},{1,9},{2,10},{3,11},{4,12},{5,13},{6,14},{7,15},{8,0},{9,1},... | collective-permute-start | bytes 368648 | tf_op jit(solution)/shard_map/ppermute | solution.py:557
  19.6 6.2 %collective-permute-start.11 = (bf16[480,128]{1,0:T(8,128)(2,1)S(1)}, bf16[480,128]{1,0:T(8,128)(2,1)S(1)}, u32[]{:S(2)}, u32[]{:S(2)}) collective-permute-start(bf16[480,128]{1,0:T(8,128)(2,1)S(1)} %get-tuple-element.41), channel_id=1, source_target_pairs={{0,1},{1,0},{2,3},{3,2},{4,5},{5,4},{6,7},{7,6},{8,16},{9,17},{10,... | collective-permute-start | bytes 368648 | tf_op jit(solution)/shard_map/ppermute | solution.py:557

commit v8 on v7

--- a/solution.py
+++ b/solution.py
@@ -320,7 +320,7 @@
 BEGUN_SLOT = 3
 
 
-def place_rows(found, box, other, right, left_star, left_corner):
+def place_rows(found, box, other, store, left_star, left_corner):
     unit = None
     if box == (0, 0):
         square = (PAIR, PAIR)
@@ -331,8 +331,7 @@
         rounded = value.astype(jnp.bfloat16)
         for index, column, place in USERS[box, other]:
             position = IMAGES[column].index((box[0] + t[0], box[1] + t[1]))
-            stored = swap_halves(value).astype(jnp.bfloat16) if place == 5 else rounded
-            right[index, place * B : (place + 1) * B, position * PAIR : (position + 1) * PAIR] = stored
+            store(index, place, position, swap_halves(value).astype(jnp.bfloat16) if place == 5 else rounded)
         if box == (0, 0):
             turned = lax.dot_general(
                 unit, rounded, (((1,), (1,)), ((), ())), preferred_element_type=jnp.float32
@@ -344,16 +343,64 @@
                 left_corner[own] = turned
 
 
-def begin_kernel(rows_ref, meta_ref, x_first, x_second, y_first, c_first, right, left_star, left_corner, begun_ref):
+def lanes_of(position):
+    return slice(position * PAIR, (position + 1) * PAIR)
+
+
+def fold_image(parts, column):
+    half = low_half((B, PAIR))
+
+    def part(s, z):
+        return parts[s][z * B : (z + 1) * B] if s in parts else jnp.zeros((B, PAIR), jnp.float32)
+
+    tiles = []
+    for pair in range(IMAGE_PAIRS):
+        one = IMAGE[2 * pair]
+        two = IMAGE[2 * pair + 1] if 2 * pair + 1 < len(IMAGE) else None
+        low = jnp.where(half, part(one, 0), swap_halves(part(two, 0)))
+        high = jnp.where(half, swap_halves(part(one, 1)), part(two, 1))
+        tiles.append((low, high))
+    return tiles
+
+
+def split_image(product, column):
+    return {s: product[:, lanes_of(position)] for position, s in enumerate(IMAGES[column])}
+
+
+INNER_Y = 3
+LATE_IMAGE = {index: targets(px, 0)[BEGUN_SLOT] for index, (px, py) in enumerate(COLUMNS) if py == 1}
+
+
+def begin_kernel(
+    a_ref,
+    rows_ref,
+    meta_ref,
+    x_first,
+    x_second,
+    y_first,
+    c_first,
+    right_late,
+    left_star,
+    left_corner,
+    begun_ref,
+    image_early,
+    begun_image,
+    right_early,
+):
     rows = Rows(rows_ref, meta_ref, {1: x_first, -1: x_second}, {1: y_first}, {1: c_first})
+
+    def store(index, place, position, value):
+        ref = right_early if index in LATE_IMAGE else right_late
+        ref[index // 2, place * B : (place + 1) * B, lanes_of(position)] = value
+
     for index, column in enumerate(COLUMNS):
         for place, (_, box, other) in enumerate(around(*column)):
             reached = {(box[0] + tx, box[1] + ty) for tx, ty in box_set(*other)}
+            if index in LATE_IMAGE and place == INNER_Y:
+                reached -= set(LATE_IMAGE[index])
             for position, s in enumerate(IMAGES[column]):
                 if s not in reached:
-                    right[index, place * B : (place + 1) * B, position * PAIR : (position + 1) * PAIR] = jnp.zeros(
-                        (B, PAIR), jnp.bfloat16
-                    )
+                    store(index, place, position, jnp.zeros((B, PAIR), jnp.bfloat16))
     for box, other in USERS:
         if (box, other) in LATE:
             continue
@@ -365,7 +412,15 @@
         found = rows.sums(box, other, slots)
         for place, t in enumerate(open_targets):
             begun_ref[BEGUN.index((box, other)), place] = found.pop(t)
-        place_rows(found, box, other, right, left_star, left_corner)
+        place_rows(found, box, other, store, left_star, left_corner)
+    for index, late in LATE_IMAGE.items():
+        product = jnp.dot(a_ref[index], right_early[index // 2], preferred_element_type=jnp.float32)
+        parts = split_image(product, COLUMNS[index])
+        for place, s in enumerate(late):
+            begun_image[index // 2, place] = parts.pop(s)
+        for pair, (low, high) in enumerate(fold_image(parts, COLUMNS[index])):
+            image_early[index // 2, 0:B, lanes_of(pair)] = low.astype(jnp.bfloat16)
+            image_early[index // 2, B:PAIR, lanes_of(pair)] = high.astype(jnp.bfloat16)
 
 
 def main_kernel(
@@ -377,6 +432,8 @@
     y_second,
     c_second,
     begun_ref,
+    image_early,
+    begun_image,
     right_in,
     left_star_in,
     left_corner_in,
@@ -385,39 +442,55 @@
     to_c_first,
     to_c_second,
     rest_ref,
-    right,
+    right_late,
     left_star,
     left_corner,
     image,
 ):
-    images = IMAGES
     rows = Rows(rows_ref, meta_ref, {1: x_first, -1: x_second}, {-1: y_second}, {-1: c_second})
+    late_rows = {index: {} for index in LATE_IMAGE}
+
+    def store(index, place, position, value):
+        if index in LATE_IMAGE:
+            late_rows[index][IMAGES[COLUMNS[index]][position]] = value
+        else:
+            right_late[index // 2, place * B : (place + 1) * B, lanes_of(position)] = value
+
     for box, other in BEGUN:
         begun = {
             t: begun_ref[BEGUN.index((box, other)), place] for place, t in enumerate(targets(*other)[BEGUN_SLOT])
         }
-        place_rows(rows.sums(box, other, [BEGUN_SLOT], begun), box, other, right, left_star, left_corner)
+        place_rows(rows.sums(box, other, [BEGUN_SLOT], begun), box, other, store, left_star, left_corner)
     for box, other in LATE:
-        place_rows(rows.sums(box, other, list(range(SLOTS))), box, other, right, left_star, left_corner)
+        place_rows(rows.sums(box, other, list(range(SLOTS))), box, other, store, left_star, left_corner)
     half = low_half((B, PAIR))
     for index, column in enumerate(COLUMNS):
-        product = jnp.dot(a_ref[index], right[index], preferred_element_type=jnp.float32)
-
-        def part(s, z):
-            if s not in images[column]:
-                return jnp.zeros((B, PAIR), jnp.float32)
-            position = images[column].index(s)
-            return product[z * B : (z + 1) * B, position * PAIR : (position + 1) * PAIR]
-
-        for pair in range(IMAGE_PAIRS):
-            one = IMAGE[2 * pair]
-            two = IMAGE[2 * pair + 1] if 2 * pair + 1 < len(IMAGE) else None
-            low = jnp.where(half, part(one, 0), swap_halves(part(two, 0)))
-            high = jnp.where(half, swap_halves(part(one, 1)), part(two, 1))
-            start = index * PAIR
-            lanes = slice(pair * PAIR, (pair + 1) * PAIR)
-            image[start : start + B, lanes] = low.astype(jnp.bfloat16)
-            image[start + B : start + PAIR, lanes] = high.astype(jnp.bfloat16)
+        start = index * PAIR
+        if index in LATE_IMAGE:
+            late = LATE_IMAGE[index]
+            more = jnp.dot(
+                a_ref[index, :, INNER_Y * B : (INNER_Y + 1) * B],
+                jnp.concatenate([late_rows[index][s] for s in late], axis=1),
+                preferred_element_type=jnp.float32,
+            )
+            parts = {
+                s: begun_image[index // 2, place] + more[:, lanes_of(place)] for place, s in enumerate(late)
+            }
+        else:
+            product = jnp.dot(a_ref[index], right_late[index // 2], preferred_element_type=jnp.float32)
+            parts = split_image(product, column)
+        for pair, (low, high) in enumerate(fold_image(parts, column)):
+            blocks = IMAGE[2 * pair : 2 * pair + 2]
+            for rows_here, tile in ((slice(0, B), low), (slice(B, PAIR), high)):
+                new = tile.astype(jnp.bfloat16)
+                if index in LATE_IMAGE:
+                    old = image_early[index // 2, rows_here, lanes_of(pair)]
+                    changed = [s in parts for s in blocks]
+                    if not any(changed):
+                        new = old
+                    elif not all(changed):
+                        new = jnp.where(half == changed[0], new, old)
+                image[start + rows_here.start : start + rows_here.stop, lanes_of(pair)] = new
     folded_half = low_half((HALF, PAIR))
 
     def fold(product):
@@ -619,17 +692,22 @@
     def sent(blocks):
         return ((len(blocks) * HALF, PAIR), bf16)
 
+    product_rows, tiles = (2, SLOTS * B, 10 * PAIR), IMAGE_PAIRS * PAIR
     lefts = [
-        ((4, SLOTS * B, 10 * PAIR), bf16),
+        (product_rows, bf16),
         ((len(STAR) * B, 4 * PAIR), bf16),
         ((4, B, PAIR), bf16),
     ]
-    *lefts_begun, begun = call(begin_kernel, [VMEM] * 6, lefts + [((len(BEGUN), 3, B, PAIR), f32)])(
-        rows, meta, x_first, x_second, y_first, c_first
-    )
+    *lefts_begun, begun, image_early, begun_image = call(
+        begin_kernel,
+        [VMEM] * 7,
+        lefts
+        + [((len(BEGUN), 3, B, PAIR), f32), ((2, PAIR, tiles), bf16), ((2, 3, PAIR, PAIR), f32)],
+        [pltpu.VMEM(product_rows, bf16)],
+    )(matrix, rows, meta, x_first, x_second, y_first, c_first)
     y_first, y_second, c_first, c_second, rest, *_ = call(
         main_kernel,
-        [VMEM] * 11,
+        [VMEM] * 13,
         [
             sent(TO_Y_FIRST),
             sent(TO_Y_SECOND),
@@ -638,8 +716,8 @@
             ((3, len(IMAGE), HALF, PAIR), f32),
         ]
         + lefts,
-        [pltpu.VMEM((4 * PAIR, IMAGE_PAIRS * PAIR), bf16)],
-        aliases={8: 5, 9: 6, 10: 7},
+        [pltpu.VMEM((4 * PAIR, tiles), bf16)],
+        aliases={10: 5, 11: 6, 12: 7},
     )(
         matrix,
         rows,
@@ -649,6 +727,8 @@
         y_second,
         c_second,
         begun,
+        image_early,
+        begun_image,
         *(pltpu.with_memory_space_constraint(left, pltpu.VMEM) for left in lefts_begun),
     )
     y_second = swapped(y_second, 0, 2)

time: 27 us -> 26.9 us (level)
  waiting for transfers between devices: 9.16 us -> 8.84 us
    ppermute x12, waiting for transfers between devices: 9.16 us -> 8.84 us  [swapped(): return lax.ppermute(value, ('sx', 'sy'), pairs)]
  transfers between devices with their start and end apart: 12 -> 12, of which waited for: 5 -> 5; matrix products, arithmetic and copies ran while one was open for 0% -> 0% of each run, Pallas kernels for 11% -> 12%
where the time goes in v8:
time: 26.9 us; the launch traced here: 26.4 us
  starting transfers between devices  10.4 us (39%)
  waiting for transfers between devices  8.84 us (33%)
  Pallas kernels  7.08 us (26%)
    ppermute x12, starting transfers between devices, swapped(): return lax.ppermute(value, ('sx', 'sy'), pairs)  10.4 us
    ppermute x12, waiting for transfers between devices, swapped(): return lax.ppermute(value, ('sx', 'sy'), pairs)  8.84 us
    pallas_call x1, Pallas kernels, per_device(): call(pack_matrix_kernel, [HBM, HBM], [((4, PAIR, 6 * B), bf16), whole], [...  1.78 us
    pallas_call x1, Pallas kernels, per_device(): call(functools.partial(pack_kernel, lax.axis_size('sy')), [HBM, HBM, HBM]...  1.48 us
    pallas_call x1, Pallas kernels, per_device(): call(main_kernel, [VMEM] * 13, [sent(TO_Y_FIRST), sent(TO_Y_SECOND), sent...  1.42 us
    pallas_call x1, Pallas kernels, per_device(): call(begin_kernel, [VMEM] * 7, lefts + [((len(BEGUN), 3, B, PAIR), f32),...  1.39 us
    pallas_call x1, Pallas kernels, per_device(): call(finish_kernel, [VMEM] * 3 + [HBM], [whole], [pltpu.VMEM((7, 7, B, B)...  0.89 us
  transfers between devices with their start and end apart: 12, of which 5 were waited for; matrix products, arithmetic and copies ran while one was open for 0% of the time, Pallas kernels for 12%

profile of v8, /device:TPU:20, one launch (start us, length us, event | category | flops | bytes accessed | tf_op | source)
XLA Modules:
  0.0 26.4 jit_solution(8271389234395499220)
XLA Ops:
  0.0 1.5 %shard_map.47 = (bf16[4,384,128]{2,1,0:T(8,128)(2,1)S(1)}, f32[32,128]{1,0:T(8,128)S(1)}, bf16[784,128]{1,0:T(8,128)(2,1)S(1)}, bf16[784,128]{1,0:T(8,128)(2,1)S...) custom-call(s32[2,2,2]{2,1,0:T(2,128)} %aggregate_hbm.1, s32[2,2,2,6]{3,2,1,0:T(2,128)} %links_hbm.3, ...), custom_call_target="tpu_custom_call" | custom-call | tf_op jit(solution)/shard_map/pallas_call | solution.py:660
  1.5 1.6 %collective-permute-start = (bf16[784,128]{1,0:T(8,128)(2,1)S(1)}, bf16[784,128]{1,0:T(8,128)(2,1)S(1)}, u32[]{:S(2)}, u32[]{:S(2)}) collective-permute-start(bf16[784,128]{1,0:T(8,128)(2,1)S(1)} %get-tuple-element.29), channel_id=1, source_target_pairs={{0,8},{1,9},{2,10},{3,11},{4,12},{5,13},{6,14},{7,15},{8,0},{9,1},... | collective-permute-start | bytes 602120 | tf_op jit(solution)/shard_map/ppermute | solution.py:630
  3.1 0.0 collective-permute-start.1
  3.1 0.6 %collective-permute-start.2 = (bf16[800,128]{1,0:T(8,128)(2,1)S(1)}, bf16[800,128]{1,0:T(8,128)(2,1)S(1)}, u32[]{:S(2)}, u32[]{:S(2)}) collective-permute-start(bf16[800,128]{1,0:T(8,128)(2,1)S(1)} %get-tuple-element.31), channel_id=1, source_target_pairs={{0,8},{1,2},{2,1},{3,4},{4,3},{5,6},{6,5},{7,15},{8,0},{9,10},{10,... | collective-permute-start | bytes 614408 | tf_op jit(solution)/shard_map/ppermute | solution.py:630
  3.7 1.0 %collective-permute-start.4 = (bf16[784,128]{1,0:T(8,128)(2,1)S(1)}, bf16[784,128]{1,0:T(8,128)(2,1)S(1)}, u32[]{:S(2)}, u32[]{:S(2)}) collective-permute-start(bf16[784,128]{1,0:T(8,128)(2,1)S(1)} %get-tuple-element.32), channel_id=1, source_target_pairs={{0,1},{1,0},{2,3},{3,2},{4,5},{5,4},{6,7},{7,6},{8,9},{9,8},{10,11... | collective-permute-start | bytes 602120 | tf_op jit(solution)/shard_map/ppermute | solution.py:630
  4.7 1.8 %shard_map.46 = (bf16[4,128,384]{2,1,0:T(8,128)(2,1)S(1)}, bf16[7,7,64,64]{3,2,1,0:T(8,128)(2,1)}) custom-call(s32[2,2,2,6]{3,2,1,0:T(2,128)} %links_hbm.3, bf16[2,2,2,7,64,64]{5,4,3,2,1,0:T(8,128)(2,1)} %a_hbm.1), custom_call_target="tpu_custom_call" | custom-call | tf_op jit(solution)/shard_map/pallas_call | solution.py:676
  6.5 1.8 %collective-permute-done.x_first = bf16[784,128]{1,0:T(8,128)(2,1)S(1)} collective-permute-done((bf16[784,128]{1,0:T(8,128)(2,1)S(1)}, bf16[784,128]{1,0:T(8,128)(2,1)S(1)}, u32[]{:S(2)}, u32[]{:S(2)}) %collective-permute-start) | collective-permute-done | bytes 200736 | tf_op jit(solution)/shard_map/ppermute | solution.py:630
  8.3 1.3 %collective-permute-done.1.x_second = bf16[784,128]{1,0:T(8,128)(2,1)S(1)} collective-permute-done((bf16[784,128]{1,0:T(8,128)(2,1)S(1)}, bf16[784,128]{1,0:T(8,128)(2,1)S(1)}, u32[]{:S(2)}, u32[]{:S(2)}) %collective-permute-start.1) | collective-permute-done | bytes 200736 | tf_op jit(solution)/shard_map/ppermute | solution.py:630
  9.6 0.0 collective-permute-start.5
  9.6 1.5 %collective-permute-start.3 = (bf16[32,128]{1,0:T(8,128)(2,1)S(1)}, bf16[32,128]{1,0:T(8,128)(2,1)S(1)}, u32[]{:S(2)}, u32[]{:S(2)}) collective-permute-start(bf16[32,128]{1,0:T(8,128)(2,1)S(1)} %shard_map.48), channel_id=1, source_target_pairs={{0,8},{1,2},{2,1},{3,4},{4,3},{5,6},{6,5},{7,15},{8,0},{9,10},{10,... | collective-permute-start | bytes 24584 | tf_op jit(solution)/shard_map/ppermute | solution.py:630
  11.1 0.0 collective-permute-done.4.y_first
  11.1 0.0 collective-permute-done.5.c_first
  11.1 1.4 %shard_map.49 = (bf16[2,384,1280]{2,1,0:T(8,128)(2,1)S(1)}, bf16[320,512]{1,0:T(8,128)(2,1)S(1)}, bf16[4,64,128]{2,1,0:T(8,128)(2,1)S(1)}, f32[4,3,64,128]{3,2,1...) custom-call(bf16[4,128,384]{2,1,0:T(8,128)(2,1)S(1)} %get-tuple-element.26._.a_ref, ...), custom_call_target="tpu_custom_call" | custom-call | tf_op jit(solution)/shard_map/pallas_call | solution.py:701
  12.5 0.0 collective-permute-done.2.y_second
  12.5 1.0 %collective-permute-done.3.c_second = bf16[32,128]{1,0:T(8,128)(2,1)S(1)} collective-permute-done((bf16[32,128]{1,0:T(8,128)(2,1)S(1)}, bf16[32,128]{1,0:T(8,128)(2,1)S(1)}, u32[]{:S(2)}, u32[]{:S(2)}) %collective-permute-start.3) | collective-permute-done | bytes 8224 | tf_op jit(solution)/shard_map/ppermute | solution.py:630
  13.6 1.4 %shard_map.50 = (bf16[1056,128]{1,0:T(8,128)(2,1)S(1)}, bf16[416,128]{1,0:T(8,128)(2,1)S(1)}, bf16[320,128]{1,0:T(8,128)(2,1)S(1)}, bf16[320,128]{1,0:T(8,128)(2...) custom-call(bf16[4,128,384]{2,1,0:T(8,128)(2,1)S(1)} %get-tuple-elem, ...), custom_call_target="tpu_custom_call", output_to_operand_aliasing={{5}: (10, {}), {6}: (11, {}), {7}: (12, {})} | custom-call | tf_op jit(solution)/shard_map/pallas_call | solution.py:708
  15.0 0.1 collective-permute-start.6
  15.1 1.6 %collective-permute-start.7 = (bf16[416,128]{1,0:T(8,128)(2,1)S(1)}, bf16[416,128]{1,0:T(8,128)(2,1)S(1)}, u32[]{:S(2)}, u32[]{:S(2)}) collective-permute-start(bf16[416,128]{1,0:T(8,128)(2,1)S(1)} %get-tuple-element.41), channel_id=1, source_target_pairs={{0,8},{1,2},{2,1},{3,4},{4,3},{5,6},{6,5},{7,15},{8,0},{9,10},{10,... | collective-permute-start | bytes 319496 | tf_op jit(solution)/shard_map/ppermute | solution.py:630
  16.7 1.0 %collective-permute-start.8 = (bf16[320,128]{1,0:T(8,128)(2,1)S(1)}, bf16[320,128]{1,0:T(8,128)(2,1)S(1)}, u32[]{:S(2)}, u32[]{:S(2)}) collective-permute-start(bf16[320,128]{1,0:T(8,128)(2,1)S(1)} %get-tuple-element.42), channel_id=1, source_target_pairs={{0,8},{1,10},{2,9},{3,12},{4,11},{5,14},{6,13},{7,15},{8,0},{9,2},... | collective-permute-start | bytes 245768 | tf_op jit(solution)/shard_map/ppermute | solution.py:630
  17.7 0.1 collective-permute-start.9
  17.8 0.0 collective-permute-done.6.y_first
  17.9 1.5 %collective-permute-start.10 = (bf16[480,128]{1,0:T(8,128)(2,1)S(1)}, bf16[480,128]{1,0:T(8,128)(2,1)S(1)}, u32[]{:S(2)}, u32[]{:S(2)}) collective-permute-start(bf16[480,128]{1,0:T(8,128)(2,1)S(1)} %get-tuple-element.44), channel_id=1, source_target_pairs={{0,8},{1,9},{2,10},{3,11},{4,12},{5,13},{6,14},{7,15},{8,0},{9,1},... | collective-permute-start | bytes 368648 | tf_op jit(solution)/shard_map/ppermute | solution.py:630
  19.4 1.3 %collective-permute-start.11 = (bf16[480,128]{1,0:T(8,128)(2,1)S(1)}, bf16[480,128]{1,0:T(8,128)(2,1)S(1)}, u32[]{:S(2)}, u32[]{:S(2)}) collective-permute-start(bf16[480,128]{1,0:T(8,128)(2,1)S(1)} %get-tuple-element.45), channel_id=1, source_target_pairs={{0,1},{1,0},{2,3},{3,2},{4,5},{5,4},{6,7},{7,6},{8,16},{9,17},{10,... | collective-permute-start | bytes 368648 | tf_op jit(solution)/shard_map/ppermute | solution.py:630
  20.7 4.0 %collective-permute-done.8.c_first = bf16[320,128]{1,0:T(8,128)(2,1)S(1)} collective-permute-done((bf16[320,128]{1,0:T(8,128)(2,1)S(1)}, bf16[320,128]{1,0:T(8,128)(2,1)S(1)}, u32[]{:S(2)}, u32[]{:S(2)}) %collective-permute-start.8) | collective-permute-done | bytes 81952 | tf_op jit(solution)/shard_map/ppermute | solution.py:630
  24.7 0.0 collective-permute-done.9.c_second
  24.7 0.0 collective-permute-done.7.y_second
  24.7 0.1 shard_map.51.own_ref
  24.8 0.0 collective-permute-done.10.x_first
  24.8 0.8 %collective-permute-done.11.x_second = bf16[480,128]{1,0:T(8,128)(2,1)S(1)} collective-permute-done((bf16[480,128]{1,0:T(8,128)(2,1)S(1)}, bf16[480,128]{1,0:T(8,128)(2,1)S(1)}, u32[]{:S(2)}, u32[]{:S(2)}) %collective-permute-start.11) | collective-permute-done | bytes 122912 | tf_op jit(solution)/shard_map/ppermute | solution.py:630
  25.6 0.9 %shard_map.53 = bf16[7,7,64,64]{3,2,1,0:T(8,128)(2,1)} custom-call(f32[23,32,128]{2,1,0:T(8,128)S(1)} %shard_map.51.own_ref, bf16[480,128]{1,0:T(8,128)(2,1)S(1)} %collective-permute-done.10.x_first, bf16[480,128]{1,0:T(8,128)(2,1)S(1)} %collective-permute-done.11.x_second, bf16[7,7,64,64]{3,2,1,0:T(8,128)(2,1)} %get-tuple-element.46._), custom_call_target="tpu_custom_call", output_to_operand_aliasing={{}: (3, {})} | custom-call | tf_op jit(solution)/shard_map/pallas_call | solution.py:742
  (2 shorter events, 0.1 us)
Async XLA Ops:
  1.5 6.8 %collective-permute-start = (bf16[784,128]{1,0:T(8,128)(2,1)S(1)}, bf16[784,128]{1,0:T(8,128)(2,1)S(1)}, u32[]{:S(2)}, u32[]{:S(2)}) collective-permute-start(bf16[784,128]{1,0:T(8,128)(2,1)S(1)} %get-tuple-element.29), channel_id=1, source_target_pairs={{0,8},{1,9},{2,10},{3,11},{4,12},{5,13},{6,14},{7,15},{8,0},{9,1},... | collective-permute-start | bytes 602120 | tf_op jit(solution)/shard_map/ppermute | solution.py:630
  3.1 6.4 %collective-permute-start.1 = (bf16[784,128]{1,0:T(8,128)(2,1)S(1)}, bf16[784,128]{1,0:T(8,128)(2,1)S(1)}, u32[]{:S(2)}, u32[]{:S(2)}) collective-permute-start(bf16[784,128]{1,0:T(8,128)(2,1)S(1)} %get-tuple-element.30), channel_id=1, source_target_pairs={{0,1},{1,0},{2,3},{3,2},{4,5},{5,4},{6,7},{7,6},{8,16},{9,17},{10,... | collective-permute-start | bytes 602120 | tf_op jit(solution)/shard_map/ppermute | solution.py:630
  3.1 9.4 %collective-permute-start.2 = (bf16[800,128]{1,0:T(8,128)(2,1)S(1)}, bf16[800,128]{1,0:T(8,128)(2,1)S(1)}, u32[]{:S(2)}, u32[]{:S(2)}) collective-permute-start(bf16[800,128]{1,0:T(8,128)(2,1)S(1)} %get-tuple-element.31), channel_id=1, source_target_pairs={{0,8},{1,2},{2,1},{3,4},{4,3},{5,6},{6,5},{7,15},{8,0},{9,10},{10,... | collective-permute-start | bytes 614408 | tf_op jit(solution)/shard_map/ppermute | solution.py:630
  3.7 7.4 %collective-permute-start.4 = (bf16[784,128]{1,0:T(8,128)(2,1)S(1)}, bf16[784,128]{1,0:T(8,128)(2,1)S(1)}, u32[]{:S(2)}, u32[]{:S(2)}) collective-permute-start(bf16[784,128]{1,0:T(8,128)(2,1)S(1)} %get-tuple-element.32), channel_id=1, source_target_pairs={{0,1},{1,0},{2,3},{3,2},{4,5},{5,4},{6,7},{7,6},{8,9},{9,8},{10,11... | collective-permute-start | bytes 602120 | tf_op jit(solution)/shard_map/ppermute | solution.py:630
  9.6 1.6 %collective-permute-start.5 = (bf16[32,128]{1,0:T(8,128)(2,1)S(1)}, bf16[32,128]{1,0:T(8,128)(2,1)S(1)}, u32[]{:S(2)}, u32[]{:S(2)}) collective-permute-start(bf16[32,128]{1,0:T(8,128)(2,1)S(1)} %shard_map.48), channel_id=1, source_target_pairs={{0,1},{1,0},{2,3},{3,2},{4,5},{5,4},{6,7},{7,6},{8,9},{9,8},{10,11... | collective-permute-start | bytes 24584 | tf_op jit(solution)/shard_map/ppermute | solution.py:630
  9.6 4.0 %collective-permute-start.3 = (bf16[32,128]{1,0:T(8,128)(2,1)S(1)}, bf16[32,128]{1,0:T(8,128)(2,1)S(1)}, u32[]{:S(2)}, u32[]{:S(2)}) collective-permute-start(bf16[32,128]{1,0:T(8,128)(2,1)S(1)} %shard_map.48), channel_id=1, source_target_pairs={{0,8},{1,2},{2,1},{3,4},{4,3},{5,6},{6,5},{7,15},{8,0},{9,10},{10,... | collective-permute-start | bytes 24584 | tf_op jit(solution)/shard_map/ppermute | solution.py:630
  15.0 2.8 %collective-permute-start.6 = (bf16[1056,128]{1,0:T(8,128)(2,1)S(1)}, bf16[1056,128]{1,0:T(8,128)(2,1)S(1)}, u32[]{:S(2)}, u32[]{:S(2)}) collective-permute-start(bf16[1056,128]{1,0:T(8,128)(2,1)S(1)} %get-tuple-element.40), channel_id=1, source_target_pairs={{0,1},{1,0},{2,3},{3,2},{4,5},{5,4},{6,7},{7,6},{8,9},{9,8},{10,11... | collective-permute-start | bytes 811016 | tf_op jit(solution)/shard_map/ppermute | solution.py:630
  15.1 9.6 %collective-permute-start.7 = (bf16[416,128]{1,0:T(8,128)(2,1)S(1)}, bf16[416,128]{1,0:T(8,128)(2,1)S(1)}, u32[]{:S(2)}, u32[]{:S(2)}) collective-permute-start(bf16[416,128]{1,0:T(8,128)(2,1)S(1)} %get-tuple-element.41), channel_id=1, source_target_pairs={{0,8},{1,2},{2,1},{3,4},{4,3},{5,6},{6,5},{7,15},{8,0},{9,10},{10,... | collective-permute-start | bytes 319496 | tf_op jit(solution)/shard_map/ppermute | solution.py:630
  16.7 8.0 %collective-permute-start.8 = (bf16[320,128]{1,0:T(8,128)(2,1)S(1)}, bf16[320,128]{1,0:T(8,128)(2,1)S(1)}, u32[]{:S(2)}, u32[]{:S(2)}) collective-permute-start(bf16[320,128]{1,0:T(8,128)(2,1)S(1)} %get-tuple-element.42), channel_id=1, source_target_pairs={{0,8},{1,10},{2,9},{3,12},{4,11},{5,14},{6,13},{7,15},{8,0},{9,2},... | collective-permute-start | bytes 245768 | tf_op jit(solution)/shard_map/ppermute | solution.py:630
  17.7 7.0 %collective-permute-start.9 = (bf16[320,128]{1,0:T(8,128)(2,1)S(1)}, bf16[320,128]{1,0:T(8,128)(2,1)S(1)}, u32[]{:S(2)}, u32[]{:S(2)}) collective-permute-start(bf16[320,128]{1,0:T(8,128)(2,1)S(1)} %get-tuple-element.43), channel_id=1, source_target_pairs={{0,1},{1,0},{2,3},{3,2},{4,5},{5,4},{6,7},{7,6},{8,16},{9,18},{10,... | collective-permute-start | bytes 245768 | tf_op jit(solution)/shard_map/ppermute | solution.py:630
  17.9 6.9 %collective-permute-start.10 = (bf16[480,128]{1,0:T(8,128)(2,1)S(1)}, bf16[480,128]{1,0:T(8,128)(2,1)S(1)}, u32[]{:S(2)}, u32[]{:S(2)}) collective-permute-start(bf16[480,128]{1,0:T(8,128)(2,1)S(1)} %get-tuple-element.44), channel_id=1, source_target_pairs={{0,8},{1,9},{2,10},{3,11},{4,12},{5,13},{6,14},{7,15},{8,0},{9,1},... | collective-permute-start | bytes 368648 | tf_op jit(solution)/shard_map/ppermute | solution.py:630
  19.4 6.2 %collective-permute-start.11 = (bf16[480,128]{1,0:T(8,128)(2,1)S(1)}, bf16[480,128]{1,0:T(8,128)(2,1)S(1)}, u32[]{:S(2)}, u32[]{:S(2)}) collective-permute-start(bf16[480,128]{1,0:T(8,128)(2,1)S(1)} %get-tuple-element.45), channel_id=1, source_target_pairs={{0,1},{1,0},{2,3},{3,2},{4,5},{5,4},{6,7},{7,6},{8,16},{9,17},{10,... | collective-permute-start | bytes 368648 | tf_op jit(solution)/shard_map/ppermute | solution.py:630

commit v9 on v7

--- a/solution.py
+++ b/solution.py
@@ -188,9 +188,10 @@
                     ref[start : start + B, :] = packed
 
 
-def notes_kernel(x_first, x_second, _, notes_ref):
-    notes_ref[0:TAIL, :] = x_first[BODY : BODY + TAIL, :]
-    notes_ref[TAIL : 2 * TAIL, :] = x_second[BODY : BODY + TAIL, :]
+def notes_kernel(x_first, x_second, _, notes_ref, again_ref):
+    for ref in (notes_ref, again_ref):
+        ref[0:TAIL, :] = x_first[BODY : BODY + TAIL, :]
+        ref[TAIL : 2 * TAIL, :] = x_second[BODY : BODY + TAIL, :]
 
 
 def pack_matrix_kernel(links_hbm, a_hbm, out_ref, whole_hbm, a_ref, links_ref, zeros, a_sems, sems):
@@ -315,9 +316,16 @@
 for _index, _column in enumerate(COLUMNS):
     for _place, (_, _box, _other) in enumerate(around(*_column)):
         USERS.setdefault((_box, _other), []).append((_index, _column, _place))
-BEGUN = [key for key in USERS if key[1][1] == 0 and key[0][1] == 0]
+BEGUN = {
+    (box, (px, py)): (1 if px == 0 else 2) if box == (0, 1) else (3 if py == 0 else 4)
+    for box, (px, py) in USERS
+    if box[1] == 1 or box[0] or (box == (0, 0) and py == 0)
+}
 LATE = [key for key in USERS if key[0][1] == -1]
-BEGUN_SLOT = 3
+
+
+def begun_targets(key):
+    return targets(*key[1])[BEGUN[key]]
 
 
 def place_rows(found, box, other, right, left_star, left_corner):
@@ -344,8 +352,8 @@
                 left_corner[own] = turned
 
 
-def begin_kernel(rows_ref, meta_ref, x_first, x_second, y_first, c_first, right, left_star, left_corner, begun_ref):
-    rows = Rows(rows_ref, meta_ref, {1: x_first, -1: x_second}, {1: y_first}, {1: c_first})
+def begin_kernel(rows_ref, meta_ref, x_first, x_second, y_first, right, left_star, left_corner, begun_ref):
+    rows = Rows(rows_ref, meta_ref, {1: x_first, -1: x_second}, {1: y_first}, {})
     for index, column in enumerate(COLUMNS):
         for place, (_, box, other) in enumerate(around(*column)):
             reached = {(box[0] + tx, box[1] + ty) for tx, ty in box_set(*other)}
@@ -360,11 +368,11 @@
         slots = list(range(SLOTS))
         open_targets = []
         if (box, other) in BEGUN:
-            slots.remove(BEGUN_SLOT)
-            open_targets = targets(*other)[BEGUN_SLOT]
+            slots.remove(BEGUN[box, other])
+            open_targets = begun_targets((box, other))
         found = rows.sums(box, other, slots)
         for place, t in enumerate(open_targets):
-            begun_ref[BEGUN.index((box, other)), place] = found.pop(t)
+            begun_ref[list(BEGUN).index((box, other)), place] = found.pop(t)
         place_rows(found, box, other, right, left_star, left_corner)
 
 
@@ -374,7 +382,9 @@
     meta_ref,
     x_first,
     x_second,
+    y_first,
     y_second,
+    c_first,
     c_second,
     begun_ref,
     right_in,
@@ -391,12 +401,10 @@
     image,
 ):
     images = IMAGES
-    rows = Rows(rows_ref, meta_ref, {1: x_first, -1: x_second}, {-1: y_second}, {-1: c_second})
-    for box, other in BEGUN:
-        begun = {
-            t: begun_ref[BEGUN.index((box, other)), place] for place, t in enumerate(targets(*other)[BEGUN_SLOT])
-        }
-        place_rows(rows.sums(box, other, [BEGUN_SLOT], begun), box, other, right, left_star, left_corner)
+    rows = Rows(rows_ref, meta_ref, {1: x_first, -1: x_second}, {1: y_first, -1: y_second}, {1: c_first, -1: c_second})
+    for number, ((box, other), slot) in enumerate(BEGUN.items()):
+        begun = {t: begun_ref[number, place] for place, t in enumerate(begun_targets((box, other)))}
+        place_rows(rows.sums(box, other, [slot], begun), box, other, right, left_star, left_corner)
     for box, other in LATE:
         place_rows(rows.sums(box, other, list(range(SLOTS))), box, other, right, left_star, left_corner)
     half = low_half((B, PAIR))
@@ -613,8 +621,11 @@
         ],
         [VMEM, HBM],
     )(*in_hbm(face_links, fine_matrix))
-    (notes,) = call(notes_kernel, [VMEM, VMEM, ANY], [((2 * TAIL, PAIR), bf16)])(x_first, x_second, matrix)
-    c_first, c_second = swapped(notes, 0, 1), swapped(notes, 0, 2)
+    note = ((2 * TAIL, PAIR), bf16)
+    notes, notes_again = call(notes_kernel, [VMEM, VMEM, ANY], [note, ((48, PAIR), bf16)])(
+        x_first, x_second, matrix
+    )
+    c_first, c_second = swapped(notes, 0, 1), swapped(notes_again, 0, 2)
 
     def sent(blocks):
         return ((len(blocks) * HALF, PAIR), bf16)
@@ -624,12 +635,12 @@
         ((len(STAR) * B, 4 * PAIR), bf16),
         ((4, B, PAIR), bf16),
     ]
-    *lefts_begun, begun = call(begin_kernel, [VMEM] * 6, lefts + [((len(BEGUN), 3, B, PAIR), f32)])(
-        rows, meta, x_first, x_second, y_first, c_first
+    *lefts_begun, begun = call(begin_kernel, [VMEM] * 5, lefts + [((len(BEGUN), 3, B, PAIR), f32)], cost=1)(
+        rows, meta, x_first, x_second, y_first
     )
     y_first, y_second, c_first, c_second, rest, *_ = call(
         main_kernel,
-        [VMEM] * 11,
+        [VMEM] * 13,
         [
             sent(TO_Y_FIRST),
             sent(TO_Y_SECOND),
@@ -639,14 +650,16 @@
         ]
         + lefts,
         [pltpu.VMEM((4 * PAIR, IMAGE_PAIRS * PAIR), bf16)],
-        aliases={8: 5, 9: 6, 10: 7},
+        aliases={10: 5, 11: 6, 12: 7},
     )(
         matrix,
         rows,
         meta,
         x_first,
         x_second,
+        y_first,
         y_second,
+        c_first,
         c_second,
         begun,
         *(pltpu.with_memory_space_constraint(left, pltpu.VMEM) for left in lefts_begun),

time: 27 us -> 26.7 us (0.989)
  starting transfers between devices: 10.5 us -> 9.56 us
  waiting for transfers between devices: 9.16 us -> 9.93 us
    ppermute x12, starting transfers between devices: 10.5 us -> 9.56 us  [swapped(): return lax.ppermute(value, ('sx', 'sy'), pairs)]
    ppermute x12, waiting for transfers between devices: 9.16 us -> 9.93 us  [swapped(): return lax.ppermute(value, ('sx', 'sy'), pairs)]
  transfers between devices with their start and end apart: 12 -> 12, of which waited for: 5 -> 7; matrix products, arithmetic and copies ran while one was open for 0% -> 0% of each run, Pallas kernels for 11% -> 11%
where the time goes in v9:
time: 26.7 us; the launch traced here: 26.5 us
  waiting for transfers between devices  9.93 us (37%)
  starting transfers between devices  9.56 us (36%)
  Pallas kernels  7 us (26%)
    ppermute x12, waiting for transfers between devices, swapped(): return lax.ppermute(value, ('sx', 'sy'), pairs)  9.93 us
    ppermute x12, starting transfers between devices, swapped(): return lax.ppermute(value, ('sx', 'sy'), pairs)  9.56 us
    pallas_call x1, Pallas kernels, per_device(): call(pack_matrix_kernel, [HBM, HBM], [((4, PAIR, 6 * B), bf16), whole], [...  1.78 us
    pallas_call x1, Pallas kernels, per_device(): call(main_kernel, [VMEM] * 13, [sent(TO_Y_FIRST), sent(TO_Y_SECOND), sent...  1.69 us
    pallas_call x1, Pallas kernels, per_device(): call(functools.partial(pack_kernel, lax.axis_size('sy')), [HBM, HBM, HBM]...  1.48 us
    pallas_call x1, Pallas kernels, per_device(): call(begin_kernel, [VMEM] * 5, lefts + [((len(BEGUN), 3, B, PAIR), f32)],...  1.02 us
    pallas_call x1, Pallas kernels, per_device(): call(finish_kernel, [VMEM] * 3 + [HBM], [whole], [pltpu.VMEM((7, 7, B, B)...  0.89 us
  transfers between devices with their start and end apart: 12, of which 7 were waited for; matrix products, arithmetic and copies ran while one was open for 0% of the time, Pallas kernels for 11%

profile of v9, /device:TPU:20, one launch (start us, length us, event | category | flops | bytes accessed | tf_op | source)
XLA Modules:
  0.0 26.5 jit_solution(6711819610966748562)
XLA Ops:
  0.0 1.5 %shard_map.47 = (bf16[4,384,128]{2,1,0:T(8,128)(2,1)S(1)}, f32[32,128]{1,0:T(8,128)S(1)}, bf16[784,128]{1,0:T(8,128)(2,1)S(1)}, bf16[784,128]{1,0:T(8,128)(2,1)S...) custom-call(s32[2,2,2]{2,1,0:T(2,128)} %aggregate_hbm.1, s32[2,2,2,6]{3,2,1,0:T(2,128)} %links_hbm.3, ...), custom_call_target="tpu_custom_call" | custom-call | tf_op jit(solution)/shard_map/pallas_call | solution.py:595
  1.5 1.6 %collective-permute-start = (bf16[784,128]{1,0:T(8,128)(2,1)S(1)}, bf16[784,128]{1,0:T(8,128)(2,1)S(1)}, u32[]{:S(2)}, u32[]{:S(2)}) collective-permute-start(bf16[784,128]{1,0:T(8,128)(2,1)S(1)} %get-tuple-element.29), channel_id=1, source_target_pairs={{0,8},{1,9},{2,10},{3,11},{4,12},{5,13},{6,14},{7,15},{8,0},{9,1},... | collective-permute-start | bytes 602120 | tf_op jit(solution)/shard_map/ppermute | solution.py:565
  3.1 0.0 collective-permute-start.1
  3.1 0.6 %collective-permute-start.3 = (bf16[800,128]{1,0:T(8,128)(2,1)S(1)}, bf16[800,128]{1,0:T(8,128)(2,1)S(1)}, u32[]{:S(2)}, u32[]{:S(2)}) collective-permute-start(bf16[800,128]{1,0:T(8,128)(2,1)S(1)} %get-tuple-element.32), channel_id=1, source_target_pairs={{0,8},{1,2},{2,1},{3,4},{4,3},{5,6},{6,5},{7,15},{8,0},{9,10},{10,... | collective-permute-start | bytes 614408 | tf_op jit(solution)/shard_map/ppermute | solution.py:565
  3.7 1.0 %collective-permute-start.2 = (bf16[784,128]{1,0:T(8,128)(2,1)S(1)}, bf16[784,128]{1,0:T(8,128)(2,1)S(1)}, u32[]{:S(2)}, u32[]{:S(2)}) collective-permute-start(bf16[784,128]{1,0:T(8,128)(2,1)S(1)} %get-tuple-element.31), channel_id=1, source_target_pairs={{0,1},{1,0},{2,3},{3,2},{4,5},{5,4},{6,7},{7,6},{8,9},{9,8},{10,11... | collective-permute-start | bytes 602120 | tf_op jit(solution)/shard_map/ppermute | solution.py:565
  4.7 1.8 %shard_map.46 = (bf16[4,128,384]{2,1,0:T(8,128)(2,1)S(1)}, bf16[7,7,64,64]{3,2,1,0:T(8,128)(2,1)}) custom-call(s32[2,2,2,6]{3,2,1,0:T(2,128)} %links_hbm.3, bf16[2,2,2,7,64,64]{5,4,3,2,1,0:T(8,128)(2,1)} %a_hbm.1), custom_call_target="tpu_custom_call" | custom-call | tf_op jit(solution)/shard_map/pallas_call | solution.py:611
  6.5 1.8 %collective-permute-done.x_first = bf16[784,128]{1,0:T(8,128)(2,1)S(1)} collective-permute-done((bf16[784,128]{1,0:T(8,128)(2,1)S(1)}, bf16[784,128]{1,0:T(8,128)(2,1)S(1)}, u32[]{:S(2)}, u32[]{:S(2)}) %collective-permute-start) | collective-permute-done | bytes 200736 | tf_op jit(solution)/shard_map/ppermute | solution.py:565
  8.3 1.3 %collective-permute-done.1.x_second = bf16[784,128]{1,0:T(8,128)(2,1)S(1)} collective-permute-done((bf16[784,128]{1,0:T(8,128)(2,1)S(1)}, bf16[784,128]{1,0:T(8,128)(2,1)S(1)}, u32[]{:S(2)}, u32[]{:S(2)}) %collective-permute-start.1) | collective-permute-done | bytes 200736 | tf_op jit(solution)/shard_map/ppermute | solution.py:565
  9.6 0.0 collective-permute-start.5
  9.6 1.6 %collective-permute-start.4 = (bf16[32,128]{1,0:T(8,128)(2,1)S(1)}, bf16[32,128]{1,0:T(8,128)(2,1)S(1)}, u32[]{:S(2)}, u32[]{:S(2)}) collective-permute-start(bf16[32,128]{1,0:T(8,128)(2,1)S(1)} %get-tuple-element.33), channel_id=1, source_target_pairs={{0,1},{1,0},{2,3},{3,2},{4,5},{5,4},{6,7},{7,6},{8,9},{9,8},{10,11... | collective-permute-start | bytes 24584 | tf_op jit(solution)/shard_map/ppermute | solution.py:565
  11.2 0.0 collective-permute-done.2.y_first
  11.2 1.0 %shard_map.49 = (bf16[4,384,1280]{2,1,0:T(8,128)(2,1)S(1)}, bf16[320,512]{1,0:T(8,128)(2,1)S(1)}, bf16[4,64,128]{2,1,0:T(8,128)(2,1)S(1)}, f32[8,3,64,128]{3,2,1,0:T(8,128)S(1)}) custom-call(bf16[4,384,128]{2,1,0:T(8,128)(2,1)S(1)} %get-tuple-element.27.rows_ref, f32[32,128]{1,0:T(8,128)S(1)} %get-tuple-element.28.meta_ref, ...), custom_call_target="tpu_custom_call" | custom-call | flops 1 | bytes 1 | tf_op jit(solution)/shard_map/pallas_call | solution.py:638
  12.2 0.0 collective-permute-done.3.y_second
  12.2 0.0 collective-permute-done.4.c_first
  12.2 1.4 %collective-permute-done.5.c_second = bf16[48,128]{1,0:T(8,128)(2,1)S(1)} collective-permute-done((bf16[48,128]{1,0:T(8,128)(2,1)S(1)}, bf16[48,128]{1,0:T(8,128)(2,1)S(1)}, u32[]{:S(2)}, u32[]{:S(2)}) %collective-permute-start.5) | collective-permute-done | bytes 12320 | tf_op jit(solution)/shard_map/ppermute | solution.py:565
  13.6 1.7 %shard_map.50 = (bf16[1056,128]{1,0:T(8,128)(2,1)S(1)}, bf16[416,128]{1,0:T(8,128)(2,1)S(1)}, bf16[320,128]{1,0:T(8,128)(2,1)S(1)}, bf16[320,128]{1,0:T(8,128)(2...) custom-call(bf16[4,128,384]{2,1,0:T(8,128)(2,1)S(1)} %get-tuple-elem, ...), custom_call_target="tpu_custom_call", output_to_operand_aliasing={{5}: (10, {}), {6}: (11, {}), {7}: (12, {})} | custom-call | tf_op jit(solution)/shard_map/pallas_call | solution.py:641
  15.3 0.1 collective-permute-start.6
  15.4 0.6 %collective-permute-start.7 = (bf16[416,128]{1,0:T(8,128)(2,1)S(1)}, bf16[416,128]{1,0:T(8,128)(2,1)S(1)}, u32[]{:S(2)}, u32[]{:S(2)}) collective-permute-start(bf16[416,128]{1,0:T(8,128)(2,1)S(1)} %get-tuple-element.41), channel_id=1, source_target_pairs={{0,8},{1,2},{2,1},{3,4},{4,3},{5,6},{6,5},{7,15},{8,0},{9,10},{10,... | collective-permute-start | bytes 319496 | tf_op jit(solution)/shard_map/ppermute | solution.py:565
  16.0 1.8 %collective-permute-start.8 = (bf16[320,128]{1,0:T(8,128)(2,1)S(1)}, bf16[320,128]{1,0:T(8,128)(2,1)S(1)}, u32[]{:S(2)}, u32[]{:S(2)}) collective-permute-start(bf16[320,128]{1,0:T(8,128)(2,1)S(1)} %get-tuple-element.42), channel_id=1, source_target_pairs={{0,8},{1,10},{2,9},{3,12},{4,11},{5,14},{6,13},{7,15},{8,0},{9,2},... | collective-permute-start | bytes 245768 | tf_op jit(solution)/shard_map/ppermute | solution.py:565
  17.8 0.0 collective-permute-start.9
  17.9 0.0 collective-permute-done.6.y_first
  17.9 1.8 %collective-permute-start.10 = (bf16[480,128]{1,0:T(8,128)(2,1)S(1)}, bf16[480,128]{1,0:T(8,128)(2,1)S(1)}, u32[]{:S(2)}, u32[]{:S(2)}) collective-permute-start(bf16[480,128]{1,0:T(8,128)(2,1)S(1)} %get-tuple-element.44), channel_id=1, source_target_pairs={{0,8},{1,9},{2,10},{3,11},{4,12},{5,13},{6,14},{7,15},{8,0},{9,1},... | collective-permute-start | bytes 368648 | tf_op jit(solution)/shard_map/ppermute | solution.py:565
  19.7 0.4 %collective-permute-start.11 = (bf16[480,128]{1,0:T(8,128)(2,1)S(1)}, bf16[480,128]{1,0:T(8,128)(2,1)S(1)}, u32[]{:S(2)}, u32[]{:S(2)}) collective-permute-start(bf16[480,128]{1,0:T(8,128)(2,1)S(1)} %get-tuple-element.45), channel_id=1, source_target_pairs={{0,1},{1,0},{2,3},{3,2},{4,5},{5,4},{6,7},{7,6},{8,16},{9,17},{10,... | collective-permute-start | bytes 368648 | tf_op jit(solution)/shard_map/ppermute | solution.py:565
  20.1 2.8 %collective-permute-done.8.c_first = bf16[320,128]{1,0:T(8,128)(2,1)S(1)} collective-permute-done((bf16[320,128]{1,0:T(8,128)(2,1)S(1)}, bf16[320,128]{1,0:T(8,128)(2,1)S(1)}, u32[]{:S(2)}, u32[]{:S(2)}) %collective-permute-start.8) | collective-permute-done | bytes 81952 | tf_op jit(solution)/shard_map/ppermute | solution.py:565
  22.9 0.9 %collective-permute-done.9.c_second = bf16[320,128]{1,0:T(8,128)(2,1)S(1)} collective-permute-done((bf16[320,128]{1,0:T(8,128)(2,1)S(1)}, bf16[320,128]{1,0:T(8,128)(2,1)S(1)}, u32[]{:S(2)}, u32[]{:S(2)}) %collective-permute-start.9) | collective-permute-done | bytes 81952 | tf_op jit(solution)/shard_map/ppermute | solution.py:565
  23.8 0.7 %collective-permute-done.7.y_second = bf16[416,128]{1,0:T(8,128)(2,1)S(1)} collective-permute-done((bf16[416,128]{1,0:T(8,128)(2,1)S(1)}, bf16[416,128]{1,0:T(8,128)(2,1)S(1)}, u32[]{:S(2)}, u32[]{:S(2)}) %collective-permute-start.7) | collective-permute-done | bytes 106528 | tf_op jit(solution)/shard_map/ppermute | solution.py:565
  24.5 0.1 shard_map.51.own_ref
  24.5 0.0 collective-permute-done.10.x_first
  24.5 1.1 %collective-permute-done.11.x_second = bf16[480,128]{1,0:T(8,128)(2,1)S(1)} collective-permute-done((bf16[480,128]{1,0:T(8,128)(2,1)S(1)}, bf16[480,128]{1,0:T(8,128)(2,1)S(1)}, u32[]{:S(2)}, u32[]{:S(2)}) %collective-permute-start.11) | collective-permute-done | bytes 122912 | tf_op jit(solution)/shard_map/ppermute | solution.py:565
  25.7 0.9 %shard_map.53 = bf16[7,7,64,64]{3,2,1,0:T(8,128)(2,1)} custom-call(f32[23,32,128]{2,1,0:T(8,128)S(1)} %shard_map.51.own_ref, bf16[480,128]{1,0:T(8,128)(2,1)S(1)} %collective-permute-done.10.x_first, bf16[480,128]{1,0:T(8,128)(2,1)S(1)} %collective-permute-done.11.x_second, bf16[7,7,64,64]{3,2,1,0:T(8,128)(2,1)} %get-tuple-element.46._), custom_call_target="tpu_custom_call", output_to_operand_aliasing={{}: (3, {})} | custom-call | tf_op jit(solution)/shard_map/pallas_call | solution.py:675
  (2 shorter events, 0.1 us)
Async XLA Ops:
  1.5 6.8 %collective-permute-start = (bf16[784,128]{1,0:T(8,128)(2,1)S(1)}, bf16[784,128]{1,0:T(8,128)(2,1)S(1)}, u32[]{:S(2)}, u32[]{:S(2)}) collective-permute-start(bf16[784,128]{1,0:T(8,128)(2,1)S(1)} %get-tuple-element.29), channel_id=1, source_target_pairs={{0,8},{1,9},{2,10},{3,11},{4,12},{5,13},{6,14},{7,15},{8,0},{9,1},... | collective-permute-start | bytes 602120 | tf_op jit(solution)/shard_map/ppermute | solution.py:565
  3.1 6.4 %collective-permute-start.1 = (bf16[784,128]{1,0:T(8,128)(2,1)S(1)}, bf16[784,128]{1,0:T(8,128)(2,1)S(1)}, u32[]{:S(2)}, u32[]{:S(2)}) collective-permute-start(bf16[784,128]{1,0:T(8,128)(2,1)S(1)} %get-tuple-element.30), channel_id=1, source_target_pairs={{0,1},{1,0},{2,3},{3,2},{4,5},{5,4},{6,7},{7,6},{8,16},{9,17},{10,... | collective-permute-start | bytes 602120 | tf_op jit(solution)/shard_map/ppermute | solution.py:565
  3.1 9.1 %collective-permute-start.3 = (bf16[800,128]{1,0:T(8,128)(2,1)S(1)}, bf16[800,128]{1,0:T(8,128)(2,1)S(1)}, u32[]{:S(2)}, u32[]{:S(2)}) collective-permute-start(bf16[800,128]{1,0:T(8,128)(2,1)S(1)} %get-tuple-element.32), channel_id=1, source_target_pairs={{0,8},{1,2},{2,1},{3,4},{4,3},{5,6},{6,5},{7,15},{8,0},{9,10},{10,... | collective-permute-start | bytes 614408 | tf_op jit(solution)/shard_map/ppermute | solution.py:565
  3.7 7.5 %collective-permute-start.2 = (bf16[784,128]{1,0:T(8,128)(2,1)S(1)}, bf16[784,128]{1,0:T(8,128)(2,1)S(1)}, u32[]{:S(2)}, u32[]{:S(2)}) collective-permute-start(bf16[784,128]{1,0:T(8,128)(2,1)S(1)} %get-tuple-element.31), channel_id=1, source_target_pairs={{0,1},{1,0},{2,3},{3,2},{4,5},{5,4},{6,7},{7,6},{8,9},{9,8},{10,11... | collective-permute-start | bytes 602120 | tf_op jit(solution)/shard_map/ppermute | solution.py:565
  9.6 4.0 %collective-permute-start.5 = (bf16[48,128]{1,0:T(8,128)(2,1)S(1)}, bf16[48,128]{1,0:T(8,128)(2,1)S(1)}, u32[]{:S(2)}, u32[]{:S(2)}) collective-permute-start(bf16[48,128]{1,0:T(8,128)(2,1)S(1)} %get-tuple-element.34), channel_id=1, source_target_pairs={{0,8},{1,2},{2,1},{3,4},{4,3},{5,6},{6,5},{7,15},{8,0},{9,10},{10,... | collective-permute-start | bytes 36872 | tf_op jit(solution)/shard_map/ppermute | solution.py:565
  9.6 2.6 %collective-permute-start.4 = (bf16[32,128]{1,0:T(8,128)(2,1)S(1)}, bf16[32,128]{1,0:T(8,128)(2,1)S(1)}, u32[]{:S(2)}, u32[]{:S(2)}) collective-permute-start(bf16[32,128]{1,0:T(8,128)(2,1)S(1)} %get-tuple-element.33), channel_id=1, source_target_pairs={{0,1},{1,0},{2,3},{3,2},{4,5},{5,4},{6,7},{7,6},{8,9},{9,8},{10,11... | collective-permute-start | bytes 24584 | tf_op jit(solution)/shard_map/ppermute | solution.py:565
  15.3 2.5 %collective-permute-start.6 = (bf16[1056,128]{1,0:T(8,128)(2,1)S(1)}, bf16[1056,128]{1,0:T(8,128)(2,1)S(1)}, u32[]{:S(2)}, u32[]{:S(2)}) collective-permute-start(bf16[1056,128]{1,0:T(8,128)(2,1)S(1)} %get-tuple-element.40), channel_id=1, source_target_pairs={{0,1},{1,0},{2,3},{3,2},{4,5},{5,4},{6,7},{7,6},{8,9},{9,8},{10,11... | collective-permute-start | bytes 811016 | tf_op jit(solution)/shard_map/ppermute | solution.py:565
  15.4 9.1 %collective-permute-start.7 = (bf16[416,128]{1,0:T(8,128)(2,1)S(1)}, bf16[416,128]{1,0:T(8,128)(2,1)S(1)}, u32[]{:S(2)}, u32[]{:S(2)}) collective-permute-start(bf16[416,128]{1,0:T(8,128)(2,1)S(1)} %get-tuple-element.41), channel_id=1, source_target_pairs={{0,8},{1,2},{2,1},{3,4},{4,3},{5,6},{6,5},{7,15},{8,0},{9,10},{10,... | collective-permute-start | bytes 319496 | tf_op jit(solution)/shard_map/ppermute | solution.py:565
  16.0 6.9 %collective-permute-start.8 = (bf16[320,128]{1,0:T(8,128)(2,1)S(1)}, bf16[320,128]{1,0:T(8,128)(2,1)S(1)}, u32[]{:S(2)}, u32[]{:S(2)}) collective-permute-start(bf16[320,128]{1,0:T(8,128)(2,1)S(1)} %get-tuple-element.42), channel_id=1, source_target_pairs={{0,8},{1,10},{2,9},{3,12},{4,11},{5,14},{6,13},{7,15},{8,0},{9,2},... | collective-permute-start | bytes 245768 | tf_op jit(solution)/shard_map/ppermute | solution.py:565
  17.8 5.9 %collective-permute-start.9 = (bf16[320,128]{1,0:T(8,128)(2,1)S(1)}, bf16[320,128]{1,0:T(8,128)(2,1)S(1)}, u32[]{:S(2)}, u32[]{:S(2)}) collective-permute-start(bf16[320,128]{1,0:T(8,128)(2,1)S(1)} %get-tuple-element.43), channel_id=1, source_target_pairs={{0,1},{1,0},{2,3},{3,2},{4,5},{5,4},{6,7},{7,6},{8,16},{9,18},{10,... | collective-permute-start | bytes 245768 | tf_op jit(solution)/shard_map/ppermute | solution.py:565
  17.9 6.6 %collective-permute-start.10 = (bf16[480,128]{1,0:T(8,128)(2,1)S(1)}, bf16[480,128]{1,0:T(8,128)(2,1)S(1)}, u32[]{:S(2)}, u32[]{:S(2)}) collective-permute-start(bf16[480,128]{1,0:T(8,128)(2,1)S(1)} %get-tuple-element.44), channel_id=1, source_target_pairs={{0,8},{1,9},{2,10},{3,11},{4,12},{5,13},{6,14},{7,15},{8,0},{9,1},... | collective-permute-start | bytes 368648 | tf_op jit(solution)/shard_map/ppermute | solution.py:565
  19.7 6.0 %collective-permute-start.11 = (bf16[480,128]{1,0:T(8,128)(2,1)S(1)}, bf16[480,128]{1,0:T(8,128)(2,1)S(1)}, u32[]{:S(2)}, u32[]{:S(2)}) collective-permute-start(bf16[480,128]{1,0:T(8,128)(2,1)S(1)} %get-tuple-element.45), channel_id=1, source_target_pairs={{0,1},{1,0},{2,3},{3,2},{4,5},{5,4},{6,7},{7,6},{8,16},{9,17},{10,... | collective-permute-start | bytes 368648 | tf_op jit(solution)/shard_map/ppermute | solution.py:565

commit v10 on v9

--- a/solution.py
+++ b/solution.py
@@ -37,14 +37,12 @@
 
 
 def around(px, py):
-    found = [(0, (0, 0), (px, py))]
-    for m in (2, 1) if px == 0 else (1, 2):
+    (mx, out_x), (my, out_y) = (2, 1) if px == 0 else (1, 2), (4, 3) if py == 0 else (3, 4)
+    found = []
+    for m in (0, 5, mx, my, out_x, out_y):
         ox, nx = divmod(px + FACES[m][0], 2)
-        found.append((m, (ox, 0), (nx, py)))
-    for m in (4, 3) if py == 0 else (3, 4):
         oy, ny = divmod(py + FACES[m][1], 2)
-        found.append((m, (0, oy), (px, ny)))
-    found.append((5, (0, 0), (px, py)))
+        found.append((m, (ox, oy), (nx, ny)))
     return found
 
 
@@ -57,7 +55,7 @@
 
 IMAGE = sorted({s for column in COLUMNS for s in image_set(*column)})
 IMAGE_PAIRS = (len(IMAGE) + 1) // 2
-STAR = [(0, 1), (0, -1), (0, 0), (1, 0), (-1, 0)]
+STAR = [(0, 1), (0, -1), (1, 0), (-1, 0), (0, 0)]
 
 
 def column_of(tx, ty):
@@ -311,7 +309,25 @@
         return {t: jnp.concatenate(parts, axis=0) for t, parts in chunks.items()}
 
 
-IMAGES = {column: image_set(*column) for column in COLUMNS}
+def couplings_of(column, s):
+    return [
+        place
+        for place, (_, (ox, oy), other) in enumerate(around(*column))
+        if (s[0] - ox, s[1] - oy) in box_set(*other)
+    ]
+
+
+def grouped_images(column):
+    groups = [[], [], []]
+    for s in image_set(*column):
+        places = couplings_of(column, s)
+        groups[1 if max(places) < 4 else 2 if min(places) > 1 else 0].append(s)
+    return groups
+
+
+GROUPS = {column: grouped_images(column) for column in COLUMNS}
+SPANS = (slice(0, 6 * B), slice(0, 4 * B), slice(2 * B, 6 * B))
+IMAGES = {column: sum(GROUPS[column], []) for column in COLUMNS}
 USERS = {}
 for _index, _column in enumerate(COLUMNS):
     for _place, (_, _box, _other) in enumerate(around(*_column)):
@@ -339,7 +355,7 @@
         rounded = value.astype(jnp.bfloat16)
         for index, column, place in USERS[box, other]:
             position = IMAGES[column].index((box[0] + t[0], box[1] + t[1]))
-            stored = swap_halves(value).astype(jnp.bfloat16) if place == 5 else rounded
+            stored = swap_halves(value).astype(jnp.bfloat16) if place == 1 else rounded
             right[index, place * B : (place + 1) * B, position * PAIR : (position + 1) * PAIR] = stored
         if box == (0, 0):
             turned = lax.dot_general(
@@ -352,13 +368,26 @@
                 left_corner[own] = turned
 
 
+def fold(product):
+    folded_half = low_half((HALF, PAIR))
+    blocks = {}
+    for pair in range(IMAGE_PAIRS):
+        tile = product[:, pair * PAIR : (pair + 1) * PAIR]
+        top, bottom = tile[:HALF], tile[HALF:]
+        blocks[IMAGE[2 * pair]] = jnp.where(folded_half, top, swap_halves(bottom))
+        if 2 * pair + 1 < len(IMAGE):
+            blocks[IMAGE[2 * pair + 1]] = jnp.where(folded_half, swap_halves(top), bottom)
+    return blocks
+
+
 def begin_kernel(rows_ref, meta_ref, x_first, x_second, y_first, right, left_star, left_corner, begun_ref):
     rows = Rows(rows_ref, meta_ref, {1: x_first, -1: x_second}, {1: y_first}, {})
     for index, column in enumerate(COLUMNS):
         for place, (_, box, other) in enumerate(around(*column)):
             reached = {(box[0] + tx, box[1] + ty) for tx, ty in box_set(*other)}
+            spans = sum(([span] * len(group) for span, group in zip(SPANS, GROUPS[column])), [])
             for position, s in enumerate(IMAGES[column]):
-                if s not in reached:
+                if s not in reached and spans[position].start <= place * B < spans[position].stop:
                     right[index, place * B : (place + 1) * B, position * PAIR : (position + 1) * PAIR] = jnp.zeros(
                         (B, PAIR), jnp.bfloat16
                     )
@@ -400,7 +429,6 @@
     left_corner,
     image,
 ):
-    images = IMAGES
     rows = Rows(rows_ref, meta_ref, {1: x_first, -1: x_second}, {1: y_first, -1: y_second}, {1: c_first, -1: c_second})
     for number, ((box, other), slot) in enumerate(BEGUN.items()):
         begun = {t: begun_ref[number, place] for place, t in enumerate(begun_targets((box, other)))}
@@ -409,13 +437,18 @@
         place_rows(rows.sums(box, other, list(range(SLOTS))), box, other, right, left_star, left_corner)
     half = low_half((B, PAIR))
     for index, column in enumerate(COLUMNS):
-        product = jnp.dot(a_ref[index], right[index], preferred_element_type=jnp.float32)
+        products, start = {}, 0
+        for span, group in zip(SPANS, GROUPS[column]):
+            lanes = slice(start * PAIR, (start + len(group)) * PAIR)
+            product = jnp.dot(a_ref[index, :, span], right[index, span, lanes], preferred_element_type=jnp.float32)
+            for place, s in enumerate(group):
+                products[s] = product[:, place * PAIR : (place + 1) * PAIR]
+            start += len(group)
 
         def part(s, z):
-            if s not in images[column]:
+            if s not in products:
                 return jnp.zeros((B, PAIR), jnp.float32)
-            position = images[column].index(s)
-            return product[z * B : (z + 1) * B, position * PAIR : (position + 1) * PAIR]
+            return products[s][z * B : (z + 1) * B]
 
         for pair in range(IMAGE_PAIRS):
             one = IMAGE[2 * pair]
@@ -426,19 +459,7 @@
             lanes = slice(pair * PAIR, (pair + 1) * PAIR)
             image[start : start + B, lanes] = low.astype(jnp.bfloat16)
             image[start + B : start + PAIR, lanes] = high.astype(jnp.bfloat16)
-    folded_half = low_half((HALF, PAIR))
-
-    def fold(product):
-        blocks = {}
-        for pair in range(IMAGE_PAIRS):
-            tile = product[:, pair * PAIR : (pair + 1) * PAIR]
-            top, bottom = tile[:HALF], tile[HALF:]
-            blocks[IMAGE[2 * pair]] = jnp.where(folded_half, top, swap_halves(bottom))
-            if 2 * pair + 1 < len(IMAGE):
-                blocks[IMAGE[2 * pair + 1]] = jnp.where(folded_half, swap_halves(top), bottom)
-        return blocks
-
-    star = jnp.dot(left_star[...], image[...], preferred_element_type=jnp.float32)
+    star = jnp.dot(left_star[0 : 4 * B, :], image[...], preferred_element_type=jnp.float32)
 
     def contribution(t):
         if t in STAR:
@@ -459,7 +480,7 @@
         parts = {t: contribution(t) for t in sorted({t for t, _ in sent})}
         for row, (t, s) in enumerate(sent):
             ref[row * HALF : (row + 1) * HALF, :] = parts[t][s].astype(jnp.bfloat16)
-    for group, tx in enumerate((0, -1, 1)):
+    for group, tx in enumerate((-1, 1)):
         parts = contribution((tx, 0))
         for position, s in enumerate(IMAGE):
             rest_ref[group, position] = parts[s]
@@ -475,7 +496,7 @@
         for row, s in enumerate(TO_X[tx]):
             value = None
             if s in IMAGE:
-                value = rest_ref[(0, -1, 1).index(tx), IMAGE.index(s)]
+                value = rest_ref[(-1, 1).index(tx), IMAGE.index(s)]
             if s in arrived:
                 more = message_block(y_first, arrived[s])
                 value = more if value is None else value + more
@@ -500,11 +521,12 @@
     )
 
 
-def own_kernel(rest_ref, y_first, y_second, c_first, c_second, own_ref):
+def own_kernel(left_star, image, y_first, y_second, c_first, c_second, own_ref):
+    centre = jnp.dot(left_star[4 * B : 5 * B, :], image[...], preferred_element_type=jnp.float32)
     has_x, has_y = inside()
     terms = {block: [] for block in STENCIL}
-    for position, s in enumerate(IMAGE):
-        terms[s].append((rest_ref[0, position], None, None))
+    for s, value in fold(centre).items():
+        terms[s].append((value, None, None))
     for s, row in relayed(0).items():
         terms[s].append((y_first, row, None))
     for row, (_, s) in enumerate(TO_Y_SECOND):
@@ -638,7 +660,7 @@
     *lefts_begun, begun = call(begin_kernel, [VMEM] * 5, lefts + [((len(BEGUN), 3, B, PAIR), f32)], cost=1)(
         rows, meta, x_first, x_second, y_first
     )
-    y_first, y_second, c_first, c_second, rest, *_ = call(
+    y_first, y_second, c_first, c_second, rest, _, left_star, _, image = call(
         main_kernel,
         [VMEM] * 13,
         [
@@ -646,10 +668,10 @@
             sent(TO_Y_SECOND),
             sent(TO_C_FIRST),
             sent(TO_C_SECOND),
-            ((3, len(IMAGE), HALF, PAIR), f32),
+            ((2, len(IMAGE), HALF, PAIR), f32),
         ]
-        + lefts,
-        [pltpu.VMEM((4 * PAIR, IMAGE_PAIRS * PAIR), bf16)],
+        + lefts
+        + [((4 * PAIR, IMAGE_PAIRS * PAIR), bf16)],
         aliases={10: 5, 11: 6, 12: 7},
     )(
         matrix,
@@ -669,8 +691,8 @@
     y_first = swapped(y_first, 0, 1)
     x_first, x_second = call(relay_kernel, [VMEM] * 2, [sent(TO_X[1]), sent(TO_X[-1])])(rest, y_first)
     x_first, x_second = swapped(x_first, 1, 0), swapped(x_second, 2, 0)
-    (own,) = call(own_kernel, [VMEM] * 5, [((len(OWN), HALF, PAIR), f32)], cost=3_000_000_000)(
-        rest, y_first, y_second, c_first, c_second
+    (own,) = call(own_kernel, [VMEM] * 6, [((len(OWN), HALF, PAIR), f32)], cost=3_000_000_000)(
+        left_star, image, y_first, y_second, c_first, c_second
     )
     (out,) = call(
         finish_kernel,

time: 26.7 us -> 26.6 us (level)
    pallas_call x1, Pallas kernels: 0.08 us -> 0.37 us  [per_device(): call(own_kernel, [VMEM] * 6, [((len(OWN), HALF, PAIR), f32)], cost=300000...]
  transfers between devices with their start and end apart: 12 -> 12, of which waited for: 7 -> 7; matrix products, arithmetic and copies ran while one was open for 0% -> 0% of each run, Pallas kernels for 11% -> 12%
where the time goes in v10:
time: 26.6 us; the launch traced here: 26.4 us
  waiting for transfers between devices  9.75 us (37%)
  starting transfers between devices  9.56 us (36%)
  Pallas kernels  7.03 us (26%)
    ppermute x12, waiting for transfers between devices, swapped(): return lax.ppermute(value, ('sx', 'sy'), pairs)  9.75 us
    ppermute x12, starting transfers between devices, swapped(): return lax.ppermute(value, ('sx', 'sy'), pairs)  9.56 us
    pallas_call x1, Pallas kernels, per_device(): call(pack_matrix_kernel, [HBM, HBM], [((4, PAIR, 6 * B), bf16), whole], [...  1.79 us
    pallas_call x1, Pallas kernels, per_device(): call(main_kernel, [VMEM] * 13, [sent(TO_Y_FIRST), sent(TO_Y_SECOND), sent...  1.55 us
    pallas_call x1, Pallas kernels, per_device(): call(functools.partial(pack_kernel, lax.axis_size('sy')), [HBM, HBM, HBM]...  1.48 us
    pallas_call x1, Pallas kernels, per_device(): call(begin_kernel, [VMEM] * 5, lefts + [((len(BEGUN), 3, B, PAIR), f32)],...  0.91 us
    pallas_call x1, Pallas kernels, per_device(): call(finish_kernel, [VMEM] * 3 + [HBM], [whole], [pltpu.VMEM((7, 7, B, B)...  0.89 us
  transfers between devices with their start and end apart: 12, of which 7 were waited for; matrix products, arithmetic and copies ran while one was open for 0% of the time, Pallas kernels for 12%

profile of v10, /device:TPU:20, one launch (start us, length us, event | category | flops | bytes accessed | tf_op | source)
XLA Modules:
  0.0 26.4 jit_solution(16537966802972260680)
XLA Ops:
  0.0 1.5 %shard_map.47 = (bf16[4,384,128]{2,1,0:T(8,128)(2,1)S(1)}, f32[32,128]{1,0:T(8,128)S(1)}, bf16[784,128]{1,0:T(8,128)(2,1)S(1)}, bf16[784,128]{1,0:T(8,128)(2,1)S...) custom-call(s32[2,2,2]{2,1,0:T(2,128)} %aggregate_hbm.1, s32[2,2,2,6]{3,2,1,0:T(2,128)} %links_hbm.3, ...), custom_call_target="tpu_custom_call" | custom-call | tf_op jit(solution)/shard_map/pallas_call | solution.py:617
  1.5 1.6 %collective-permute-start = (bf16[784,128]{1,0:T(8,128)(2,1)S(1)}, bf16[784,128]{1,0:T(8,128)(2,1)S(1)}, u32[]{:S(2)}, u32[]{:S(2)}) collective-permute-start(bf16[784,128]{1,0:T(8,128)(2,1)S(1)} %get-tuple-element.31), channel_id=1, source_target_pairs={{0,8},{1,9},{2,10},{3,11},{4,12},{5,13},{6,14},{7,15},{8,0},{9,1},... | collective-permute-start | bytes 602120 | tf_op jit(solution)/shard_map/ppermute | solution.py:587
  3.1 0.0 collective-permute-start.1
  3.1 0.6 %collective-permute-start.3 = (bf16[800,128]{1,0:T(8,128)(2,1)S(1)}, bf16[800,128]{1,0:T(8,128)(2,1)S(1)}, u32[]{:S(2)}, u32[]{:S(2)}) collective-permute-start(bf16[800,128]{1,0:T(8,128)(2,1)S(1)} %get-tuple-element.34), channel_id=1, source_target_pairs={{0,8},{1,2},{2,1},{3,4},{4,3},{5,6},{6,5},{7,15},{8,0},{9,10},{10,... | collective-permute-start | bytes 614408 | tf_op jit(solution)/shard_map/ppermute | solution.py:587
  3.7 1.0 %collective-permute-start.2 = (bf16[784,128]{1,0:T(8,128)(2,1)S(1)}, bf16[784,128]{1,0:T(8,128)(2,1)S(1)}, u32[]{:S(2)}, u32[]{:S(2)}) collective-permute-start(bf16[784,128]{1,0:T(8,128)(2,1)S(1)} %get-tuple-element.33), channel_id=1, source_target_pairs={{0,1},{1,0},{2,3},{3,2},{4,5},{5,4},{6,7},{7,6},{8,9},{9,8},{10,11... | collective-permute-start | bytes 602120 | tf_op jit(solution)/shard_map/ppermute | solution.py:587
  4.7 1.8 %shard_map.46 = (bf16[4,128,384]{2,1,0:T(8,128)(2,1)S(1)}, bf16[7,7,64,64]{3,2,1,0:T(8,128)(2,1)}) custom-call(s32[2,2,2,6]{3,2,1,0:T(2,128)} %links_hbm.3, bf16[2,2,2,7,64,64]{5,4,3,2,1,0:T(8,128)(2,1)} %a_hbm.1), custom_call_target="tpu_custom_call" | custom-call | tf_op jit(solution)/shard_map/pallas_call | solution.py:633
  6.5 1.7 %collective-permute-done.x_first = bf16[784,128]{1,0:T(8,128)(2,1)S(1)} collective-permute-done((bf16[784,128]{1,0:T(8,128)(2,1)S(1)}, bf16[784,128]{1,0:T(8,128)(2,1)S(1)}, u32[]{:S(2)}, u32[]{:S(2)}) %collective-permute-start) | collective-permute-done | bytes 200736 | tf_op jit(solution)/shard_map/ppermute | solution.py:587
  8.3 1.3 %collective-permute-done.1.x_second = bf16[784,128]{1,0:T(8,128)(2,1)S(1)} collective-permute-done((bf16[784,128]{1,0:T(8,128)(2,1)S(1)}, bf16[784,128]{1,0:T(8,128)(2,1)S(1)}, u32[]{:S(2)}, u32[]{:S(2)}) %collective-permute-start.1) | collective-permute-done | bytes 200736 | tf_op jit(solution)/shard_map/ppermute | solution.py:587
  9.6 0.0 collective-permute-start.5
  9.6 1.6 %collective-permute-start.4 = (bf16[32,128]{1,0:T(8,128)(2,1)S(1)}, bf16[32,128]{1,0:T(8,128)(2,1)S(1)}, u32[]{:S(2)}, u32[]{:S(2)}) collective-permute-start(bf16[32,128]{1,0:T(8,128)(2,1)S(1)} %get-tuple-element.35), channel_id=1, source_target_pairs={{0,1},{1,0},{2,3},{3,2},{4,5},{5,4},{6,7},{7,6},{8,9},{9,8},{10,11... | collective-permute-start | bytes 24584 | tf_op jit(solution)/shard_map/ppermute | solution.py:587
  11.2 0.0 collective-permute-done.2.y_first
  11.2 0.9 %shard_map.49 = (bf16[4,384,1280]{2,1,0:T(8,128)(2,1)S(1)}, bf16[320,512]{1,0:T(8,128)(2,1)S(1)}, bf16[4,64,128]{2,1,0:T(8,128)(2,1)S(1)}, f32[8,3,64,128]{3,2,1,0:T(8,128)S(1)}) custom-call(bf16[4,384,128]{2,1,0:T(8,128)(2,1)S(1)} %get-tuple-element.29.rows_ref, f32[32,128]{1,0:T(8,128)S(1)} %get-tuple-element.30.meta_ref, ...), custom_call_target="tpu_custom_call" | custom-call | flops 1 | bytes 1 | tf_op jit(solution)/shard_map/pallas_call | solution.py:660
  12.1 0.0 collective-permute-done.3.y_second
  12.1 0.0 collective-permute-done.4.c_first
  12.1 1.5 %collective-permute-done.5.c_second = bf16[48,128]{1,0:T(8,128)(2,1)S(1)} collective-permute-done((bf16[48,128]{1,0:T(8,128)(2,1)S(1)}, bf16[48,128]{1,0:T(8,128)(2,1)S(1)}, u32[]{:S(2)}, u32[]{:S(2)}) %collective-permute-start.5) | collective-permute-done | bytes 12320 | tf_op jit(solution)/shard_map/ppermute | solution.py:587
  13.6 1.5 %shard_map.50 = (bf16[1056,128]{1,0:T(8,128)(2,1)S(1)}, bf16[416,128]{1,0:T(8,128)(2,1)S(1)}, bf16[320,128]{1,0:T(8,128)(2,1)S(1)}, bf16[320,128]{1,0:T(8,128)(2...) custom-call(bf16[4,128,384]{2,1,0:T(8,128)(2,1)S(1)} %get-tuple-elem, ...), custom_call_target="tpu_custom_call", output_to_operand_aliasing={{5}: (10, {}), {6}: (11, {}), {7}: (12, {})} | custom-call | tf_op jit(solution)/shard_map/pallas_call | solution.py:663
  15.2 0.1 collective-permute-start.6
  15.2 0.6 %collective-permute-start.7 = (bf16[416,128]{1,0:T(8,128)(2,1)S(1)}, bf16[416,128]{1,0:T(8,128)(2,1)S(1)}, u32[]{:S(2)}, u32[]{:S(2)}) collective-permute-start(bf16[416,128]{1,0:T(8,128)(2,1)S(1)} %get-tuple-element.44), channel_id=1, source_target_pairs={{0,8},{1,2},{2,1},{3,4},{4,3},{5,6},{6,5},{7,15},{8,0},{9,10},{10,... | collective-permute-start | bytes 319496 | tf_op jit(solution)/shard_map/ppermute | solution.py:587
  15.9 1.8 %collective-permute-start.8 = (bf16[320,128]{1,0:T(8,128)(2,1)S(1)}, bf16[320,128]{1,0:T(8,128)(2,1)S(1)}, u32[]{:S(2)}, u32[]{:S(2)}) collective-permute-start(bf16[320,128]{1,0:T(8,128)(2,1)S(1)} %get-tuple-element.45), channel_id=1, source_target_pairs={{0,8},{1,10},{2,9},{3,12},{4,11},{5,14},{6,13},{7,15},{8,0},{9,2},... | collective-permute-start | bytes 245768 | tf_op jit(solution)/shard_map/ppermute | solution.py:587
  17.7 0.0 collective-permute-start.9
  17.7 0.0 collective-permute-done.6.y_first
  17.8 1.8 %collective-permute-start.10 = (bf16[480,128]{1,0:T(8,128)(2,1)S(1)}, bf16[480,128]{1,0:T(8,128)(2,1)S(1)}, u32[]{:S(2)}, u32[]{:S(2)}) collective-permute-start(bf16[480,128]{1,0:T(8,128)(2,1)S(1)} %get-tuple-element.48), channel_id=1, source_target_pairs={{0,8},{1,9},{2,10},{3,11},{4,12},{5,13},{6,14},{7,15},{8,0},{9,1},... | collective-permute-start | bytes 368648 | tf_op jit(solution)/shard_map/ppermute | solution.py:587
  19.5 0.4 %collective-permute-start.11 = (bf16[480,128]{1,0:T(8,128)(2,1)S(1)}, bf16[480,128]{1,0:T(8,128)(2,1)S(1)}, u32[]{:S(2)}, u32[]{:S(2)}) collective-permute-start(bf16[480,128]{1,0:T(8,128)(2,1)S(1)} %get-tuple-element.49), channel_id=1, source_target_pairs={{0,1},{1,0},{2,3},{3,2},{4,5},{5,4},{6,7},{7,6},{8,16},{9,17},{10,... | collective-permute-start | bytes 368648 | tf_op jit(solution)/shard_map/ppermute | solution.py:587
  19.9 2.8 %collective-permute-done.8.c_first = bf16[320,128]{1,0:T(8,128)(2,1)S(1)} collective-permute-done((bf16[320,128]{1,0:T(8,128)(2,1)S(1)}, bf16[320,128]{1,0:T(8,128)(2,1)S(1)}, u32[]{:S(2)}, u32[]{:S(2)}) %collective-permute-start.8) | collective-permute-done | bytes 81952 | tf_op jit(solution)/shard_map/ppermute | solution.py:587
  22.8 0.9 %collective-permute-done.9.c_second = bf16[320,128]{1,0:T(8,128)(2,1)S(1)} collective-permute-done((bf16[320,128]{1,0:T(8,128)(2,1)S(1)}, bf16[320,128]{1,0:T(8,128)(2,1)S(1)}, u32[]{:S(2)}, u32[]{:S(2)}) %collective-permute-start.9) | collective-permute-done | bytes 81952 | tf_op jit(solution)/shard_map/ppermute | solution.py:587
  23.6 0.7 %collective-permute-done.7.y_second = bf16[416,128]{1,0:T(8,128)(2,1)S(1)} collective-permute-done((bf16[416,128]{1,0:T(8,128)(2,1)S(1)}, bf16[416,128]{1,0:T(8,128)(2,1)S(1)}, u32[]{:S(2)}, u32[]{:S(2)}) %collective-permute-start.7) | collective-permute-done | bytes 106528 | tf_op jit(solution)/shard_map/ppermute | solution.py:587
  24.3 0.4 %shard_map.51.own_ref = f32[23,32,128]{2,1,0:T(8,128)S(1)} custom-call(bf16[320,512]{1,0:T(8,128)(2,1)S(1)} %get-tuple-element.41.left_star, bf16[512,896]{1,0:T(8,128)(2,1)S(1)} %get-tuple-element.42.image, bf16[1056,128]{1,0:T(8,128)(2,1)S(1)} %collective-permute-done.6.y_first, bf16[416,128]{1,0:T(8,128)(2,1)S(1)} %collective-permute-done.7.y_second, ...), custom_call_target="tpu_custom_call" | custom-call | flops 3000000000 | bytes 1 | tf_op jit(solution)/shard_map/pallas_call | solution.py:694
  24.7 0.0 collective-permute-done.10.x_first
  24.7 0.8 %collective-permute-done.11.x_second = bf16[480,128]{1,0:T(8,128)(2,1)S(1)} collective-permute-done((bf16[480,128]{1,0:T(8,128)(2,1)S(1)}, bf16[480,128]{1,0:T(8,128)(2,1)S(1)}, u32[]{:S(2)}, u32[]{:S(2)}) %collective-permute-start.11) | collective-permute-done | bytes 122912 | tf_op jit(solution)/shard_map/ppermute | solution.py:587
  25.5 0.9 %shard_map.53 = bf16[7,7,64,64]{3,2,1,0:T(8,128)(2,1)} custom-call(f32[23,32,128]{2,1,0:T(8,128)S(1)} %shard_map.51.own_ref, bf16[480,128]{1,0:T(8,128)(2,1)S(1)} %collective-permute-done.10.x_first, bf16[480,128]{1,0:T(8,128)(2,1)S(1)} %collective-permute-done.11.x_second, bf16[7,7,64,64]{3,2,1,0:T(8,128)(2,1)} %get-tuple-element.50._), custom_call_target="tpu_custom_call", output_to_operand_aliasing={{}: (3, {})} | custom-call | tf_op jit(solution)/shard_map/pallas_call | solution.py:697
  (2 shorter events, 0.1 us)
Async XLA Ops:
  1.5 6.8 %collective-permute-start = (bf16[784,128]{1,0:T(8,128)(2,1)S(1)}, bf16[784,128]{1,0:T(8,128)(2,1)S(1)}, u32[]{:S(2)}, u32[]{:S(2)}) collective-permute-start(bf16[784,128]{1,0:T(8,128)(2,1)S(1)} %get-tuple-element.31), channel_id=1, source_target_pairs={{0,8},{1,9},{2,10},{3,11},{4,12},{5,13},{6,14},{7,15},{8,0},{9,1},... | collective-permute-start | bytes 602120 | tf_op jit(solution)/shard_map/ppermute | solution.py:587
  3.1 6.4 %collective-permute-start.1 = (bf16[784,128]{1,0:T(8,128)(2,1)S(1)}, bf16[784,128]{1,0:T(8,128)(2,1)S(1)}, u32[]{:S(2)}, u32[]{:S(2)}) collective-permute-start(bf16[784,128]{1,0:T(8,128)(2,1)S(1)} %get-tuple-element.32), channel_id=1, source_target_pairs={{0,1},{1,0},{2,3},{3,2},{4,5},{5,4},{6,7},{7,6},{8,16},{9,17},{10,... | collective-permute-start | bytes 602120 | tf_op jit(solution)/shard_map/ppermute | solution.py:587
  3.1 9.0 %collective-permute-start.3 = (bf16[800,128]{1,0:T(8,128)(2,1)S(1)}, bf16[800,128]{1,0:T(8,128)(2,1)S(1)}, u32[]{:S(2)}, u32[]{:S(2)}) collective-permute-start(bf16[800,128]{1,0:T(8,128)(2,1)S(1)} %get-tuple-element.34), channel_id=1, source_target_pairs={{0,8},{1,2},{2,1},{3,4},{4,3},{5,6},{6,5},{7,15},{8,0},{9,10},{10,... | collective-permute-start | bytes 614408 | tf_op jit(solution)/shard_map/ppermute | solution.py:587
  3.7 7.5 %collective-permute-start.2 = (bf16[784,128]{1,0:T(8,128)(2,1)S(1)}, bf16[784,128]{1,0:T(8,128)(2,1)S(1)}, u32[]{:S(2)}, u32[]{:S(2)}) collective-permute-start(bf16[784,128]{1,0:T(8,128)(2,1)S(1)} %get-tuple-element.33), channel_id=1, source_target_pairs={{0,1},{1,0},{2,3},{3,2},{4,5},{5,4},{6,7},{7,6},{8,9},{9,8},{10,11... | collective-permute-start | bytes 602120 | tf_op jit(solution)/shard_map/ppermute | solution.py:587
  9.6 4.0 %collective-permute-start.5 = (bf16[48,128]{1,0:T(8,128)(2,1)S(1)}, bf16[48,128]{1,0:T(8,128)(2,1)S(1)}, u32[]{:S(2)}, u32[]{:S(2)}) collective-permute-start(bf16[48,128]{1,0:T(8,128)(2,1)S(1)} %get-tuple-element.36), channel_id=1, source_target_pairs={{0,8},{1,2},{2,1},{3,4},{4,3},{5,6},{6,5},{7,15},{8,0},{9,10},{10,... | collective-permute-start | bytes 36872 | tf_op jit(solution)/shard_map/ppermute | solution.py:587
  9.6 2.5 %collective-permute-start.4 = (bf16[32,128]{1,0:T(8,128)(2,1)S(1)}, bf16[32,128]{1,0:T(8,128)(2,1)S(1)}, u32[]{:S(2)}, u32[]{:S(2)}) collective-permute-start(bf16[32,128]{1,0:T(8,128)(2,1)S(1)} %get-tuple-element.35), channel_id=1, source_target_pairs={{0,1},{1,0},{2,3},{3,2},{4,5},{5,4},{6,7},{7,6},{8,9},{9,8},{10,11... | collective-permute-start | bytes 24584 | tf_op jit(solution)/shard_map/ppermute | solution.py:587
  15.2 2.6 %collective-permute-start.6 = (bf16[1056,128]{1,0:T(8,128)(2,1)S(1)}, bf16[1056,128]{1,0:T(8,128)(2,1)S(1)}, u32[]{:S(2)}, u32[]{:S(2)}) collective-permute-start(bf16[1056,128]{1,0:T(8,128)(2,1)S(1)} %get-tuple-element.43), channel_id=1, source_target_pairs={{0,1},{1,0},{2,3},{3,2},{4,5},{5,4},{6,7},{7,6},{8,9},{9,8},{10,11... | collective-permute-start | bytes 811016 | tf_op jit(solution)/shard_map/ppermute | solution.py:587
  15.2 9.1 %collective-permute-start.7 = (bf16[416,128]{1,0:T(8,128)(2,1)S(1)}, bf16[416,128]{1,0:T(8,128)(2,1)S(1)}, u32[]{:S(2)}, u32[]{:S(2)}) collective-permute-start(bf16[416,128]{1,0:T(8,128)(2,1)S(1)} %get-tuple-element.44), channel_id=1, source_target_pairs={{0,8},{1,2},{2,1},{3,4},{4,3},{5,6},{6,5},{7,15},{8,0},{9,10},{10,... | collective-permute-start | bytes 319496 | tf_op jit(solution)/shard_map/ppermute | solution.py:587
  15.9 6.9 %collective-permute-start.8 = (bf16[320,128]{1,0:T(8,128)(2,1)S(1)}, bf16[320,128]{1,0:T(8,128)(2,1)S(1)}, u32[]{:S(2)}, u32[]{:S(2)}) collective-permute-start(bf16[320,128]{1,0:T(8,128)(2,1)S(1)} %get-tuple-element.45), channel_id=1, source_target_pairs={{0,8},{1,10},{2,9},{3,12},{4,11},{5,14},{6,13},{7,15},{8,0},{9,2},... | collective-permute-start | bytes 245768 | tf_op jit(solution)/shard_map/ppermute | solution.py:587
  17.7 5.9 %collective-permute-start.9 = (bf16[320,128]{1,0:T(8,128)(2,1)S(1)}, bf16[320,128]{1,0:T(8,128)(2,1)S(1)}, u32[]{:S(2)}, u32[]{:S(2)}) collective-permute-start(bf16[320,128]{1,0:T(8,128)(2,1)S(1)} %get-tuple-element.46), channel_id=1, source_target_pairs={{0,1},{1,0},{2,3},{3,2},{4,5},{5,4},{6,7},{7,6},{8,16},{9,18},{10,... | collective-permute-start | bytes 245768 | tf_op jit(solution)/shard_map/ppermute | solution.py:587
  17.8 6.9 %collective-permute-start.10 = (bf16[480,128]{1,0:T(8,128)(2,1)S(1)}, bf16[480,128]{1,0:T(8,128)(2,1)S(1)}, u32[]{:S(2)}, u32[]{:S(2)}) collective-permute-start(bf16[480,128]{1,0:T(8,128)(2,1)S(1)} %get-tuple-element.48), channel_id=1, source_target_pairs={{0,8},{1,9},{2,10},{3,11},{4,12},{5,13},{6,14},{7,15},{8,0},{9,1},... | collective-permute-start | bytes 368648 | tf_op jit(solution)/shard_map/ppermute | solution.py:587
  19.5 6.0 %collective-permute-start.11 = (bf16[480,128]{1,0:T(8,128)(2,1)S(1)}, bf16[480,128]{1,0:T(8,128)(2,1)S(1)}, u32[]{:S(2)}, u32[]{:S(2)}) collective-permute-start(bf16[480,128]{1,0:T(8,128)(2,1)S(1)} %get-tuple-element.49), channel_id=1, source_target_pairs={{0,1},{1,0},{2,3},{3,2},{4,5},{5,4},{6,7},{7,6},{8,16},{9,17},{10,... | collective-permute-start | bytes 368648 | tf_op jit(solution)/shard_map/ppermute | solution.py:587

commit v11 on v10

--- a/solution.py
+++ b/solution.py
@@ -423,7 +423,6 @@
     to_y_second,
     to_c_first,
     to_c_second,
-    rest_ref,
     right,
     left_star,
     left_corner,
@@ -459,7 +458,7 @@
             lanes = slice(pair * PAIR, (pair + 1) * PAIR)
             image[start : start + B, lanes] = low.astype(jnp.bfloat16)
             image[start + B : start + PAIR, lanes] = high.astype(jnp.bfloat16)
-    star = jnp.dot(left_star[0 : 4 * B, :], image[...], preferred_element_type=jnp.float32)
+    star = jnp.dot(left_star[0 : 2 * B, :], image[...], preferred_element_type=jnp.float32)
 
     def contribution(t):
         if t in STAR:
@@ -480,23 +479,21 @@
         parts = {t: contribution(t) for t in sorted({t for t, _ in sent})}
         for row, (t, s) in enumerate(sent):
             ref[row * HALF : (row + 1) * HALF, :] = parts[t][s].astype(jnp.bfloat16)
-    for group, tx in enumerate((-1, 1)):
-        parts = contribution((tx, 0))
-        for position, s in enumerate(IMAGE):
-            rest_ref[group, position] = parts[s]
 
 
 def message_block(ref, row):
     return ref[row * HALF : (row + 1) * HALF, :].astype(jnp.float32)
 
 
-def relay_kernel(rest_ref, y_first, x_first, x_second):
+def relay_kernel(left_star, image, y_first, x_first, x_second):
+    beside = jnp.dot(left_star[2 * B : 4 * B, :], image[...], preferred_element_type=jnp.float32)
+    parts = {1: fold(beside[:B]), -1: fold(beside[B:])}
     for ref, tx in ((x_first, 1), (x_second, -1)):
         arrived = relayed(tx)
         for row, s in enumerate(TO_X[tx]):
             value = None
             if s in IMAGE:
-                value = rest_ref[(-1, 1).index(tx), IMAGE.index(s)]
+                value = parts[tx][s]
             if s in arrived:
                 more = message_block(y_first, arrived[s])
                 value = more if value is None else value + more
@@ -660,7 +657,7 @@
     *lefts_begun, begun = call(begin_kernel, [VMEM] * 5, lefts + [((len(BEGUN), 3, B, PAIR), f32)], cost=1)(
         rows, meta, x_first, x_second, y_first
     )
-    y_first, y_second, c_first, c_second, rest, _, left_star, _, image = call(
+    y_first, y_second, c_first, c_second, _, left_star, _, image = call(
         main_kernel,
         [VMEM] * 13,
         [
@@ -668,11 +665,10 @@
             sent(TO_Y_SECOND),
             sent(TO_C_FIRST),
             sent(TO_C_SECOND),
-            ((2, len(IMAGE), HALF, PAIR), f32),
         ]
         + lefts
         + [((4 * PAIR, IMAGE_PAIRS * PAIR), bf16)],
-        aliases={10: 5, 11: 6, 12: 7},
+        aliases={10: 4, 11: 5, 12: 6},
     )(
         matrix,
         rows,
@@ -689,7 +685,7 @@
     y_second = swapped(y_second, 0, 2)
     c_first, c_second = swapped(c_first, 1, 2), swapped(c_second, 2, 2)
     y_first = swapped(y_first, 0, 1)
-    x_first, x_second = call(relay_kernel, [VMEM] * 2, [sent(TO_X[1]), sent(TO_X[-1])])(rest, y_first)
+    x_first, x_second = call(relay_kernel, [VMEM] * 3, [sent(TO_X[1]), sent(TO_X[-1])])(left_star, image, y_first)
     x_first, x_second = swapped(x_first, 1, 0), swapped(x_second, 2, 0)
     (own,) = call(own_kernel, [VMEM] * 6, [((len(OWN), HALF, PAIR), f32)], cost=3_000_000_000)(
         left_star, image, y_first, y_second, c_first, c_second

time: 26.6 us -> 26.6 us (level)
    pallas_call x1, Pallas kernels: 0.05 us -> 0.39 us  [per_device(): call(relay_kernel, [VMEM] * 3, [sent(TO_X[1]), sent(TO_X[-1])])]
  transfers between devices with their start and end apart: 12 -> 12, of which waited for: 7 -> 7; matrix products, arithmetic and copies ran while one was open for 0% -> 0% of each run, Pallas kernels for 12% -> 13%
where the time goes in v11:
time: 26.6 us; the launch traced here: 26.4 us
  starting transfers between devices  9.56 us (36%)
  waiting for transfers between devices  9.54 us (36%)
  Pallas kernels  7.24 us (27%)
    ppermute x12, starting transfers between devices, swapped(): return lax.ppermute(value, ('sx', 'sy'), pairs)  9.56 us
    ppermute x12, waiting for transfers between devices, swapped(): return lax.ppermute(value, ('sx', 'sy'), pairs)  9.54 us
    pallas_call x1, Pallas kernels, per_device(): call(pack_matrix_kernel, [HBM, HBM], [((4, PAIR, 6 * B), bf16), whole], [...  1.79 us
    pallas_call x1, Pallas kernels, per_device(): call(functools.partial(pack_kernel, lax.axis_size('sy')), [HBM, HBM, HBM]...  1.48 us
    pallas_call x1, Pallas kernels, per_device(): call(main_kernel, [VMEM] * 13, [sent(TO_Y_FIRST), sent(TO_Y_SECOND), sent...  1.41 us
    pallas_call x1, Pallas kernels, per_device(): call(begin_kernel, [VMEM] * 5, lefts + [((len(BEGUN), 3, B, PAIR), f32)],...  0.91 us
    pallas_call x1, Pallas kernels, per_device(): call(finish_kernel, [VMEM] * 3 + [HBM], [whole], [pltpu.VMEM((7, 7, B, B)...  0.89 us
  transfers between devices with their start and end apart: 12, of which 7 were waited for; matrix products, arithmetic and copies ran while one was open for 0% of the time, Pallas kernels for 13%

profile of v11, /device:TPU:20, one launch (start us, length us, event | category | flops | bytes accessed | tf_op | source)
XLA Modules:
  0.0 26.4 jit_solution(10574548400026141421)
XLA Ops:
  0.0 1.5 %shard_map.47 = (bf16[4,384,128]{2,1,0:T(8,128)(2,1)S(1)}, f32[32,128]{1,0:T(8,128)S(1)}, bf16[784,128]{1,0:T(8,128)(2,1)S(1)}, bf16[784,128]{1,0:T(8,128)(2,1)S...) custom-call(s32[2,2,2]{2,1,0:T(2,128)} %aggregate_hbm.1, s32[2,2,2,6]{3,2,1,0:T(2,128)} %links_hbm.3, ...), custom_call_target="tpu_custom_call" | custom-call | tf_op jit(solution)/shard_map/pallas_call | solution.py:614
  1.5 1.6 %collective-permute-start = (bf16[784,128]{1,0:T(8,128)(2,1)S(1)}, bf16[784,128]{1,0:T(8,128)(2,1)S(1)}, u32[]{:S(2)}, u32[]{:S(2)}) collective-permute-start(bf16[784,128]{1,0:T(8,128)(2,1)S(1)} %get-tuple-element.30), channel_id=1, source_target_pairs={{0,8},{1,9},{2,10},{3,11},{4,12},{5,13},{6,14},{7,15},{8,0},{9,1},... | collective-permute-start | bytes 602120 | tf_op jit(solution)/shard_map/ppermute | solution.py:584
  3.1 0.0 collective-permute-start.1
  3.1 0.6 %collective-permute-start.3 = (bf16[800,128]{1,0:T(8,128)(2,1)S(1)}, bf16[800,128]{1,0:T(8,128)(2,1)S(1)}, u32[]{:S(2)}, u32[]{:S(2)}) collective-permute-start(bf16[800,128]{1,0:T(8,128)(2,1)S(1)} %get-tuple-element.33), channel_id=1, source_target_pairs={{0,8},{1,2},{2,1},{3,4},{4,3},{5,6},{6,5},{7,15},{8,0},{9,10},{10,... | collective-permute-start | bytes 614408 | tf_op jit(solution)/shard_map/ppermute | solution.py:584
  3.7 1.0 %collective-permute-start.2 = (bf16[784,128]{1,0:T(8,128)(2,1)S(1)}, bf16[784,128]{1,0:T(8,128)(2,1)S(1)}, u32[]{:S(2)}, u32[]{:S(2)}) collective-permute-start(bf16[784,128]{1,0:T(8,128)(2,1)S(1)} %get-tuple-element.32), channel_id=1, source_target_pairs={{0,1},{1,0},{2,3},{3,2},{4,5},{5,4},{6,7},{7,6},{8,9},{9,8},{10,11... | collective-permute-start | bytes 602120 | tf_op jit(solution)/shard_map/ppermute | solution.py:584
  4.7 1.8 %shard_map.46 = (bf16[4,128,384]{2,1,0:T(8,128)(2,1)S(1)}, bf16[7,7,64,64]{3,2,1,0:T(8,128)(2,1)}) custom-call(s32[2,2,2,6]{3,2,1,0:T(2,128)} %links_hbm.3, bf16[2,2,2,7,64,64]{5,4,3,2,1,0:T(8,128)(2,1)} %a_hbm.1), custom_call_target="tpu_custom_call" | custom-call | tf_op jit(solution)/shard_map/pallas_call | solution.py:630
  6.5 1.7 %collective-permute-done.x_first = bf16[784,128]{1,0:T(8,128)(2,1)S(1)} collective-permute-done((bf16[784,128]{1,0:T(8,128)(2,1)S(1)}, bf16[784,128]{1,0:T(8,128)(2,1)S(1)}, u32[]{:S(2)}, u32[]{:S(2)}) %collective-permute-start) | collective-permute-done | bytes 200736 | tf_op jit(solution)/shard_map/ppermute | solution.py:584
  8.3 1.3 %collective-permute-done.1.x_second = bf16[784,128]{1,0:T(8,128)(2,1)S(1)} collective-permute-done((bf16[784,128]{1,0:T(8,128)(2,1)S(1)}, bf16[784,128]{1,0:T(8,128)(2,1)S(1)}, u32[]{:S(2)}, u32[]{:S(2)}) %collective-permute-start.1) | collective-permute-done | bytes 200736 | tf_op jit(solution)/shard_map/ppermute | solution.py:584
  9.6 0.0 collective-permute-start.5
  9.6 1.6 %collective-permute-start.4 = (bf16[32,128]{1,0:T(8,128)(2,1)S(1)}, bf16[32,128]{1,0:T(8,128)(2,1)S(1)}, u32[]{:S(2)}, u32[]{:S(2)}) collective-permute-start(bf16[32,128]{1,0:T(8,128)(2,1)S(1)} %get-tuple-element.34), channel_id=1, source_target_pairs={{0,1},{1,0},{2,3},{3,2},{4,5},{5,4},{6,7},{7,6},{8,9},{9,8},{10,11... | collective-permute-start | bytes 24584 | tf_op jit(solution)/shard_map/ppermute | solution.py:584
  11.2 0.0 collective-permute-done.2.y_first
  11.2 0.9 %shard_map.49 = (bf16[4,384,1280]{2,1,0:T(8,128)(2,1)S(1)}, bf16[320,512]{1,0:T(8,128)(2,1)S(1)}, bf16[4,64,128]{2,1,0:T(8,128)(2,1)S(1)}, f32[8,3,64,128]{3,2,1,0:T(8,128)S(1)}) custom-call(bf16[4,384,128]{2,1,0:T(8,128)(2,1)S(1)} %get-tuple-element.28.rows_ref, f32[32,128]{1,0:T(8,128)S(1)} %get-tuple-element.29.meta_ref, ...), custom_call_target="tpu_custom_call" | custom-call | flops 1 | bytes 1 | tf_op jit(solution)/shard_map/pallas_call | solution.py:657
  12.1 0.0 collective-permute-done.3.y_second
  12.1 0.0 collective-permute-done.4.c_first
  12.1 1.5 %collective-permute-done.5.c_second = bf16[48,128]{1,0:T(8,128)(2,1)S(1)} collective-permute-done((bf16[48,128]{1,0:T(8,128)(2,1)S(1)}, bf16[48,128]{1,0:T(8,128)(2,1)S(1)}, u32[]{:S(2)}, u32[]{:S(2)}) %collective-permute-start.5) | collective-permute-done | bytes 12320 | tf_op jit(solution)/shard_map/ppermute | solution.py:584
  13.6 1.4 %shard_map.50 = (bf16[1056,128]{1,0:T(8,128)(2,1)S(1)}, bf16[416,128]{1,0:T(8,128)(2,1)S(1)}, bf16[320,128]{1,0:T(8,128)(2,1)S(1)}, bf16[320,128]{1,0:T(8,128)(2...) custom-call(bf16[4,128,384]{2,1,0:T(8,128)(2,1)S(1)} %get-tuple-elem, ...), custom_call_target="tpu_custom_call", output_to_operand_aliasing={{4}: (10, {}), {5}: (11, {}), {6}: (12, {})} | custom-call | tf_op jit(solution)/shard_map/pallas_call | solution.py:660
  15.0 0.1 collective-permute-start.6
  15.1 0.6 %collective-permute-start.7 = (bf16[416,128]{1,0:T(8,128)(2,1)S(1)}, bf16[416,128]{1,0:T(8,128)(2,1)S(1)}, u32[]{:S(2)}, u32[]{:S(2)}) collective-permute-start(bf16[416,128]{1,0:T(8,128)(2,1)S(1)} %get-tuple-element.43), channel_id=1, source_target_pairs={{0,8},{1,2},{2,1},{3,4},{4,3},{5,6},{6,5},{7,15},{8,0},{9,10},{10,... | collective-permute-start | bytes 319496 | tf_op jit(solution)/shard_map/ppermute | solution.py:584
  15.7 1.8 %collective-permute-start.8 = (bf16[320,128]{1,0:T(8,128)(2,1)S(1)}, bf16[320,128]{1,0:T(8,128)(2,1)S(1)}, u32[]{:S(2)}, u32[]{:S(2)}) collective-permute-start(bf16[320,128]{1,0:T(8,128)(2,1)S(1)} %get-tuple-element.44), channel_id=1, source_target_pairs={{0,8},{1,10},{2,9},{3,12},{4,11},{5,14},{6,13},{7,15},{8,0},{9,2},... | collective-permute-start | bytes 245768 | tf_op jit(solution)/shard_map/ppermute | solution.py:584
  17.6 0.0 collective-permute-start.9
  17.6 0.0 collective-permute-done.6.y_first
  17.6 0.4 %shard_map.52 = (bf16[480,128]{1,0:T(8,128)(2,1)S(1)}, bf16[480,128]{1,0:T(8,128)(2,1)S(1)}) custom-call(bf16[320,512]{1,0:T(8,128)(2,1)S(1)} %get-tuple-element.40.left_star, bf16[512,896]{1,0:T(8,128)(2,1)S(1)} %get-tuple-element.41.image, bf16[1056,128]{1,0:T(8,128)(2,1)S(1)} %collective-permute-done.6.y_first), custom_call_target="tpu_custom_call" | custom-call | tf_op jit(solution)/shard_map/pallas_call | solution.py:688
  18.0 1.8 %collective-permute-start.10 = (bf16[480,128]{1,0:T(8,128)(2,1)S(1)}, bf16[480,128]{1,0:T(8,128)(2,1)S(1)}, u32[]{:S(2)}, u32[]{:S(2)}) collective-permute-start(bf16[480,128]{1,0:T(8,128)(2,1)S(1)} %get-tuple-element.46), channel_id=1, source_target_pairs={{0,8},{1,9},{2,10},{3,11},{4,12},{5,13},{6,14},{7,15},{8,0},{9,1},... | collective-permute-start | bytes 368648 | tf_op jit(solution)/shard_map/ppermute | solution.py:584
  19.7 0.4 %collective-permute-start.11 = (bf16[480,128]{1,0:T(8,128)(2,1)S(1)}, bf16[480,128]{1,0:T(8,128)(2,1)S(1)}, u32[]{:S(2)}, u32[]{:S(2)}) collective-permute-start(bf16[480,128]{1,0:T(8,128)(2,1)S(1)} %get-tuple-element.47), channel_id=1, source_target_pairs={{0,1},{1,0},{2,3},{3,2},{4,5},{5,4},{6,7},{7,6},{8,16},{9,17},{10,... | collective-permute-start | bytes 368648 | tf_op jit(solution)/shard_map/ppermute | solution.py:584
  20.1 2.5 %collective-permute-done.8.c_first = bf16[320,128]{1,0:T(8,128)(2,1)S(1)} collective-permute-done((bf16[320,128]{1,0:T(8,128)(2,1)S(1)}, bf16[320,128]{1,0:T(8,128)(2,1)S(1)}, u32[]{:S(2)}, u32[]{:S(2)}) %collective-permute-start.8) | collective-permute-done | bytes 81952 | tf_op jit(solution)/shard_map/ppermute | solution.py:584
  22.6 0.9 %collective-permute-done.9.c_second = bf16[320,128]{1,0:T(8,128)(2,1)S(1)} collective-permute-done((bf16[320,128]{1,0:T(8,128)(2,1)S(1)}, bf16[320,128]{1,0:T(8,128)(2,1)S(1)}, u32[]{:S(2)}, u32[]{:S(2)}) %collective-permute-start.9) | collective-permute-done | bytes 81952 | tf_op jit(solution)/shard_map/ppermute | solution.py:584
  23.5 0.7 %collective-permute-done.7.y_second = bf16[416,128]{1,0:T(8,128)(2,1)S(1)} collective-permute-done((bf16[416,128]{1,0:T(8,128)(2,1)S(1)}, bf16[416,128]{1,0:T(8,128)(2,1)S(1)}, u32[]{:S(2)}, u32[]{:S(2)}) %collective-permute-start.7) | collective-permute-done | bytes 106528 | tf_op jit(solution)/shard_map/ppermute | solution.py:584
  24.2 0.4 %shard_map.51.own_ref = f32[23,32,128]{2,1,0:T(8,128)S(1)} custom-call(bf16[320,512]{1,0:T(8,128)(2,1)S(1)} %get-tuple-element.40.left_star, bf16[512,896]{1,0:T(8,128)(2,1)S(1)} %get-tuple-element.41.image, bf16[1056,128]{1,0:T(8,128)(2,1)S(1)} %collective-permute-done.6.y_first, bf16[416,128]{1,0:T(8,128)(2,1)S(1)} %collective-permute-done.7.y_second, ...), custom_call_target="tpu_custom_call" | custom-call | flops 3000000000 | bytes 1 | tf_op jit(solution)/shard_map/pallas_call | solution.py:690
  24.5 0.0 collective-permute-done.10.x_first
  24.6 1.0 %collective-permute-done.11.x_second = bf16[480,128]{1,0:T(8,128)(2,1)S(1)} collective-permute-done((bf16[480,128]{1,0:T(8,128)(2,1)S(1)}, bf16[480,128]{1,0:T(8,128)(2,1)S(1)}, u32[]{:S(2)}, u32[]{:S(2)}) %collective-permute-start.11) | collective-permute-done | bytes 122912 | tf_op jit(solution)/shard_map/ppermute | solution.py:584
  25.5 0.9 %shard_map.53 = bf16[7,7,64,64]{3,2,1,0:T(8,128)(2,1)} custom-call(f32[23,32,128]{2,1,0:T(8,128)S(1)} %shard_map.51.own_ref, bf16[480,128]{1,0:T(8,128)(2,1)S(1)} %collective-permute-done.10.x_first, bf16[480,128]{1,0:T(8,128)(2,1)S(1)} %collective-permute-done.11.x_second, bf16[7,7,64,64]{3,2,1,0:T(8,128)(2,1)} %get-tuple-element.48._), custom_call_target="tpu_custom_call", output_to_operand_aliasing={{}: (3, {})} | custom-call | tf_op jit(solution)/shard_map/pallas_call | solution.py:693
  (1 shorter events, 0.0 us)
Async XLA Ops:
  1.5 6.8 %collective-permute-start = (bf16[784,128]{1,0:T(8,128)(2,1)S(1)}, bf16[784,128]{1,0:T(8,128)(2,1)S(1)}, u32[]{:S(2)}, u32[]{:S(2)}) collective-permute-start(bf16[784,128]{1,0:T(8,128)(2,1)S(1)} %get-tuple-element.30), channel_id=1, source_target_pairs={{0,8},{1,9},{2,10},{3,11},{4,12},{5,13},{6,14},{7,15},{8,0},{9,1},... | collective-permute-start | bytes 602120 | tf_op jit(solution)/shard_map/ppermute | solution.py:584
  3.1 6.4 %collective-permute-start.1 = (bf16[784,128]{1,0:T(8,128)(2,1)S(1)}, bf16[784,128]{1,0:T(8,128)(2,1)S(1)}, u32[]{:S(2)}, u32[]{:S(2)}) collective-permute-start(bf16[784,128]{1,0:T(8,128)(2,1)S(1)} %get-tuple-element.31), channel_id=1, source_target_pairs={{0,1},{1,0},{2,3},{3,2},{4,5},{5,4},{6,7},{7,6},{8,16},{9,17},{10,... | collective-permute-start | bytes 602120 | tf_op jit(solution)/shard_map/ppermute | solution.py:584
  3.1 9.0 %collective-permute-start.3 = (bf16[800,128]{1,0:T(8,128)(2,1)S(1)}, bf16[800,128]{1,0:T(8,128)(2,1)S(1)}, u32[]{:S(2)}, u32[]{:S(2)}) collective-permute-start(bf16[800,128]{1,0:T(8,128)(2,1)S(1)} %get-tuple-element.33), channel_id=1, source_target_pairs={{0,8},{1,2},{2,1},{3,4},{4,3},{5,6},{6,5},{7,15},{8,0},{9,10},{10,... | collective-permute-start | bytes 614408 | tf_op jit(solution)/shard_map/ppermute | solution.py:584
  3.7 7.5 %collective-permute-start.2 = (bf16[784,128]{1,0:T(8,128)(2,1)S(1)}, bf16[784,128]{1,0:T(8,128)(2,1)S(1)}, u32[]{:S(2)}, u32[]{:S(2)}) collective-permute-start(bf16[784,128]{1,0:T(8,128)(2,1)S(1)} %get-tuple-element.32), channel_id=1, source_target_pairs={{0,1},{1,0},{2,3},{3,2},{4,5},{5,4},{6,7},{7,6},{8,9},{9,8},{10,11... | collective-permute-start | bytes 602120 | tf_op jit(solution)/shard_map/ppermute | solution.py:584
  9.6 4.0 %collective-permute-start.5 = (bf16[48,128]{1,0:T(8,128)(2,1)S(1)}, bf16[48,128]{1,0:T(8,128)(2,1)S(1)}, u32[]{:S(2)}, u32[]{:S(2)}) collective-permute-start(bf16[48,128]{1,0:T(8,128)(2,1)S(1)} %get-tuple-element.35), channel_id=1, source_target_pairs={{0,8},{1,2},{2,1},{3,4},{4,3},{5,6},{6,5},{7,15},{8,0},{9,10},{10,... | collective-permute-start | bytes 36872 | tf_op jit(solution)/shard_map/ppermute | solution.py:584
  9.6 2.5 %collective-permute-start.4 = (bf16[32,128]{1,0:T(8,128)(2,1)S(1)}, bf16[32,128]{1,0:T(8,128)(2,1)S(1)}, u32[]{:S(2)}, u32[]{:S(2)}) collective-permute-start(bf16[32,128]{1,0:T(8,128)(2,1)S(1)} %get-tuple-element.34), channel_id=1, source_target_pairs={{0,1},{1,0},{2,3},{3,2},{4,5},{5,4},{6,7},{7,6},{8,9},{9,8},{10,11... | collective-permute-start | bytes 24584 | tf_op jit(solution)/shard_map/ppermute | solution.py:584
  15.0 2.6 %collective-permute-start.6 = (bf16[1056,128]{1,0:T(8,128)(2,1)S(1)}, bf16[1056,128]{1,0:T(8,128)(2,1)S(1)}, u32[]{:S(2)}, u32[]{:S(2)}) collective-permute-start(bf16[1056,128]{1,0:T(8,128)(2,1)S(1)} %get-tuple-element.42), channel_id=1, source_target_pairs={{0,1},{1,0},{2,3},{3,2},{4,5},{5,4},{6,7},{7,6},{8,9},{9,8},{10,11... | collective-permute-start | bytes 811016 | tf_op jit(solution)/shard_map/ppermute | solution.py:584
  15.1 9.1 %collective-permute-start.7 = (bf16[416,128]{1,0:T(8,128)(2,1)S(1)}, bf16[416,128]{1,0:T(8,128)(2,1)S(1)}, u32[]{:S(2)}, u32[]{:S(2)}) collective-permute-start(bf16[416,128]{1,0:T(8,128)(2,1)S(1)} %get-tuple-element.43), channel_id=1, source_target_pairs={{0,8},{1,2},{2,1},{3,4},{4,3},{5,6},{6,5},{7,15},{8,0},{9,10},{10,... | collective-permute-start | bytes 319496 | tf_op jit(solution)/shard_map/ppermute | solution.py:584
  15.7 6.9 %collective-permute-start.8 = (bf16[320,128]{1,0:T(8,128)(2,1)S(1)}, bf16[320,128]{1,0:T(8,128)(2,1)S(1)}, u32[]{:S(2)}, u32[]{:S(2)}) collective-permute-start(bf16[320,128]{1,0:T(8,128)(2,1)S(1)} %get-tuple-element.44), channel_id=1, source_target_pairs={{0,8},{1,10},{2,9},{3,12},{4,11},{5,14},{6,13},{7,15},{8,0},{9,2},... | collective-permute-start | bytes 245768 | tf_op jit(solution)/shard_map/ppermute | solution.py:584
  17.6 5.9 %collective-permute-start.9 = (bf16[320,128]{1,0:T(8,128)(2,1)S(1)}, bf16[320,128]{1,0:T(8,128)(2,1)S(1)}, u32[]{:S(2)}, u32[]{:S(2)}) collective-permute-start(bf16[320,128]{1,0:T(8,128)(2,1)S(1)} %get-tuple-element.45), channel_id=1, source_target_pairs={{0,1},{1,0},{2,3},{3,2},{4,5},{5,4},{6,7},{7,6},{8,16},{9,18},{10,... | collective-permute-start | bytes 245768 | tf_op jit(solution)/shard_map/ppermute | solution.py:584
  18.0 6.6 %collective-permute-start.10 = (bf16[480,128]{1,0:T(8,128)(2,1)S(1)}, bf16[480,128]{1,0:T(8,128)(2,1)S(1)}, u32[]{:S(2)}, u32[]{:S(2)}) collective-permute-start(bf16[480,128]{1,0:T(8,128)(2,1)S(1)} %get-tuple-element.46), channel_id=1, source_target_pairs={{0,8},{1,9},{2,10},{3,11},{4,12},{5,13},{6,14},{7,15},{8,0},{9,1},... | collective-permute-start | bytes 368648 | tf_op jit(solution)/shard_map/ppermute | solution.py:584
  19.7 5.8 %collective-permute-start.11 = (bf16[480,128]{1,0:T(8,128)(2,1)S(1)}, bf16[480,128]{1,0:T(8,128)(2,1)S(1)}, u32[]{:S(2)}, u32[]{:S(2)}) collective-permute-start(bf16[480,128]{1,0:T(8,128)(2,1)S(1)} %get-tuple-element.47), channel_id=1, source_target_pairs={{0,1},{1,0},{2,3},{3,2},{4,5},{5,4},{6,7},{7,6},{8,16},{9,17},{10,... | collective-permute-start | bytes 368648 | tf_op jit(solution)/shard_map/ppermute | solution.py:584

commit v12 on v11

--- a/solution.py
+++ b/solution.py
@@ -130,8 +130,6 @@
     meta_ref,
     x_first,
     x_second,
-    y_first,
-    y_second,
     p_ref,
     aggregate_ref,
     links_ref,
@@ -169,8 +167,6 @@
     messages = (
         (x_first, ((1, 0), (1, 1))),
         (x_second, ((0, 0), (0, 1))),
-        (y_first, ((0, 1), (1, 1))),
-        (y_second, ((0, 0), (1, 0))),
     )
     for ref, columns in messages:
         tail = fill_rows(TAIL, states + links[columns[0]] + links[columns[1]])
@@ -184,6 +180,17 @@
                 if column in columns:
                     start = columns.index(column) * BLOCK_ROWS + m * B
                     ref[start : start + B, :] = packed
+
+
+def pack_y_kernel(rows_ref, meta_ref, y_first, y_second):
+    meta = meta_ref[...]
+    for ref, columns in ((y_first, (1, 3)), (y_second, (0, 2))):
+        parts = [meta[0:4]]
+        for place, index in enumerate(columns):
+            ref[place * BLOCK_ROWS : (place + 1) * BLOCK_ROWS, :] = rows_ref[index]
+            parts.append(meta[4 + (SLOTS - 1) * index : 4 + (SLOTS - 1) * (index + 1)])
+        parts.append(jnp.zeros((2, PAIR), jnp.float32))
+        ref[BODY : BODY + TAIL, :] = jnp.concatenate(parts, axis=0).astype(jnp.bfloat16)
 
 
 def notes_kernel(x_first, x_second, _, notes_ref, again_ref):
@@ -611,10 +618,10 @@
     bf16, f32 = jnp.bfloat16, jnp.float32
     message = ((BODY + TAIL, PAIR), bf16)
     longer = ((BODY + 2 * TAIL, PAIR), bf16)
-    rows, meta, x_first, x_second, y_first, y_second = call(
+    rows, meta, x_first, x_second = call(
         functools.partial(pack_kernel, lax.axis_size("sy")),
         [HBM, HBM, HBM],
-        [((4, BLOCK_ROWS, PAIR), bf16), ((32, PAIR), f32), message, message, message, longer],
+        [((4, BLOCK_ROWS, PAIR), bf16), ((32, PAIR), f32), message, message],
         [
             pltpu.VMEM((4, 2, 7, B, B), bf16),
             pltpu.SMEM((2, 2, 2), jnp.int32),
@@ -623,6 +630,7 @@
             pltpu.SemaphoreType.DMA((2,)),
         ],
     )(*in_hbm(aggregate, face_links, prolongator))
+    y_first, y_second = call(pack_y_kernel, [VMEM] * 2, [message, longer])(rows, meta)
     y_second = swapped(y_second, 0, 2)
     x_first, x_second = swapped(x_first, 1, 0), swapped(x_second, 2, 0)
     y_first = swapped(y_first, 0, 1)

time: 26.6 us -> 26.5 us (level)
  no operation moved by 1% of the time
where the time goes in v12:
time: 26.5 us; the launch traced here: 26.4 us
  starting transfers between devices  9.63 us (36%)
  waiting for transfers between devices  9.44 us (36%)
  Pallas kernels  7.21 us (27%)
    ppermute x12, starting transfers between devices, swapped(): return lax.ppermute(value, ('sx', 'sy'), pairs)  9.63 us
    ppermute x12, waiting for transfers between devices, swapped(): return lax.ppermute(value, ('sx', 'sy'), pairs)  9.44 us
    pallas_call x1, Pallas kernels, per_device(): call(pack_matrix_kernel, [HBM, HBM], [((4, PAIR, 6 * B), bf16), whole], [...  1.79 us
    pallas_call x1, Pallas kernels, per_device(): call(functools.partial(pack_kernel, lax.axis_size('sy')), [HBM, HBM, HBM]...  1.43 us
    pallas_call x1, Pallas kernels, per_device(): call(main_kernel, [VMEM] * 13, [sent(TO_Y_FIRST), sent(TO_Y_SECOND), sent...  1.41 us
    pallas_call x1, Pallas kernels, per_device(): call(begin_kernel, [VMEM] * 5, lefts + [((len(BEGUN), 3, B, PAIR), f32)],...  0.91 us
    pallas_call x1, Pallas kernels, per_device(): call(finish_kernel, [VMEM] * 3 + [HBM], [whole], [pltpu.VMEM((7, 7, B, B)...  0.89 us
  transfers between devices with their start and end apart: 12, of which 7 were waited for; matrix products, arithmetic and copies ran while one was open for 0% of the time, Pallas kernels for 13%

profile of v12, /device:TPU:20, one launch (start us, length us, event | category | flops | bytes accessed | tf_op | source)
XLA Modules:
  0.0 26.4 jit_solution(11866581761010144636)
XLA Ops:
  0.0 1.4 %shard_map.47 = (bf16[4,384,128]{2,1,0:T(8,128)(2,1)S(1)}, f32[32,128]{1,0:T(8,128)S(1)}, bf16[784,128]{1,0:T(8,128)(2,1)S(1)}, bf16[784,128]{1,0:T(8,128)(2,1)S(1)}) custom-call(s32[2,2,2]{2,1,0:T(2,128)} %aggregate_hbm.1, s32[2,2,2,6]{3,2,1,0:T(2,128)} %links_hbm.3, bf16[2,2,2,7,64,64]{5,4,3,2,1,0:T(8,128)(2,1)} %p_hbm.1), custom_call_target="tpu_custom_call" | custom-call | tf_op jit(solution)/shard_map/pallas_call | solution.py:621
  1.4 1.6 %collective-permute-start = (bf16[784,128]{1,0:T(8,128)(2,1)S(1)}, bf16[784,128]{1,0:T(8,128)(2,1)S(1)}, u32[]{:S(2)}, u32[]{:S(2)}) collective-permute-start(bf16[784,128]{1,0:T(8,128)(2,1)S(1)} %get-tuple-element.30), channel_id=1, source_target_pairs={{0,8},{1,9},{2,10},{3,11},{4,12},{5,13},{6,14},{7,15},{8,0},{9,1},... | collective-permute-start | bytes 602120 | tf_op jit(solution)/shard_map/ppermute | solution.py:591
  3.1 0.0 collective-permute-start.1
  3.1 0.7 %collective-permute-start.3 = (bf16[800,128]{1,0:T(8,128)(2,1)S(1)}, bf16[800,128]{1,0:T(8,128)(2,1)S(1)}, u32[]{:S(2)}, u32[]{:S(2)}) collective-permute-start(bf16[800,128]{1,0:T(8,128)(2,1)S(1)} %get-tuple-element.33), channel_id=1, source_target_pairs={{0,8},{1,2},{2,1},{3,4},{4,3},{5,6},{6,5},{7,15},{8,0},{9,10},{10,... | collective-permute-start | bytes 614408 | tf_op jit(solution)/shard_map/ppermute | solution.py:591
  3.8 1.0 %collective-permute-start.2 = (bf16[784,128]{1,0:T(8,128)(2,1)S(1)}, bf16[784,128]{1,0:T(8,128)(2,1)S(1)}, u32[]{:S(2)}, u32[]{:S(2)}) collective-permute-start(bf16[784,128]{1,0:T(8,128)(2,1)S(1)} %get-tuple-element.32), channel_id=1, source_target_pairs={{0,1},{1,0},{2,3},{3,2},{4,5},{5,4},{6,7},{7,6},{8,9},{9,8},{10,11... | collective-permute-start | bytes 602120 | tf_op jit(solution)/shard_map/ppermute | solution.py:591
  4.8 1.8 %shard_map.46 = (bf16[4,128,384]{2,1,0:T(8,128)(2,1)S(1)}, bf16[7,7,64,64]{3,2,1,0:T(8,128)(2,1)}) custom-call(s32[2,2,2,6]{3,2,1,0:T(2,128)} %links_hbm.3, bf16[2,2,2,7,64,64]{5,4,3,2,1,0:T(8,128)(2,1)} %a_hbm.1), custom_call_target="tpu_custom_call" | custom-call | tf_op jit(solution)/shard_map/pallas_call | solution.py:638
  6.6 1.7 %collective-permute-done.x_first = bf16[784,128]{1,0:T(8,128)(2,1)S(1)} collective-permute-done((bf16[784,128]{1,0:T(8,128)(2,1)S(1)}, bf16[784,128]{1,0:T(8,128)(2,1)S(1)}, u32[]{:S(2)}, u32[]{:S(2)}) %collective-permute-start) | collective-permute-done | bytes 200736 | tf_op jit(solution)/shard_map/ppermute | solution.py:591
  8.2 1.3 %collective-permute-done.1.x_second = bf16[784,128]{1,0:T(8,128)(2,1)S(1)} collective-permute-done((bf16[784,128]{1,0:T(8,128)(2,1)S(1)}, bf16[784,128]{1,0:T(8,128)(2,1)S(1)}, u32[]{:S(2)}, u32[]{:S(2)}) %collective-permute-start.1) | collective-permute-done | bytes 200736 | tf_op jit(solution)/shard_map/ppermute | solution.py:591
  9.5 0.0 collective-permute-start.5
  9.5 1.6 %collective-permute-start.4 = (bf16[32,128]{1,0:T(8,128)(2,1)S(1)}, bf16[32,128]{1,0:T(8,128)(2,1)S(1)}, u32[]{:S(2)}, u32[]{:S(2)}) collective-permute-start(bf16[32,128]{1,0:T(8,128)(2,1)S(1)} %get-tuple-element.34), channel_id=1, source_target_pairs={{0,1},{1,0},{2,3},{3,2},{4,5},{5,4},{6,7},{7,6},{8,9},{9,8},{10,11... | collective-permute-start | bytes 24584 | tf_op jit(solution)/shard_map/ppermute | solution.py:591
  11.1 0.0 collective-permute-done.2.y_first
  11.1 0.9 %shard_map.50 = (bf16[4,384,1280]{2,1,0:T(8,128)(2,1)S(1)}, bf16[320,512]{1,0:T(8,128)(2,1)S(1)}, bf16[4,64,128]{2,1,0:T(8,128)(2,1)S(1)}, f32[8,3,64,128]{3,2,1,0:T(8,128)S(1)}) custom-call(bf16[4,384,128]{2,1,0:T(8,128)(2,1)S(1)} %get-tuple-element.28.rows_ref, f32[32,128]{1,0:T(8,128)S(1)} %get-tuple-element.29.meta_ref, ...), custom_call_target="tpu_custom_call" | custom-call | flops 1 | bytes 1 | tf_op jit(solution)/shard_map/pallas_call | solution.py:665
  12.1 0.0 collective-permute-done.3.y_second
  12.1 0.0 collective-permute-done.4.c_first
  12.1 1.5 %collective-permute-done.5.c_second = bf16[48,128]{1,0:T(8,128)(2,1)S(1)} collective-permute-done((bf16[48,128]{1,0:T(8,128)(2,1)S(1)}, bf16[48,128]{1,0:T(8,128)(2,1)S(1)}, u32[]{:S(2)}, u32[]{:S(2)}) %collective-permute-start.5) | collective-permute-done | bytes 12320 | tf_op jit(solution)/shard_map/ppermute | solution.py:591
  13.6 1.4 %shard_map.51 = (bf16[1056,128]{1,0:T(8,128)(2,1)S(1)}, bf16[416,128]{1,0:T(8,128)(2,1)S(1)}, bf16[320,128]{1,0:T(8,128)(2,1)S(1)}, bf16[320,128]{1,0:T(8,128)(2...) custom-call(bf16[4,128,384]{2,1,0:T(8,128)(2,1)S(1)} %get-tuple-elem, ...), custom_call_target="tpu_custom_call", output_to_operand_aliasing={{4}: (10, {}), {5}: (11, {}), {6}: (12, {})} | custom-call | tf_op jit(solution)/shard_map/pallas_call | solution.py:668
  15.0 0.1 collective-permute-start.6
  15.0 0.6 %collective-permute-start.7 = (bf16[416,128]{1,0:T(8,128)(2,1)S(1)}, bf16[416,128]{1,0:T(8,128)(2,1)S(1)}, u32[]{:S(2)}, u32[]{:S(2)}) collective-permute-start(bf16[416,128]{1,0:T(8,128)(2,1)S(1)} %get-tuple-element.43), channel_id=1, source_target_pairs={{0,8},{1,2},{2,1},{3,4},{4,3},{5,6},{6,5},{7,15},{8,0},{9,10},{10,... | collective-permute-start | bytes 319496 | tf_op jit(solution)/shard_map/ppermute | solution.py:591
  15.7 1.8 %collective-permute-start.8 = (bf16[320,128]{1,0:T(8,128)(2,1)S(1)}, bf16[320,128]{1,0:T(8,128)(2,1)S(1)}, u32[]{:S(2)}, u32[]{:S(2)}) collective-permute-start(bf16[320,128]{1,0:T(8,128)(2,1)S(1)} %get-tuple-element.44), channel_id=1, source_target_pairs={{0,8},{1,10},{2,9},{3,12},{4,11},{5,14},{6,13},{7,15},{8,0},{9,2},... | collective-permute-start | bytes 245768 | tf_op jit(solution)/shard_map/ppermute | solution.py:591
  17.5 0.0 collective-permute-start.9
  17.5 0.0 collective-permute-done.6.y_first
  17.5 0.4 %shard_map.53 = (bf16[480,128]{1,0:T(8,128)(2,1)S(1)}, bf16[480,128]{1,0:T(8,128)(2,1)S(1)}) custom-call(bf16[320,512]{1,0:T(8,128)(2,1)S(1)} %get-tuple-element.40.left_star, bf16[512,896]{1,0:T(8,128)(2,1)S(1)} %get-tuple-element.41.image, bf16[1056,128]{1,0:T(8,128)(2,1)S(1)} %collective-permute-done.6.y_first), custom_call_target="tpu_custom_call" | custom-call | tf_op jit(solution)/shard_map/pallas_call | solution.py:696
  17.9 1.8 %collective-permute-start.10 = (bf16[480,128]{1,0:T(8,128)(2,1)S(1)}, bf16[480,128]{1,0:T(8,128)(2,1)S(1)}, u32[]{:S(2)}, u32[]{:S(2)}) collective-permute-start(bf16[480,128]{1,0:T(8,128)(2,1)S(1)} %get-tuple-element.46), channel_id=1, source_target_pairs={{0,8},{1,9},{2,10},{3,11},{4,12},{5,13},{6,14},{7,15},{8,0},{9,1},... | collective-permute-start | bytes 368648 | tf_op jit(solution)/shard_map/ppermute | solution.py:591
  19.7 0.4 %collective-permute-start.11 = (bf16[480,128]{1,0:T(8,128)(2,1)S(1)}, bf16[480,128]{1,0:T(8,128)(2,1)S(1)}, u32[]{:S(2)}, u32[]{:S(2)}) collective-permute-start(bf16[480,128]{1,0:T(8,128)(2,1)S(1)} %get-tuple-element.47), channel_id=1, source_target_pairs={{0,1},{1,0},{2,3},{3,2},{4,5},{5,4},{6,7},{7,6},{8,16},{9,17},{10,... | collective-permute-start | bytes 368648 | tf_op jit(solution)/shard_map/ppermute | solution.py:591
  20.1 2.5 %collective-permute-done.8.c_first = bf16[320,128]{1,0:T(8,128)(2,1)S(1)} collective-permute-done((bf16[320,128]{1,0:T(8,128)(2,1)S(1)}, bf16[320,128]{1,0:T(8,128)(2,1)S(1)}, u32[]{:S(2)}, u32[]{:S(2)}) %collective-permute-start.8) | collective-permute-done | bytes 81952 | tf_op jit(solution)/shard_map/ppermute | solution.py:591
  22.6 0.9 %collective-permute-done.9.c_second = bf16[320,128]{1,0:T(8,128)(2,1)S(1)} collective-permute-done((bf16[320,128]{1,0:T(8,128)(2,1)S(1)}, bf16[320,128]{1,0:T(8,128)(2,1)S(1)}, u32[]{:S(2)}, u32[]{:S(2)}) %collective-permute-start.9) | collective-permute-done | bytes 81952 | tf_op jit(solution)/shard_map/ppermute | solution.py:591
  23.4 0.7 %collective-permute-done.7.y_second = bf16[416,128]{1,0:T(8,128)(2,1)S(1)} collective-permute-done((bf16[416,128]{1,0:T(8,128)(2,1)S(1)}, bf16[416,128]{1,0:T(8,128)(2,1)S(1)}, u32[]{:S(2)}, u32[]{:S(2)}) %collective-permute-start.7) | collective-permute-done | bytes 106528 | tf_op jit(solution)/shard_map/ppermute | solution.py:591
  24.1 0.4 %shard_map.52.own_ref = f32[23,32,128]{2,1,0:T(8,128)S(1)} custom-call(bf16[320,512]{1,0:T(8,128)(2,1)S(1)} %get-tuple-element.40.left_star, bf16[512,896]{1,0:T(8,128)(2,1)S(1)} %get-tuple-element.41.image, bf16[1056,128]{1,0:T(8,128)(2,1)S(1)} %collective-permute-done.6.y_first, bf16[416,128]{1,0:T(8,128)(2,1)S(1)} %collective-permute-done.7.y_second, ...), custom_call_target="tpu_custom_call" | custom-call | flops 3000000000 | bytes 1 | tf_op jit(solution)/shard_map/pallas_call | solution.py:698
  24.5 0.0 collective-permute-done.10.x_first
  24.5 1.0 %collective-permute-done.11.x_second = bf16[480,128]{1,0:T(8,128)(2,1)S(1)} collective-permute-done((bf16[480,128]{1,0:T(8,128)(2,1)S(1)}, bf16[480,128]{1,0:T(8,128)(2,1)S(1)}, u32[]{:S(2)}, u32[]{:S(2)}) %collective-permute-start.11) | collective-permute-done | bytes 122912 | tf_op jit(solution)/shard_map/ppermute | solution.py:591
  25.5 0.9 %shard_map.54 = bf16[7,7,64,64]{3,2,1,0:T(8,128)(2,1)} custom-call(f32[23,32,128]{2,1,0:T(8,128)S(1)} %shard_map.52.own_ref, bf16[480,128]{1,0:T(8,128)(2,1)S(1)} %collective-permute-done.10.x_first, bf16[480,128]{1,0:T(8,128)(2,1)S(1)} %collective-permute-done.11.x_second, bf16[7,7,64,64]{3,2,1,0:T(8,128)(2,1)} %get-tuple-element.48._), custom_call_target="tpu_custom_call", output_to_operand_aliasing={{}: (3, {})} | custom-call | tf_op jit(solution)/shard_map/pallas_call | solution.py:701
  (2 shorter events, 0.0 us)
Async XLA Ops:
  1.4 6.8 %collective-permute-start = (bf16[784,128]{1,0:T(8,128)(2,1)S(1)}, bf16[784,128]{1,0:T(8,128)(2,1)S(1)}, u32[]{:S(2)}, u32[]{:S(2)}) collective-permute-start(bf16[784,128]{1,0:T(8,128)(2,1)S(1)} %get-tuple-element.30), channel_id=1, source_target_pairs={{0,8},{1,9},{2,10},{3,11},{4,12},{5,13},{6,14},{7,15},{8,0},{9,1},... | collective-permute-start | bytes 602120 | tf_op jit(solution)/shard_map/ppermute | solution.py:591
  3.1 6.4 %collective-permute-start.1 = (bf16[784,128]{1,0:T(8,128)(2,1)S(1)}, bf16[784,128]{1,0:T(8,128)(2,1)S(1)}, u32[]{:S(2)}, u32[]{:S(2)}) collective-permute-start(bf16[784,128]{1,0:T(8,128)(2,1)S(1)} %get-tuple-element.31), channel_id=1, source_target_pairs={{0,1},{1,0},{2,3},{3,2},{4,5},{5,4},{6,7},{7,6},{8,16},{9,17},{10,... | collective-permute-start | bytes 602120 | tf_op jit(solution)/shard_map/ppermute | solution.py:591
  3.1 8.9 %collective-permute-start.3 = (bf16[800,128]{1,0:T(8,128)(2,1)S(1)}, bf16[800,128]{1,0:T(8,128)(2,1)S(1)}, u32[]{:S(2)}, u32[]{:S(2)}) collective-permute-start(bf16[800,128]{1,0:T(8,128)(2,1)S(1)} %get-tuple-element.33), channel_id=1, source_target_pairs={{0,8},{1,2},{2,1},{3,4},{4,3},{5,6},{6,5},{7,15},{8,0},{9,10},{10,... | collective-permute-start | bytes 614408 | tf_op jit(solution)/shard_map/ppermute | solution.py:591
  3.8 7.4 %collective-permute-start.2 = (bf16[784,128]{1,0:T(8,128)(2,1)S(1)}, bf16[784,128]{1,0:T(8,128)(2,1)S(1)}, u32[]{:S(2)}, u32[]{:S(2)}) collective-permute-start(bf16[784,128]{1,0:T(8,128)(2,1)S(1)} %get-tuple-element.32), channel_id=1, source_target_pairs={{0,1},{1,0},{2,3},{3,2},{4,5},{5,4},{6,7},{7,6},{8,9},{9,8},{10,11... | collective-permute-start | bytes 602120 | tf_op jit(solution)/shard_map/ppermute | solution.py:591
  9.5 4.0 %collective-permute-start.5 = (bf16[48,128]{1,0:T(8,128)(2,1)S(1)}, bf16[48,128]{1,0:T(8,128)(2,1)S(1)}, u32[]{:S(2)}, u32[]{:S(2)}) collective-permute-start(bf16[48,128]{1,0:T(8,128)(2,1)S(1)} %get-tuple-element.35), channel_id=1, source_target_pairs={{0,8},{1,2},{2,1},{3,4},{4,3},{5,6},{6,5},{7,15},{8,0},{9,10},{10,... | collective-permute-start | bytes 36872 | tf_op jit(solution)/shard_map/ppermute | solution.py:591
  9.5 2.5 %collective-permute-start.4 = (bf16[32,128]{1,0:T(8,128)(2,1)S(1)}, bf16[32,128]{1,0:T(8,128)(2,1)S(1)}, u32[]{:S(2)}, u32[]{:S(2)}) collective-permute-start(bf16[32,128]{1,0:T(8,128)(2,1)S(1)} %get-tuple-element.34), channel_id=1, source_target_pairs={{0,1},{1,0},{2,3},{3,2},{4,5},{5,4},{6,7},{7,6},{8,9},{9,8},{10,11... | collective-permute-start | bytes 24584 | tf_op jit(solution)/shard_map/ppermute | solution.py:591
  15.0 2.5 %collective-permute-start.6 = (bf16[1056,128]{1,0:T(8,128)(2,1)S(1)}, bf16[1056,128]{1,0:T(8,128)(2,1)S(1)}, u32[]{:S(2)}, u32[]{:S(2)}) collective-permute-start(bf16[1056,128]{1,0:T(8,128)(2,1)S(1)} %get-tuple-element.42), channel_id=1, source_target_pairs={{0,1},{1,0},{2,3},{3,2},{4,5},{5,4},{6,7},{7,6},{8,9},{9,8},{10,11... | collective-permute-start | bytes 811016 | tf_op jit(solution)/shard_map/ppermute | solution.py:591
  15.0 9.1 %collective-permute-start.7 = (bf16[416,128]{1,0:T(8,128)(2,1)S(1)}, bf16[416,128]{1,0:T(8,128)(2,1)S(1)}, u32[]{:S(2)}, u32[]{:S(2)}) collective-permute-start(bf16[416,128]{1,0:T(8,128)(2,1)S(1)} %get-tuple-element.43), channel_id=1, source_target_pairs={{0,8},{1,2},{2,1},{3,4},{4,3},{5,6},{6,5},{7,15},{8,0},{9,10},{10,... | collective-permute-start | bytes 319496 | tf_op jit(solution)/shard_map/ppermute | solution.py:591
  15.7 6.9 %collective-permute-start.8 = (bf16[320,128]{1,0:T(8,128)(2,1)S(1)}, bf16[320,128]{1,0:T(8,128)(2,1)S(1)}, u32[]{:S(2)}, u32[]{:S(2)}) collective-permute-start(bf16[320,128]{1,0:T(8,128)(2,1)S(1)} %get-tuple-element.44), channel_id=1, source_target_pairs={{0,8},{1,10},{2,9},{3,12},{4,11},{5,14},{6,13},{7,15},{8,0},{9,2},... | collective-permute-start | bytes 245768 | tf_op jit(solution)/shard_map/ppermute | solution.py:591
  17.5 5.9 %collective-permute-start.9 = (bf16[320,128]{1,0:T(8,128)(2,1)S(1)}, bf16[320,128]{1,0:T(8,128)(2,1)S(1)}, u32[]{:S(2)}, u32[]{:S(2)}) collective-permute-start(bf16[320,128]{1,0:T(8,128)(2,1)S(1)} %get-tuple-element.45), channel_id=1, source_target_pairs={{0,1},{1,0},{2,3},{3,2},{4,5},{5,4},{6,7},{7,6},{8,16},{9,18},{10,... | collective-permute-start | bytes 245768 | tf_op jit(solution)/shard_map/ppermute | solution.py:591
  17.9 6.6 %collective-permute-start.10 = (bf16[480,128]{1,0:T(8,128)(2,1)S(1)}, bf16[480,128]{1,0:T(8,128)(2,1)S(1)}, u32[]{:S(2)}, u32[]{:S(2)}) collective-permute-start(bf16[480,128]{1,0:T(8,128)(2,1)S(1)} %get-tuple-element.46), channel_id=1, source_target_pairs={{0,8},{1,9},{2,10},{3,11},{4,12},{5,13},{6,14},{7,15},{8,0},{9,1},... | collective-permute-start | bytes 368648 | tf_op jit(solution)/shard_map/ppermute | solution.py:591
  19.7 5.8 %collective-permute-start.11 = (bf16[480,128]{1,0:T(8,128)(2,1)S(1)}, bf16[480,128]{1,0:T(8,128)(2,1)S(1)}, u32[]{:S(2)}, u32[]{:S(2)}) collective-permute-start(bf16[480,128]{1,0:T(8,128)(2,1)S(1)} %get-tuple-element.47), channel_id=1, source_target_pairs={{0,1},{1,0},{2,3},{3,2},{4,5},{5,4},{6,7},{7,6},{8,16},{9,17},{10,... | collective-permute-start | bytes 368648 | tf_op jit(solution)/shard_map/ppermute | solution.py:591

commit v13 on v12

--- a/solution.py
+++ b/solution.py
@@ -92,6 +92,8 @@
 
 
 def swap_halves(value):
+    if value.dtype == jnp.bfloat16:
+        return jnp.concatenate([value[..., B:], value[..., :B]], axis=-1)
     return pltpu.roll(value, B, value.ndim - 1)
 
 
@@ -448,12 +450,12 @@
             lanes = slice(start * PAIR, (start + len(group)) * PAIR)
             product = jnp.dot(a_ref[index, :, span], right[index, span, lanes], preferred_element_type=jnp.float32)
             for place, s in enumerate(group):
-                products[s] = product[:, place * PAIR : (place + 1) * PAIR]
+                products[s] = product[:, place * PAIR : (place + 1) * PAIR].astype(jnp.bfloat16)
             start += len(group)
 
         def part(s, z):
             if s not in products:
-                return jnp.zeros((B, PAIR), jnp.float32)
+                return jnp.zeros((B, PAIR), jnp.bfloat16)
             return products[s][z * B : (z + 1) * B]
 
         for pair in range(IMAGE_PAIRS):
@@ -463,8 +465,8 @@
             high = jnp.where(half, swap_halves(part(one, 1)), part(two, 1))
             start = index * PAIR
             lanes = slice(pair * PAIR, (pair + 1) * PAIR)
-            image[start : start + B, lanes] = low.astype(jnp.bfloat16)
-            image[start + B : start + PAIR, lanes] = high.astype(jnp.bfloat16)
+            image[start : start + B, lanes] = low
+            image[start + B : start + PAIR, lanes] = high
     star = jnp.dot(left_star[0 : 2 * B, :], image[...], preferred_element_type=jnp.float32)
 
     def contribution(t):

time: 26.5 us -> 26.5 us (level)
  no operation moved by 1% of the time
where the time goes in v13:
time: 26.5 us; the launch traced here: 26.3 us
  starting transfers between devices  9.62 us (36%)
  waiting for transfers between devices  9.44 us (36%)
  Pallas kernels  7.21 us (27%)
    ppermute x12, starting transfers between devices, swapped(): return lax.ppermute(value, ('sx', 'sy'), pairs)  9.62 us
    ppermute x12, waiting for transfers between devices, swapped(): return lax.ppermute(value, ('sx', 'sy'), pairs)  9.44 us
    pallas_call x1, Pallas kernels, per_device(): call(pack_matrix_kernel, [HBM, HBM], [((4, PAIR, 6 * B), bf16), whole], [...  1.79 us
    pallas_call x1, Pallas kernels, per_device(): call(functools.partial(pack_kernel, lax.axis_size('sy')), [HBM, HBM, HBM]...  1.43 us
    pallas_call x1, Pallas kernels, per_device(): call(main_kernel, [VMEM] * 13, [sent(TO_Y_FIRST), sent(TO_Y_SECOND), sent...  1.4 us
    pallas_call x1, Pallas kernels, per_device(): call(begin_kernel, [VMEM] * 5, lefts + [((len(BEGUN), 3, B, PAIR), f32)],...  0.91 us
    pallas_call x1, Pallas kernels, per_device(): call(finish_kernel, [VMEM] * 3 + [HBM], [whole], [pltpu.VMEM((7, 7, B, B)...  0.89 us
  transfers between devices with their start and end apart: 12, of which 7 were waited for; matrix products, arithmetic and copies ran while one was open for 0% of the time, Pallas kernels for 13%

profile of v13, /device:TPU:20, one launch (start us, length us, event | category | flops | bytes accessed | tf_op | source)
XLA Modules:
  0.0 26.3 jit_solution(9993190439161756355)
XLA Ops:
  0.0 1.4 %shard_map.47 = (bf16[4,384,128]{2,1,0:T(8,128)(2,1)S(1)}, f32[32,128]{1,0:T(8,128)S(1)}, bf16[784,128]{1,0:T(8,128)(2,1)S(1)}, bf16[784,128]{1,0:T(8,128)(2,1)S(1)}) custom-call(s32[2,2,2]{2,1,0:T(2,128)} %aggregate_hbm.1, s32[2,2,2,6]{3,2,1,0:T(2,128)} %links_hbm.3, bf16[2,2,2,7,64,64]{5,4,3,2,1,0:T(8,128)(2,1)} %p_hbm.1), custom_call_target="tpu_custom_call" | custom-call | tf_op jit(solution)/shard_map/pallas_call | solution.py:623
  1.4 1.6 %collective-permute-start = (bf16[784,128]{1,0:T(8,128)(2,1)S(1)}, bf16[784,128]{1,0:T(8,128)(2,1)S(1)}, u32[]{:S(2)}, u32[]{:S(2)}) collective-permute-start(bf16[784,128]{1,0:T(8,128)(2,1)S(1)} %get-tuple-element.30), channel_id=1, source_target_pairs={{0,8},{1,9},{2,10},{3,11},{4,12},{5,13},{6,14},{7,15},{8,0},{9,1},... | collective-permute-start | bytes 602120 | tf_op jit(solution)/shard_map/ppermute | solution.py:593
  3.1 0.0 collective-permute-start.1
  3.1 0.7 %collective-permute-start.3 = (bf16[800,128]{1,0:T(8,128)(2,1)S(1)}, bf16[800,128]{1,0:T(8,128)(2,1)S(1)}, u32[]{:S(2)}, u32[]{:S(2)}) collective-permute-start(bf16[800,128]{1,0:T(8,128)(2,1)S(1)} %get-tuple-element.33), channel_id=1, source_target_pairs={{0,8},{1,2},{2,1},{3,4},{4,3},{5,6},{6,5},{7,15},{8,0},{9,10},{10,... | collective-permute-start | bytes 614408 | tf_op jit(solution)/shard_map/ppermute | solution.py:593
  3.8 1.0 %collective-permute-start.2 = (bf16[784,128]{1,0:T(8,128)(2,1)S(1)}, bf16[784,128]{1,0:T(8,128)(2,1)S(1)}, u32[]{:S(2)}, u32[]{:S(2)}) collective-permute-start(bf16[784,128]{1,0:T(8,128)(2,1)S(1)} %get-tuple-element.32), channel_id=1, source_target_pairs={{0,1},{1,0},{2,3},{3,2},{4,5},{5,4},{6,7},{7,6},{8,9},{9,8},{10,11... | collective-permute-start | bytes 602120 | tf_op jit(solution)/shard_map/ppermute | solution.py:593
  4.8 1.8 %shard_map.46 = (bf16[4,128,384]{2,1,0:T(8,128)(2,1)S(1)}, bf16[7,7,64,64]{3,2,1,0:T(8,128)(2,1)}) custom-call(s32[2,2,2,6]{3,2,1,0:T(2,128)} %links_hbm.3, bf16[2,2,2,7,64,64]{5,4,3,2,1,0:T(8,128)(2,1)} %a_hbm.1), custom_call_target="tpu_custom_call" | custom-call | tf_op jit(solution)/shard_map/pallas_call | solution.py:640
  6.6 1.7 %collective-permute-done.x_first = bf16[784,128]{1,0:T(8,128)(2,1)S(1)} collective-permute-done((bf16[784,128]{1,0:T(8,128)(2,1)S(1)}, bf16[784,128]{1,0:T(8,128)(2,1)S(1)}, u32[]{:S(2)}, u32[]{:S(2)}) %collective-permute-start) | collective-permute-done | bytes 200736 | tf_op jit(solution)/shard_map/ppermute | solution.py:593
  8.2 1.3 %collective-permute-done.1.x_second = bf16[784,128]{1,0:T(8,128)(2,1)S(1)} collective-permute-done((bf16[784,128]{1,0:T(8,128)(2,1)S(1)}, bf16[784,128]{1,0:T(8,128)(2,1)S(1)}, u32[]{:S(2)}, u32[]{:S(2)}) %collective-permute-start.1) | collective-permute-done | bytes 200736 | tf_op jit(solution)/shard_map/ppermute | solution.py:593
  9.5 0.0 collective-permute-start.5
  9.5 1.6 %collective-permute-start.4 = (bf16[32,128]{1,0:T(8,128)(2,1)S(1)}, bf16[32,128]{1,0:T(8,128)(2,1)S(1)}, u32[]{:S(2)}, u32[]{:S(2)}) collective-permute-start(bf16[32,128]{1,0:T(8,128)(2,1)S(1)} %get-tuple-element.34), channel_id=1, source_target_pairs={{0,1},{1,0},{2,3},{3,2},{4,5},{5,4},{6,7},{7,6},{8,9},{9,8},{10,11... | collective-permute-start | bytes 24584 | tf_op jit(solution)/shard_map/ppermute | solution.py:593
  11.1 0.0 collective-permute-done.2.y_first
  11.1 0.9 %shard_map.50 = (bf16[4,384,1280]{2,1,0:T(8,128)(2,1)S(1)}, bf16[320,512]{1,0:T(8,128)(2,1)S(1)}, bf16[4,64,128]{2,1,0:T(8,128)(2,1)S(1)}, f32[8,3,64,128]{3,2,1,0:T(8,128)S(1)}) custom-call(bf16[4,384,128]{2,1,0:T(8,128)(2,1)S(1)} %get-tuple-element.28.rows_ref, f32[32,128]{1,0:T(8,128)S(1)} %get-tuple-element.29.meta_ref, ...), custom_call_target="tpu_custom_call" | custom-call | flops 1 | bytes 1 | tf_op jit(solution)/shard_map/pallas_call | solution.py:667
  12.1 0.0 collective-permute-done.3.y_second
  12.1 0.0 collective-permute-done.4.c_first
  12.1 1.5 %collective-permute-done.5.c_second = bf16[48,128]{1,0:T(8,128)(2,1)S(1)} collective-permute-done((bf16[48,128]{1,0:T(8,128)(2,1)S(1)}, bf16[48,128]{1,0:T(8,128)(2,1)S(1)}, u32[]{:S(2)}, u32[]{:S(2)}) %collective-permute-start.5) | collective-permute-done | bytes 12320 | tf_op jit(solution)/shard_map/ppermute | solution.py:593
  13.6 1.4 %shard_map.51 = (bf16[1056,128]{1,0:T(8,128)(2,1)S(1)}, bf16[416,128]{1,0:T(8,128)(2,1)S(1)}, bf16[320,128]{1,0:T(8,128)(2,1)S(1)}, bf16[320,128]{1,0:T(8,128)(2...) custom-call(bf16[4,128,384]{2,1,0:T(8,128)(2,1)S(1)} %get-tuple-elem, ...), custom_call_target="tpu_custom_call", output_to_operand_aliasing={{4}: (10, {}), {5}: (11, {}), {6}: (12, {})} | custom-call | tf_op jit(solution)/shard_map/pallas_call | solution.py:670
  15.0 0.1 collective-permute-start.6
  15.0 0.6 %collective-permute-start.7 = (bf16[416,128]{1,0:T(8,128)(2,1)S(1)}, bf16[416,128]{1,0:T(8,128)(2,1)S(1)}, u32[]{:S(2)}, u32[]{:S(2)}) collective-permute-start(bf16[416,128]{1,0:T(8,128)(2,1)S(1)} %get-tuple-element.43), channel_id=1, source_target_pairs={{0,8},{1,2},{2,1},{3,4},{4,3},{5,6},{6,5},{7,15},{8,0},{9,10},{10,... | collective-permute-start | bytes 319496 | tf_op jit(solution)/shard_map/ppermute | solution.py:593
  15.7 1.8 %collective-permute-start.8 = (bf16[320,128]{1,0:T(8,128)(2,1)S(1)}, bf16[320,128]{1,0:T(8,128)(2,1)S(1)}, u32[]{:S(2)}, u32[]{:S(2)}) collective-permute-start(bf16[320,128]{1,0:T(8,128)(2,1)S(1)} %get-tuple-element.44), channel_id=1, source_target_pairs={{0,8},{1,10},{2,9},{3,12},{4,11},{5,14},{6,13},{7,15},{8,0},{9,2},... | collective-permute-start | bytes 245768 | tf_op jit(solution)/shard_map/ppermute | solution.py:593
  17.5 0.0 collective-permute-start.9
  17.5 0.0 collective-permute-done.6.y_first
  17.5 0.4 %shard_map.53 = (bf16[480,128]{1,0:T(8,128)(2,1)S(1)}, bf16[480,128]{1,0:T(8,128)(2,1)S(1)}) custom-call(bf16[320,512]{1,0:T(8,128)(2,1)S(1)} %get-tuple-element.40.left_star, bf16[512,896]{1,0:T(8,128)(2,1)S(1)} %get-tuple-element.41.image, bf16[1056,128]{1,0:T(8,128)(2,1)S(1)} %collective-permute-done.6.y_first), custom_call_target="tpu_custom_call" | custom-call | tf_op jit(solution)/shard_map/pallas_call | solution.py:698
  17.9 1.8 %collective-permute-start.10 = (bf16[480,128]{1,0:T(8,128)(2,1)S(1)}, bf16[480,128]{1,0:T(8,128)(2,1)S(1)}, u32[]{:S(2)}, u32[]{:S(2)}) collective-permute-start(bf16[480,128]{1,0:T(8,128)(2,1)S(1)} %get-tuple-element.46), channel_id=1, source_target_pairs={{0,8},{1,9},{2,10},{3,11},{4,12},{5,13},{6,14},{7,15},{8,0},{9,1},... | collective-permute-start | bytes 368648 | tf_op jit(solution)/shard_map/ppermute | solution.py:593
  19.7 0.4 %collective-permute-start.11 = (bf16[480,128]{1,0:T(8,128)(2,1)S(1)}, bf16[480,128]{1,0:T(8,128)(2,1)S(1)}, u32[]{:S(2)}, u32[]{:S(2)}) collective-permute-start(bf16[480,128]{1,0:T(8,128)(2,1)S(1)} %get-tuple-element.47), channel_id=1, source_target_pairs={{0,1},{1,0},{2,3},{3,2},{4,5},{5,4},{6,7},{7,6},{8,16},{9,17},{10,... | collective-permute-start | bytes 368648 | tf_op jit(solution)/shard_map/ppermute | solution.py:593
  20.1 2.5 %collective-permute-done.8.c_first = bf16[320,128]{1,0:T(8,128)(2,1)S(1)} collective-permute-done((bf16[320,128]{1,0:T(8,128)(2,1)S(1)}, bf16[320,128]{1,0:T(8,128)(2,1)S(1)}, u32[]{:S(2)}, u32[]{:S(2)}) %collective-permute-start.8) | collective-permute-done | bytes 81952 | tf_op jit(solution)/shard_map/ppermute | solution.py:593
  22.6 0.9 %collective-permute-done.9.c_second = bf16[320,128]{1,0:T(8,128)(2,1)S(1)} collective-permute-done((bf16[320,128]{1,0:T(8,128)(2,1)S(1)}, bf16[320,128]{1,0:T(8,128)(2,1)S(1)}, u32[]{:S(2)}, u32[]{:S(2)}) %collective-permute-start.9) | collective-permute-done | bytes 81952 | tf_op jit(solution)/shard_map/ppermute | solution.py:593
  23.4 0.7 %collective-permute-done.7.y_second = bf16[416,128]{1,0:T(8,128)(2,1)S(1)} collective-permute-done((bf16[416,128]{1,0:T(8,128)(2,1)S(1)}, bf16[416,128]{1,0:T(8,128)(2,1)S(1)}, u32[]{:S(2)}, u32[]{:S(2)}) %collective-permute-start.7) | collective-permute-done | bytes 106528 | tf_op jit(solution)/shard_map/ppermute | solution.py:593
  24.1 0.4 %shard_map.52.own_ref = f32[23,32,128]{2,1,0:T(8,128)S(1)} custom-call(bf16[320,512]{1,0:T(8,128)(2,1)S(1)} %get-tuple-element.40.left_star, bf16[512,896]{1,0:T(8,128)(2,1)S(1)} %get-tuple-element.41.image, bf16[1056,128]{1,0:T(8,128)(2,1)S(1)} %collective-permute-done.6.y_first, bf16[416,128]{1,0:T(8,128)(2,1)S(1)} %collective-permute-done.7.y_second, ...), custom_call_target="tpu_custom_call" | custom-call | flops 3000000000 | bytes 1 | tf_op jit(solution)/shard_map/pallas_call | solution.py:700
  24.5 0.0 collective-permute-done.10.x_first
  24.5 1.0 %collective-permute-done.11.x_second = bf16[480,128]{1,0:T(8,128)(2,1)S(1)} collective-permute-done((bf16[480,128]{1,0:T(8,128)(2,1)S(1)}, bf16[480,128]{1,0:T(8,128)(2,1)S(1)}, u32[]{:S(2)}, u32[]{:S(2)}) %collective-permute-start.11) | collective-permute-done | bytes 122912 | tf_op jit(solution)/shard_map/ppermute | solution.py:593
  25.5 0.9 %shard_map.54 = bf16[7,7,64,64]{3,2,1,0:T(8,128)(2,1)} custom-call(f32[23,32,128]{2,1,0:T(8,128)S(1)} %shard_map.52.own_ref, bf16[480,128]{1,0:T(8,128)(2,1)S(1)} %collective-permute-done.10.x_first, bf16[480,128]{1,0:T(8,128)(2,1)S(1)} %collective-permute-done.11.x_second, bf16[7,7,64,64]{3,2,1,0:T(8,128)(2,1)} %get-tuple-element.48._), custom_call_target="tpu_custom_call", output_to_operand_aliasing={{}: (3, {})} | custom-call | tf_op jit(solution)/shard_map/pallas_call | solution.py:703
  (2 shorter events, 0.0 us)
Async XLA Ops:
  1.4 6.8 %collective-permute-start = (bf16[784,128]{1,0:T(8,128)(2,1)S(1)}, bf16[784,128]{1,0:T(8,128)(2,1)S(1)}, u32[]{:S(2)}, u32[]{:S(2)}) collective-permute-start(bf16[784,128]{1,0:T(8,128)(2,1)S(1)} %get-tuple-element.30), channel_id=1, source_target_pairs={{0,8},{1,9},{2,10},{3,11},{4,12},{5,13},{6,14},{7,15},{8,0},{9,1},... | collective-permute-start | bytes 602120 | tf_op jit(solution)/shard_map/ppermute | solution.py:593
  3.1 6.4 %collective-permute-start.1 = (bf16[784,128]{1,0:T(8,128)(2,1)S(1)}, bf16[784,128]{1,0:T(8,128)(2,1)S(1)}, u32[]{:S(2)}, u32[]{:S(2)}) collective-permute-start(bf16[784,128]{1,0:T(8,128)(2,1)S(1)} %get-tuple-element.31), channel_id=1, source_target_pairs={{0,1},{1,0},{2,3},{3,2},{4,5},{5,4},{6,7},{7,6},{8,16},{9,17},{10,... | collective-permute-start | bytes 602120 | tf_op jit(solution)/shard_map/ppermute | solution.py:593
  3.1 8.9 %collective-permute-start.3 = (bf16[800,128]{1,0:T(8,128)(2,1)S(1)}, bf16[800,128]{1,0:T(8,128)(2,1)S(1)}, u32[]{:S(2)}, u32[]{:S(2)}) collective-permute-start(bf16[800,128]{1,0:T(8,128)(2,1)S(1)} %get-tuple-element.33), channel_id=1, source_target_pairs={{0,8},{1,2},{2,1},{3,4},{4,3},{5,6},{6,5},{7,15},{8,0},{9,10},{10,... | collective-permute-start | bytes 614408 | tf_op jit(solution)/shard_map/ppermute | solution.py:593
  3.8 7.4 %collective-permute-start.2 = (bf16[784,128]{1,0:T(8,128)(2,1)S(1)}, bf16[784,128]{1,0:T(8,128)(2,1)S(1)}, u32[]{:S(2)}, u32[]{:S(2)}) collective-permute-start(bf16[784,128]{1,0:T(8,128)(2,1)S(1)} %get-tuple-element.32), channel_id=1, source_target_pairs={{0,1},{1,0},{2,3},{3,2},{4,5},{5,4},{6,7},{7,6},{8,9},{9,8},{10,11... | collective-permute-start | bytes 602120 | tf_op jit(solution)/shard_map/ppermute | solution.py:593
  9.5 4.0 %collective-permute-start.5 = (bf16[48,128]{1,0:T(8,128)(2,1)S(1)}, bf16[48,128]{1,0:T(8,128)(2,1)S(1)}, u32[]{:S(2)}, u32[]{:S(2)}) collective-permute-start(bf16[48,128]{1,0:T(8,128)(2,1)S(1)} %get-tuple-element.35), channel_id=1, source_target_pairs={{0,8},{1,2},{2,1},{3,4},{4,3},{5,6},{6,5},{7,15},{8,0},{9,10},{10,... | collective-permute-start | bytes 36872 | tf_op jit(solution)/shard_map/ppermute | solution.py:593
  9.5 2.5 %collective-permute-start.4 = (bf16[32,128]{1,0:T(8,128)(2,1)S(1)}, bf16[32,128]{1,0:T(8,128)(2,1)S(1)}, u32[]{:S(2)}, u32[]{:S(2)}) collective-permute-start(bf16[32,128]{1,0:T(8,128)(2,1)S(1)} %get-tuple-element.34), channel_id=1, source_target_pairs={{0,1},{1,0},{2,3},{3,2},{4,5},{5,4},{6,7},{7,6},{8,9},{9,8},{10,11... | collective-permute-start | bytes 24584 | tf_op jit(solution)/shard_map/ppermute | solution.py:593
  15.0 2.6 %collective-permute-start.6 = (bf16[1056,128]{1,0:T(8,128)(2,1)S(1)}, bf16[1056,128]{1,0:T(8,128)(2,1)S(1)}, u32[]{:S(2)}, u32[]{:S(2)}) collective-permute-start(bf16[1056,128]{1,0:T(8,128)(2,1)S(1)} %get-tuple-element.42), channel_id=1, source_target_pairs={{0,1},{1,0},{2,3},{3,2},{4,5},{5,4},{6,7},{7,6},{8,9},{9,8},{10,11... | collective-permute-start | bytes 811016 | tf_op jit(solution)/shard_map/ppermute | solution.py:593
  15.0 9.1 %collective-permute-start.7 = (bf16[416,128]{1,0:T(8,128)(2,1)S(1)}, bf16[416,128]{1,0:T(8,128)(2,1)S(1)}, u32[]{:S(2)}, u32[]{:S(2)}) collective-permute-start(bf16[416,128]{1,0:T(8,128)(2,1)S(1)} %get-tuple-element.43), channel_id=1, source_target_pairs={{0,8},{1,2},{2,1},{3,4},{4,3},{5,6},{6,5},{7,15},{8,0},{9,10},{10,... | collective-permute-start | bytes 319496 | tf_op jit(solution)/shard_map/ppermute | solution.py:593
  15.7 6.9 %collective-permute-start.8 = (bf16[320,128]{1,0:T(8,128)(2,1)S(1)}, bf16[320,128]{1,0:T(8,128)(2,1)S(1)}, u32[]{:S(2)}, u32[]{:S(2)}) collective-permute-start(bf16[320,128]{1,0:T(8,128)(2,1)S(1)} %get-tuple-element.44), channel_id=1, source_target_pairs={{0,8},{1,10},{2,9},{3,12},{4,11},{5,14},{6,13},{7,15},{8,0},{9,2},... | collective-permute-start | bytes 245768 | tf_op jit(solution)/shard_map/ppermute | solution.py:593
  17.5 5.9 %collective-permute-start.9 = (bf16[320,128]{1,0:T(8,128)(2,1)S(1)}, bf16[320,128]{1,0:T(8,128)(2,1)S(1)}, u32[]{:S(2)}, u32[]{:S(2)}) collective-permute-start(bf16[320,128]{1,0:T(8,128)(2,1)S(1)} %get-tuple-element.45), channel_id=1, source_target_pairs={{0,1},{1,0},{2,3},{3,2},{4,5},{5,4},{6,7},{7,6},{8,16},{9,18},{10,... | collective-permute-start | bytes 245768 | tf_op jit(solution)/shard_map/ppermute | solution.py:593
  17.9 6.6 %collective-permute-start.10 = (bf16[480,128]{1,0:T(8,128)(2,1)S(1)}, bf16[480,128]{1,0:T(8,128)(2,1)S(1)}, u32[]{:S(2)}, u32[]{:S(2)}) collective-permute-start(bf16[480,128]{1,0:T(8,128)(2,1)S(1)} %get-tuple-element.46), channel_id=1, source_target_pairs={{0,8},{1,9},{2,10},{3,11},{4,12},{5,13},{6,14},{7,15},{8,0},{9,1},... | collective-permute-start | bytes 368648 | tf_op jit(solution)/shard_map/ppermute | solution.py:593
  19.7 5.8 %collective-permute-start.11 = (bf16[480,128]{1,0:T(8,128)(2,1)S(1)}, bf16[480,128]{1,0:T(8,128)(2,1)S(1)}, u32[]{:S(2)}, u32[]{:S(2)}) collective-permute-start(bf16[480,128]{1,0:T(8,128)(2,1)S(1)} %get-tuple-element.47), channel_id=1, source_target_pairs={{0,1},{1,0},{2,3},{3,2},{4,5},{5,4},{6,7},{7,6},{8,16},{9,17},{10,... | collective-permute-start | bytes 368648 | tf_op jit(solution)/shard_map/ppermute | solution.py:593
